TPU v7x, 128 devices: a whole 4x4x4 slice. The times are simulated.
128 devices in a mesh: aux: 16 (over z, x_lo, core), pair: 8 (over x_hi, y).
Axes of the slice: x: 4 (x_hi: 2, x_lo: 2; x = x_hi * 2 + x_lo), y: 4, z: 4, core: 2. Of those that a mesh axis runs over, the one named last changes fastest.
Arguments:
- coeffs: bfloat16 [12288, 49152], P('aux', 'pair'), may hold values from -0.0390625 to 0.0390625
- occ_index: int32 [49152], P('pair'), may hold values from 0 to 4095
- virt_index: int32 [49152], P('pair'), may hold values from 0 to 32767
- occ_energy: float32 [4096], replicated, may hold values from -1.5 to -0.25
- virt_energy: float32 [32768], replicated, may hold values from 0.02 to 3
Outputs:
- band: float32 [7, 12288, 768], P(None, ('aux', 'pair'))
All inputs are finite; a program needn't handle non-finite values.
Results may differ from a plain program's by a relative error of at most 0.0011.
Values may be sent and summed in bfloat16 or wider, within the bound.
No kernel may reach another device: no remote copies, remote signals or barrier semaphores. Data moves between devices by JAX's collectives and lax.ppermute only.
A program may use at most 128 MiB of HBM per device.

v0:
```python
import jax
import jax.numpy as jnp
from jax import lax
from jax.sharding import PartitionSpec as P

STEPS = 4


freq_point = 0.5


def shifted(value, axis, by):
    peers = lax.axis_size(axis)
    return lax.ppermute(value, axis, [(i, (i + by) % peers) for i in range(peers)])


def pair_weights(occ_index, virt_index, occ_energy, virt_energy):
    gap = virt_energy[virt_index] - occ_energy[occ_index]
    return 4.0 * gap / (gap * gap + freq_point * freq_point)


def tile_term(left, right):
    return -lax.dot_general(
        left, right, (((1,), (1,)), ((), ())), preferred_element_type=jnp.float32
    )


def tile_sum(left, right):
    return lax.psum_scatter(tile_term(left, right), "pair", scatter_dimension=0, tiled=True)


def local(coeffs, occ_index, virt_index, occ_energy, virt_energy):
    weight = pair_weights(occ_index, virt_index, occ_energy, virt_energy)
    scaled = (coeffs.astype(jnp.float32) * weight[None, :]).astype(jnp.bfloat16)
    panel_list = [coeffs]
    for offset in range(1, STEPS):
        panel_list.append(shifted(panel_list[-1], "aux", 1))
    crossed_list = []
    products = [(scaled, panel) for panel in panel_list]
    lower = [tile_sum(left, right) for left, right in products]
    for offset in range(1, STEPS):
        crossed = lax.all_to_all(lower[offset], "pair", split_axis=1, concat_axis=0, tiled=True)
        crossed_list.append(crossed.T)
    upper = []
    for offset in range(1, STEPS):
        upper.append(shifted(crossed_list[offset - 1], "aux", -offset))
    return jnp.stack(lower[::-1] + upper)


def solution(mesh):
    return jax.shard_map(
        local,
        mesh=mesh,
        in_specs=(P("aux", "pair"), P("pair"), P("pair"), P(), P()),
        out_specs=P(None, ("aux", "pair"), None),
        check_vma=False,
    )
```

profile of v0, /device:TPU:3, one launch (start us, length us, event | category | flops | bytes accessed | tf_op | source)
XLA Modules:
  0.0 577.4 jit_solution(155076488983013447)
XLA Ops:
  6.5 2.2 collective-permute-start
  8.7 101.9 %collective-permute-done = bf16[768,6144]{1,0:T(8,128)(2,1)} collective-permute-done((bf16[768,6144]{1,0:T(8,128)(2,1)}, bf16[768,6144]{1,0:T(8,128)(2,1)}, u32[]{:S(2)}, u32[]{:S(2)}) %collective-permute-start) | collective-permute-done | bytes 9437216 | tf_op jit(solution)/shard_map/ppermute | solution.py:14
  110.7 3.4 collective-permute-start.1
  114.0 0.8 fusion.12
  114.8 34.3 %gather_fusion = f32[6144]{0:T(1024)S(1)} fusion(f32[32768]{0:T(1024)S(1)} %copy-done, s32[6144]{0:T(1024)S(1)} %get-tuple-element.5), kind=kCustom, calls=%fused_computation | custom fusion | bytes 73728 | tf_op jit(solution)/shard_map/gather | solution.py:18
  149.1 34.3 %gather_fusion.1 = f32[6144]{0:T(1024)S(1)} fusion(f32[4096]{0:T(1024)S(1)} %copy-done.1, s32[6144]{0:T(1024)S(1)} %get-tuple-element.6), kind=kCustom, calls=%fused_computation.1 | custom fusion | bytes 73728 | tf_op jit(solution)/shard_map/gather | solution.py:18
  183.4 32.5 %collective-permute-done.1 = bf16[768,6144]{1,0:T(8,128)(2,1)} collective-permute-done((bf16[768,6144]{1,0:T(8,128)(2,1)}, bf16[768,6144]{1,0:T(8,128)(2,1)}, u32[]{:S(2)}, u32[]{:S(2)}) %collective-permute-start.1) | collective-permute-done | bytes 9437216 | tf_op jit(solution)/shard_map/ppermute | solution.py:14
  216.0 3.4 collective-permute-start.2
  219.4 13.9 %fusion.10 = f32[768,768]{1,0:T(8,128)} fusion(bf16[768,6144]{1,0:T(8,128)(2,1)} %collective-permute-done, bf16[768,6144]{1,0:T(8,128)(2,1)} %param.5, f32[6144]{0:T(1024)S(1)} %add_divide_fusion), kind=kOutput, calls=%fused_computation.13 | convolution fusion | flops 7262502912 | bytes 21258240 | tf_op jit(solution)/shard_map/dot_general | solution.py:23
  233.3 13.9 %fusion.9 = f32[768,768]{1,0:T(8,128)} fusion(bf16[768,6144]{1,0:T(8,128)(2,1)} %collective-permute-done.1, bf16[768,6144]{1,0:T(8,128)(2,1)} %param.5, f32[6144]{0:T(1024)S(1)} %add_divide_fusion), kind=kOutput, calls=%fused_computation.12 | convolution fusion | flops 7262502912 | bytes 21258240 | tf_op jit(solution)/shard_map/dot_general | solution.py:23
  247.5 92.8 %collective-permute-done.2 = bf16[768,6144]{1,0:T(8,128)(2,1)} collective-permute-done((bf16[768,6144]{1,0:T(8,128)(2,1)}, bf16[768,6144]{1,0:T(8,128)(2,1)}, u32[]{:S(2)}, u32[]{:S(2)}) %collective-permute-start.2) | collective-permute-done | bytes 9437216 | tf_op jit(solution)/shard_map/ppermute | solution.py:14
  340.3 14.2 %fusion.8 = f32[768,768]{1,0:T(8,128)} fusion(bf16[768,6144]{1,0:T(8,128)(2,1)} %collective-permute-done.2, bf16[768,6144]{1,0:T(8,128)(2,1)} %param.5, f32[6144]{0:T(1024)S(1)} %add_divide_fusion), kind=kOutput, calls=%fused_computation.11 | convolution fusion | flops 7262502912 | bytes 21258240 | tf_op jit(solution)/shard_map/dot_general | solution.py:23
  354.5 15.2 %fusion.11 = f32[768,768]{1,0:T(8,128)} fusion(bf16[768,6144]{1,0:T(8,128)(2,1)} %param.5, f32[6144]{0:T(1024)S(1)} %add_divide_fusion), kind=kOutput, calls=%fused_computation.14 | convolution fusion | flops 7262502912 | bytes 11821056 | tf_op jit(solution)/shard_map/dot_general | solution.py:23
  369.8 1.9 copy.18
  371.7 6.2 %all-to-all-start = ((f32[96,8,96]{0,2,1:T(8,128)}), f32[96,8,96]{0,2,1:T(8,128)S(1)}, u32[]{:S(2)}, u32[]{:S(2)}) async-start(f32[96,8,96]{0,2,1:T(8,128)} %bitcast.4), calls=%async_computation.4 | async-start | bytes 786432 | tf_op jit(solution)/shard_map/all_to_all | solution.py:42
  377.9 19.0 %reduce-scatter.7.cloned.1.call-done = f32[96,768]{1,0:T(8,128)} async-done(((f32[768,768]{1,0:T(8,128)}), f32[96,768]{1,0:T(8,128)}) %reduce-scatter.7.cloned.1.call-update) | async-done | bytes 294928 | tf_op jit(solution)/shard_map/reduce_scatter | solution.py:29
  396.8 1.9 copy.19
  398.7 3.5 all-to-all-start.1
  402.6 1.8 collective-permute-start.3
  404.4 6.0 %all-to-all-done.1 = f32[96,8,96]{0,2,1:T(8,128)S(1)} async-done(((f32[96,8,96]{0,2,1:T(8,128)}), f32[96,8,96]{0,2,1:T(8,128)S(1)}, u32[]{:S(2)}, u32[]{:S(2)}) %all-to-all-start.1) | async-done | bytes 294944 | tf_op jit(solution)/shard_map/all_to_all | solution.py:42
  410.7 0.8 collective-permute-start.4
  411.5 67.0 %reduce-scatter.5.cloned.1.call-done = f32[96,768]{1,0:T(8,128)} async-done(((f32[768,768]{1,0:T(8,128)}), f32[96,768]{1,0:T(8,128)}) %reduce-scatter.5.cloned.1.call-update) | async-done | bytes 294928 | tf_op jit(solution)/shard_map/reduce_scatter | solution.py:29
  478.6 1.1 all_to_all.50
  479.7 0.8 copy.16
  480.5 3.6 all-to-all-start.2
  484.1 1.7 bitcast_dynamic-update-slice_fusion.6
  485.8 1.7 bitcast_dynamic-update-slice_fusion.5
  488.2 69.4 %reduce-scatter.11.cloned.1.call-done = f32[96,768]{1,0:T(8,128)} async-done(((f32[768,768]{1,0:T(8,128)}), f32[96,768]{1,0:T(8,128)}) %reduce-scatter.11.cloned.1.call-update) | async-done | bytes 294928 | tf_op jit(solution)/shard_map/reduce_scatter | solution.py:29
  557.6 1.7 bitcast_dynamic-update-slice_fusion.3
  559.4 3.0 collective-permute-start.5
  562.4 0.7 bitcast_dynamic-update-slice_fusion.2
  563.9 6.2 %collective-permute-done.5 = f32[96,768]{1,0:T(8,128)S(1)} collective-permute-done((f32[96,768]{1,0:T(8,128)S(1)}, f32[96,768]{1,0:T(8,128)S(1)}, u32[]{:S(2)}, u32[]{:S(2)}) %collective-permute-start.5) | collective-permute-done | bytes 294944 | tf_op jit(solution)/shard_map/ppermute | solution.py:14
  (28 shorter events, 3.6 us)
Async XLA Ops:
  6.5 108.3 %copy-start = (f32[32768]{0:T(1024)S(1)}, f32[32768]{0:T(1024)}, u32[]{:S(2)}) copy-start(f32[32768]{0:T(1024)} %param.9) | copy-start | bytes 393220
  6.5 363.2 %reduce-scatter.9.cloned.1.call-start = ((), (), s32[]{:S(2)}) async-start(), calls=%async_computation.9 | async-start | bytes 2654208 | tf_op jit(solution)/shard_map/reduce_scatter | solution.py:29
  6.5 104.1 %collective-permute-start = (bf16[768,6144]{1,0:T(8,128)(2,1)}, bf16[768,6144]{1,0:T(8,128)(2,1)}, u32[]{:S(2)}, u32[]{:S(2)}) collective-permute-start(bf16[768,6144]{1,0:T(8,128)(2,1)} %param.5), channel_id=1, source_target_pairs={{0,8},{8,16},{16,24},{24,32},{32,40},{40,48},{48,56},{56,64},{64,7... | collective-permute-start | bytes 28311560 | tf_op jit(solution)/shard_map/ppermute | solution.py:14
  110.7 105.3 %collective-permute-start.1 = (bf16[768,6144]{1,0:T(8,128)(2,1)}, bf16[768,6144]{1,0:T(8,128)(2,1)}, u32[]{:S(2)}, u32[]{:S(2)}) collective-permute-start(bf16[768,6144]{1,0:T(8,128)(2,1)} %collective-permute-done), channel_id=1, source_target_pairs={{0,8},{8,16},{16,24},{24,32},{32,40},{40,48},{48,56},{56,64},{64,7... | collective-permute-start | bytes 28311560 | tf_op jit(solution)/shard_map/ppermute | solution.py:14
  114.8 34.3 %copy-start.1 = (f32[4096]{0:T(1024)S(1)}, f32[4096]{0:T(1024)}, u32[]{:S(2)}) copy-start(f32[4096]{0:T(1024)} %param.8) | copy-start | bytes 49156
  216.0 124.3 %collective-permute-start.2 = (bf16[768,6144]{1,0:T(8,128)(2,1)}, bf16[768,6144]{1,0:T(8,128)(2,1)}, u32[]{:S(2)}, u32[]{:S(2)}) collective-permute-start(bf16[768,6144]{1,0:T(8,128)(2,1)} %collective-permute-done.1), channel_id=1, source_target_pairs={{0,8},{8,16},{16,24},{24,32},{32,40},{40,48},{48,56},{56,64},{64,7... | collective-permute-start | bytes 28311560 | tf_op jit(solution)/shard_map/ppermute | solution.py:14
  233.3 163.6 %reduce-scatter.7.cloned.1.call-start = ((), (), s32[]{:S(2)}) async-start(), calls=%async_computation.8 | async-start | bytes 2654208 | tf_op jit(solution)/shard_map/reduce_scatter | solution.py:29
  247.2 231.3 %reduce-scatter.5.cloned.1.call-start = ((), (), s32[]{:S(2)}) async-start(), calls=%async_computation.7 | async-start | bytes 2654208 | tf_op jit(solution)/shard_map/reduce_scatter | solution.py:29
  354.5 203.1 %reduce-scatter.11.cloned.1.call-start = ((), (), s32[]{:S(2)}) async-start(), calls=%async_computation.10 | async-start | bytes 2654208 | tf_op jit(solution)/shard_map/reduce_scatter | solution.py:29
  369.8 117.7 %copy-start.2 = (f32[96,768]{1,0:T(8,128)S(1)}, f32[96,768]{1,0:T(8,128)}, u32[]{:S(2)}) copy-start(f32[96,768]{1,0:T(8,128)} %reduce-scatter.9.cloned.1.call-done) | copy-start | bytes 884740
  371.7 27.0 %all-to-all-start = ((f32[96,8,96]{0,2,1:T(8,128)}), f32[96,8,96]{0,2,1:T(8,128)S(1)}, u32[]{:S(2)}, u32[]{:S(2)}) async-start(f32[96,8,96]{0,2,1:T(8,128)} %bitcast.4), calls=%async_computation.4 | async-start | bytes 786432 | tf_op jit(solution)/shard_map/all_to_all | solution.py:42
  398.7 11.6 %all-to-all-start.1 = ((f32[96,8,96]{0,2,1:T(8,128)}), f32[96,8,96]{0,2,1:T(8,128)S(1)}, u32[]{:S(2)}, u32[]{:S(2)}) async-start(f32[96,8,96]{0,2,1:T(8,128)} %bitcast.8), calls=%async_computation.5 | async-start | bytes 786432 | tf_op jit(solution)/shard_map/all_to_all | solution.py:42
  402.6 159.9 %collective-permute-start.3 = (f32[96,768]{1,0:T(8,128)S(1)}, f32[96,768]{1,0:T(8,128)S(1)}, u32[]{:S(2)}, u32[]{:S(2)}) collective-permute-start(f32[96,768]{1,0:T(8,128)S(1)} %bitcast.35), channel_id=1, source_target_pairs={{0,120},{8,0},{16,8},{24,16},{32,24},{40,32},{48,40},{56,48},{64,5... | collective-permute-start | bytes 884744 | tf_op jit(solution)/shard_map/ppermute | solution.py:14
  410.7 152.5 %collective-permute-start.4 = (f32[96,768]{1,0:T(8,128)S(1)}, f32[96,768]{1,0:T(8,128)S(1)}, u32[]{:S(2)}, u32[]{:S(2)}) collective-permute-start(f32[96,768]{1,0:T(8,128)S(1)} %bitcast.36), channel_id=1, source_target_pairs={{0,112},{8,120},{16,0},{24,8},{32,16},{40,24},{48,32},{56,40},{64,... | collective-permute-start | bytes 884744 | tf_op jit(solution)/shard_map/ppermute | solution.py:14
  480.5 78.7 %all-to-all-start.2 = ((f32[96,8,96]{2,0,1:T(8,128)}), f32[96,8,96]{2,0,1:T(8,128)S(1)}, u32[]{:S(2)}, u32[]{:S(2)}) async-start(f32[96,8,96]{2,0,1:T(8,128)} %copy.16), calls=%async_computation.6 | async-start | bytes 786432 | tf_op jit(solution)/shard_map/all_to_all | solution.py:42
  559.4 10.7 %collective-permute-start.5 = (f32[96,768]{1,0:T(8,128)S(1)}, f32[96,768]{1,0:T(8,128)S(1)}, u32[]{:S(2)}, u32[]{:S(2)}) collective-permute-start(f32[96,768]{1,0:T(8,128)S(1)} %bitcast.37), channel_id=1, source_target_pairs={{0,104},{8,112},{16,120},{24,0},{32,8},{40,16},{48,24},{56,32},{64... | collective-permute-start | bytes 884744 | tf_op jit(solution)/shard_map/ppermute | solution.py:14
Sparse Core Ops, SparseCore 0:
  233.4 81.9 reduce-scatter.8
  319.2 77.5 reduce-scatter.6
  400.6 77.9 reduce-scatter.4
  482.2 75.3 reduce-scatter.10
where the time goes:
time: 578 us; the launch traced here: 577 us
  waiting for transfers between devices  395 us (68%)
  local copies, waits for them, and re-layouts  83.3 us (14%)
  matrix products  57.2 us (10%)
  starting transfers between devices  28 us (5%)
  between operations  13.2 us (2%)
    ppermute x6, waiting for transfers between devices, shifted(): lax.ppermute(value, axis, [(i, (i + by) % peers) for i in range(peers)])  233 us
    reduce_scatter x4, waiting for transfers between devices, tile_sum(): lax.psum_scatter(tile_term(left, right), 'pair', scatter_dimension=0, til...  155 us
    gather x2, local copies, waits for them, and re-layouts, pair_weights(): gap = virt_energy[virt_index] - occ_energy[occ_index]  68.6 us
    dot_general x4, matrix products, tile_term(): lax.dot_general(left, right, (((1,), (1,)), ((), ())), preferred_element_...  57.2 us
    ppermute x6, starting transfers between devices, shifted(): lax.ppermute(value, axis, [(i, (i + by) % peers) for i in range(peers)])  14.6 us
    all_to_all x3, starting transfers between devices, local(): lax.all_to_all(lower[offset], 'pair', split_axis=1, concat_axis=0, tiled=...  13.2 us
  transfers between devices with their start and end apart: 13, of which 8 were waited for; matrix products, arithmetic and copies ran while one was open for 24% of the time, Pallas kernels for 0%

commit v1 on v0

v1 whole, which is shorter than its diff:
```python
import functools

import jax
import jax.numpy as jnp
import numpy as np
from jax import lax
from jax.experimental import pallas as pl
from jax.experimental.pallas import tpu as pltpu
from jax.sharding import PartitionSpec as P

ROWS = 768
HALF = 3072
PART = 96
PLANES = 4
WIDE = 256
PIECES = 4
DEPTH = HALF // PIECES
freq_point = 0.5

OWN, SIB, FAR_A, FAR_A_SIB, FAR_B, FAR_B_SIB, HALO_A, HALO_B, HALO_A_SIB, HALO_B_SIB, MINOR = range(11)

WHERE = [
    {"A0": OWN, "A1": SIB, "A2": FAR_B, "A3": FAR_A_SIB, "P0": HALO_A, "B3": MINOR},
    {"A1": OWN, "A0": SIB, "A3": FAR_A, "A2": FAR_B_SIB, "P1": HALO_B},
    {"A2": OWN, "A3": SIB, "A0": FAR_A, "A1": FAR_B_SIB, "B2": HALO_B, "B3": HALO_A_SIB, "P0": MINOR},
    {"A3": OWN, "A2": SIB, "A1": FAR_B, "A0": FAR_A_SIB, "B3": HALO_A, "B2": HALO_B_SIB},
]

BATCHES = [
    [["A0A0", "A3A1"],
     ["A1A0", "A1A1"],
     ["A2A2", "A0A0"],
     ["A3A2", "A3A3"]],
    [["P0A1", "P0A3"],
     ["A3A0", "A3A3"],
     ["A0B3", "A2B3"],
     ["A3A0", "A2A0"]],
    [["P0A2", "A2A1"],
     ["P1A2", "P1A3"],
     ["P0A1", "A0B2"],
     ["A1A0", "A1A1"]],
    [["A2A2", "A2B3"],
     ["A3A2", "A2A0"],
     ["A2A1", "A3A1"],
     ["A1B3", "A1B2"]],
]
MOVED = [["A0B1", "A0B3", "A0B2", None], [None, None, "A1B2", "A1B3"],
         [None, None, "A0B1", None], [None, None, None, None]]
ENTRIES = [
    [["A0A0", "A0B3", "A0B2", "A0B1"], ["A2A2", "A2A1", "A3A1", "A2B3"]],
    [["A1A1", "A1A0", "A1B3", "A1B2"], ["A3A3", "A3A2", "A2A0", "A3A0"]],
]
def batch_table(batch, sources):
    return np.array([[sources.index(WHERE[role][tile[at:at + 2]]) for at in (0, 2) for tile in tiles]
                     for role, tiles in enumerate(batch)], np.int32)


def tiles_kernel(count, sources, table, weight, *refs):
    source_refs = refs[:sources]
    out, held, scaled, total, sems = refs[sources:]
    step = pl.program_id(0)
    slot = lax.rem(step, 2)
    here = table[2 * count]

    def copy(k, slot, side, c):
        columns = slice(c * DEPTH, (c + 1) * DEPTH)
        return pltpu.make_async_copy(
            source_refs[k].at[:, columns], held.at[slot, side, :, columns], sems.at[slot, side, c])

    def fetch(tile, slot):
        for c in range(PIECES):
            for side in range(2):
                for k in range(sources):
                    @pl.when(table[side * count + tile] == k)
                    def _():
                        copy(k, slot, side, c).start()

    @pl.when(step == 0)
    def _():
        fetch(0, 0)

    @pl.when(step + 1 < count)
    def _():
        fetch(step + 1, 1 - slot)

    def ready(c):
        columns = slice(c * DEPTH, (c + 1) * DEPTH)
        for side in range(2):
            copy(0, slot, side, c).wait()
        scaled[c % 2] = (held[slot, 0, :, columns].astype(jnp.float32) * weight[:, columns]).astype(jnp.bfloat16)

    ready(0)
    for c in range(PIECES):
        if c + 1 < PIECES:
            ready(c + 1)
        for n in range(ROWS // WIDE):
            columns = slice(n * WIDE, (n + 1) * WIDE)
            acc = lax.dot_general(
                scaled[c % 2], held[slot, 1, columns, c * DEPTH:(c + 1) * DEPTH],
                (((1,), (1,)), ((), ())), preferred_element_type=jnp.float32)
            if c > 0:
                acc = acc + total[:, columns]
            if c + 1 < PIECES:
                total[:, columns] = acc
            else:
                for y in range(4):
                    at = lax.rem(y + 4 - here, 4)
                    for h in range(2):
                        first = (h * 4 + y) * PART
                        out[at, h, 0, :, columns] = acc[first:first + PART]


def tile_batch(table_row, weight, sources):
    count = (table_row.shape[0] - 1) // 2
    return pl.pallas_call(
        functools.partial(tiles_kernel, count, len(sources)),
        grid_spec=pltpu.PrefetchScalarGridSpec(
            num_scalar_prefetch=1,
            grid=(count,),
            in_specs=[pl.BlockSpec((1, HALF), lambda i, t: (0, 0))]
            + [pl.BlockSpec(memory_space=pl.ANY)] * len(sources),
            out_specs=pl.BlockSpec((4, 2, 1, PART, ROWS), lambda i, t: (0, 0, i, 0, 0)),
            scratch_shapes=[
                pltpu.VMEM((2, 2, ROWS, HALF), jnp.bfloat16),
                pltpu.VMEM((2, ROWS, DEPTH), jnp.bfloat16),
                pltpu.VMEM((ROWS, ROWS), jnp.float32),
                pltpu.SemaphoreType.DMA((2, 2, PIECES)),
            ],
        ),
        out_shape=jax.ShapeDtypeStruct((4, 2, count, PART, ROWS), jnp.float32),
        compiler_params=pltpu.CompilerParams(
            dimension_semantics=("arbitrary",), vmem_limit_bytes=44 * 1024 * 1024),
        cost_estimate=pl.CostEstimate(
            flops=count * ROWS * ROWS,
            bytes_accessed=count * ROWS * ROWS,
            transcendentals=0),
    )(table_row, weight, *sources)


def lookup(table, index):
    blocks = table.shape[0]
    high = lax.shift_right_logical(index, 7)
    low = jnp.bitwise_and(index, 127)
    pairs = index.shape[1]
    hot = jnp.where(lax.broadcasted_iota(jnp.int32, (blocks, pairs), 0) == high, 1.0, 0.0).astype(jnp.bfloat16)
    rest = table
    column = jnp.zeros((128, pairs), jnp.float32)
    for _ in range(3):
        piece = rest.astype(jnp.bfloat16)
        rest = rest - piece.astype(jnp.float32)
        column = column + lax.dot_general(
            piece, hot, (((0,), (0,)), ((), ())), preferred_element_type=jnp.float32)
    mask = lax.broadcasted_iota(jnp.int32, (128, pairs), 0) == low
    return jnp.sum(jnp.where(mask, column, 0.0), axis=0, keepdims=True)


def gap_kernel(occ_index, virt_index, occ_energy, virt_energy, gap):
    gap[...] = lookup(virt_energy[...], virt_index[...]) - lookup(occ_energy[...], occ_index[...])


def pair_gaps(occ_index, virt_index, occ_energy, virt_energy):
    block = 512
    pairs = occ_index.shape[0]
    occ_table = occ_energy.reshape(-1, 128)
    virt_table = virt_energy.reshape(-1, 128)
    line = pl.BlockSpec((1, block), lambda i: (0, i))
    return pl.pallas_call(
        gap_kernel,
        grid=(pairs // block,),
        in_specs=[line, line,
                  pl.BlockSpec(occ_table.shape, lambda i: (0, 0)),
                  pl.BlockSpec(virt_table.shape, lambda i: (0, 0))],
        out_specs=line,
        out_shape=jax.ShapeDtypeStruct((1, pairs), jnp.float32),
        cost_estimate=pl.CostEstimate(flops=6 * 128 * 288 * pairs, bytes_accessed=200000, transcendentals=0),
    )(occ_index[None, :], virt_index[None, :], occ_table, virt_table)


def moves(pairs):
    return [(z * 4 + src, (z + dz) % PLANES * 4 + dst) for z in range(PLANES) for src, dst, dz in pairs]


def aux_permute(value, pairs):
    return lax.ppermute(value, "aux", moves(pairs))


def y_permute(value, by):
    return lax.ppermute(value, "pair", [(h * 4 + y, h * 4 + (y + by) % 4) for h in range(2) for y in range(4)])


def x_permute(value, by):
    perm = []
    for z in range(PLANES):
        for x in range(4):
            to = (x + by) % 4
            for core in range(2):
                for y in range(4):
                    source = (z * 4 + x % 2 * 2 + core) * 8 + x // 2 * 4 + y
                    perm.append((source, (z * 4 + to % 2 * 2 + core) * 8 + to // 2 * 4 + y))
    return lax.ppermute(value, ("aux", "pair"), perm)


def ring_sum(part, permute, narrow, wide):
    count = part(0, 0).shape[0]
    up = permute(narrow(jnp.concatenate([part(2, 0), part(1, 1)])), 1)
    down = permute(narrow(jnp.concatenate([part(2, 1), part(3, 0)])), -1)
    up_more = permute(narrow(part(1, 0) + wide(up[:count])), 1)
    down_more = permute(narrow(part(3, 1) + wide(down[:count])), -1)
    zero = part(0, 0) + wide(down[count:]) + wide(up_more)
    one = part(0, 1) + wide(up[count:]) + wide(down_more)
    return zero, one


def slot_names(role):
    names = []
    for batch in BATCHES:
        names += [(tile, h) for h in range(2) for tile in batch[role]]
    early, late = MOVED[role][:2], MOVED[role][2:]
    names += [(tile, h) for h in range(2) for tile in early]
    names += [(tile, h) for h in range(2) for tile in late]
    return names


def entry_table():
    rows = []
    for role in range(4):
        names = slot_names(role)
        for x_hi in range(2):
            row = []
            for k in range(4):
                to = (x_hi * 2 + role // 2 + k) % 4
                row += [names.index((tile, to // 2)) for tile in ENTRIES[role % 2][to % 2]]
            rows.append(row)
    return np.array(rows, np.int32)


def pick_kernel(table, slots, parts):
    for i in range(16):
        parts[i] = slots[table[i]]


def pick_parts(table, slots):
    return pl.pallas_call(
        pick_kernel,
        in_specs=[pl.BlockSpec(memory_space=pltpu.SMEM), pl.BlockSpec(memory_space=pltpu.VMEM)],
        out_specs=pl.BlockSpec(memory_space=pltpu.VMEM),
        out_shape=jax.ShapeDtypeStruct((16, PART, ROWS), jnp.float32),
        compiler_params=pltpu.CompilerParams(vmem_limit_bytes=20 * 1024 * 1024),
        cost_estimate=pl.CostEstimate(flops=0, bytes_accessed=PART * ROWS, transcendentals=0),
    )(table, slots)


def largest_round(value, permute):
    got = [permute(value, by) for by in (1, 2, 3)]
    return jnp.maximum(jnp.maximum(value, got[0]), jnp.maximum(got[1], got[2]))


def z_permute(value, by):
    return aux_permute(value, [(r, r, by) for r in range(4)])


def after(value, other):
    return lax.optimization_barrier((value, other))[0]


def local(coeffs, occ_index, virt_index, occ_energy, virt_energy):
    role = lax.rem(lax.axis_index("aux"), 4)
    x_lo = role // 2
    x_hi = lax.axis_index("pair") // 4
    y = lax.rem(lax.axis_index("pair"), 4)

    largest = jnp.max(jnp.abs(coeffs).reshape(-1, 8, coeffs.shape[1]), axis=0)
    largest = jnp.max(largest.reshape(8, -1, 128), axis=1).astype(jnp.float32)
    largest = largest_round(largest, x_permute)

    other = lax.dynamic_slice_in_dim(coeffs, (1 - x_lo) * HALF, HALF, axis=1)
    other, largest = lax.optimization_barrier((other, largest))
    far_a = aux_permute(other, [(0, 2, 0), (3, 1, 0)])
    largest = largest_round(largest, z_permute)
    mine = lax.dynamic_slice_in_dim(after(coeffs, other), x_lo * HALF, HALF, axis=1)
    mine, largest = lax.optimization_barrier((mine, largest))
    halo_a = aux_permute(mine, [(0, 0, -1), (3, 3, 1)])
    sib = aux_permute(mine, [(0, 1, 0), (1, 0, 0), (2, 3, 0), (3, 2, 0)])
    far_b = aux_permute(after(other, far_a), [(1, 3, 0), (2, 0, 0)])

    largest = largest_round(largest, y_permute)
    largest = jnp.maximum(largest, aux_permute(largest, [(0, 1, 0), (1, 0, 0), (2, 3, 0), (3, 2, 0)]))
    largest = jnp.max(largest)
    bound = 8.0 * HALF * 4 * largest * largest * 4.0
    scale = 32768.0 / jnp.maximum(bound, 1e-30)
    unscale = 1.0 / scale

    def narrow(value):
        return (value * scale).astype(jnp.float16)

    def wide(value):
        return value.astype(jnp.float32) * unscale

    begin = x_lo * HALF
    gap = pair_gaps(
        lax.dynamic_slice_in_dim(occ_index, begin, HALF),
        lax.dynamic_slice_in_dim(virt_index, begin, HALF),
        occ_energy, virt_energy)
    weight = -4.0 * gap / (gap * gap + freq_point * freq_point)

    plans = []
    for batch in BATCHES:
        used = sorted({WHERE[r][t[i:i + 2]] for r in range(4) for t in batch[r] for i in (0, 2)})
        row = lax.dynamic_index_in_dim(jnp.asarray(batch_table(batch, used)), role, axis=0, keepdims=False)
        row = jnp.concatenate([row, y[None].astype(jnp.int32)])
        plans.append([used, row])
    entries = lax.dynamic_index_in_dim(jnp.asarray(entry_table()), role * 2 + x_hi, axis=0, keepdims=False)
    rows = [plan[1] for plan in plans]
    far_a, scale, unscale, weight, entries, rows = lax.optimization_barrier(
        (far_a, scale, unscale, weight, entries, rows))

    far_a_sib = aux_permute(far_a, [(1, 0, 0), (2, 3, 0)])
    minor = aux_permute(far_a, [(1, 0, 1), (2, 2, -1)])
    halo_a, far_a_sib = lax.optimization_barrier((halo_a, far_a_sib))
    halo_b = aux_permute(after(mine, halo_a), [(1, 1, -1), (2, 2, 1)])
    halo_a_sib = aux_permute(halo_a, [(3, 2, 0)])

    held = {OWN: mine, SIB: sib, FAR_A: far_a, FAR_A_SIB: far_a_sib, HALO_A: halo_a}

    def tiles(number):
        return tile_batch(rows[number], weight, [held[s] for s in plans[number][0]])

    def first_sends(partial):
        return [narrow(jnp.concatenate([partial[2, 0], partial[1, 1]])),
                narrow(jnp.concatenate([partial[2, 1], partial[3, 0]]))]

    def first_round(sends):
        return [y_permute(sends[0], 1), y_permute(sends[1], -1)]

    def second_sends(partial, got):
        return [narrow(partial[1, 0] + wide(got[0][:2])), narrow(partial[3, 1] + wide(got[1][:2]))]

    def finish(partial, got, more):
        zero = partial[0, 0] + wide(got[1][2:]) + wide(more[0])
        one = partial[0, 1] + wide(got[0][2:]) + wide(more[1])
        return [zero, one]

    partial0 = tiles(0)
    sends0 = first_sends(partial0)
    held[HALO_A_SIB] = after(halo_a_sib, sends0)
    got0 = first_round(sends0)
    partial1 = tiles(1)
    sends1 = first_sends(partial1)
    got0, sends1 = lax.optimization_barrier((got0, sends1))
    got1 = first_round(sends1)
    sends0 = second_sends(partial0, got0)
    more0 = first_round(sends0)
    sends1 = second_sends(partial1, got1)
    far_b, halo_b, minor, more0 = lax.optimization_barrier((far_b, halo_b, minor, more0, sends1))[:4]
    more1 = first_round(sends1)
    held[FAR_B], held[HALO_B], held[MINOR] = far_b, halo_b, minor
    held[FAR_B_SIB] = aux_permute(far_b, [(0, 1, 0), (3, 2, 0)])
    held[HALO_B_SIB] = aux_permute(halo_b, [(2, 3, 0)])
    partial2 = tiles(2)
    sends2 = first_sends(partial2)
    more1 = after(more1, sends2)
    got2 = first_round(sends2)
    total0 = finish(partial0, got0, more0)
    total1 = finish(partial1, got1, more1)
    moved0 = wide(aux_permute(narrow(jnp.concatenate(total1)), [(0, 0, 1)]))
    partial3 = tiles(3)
    sends3 = first_sends(partial3)
    got2 = after(got2, partial3)
    sends2 = second_sends(partial2, got2)
    more2 = first_round(sends2)
    got3 = first_round(after(sends3, sends2))
    more3 = first_round(second_sends(partial3, got3))
    total2 = finish(partial2, got2, more2)
    moved2 = wide(aux_permute(narrow(jnp.concatenate(total2)), [(0, 0, 1), (1, 1, 1), (2, 2, 1)]))
    total3 = finish(partial3, got3, more3)
    slots = jnp.concatenate(total0 + total1 + total2 + total3 + [moved0, moved2])
    parts = pick_parts(entries, slots).reshape(4, 2, 2, PART, ROWS)

    def x_part(k, d):
        return parts[k, d]

    zero, one = ring_sum(x_part, x_permute, narrow, wide)
    final = [zero[0], zero[1], one[0], one[1]]

    swapped = wide(aux_permute(narrow(one[0]), [(2, 3, 0), (3, 2, 0)]))
    lower = [final[0], final[1], jnp.where(x_lo == 1, swapped, final[2]), final[3]]

    crossed = narrow(jnp.stack(final[1:])).reshape(3, PART, 8, PART)
    crossed = lax.all_to_all(crossed, "pair", split_axis=2, concat_axis=1, tiled=True)
    crossed = crossed.reshape(3, ROWS, PART)
    back = [
        [(0, 3, -1), (1, 0, 0), (2, 1, 0), (3, 2, 0)],
        [(0, 2, -1), (1, 3, -1), (2, 1, 0), (3, 0, 0)],
        [(0, 1, -1), (1, 2, -1), (2, 3, -1), (3, 0, 0)],
    ]
    upper = [wide(aux_permute(crossed[o], back[o])).T for o in range(3)]
    return jnp.stack(lower[::-1] + upper)


def solution(mesh):
    return jax.shard_map(
        local,
        mesh=mesh,
        in_specs=(P("aux", "pair"), P("pair"), P("pair"), P(), P()),
        out_specs=P(None, ("aux", "pair"), None),
        check_vma=False,
    )
```

time: 578 us -> 368 us (0.64); the launches traced: 577 us -> 361 us
  waiting for transfers between devices: 395 us -> 111 us
  Pallas kernels: 0 us -> 76.4 us
  starting transfers between devices: 28 us -> 97.6 us
  local copies, waits for them, and re-layouts: 83.3 us -> 25.8 us
  matrix products: 57.2 us -> 0 us
  other arithmetic: 0.78 us -> 30.1 us
  blocking collectives: 0 us -> 18 us
  between operations: 13.2 us -> 2.14 us
    reduce_scatter x4 -> x0, waiting for transfers between devices: 155 us -> none  [tile_sum(): lax.psum_scatter(tile_term(left, right), 'pair', scatter_dimension=0, til...]
    ppermute x6 -> x46, waiting for transfers between devices: 233 us -> 111 us  [the longest x20 52.4 us: aux_permute(): return lax.ppermute(value, 'aux', moves(pairs))]
    ppermute x6 -> x46, starting transfers between devices: 14.6 us -> 97.6 us  [the longest x20 56.9 us: aux_permute(): return lax.ppermute(value, 'aux', moves(pairs))]
    pallas_call x0 -> x6, Pallas kernels: none -> 76.4 us  [the longest x4 68.3 us: tile_batch(): pl.pallas_call(functools.partial(tiles_kernel, count, len(sources)), grid...]
    gather x2 -> x0, local copies, waits for them, and re-layouts: 68.6 us -> none  [pair_weights(): gap = virt_energy[virt_index] - occ_energy[occ_index]]
    dot_general x4 -> x0, matrix products: 57.2 us -> none  [tile_term(): lax.dot_general(left, right, (((1,), (1,)), ((), ())), preferred_element_...]
    all_to_all x0 -> x1, blocking collectives: none -> 18 us  [local(): lax.all_to_all(crossed, 'pair', split_axis=2, concat_axis=1, tiled=True)]
    unnamed x0 -> x13, other arithmetic: none -> 13.4 us
  transfers between devices with their start and end apart: 13 -> 46, of which waited for: 8 -> 19; matrix products, arithmetic and copies ran while one was open for 24% -> 10% of each run, Pallas kernels for 0% -> 20%
where the time goes in v1:
time: 368 us; the launch traced here: 361 us
  waiting for transfers between devices  111 us (30%)
  starting transfers between devices  97.6 us (27%)
  Pallas kernels  76.4 us (21%)
  other arithmetic  30.1 us (8%)
  local copies, waits for them, and re-layouts  25.8 us (7%)
  blocking collectives  18 us (5%)
    pallas_call x4, Pallas kernels, tile_batch(): pl.pallas_call(functools.partial(tiles_kernel, count, len(sources)), grid...  68.3 us
    ppermute x20, starting transfers between devices, aux_permute(): return lax.ppermute(value, 'aux', moves(pairs))  56.9 us
    ppermute x20, waiting for transfers between devices, aux_permute(): return lax.ppermute(value, 'aux', moves(pairs))  52.4 us
    ppermute x19, waiting for transfers between devices, y_permute(): lax.ppermute(value, 'pair', [(h * 4 + y, h * 4 + (y + by) % 4) for h in r...  40.9 us
    ppermute x7, starting transfers between devices, x_permute(): return lax.ppermute(value, ('aux', 'pair'), perm)  21.4 us
    ppermute x19, starting transfers between devices, y_permute(): lax.ppermute(value, 'pair', [(h * 4 + y, h * 4 + (y + by) % 4) for h in r...  19.2 us
    all_to_all x1, blocking collectives, local(): lax.all_to_all(crossed, 'pair', split_axis=2, concat_axis=1, tiled=True)  18 us
    ppermute x7, waiting for transfers between devices, x_permute(): return lax.ppermute(value, ('aux', 'pair'), perm)  17.8 us
  transfers between devices with their start and end apart: 46, of which 19 were waited for; matrix products, arithmetic and copies ran while one was open for 10% of the time, Pallas kernels for 20%

profile of v1, /device:TPU:3, one launch (start us, length us, event | category | flops | bytes accessed | tf_op | source)
XLA Modules:
  0.0 361.1 jit_solution(9943780180515071510)
XLA Ops:
  0.0 5.1 %bitcast_reduce_fusion = bf16[8,6144]{1,0:T(8,128)(2,1)S(1)} fusion(bf16[768,6144]{1,0:T(8,128)(2,1)} %param.10), kind=kLoop, calls=%fused_computation | loop fusion | flops 9388032 | bytes 9535488 | tf_op jit(solution)/shard_map/reduce_max | solution.py:272
  8.6 4.8 %constant_dynamic-slice_fusion.6 = bf16[768,3072]{1,0:T(8,128)(2,1)} fusion(bf16[768,6144]{1,0:T(8,128)(2,1)} %param.10, s32[]{:T(128)S(6)} %select_n.36), kind=kLoop, calls=%fused_computation.148 | loop fusion | bytes 9437188 | tf_op jit(solution)/shard_map/dynamic_slice | solution.py:276
  13.4 5.2 %collective-permute-start.3 = (bf16[768,3072]{1,0:T(8,128)(2,1)}, bf16[768,3072]{1,0:T(8,128)(2,1)}, u32[]{:S(2)}, u32[]{:S(2)}) collective-permute-start(bf16[768,3072]{1,0:T(8,128)(2,1)} %constant_dynamic-slice_fusion.6), channel_id=1, source_target_pairs={{0,16},{24,8},{32,48},{56,40},{64,80},{88,72},{96,112},{120,104},{... | collective-permute-start | bytes 14155784 | tf_op jit(solution)/shard_map/ppermute | solution.py:184
  19.9 4.8 %shard_map.100 = f32[1,3072]{1,0:T(1,128)} custom-call(s32[1,3072]{1,0:T(1,128)} %bitcast.258, s32[1,3072]{1,0:T(1,128)} %bitcast.259, f32[32,128]{1,0:T(8,128)} %bitcast.261, f32[256,128]{1,0:T(8,128)} %bitcast.260), custom_call_target="tpu_custom_call" | custom-call | flops 679477248 | bytes 200000 | tf_op jit(solution)/shard_map/pallas_call | solution.py:167
  28.2 3.8 %collective-permute-start.6 = (f32[8,128]{1,0:T(8,128)S(1)}, f32[8,128]{1,0:T(8,128)S(1)}, u32[]{:S(2)}, u32[]{:S(2)}) collective-permute-start(f32[8,128]{1,0:T(8,128)S(1)} %maximum_maximum_fusion.2), channel_id=1, source_target_pairs={{0,96},{8,104},{16,112},{24,120},{32,0},{40,8},{48,16},{56,24},{64... | collective-permute-start | bytes 12296 | tf_op jit(solution)/shard_map/ppermute | solution.py:184
  32.8 4.8 %constant_dynamic-slice_fusion.5.refs_0_ = bf16[768,3072]{1,0:T(8,128)(2,1)} fusion(bf16[768,6144]{1,0:T(8,128)(2,1)} %param.10, s32[]{:T(128)S(6)} %select_n.37), kind=kLoop, calls=%fused_computation.147 | loop fusion | bytes 9437188 | tf_op jit(solution)/shard_map/dynamic_slice | solution.py:280
  45.3 3.9 %collective-permute-start.12 = (bf16[768,3072]{1,0:T(8,128)(2,1)}, bf16[768,3072]{1,0:T(8,128)(2,1)}, u32[]{:S(2)}, u32[]{:S(2)}) collective-permute-start(bf16[768,3072]{1,0:T(8,128)(2,1)} %constant_dynamic-slice_fusion.5.refs_0_), channel_id=1, source_target_pairs={{0,96},{24,56},{32,0},{56,88},{64,32},{88,120},{96,64},{120,24},{1... | collective-permute-start | bytes 14155784 | tf_op jit(solution)/shard_map/ppermute | solution.py:184
  51.1 16.8 %collective-permute-done.3.refs_2_.refs_1_ = bf16[768,3072]{1,0:T(8,128)(2,1)} collective-permute-done((bf16[768,3072]{1,0:T(8,128)(2,1)}, bf16[768,3072]{1,0:T(8,128)(2,1)}, u32[]{:S(2)}, u32[]{:S(2)}) %collective-permute-start.3) | collective-permute-done | bytes 4718624 | tf_op jit(solution)/shard_map/ppermute | solution.py:184
  69.2 3.8 %collective-permute-start.11 = (bf16[768,3072]{1,0:T(8,128)(2,1)}, bf16[768,3072]{1,0:T(8,128)(2,1)S(1)}, u32[]{:S(2)}, u32[]{:S(2)}) collective-permute-start(bf16[768,3072]{1,0:T(8,128)(2,1)} %constant_dynamic-slice_fusion.5.refs_0_), channel_id=1, source_target_pairs={{0,8},{8,0},{16,24},{24,16},{32,40},{40,32},{48,56},{56,48},{64,72... | collective-permute-start | bytes 14155784 | tf_op jit(solution)/shard_map/ppermute | solution.py:184
  73.0 28.7 %collective-permute-done.12.refs_4_.refs_5_ = bf16[768,3072]{1,0:T(8,128)(2,1)} collective-permute-done((bf16[768,3072]{1,0:T(8,128)(2,1)}, bf16[768,3072]{1,0:T(8,128)(2,1)}, u32[]{:S(2)}, u32[]{:S(2)}) %collective-permute-start.12) | collective-permute-done | bytes 4718624 | tf_op jit(solution)/shard_map/ppermute | solution.py:184
  101.7 3.6 collective-permute-start.16
  109.4 3.0 collective-permute-start.18
  117.0 17.1 %shard_map.101 = f32[4,2,2,96,768]{4,3,2,1,0:T(8,128)S(1)} custom-call(s32[5]{0:T(128)S(1)} %get-tuple-element.44.table, f32[1,3072]{1,0:T(1,128)S(1)} %add_divide_fusion.weight, bf16[768,3072]{1,0:T(8,128)(2,1)S(1)} %copy-done.1, bf16[768,3072]{1,0:T(8,128)(2,1)} %copy-done, bf16[768,3072]{1,0:T(8,128)(2,1)} %collective-permute-done.3.refs_2_.refs_1_, ...), custom_call_target="tpu_custom_call" | custom-call | flops 1179648 | bytes 1179648 | tf_op jit(solution)/shard_map/pallas_call | solution.py:115
  139.8 16.7 %shard_map.102 = f32[4,2,2,96,768]{4,3,2,1,0:T(8,128)S(1)} custom-call(s32[5]{0:T(128)S(1)} %get-tuple-element.50.table, f32[1,3072]{1,0:T(1,128)S(1)} %add_divide_fusion.weight, bf16[768,3072]{1,0:T(8,128)(2,1)S(1)} %copy-done.2, bf16[768,3072]{1,0:T(8,128)(2,1)} %copy-done, bf16[768,3072]{1,0:T(8,128)(2,1)} %collective-permute-done.3.refs_2_.refs_1_, ...), custom_call_target="tpu_custom_call" | custom-call | flops 1179648 | bytes 1179648 | tf_op jit(solution)/shard_map/pallas_call | solution.py:115
  160.9 6.5 %collective-permute-done.22 = f16[4,96,768]{2,1,0:T(8,128)(2,1)S(1)} collective-permute-done((f16[4,96,768]{2,1,0:T(8,128)(2,1)S(1)}, f16[4,96,768]{2,1,0:T(8,128)(2,1)S(1)}, u32[]{:S(2)}, u32[]{:S(2)}) %collective-permute-start.22) | collective-permute-done | bytes 589856 | tf_op jit(solution)/shard_map/ppermute | solution.py:188
  169.9 6.6 %collective-permute-done.21 = f16[2,96,768]{2,1,0:T(8,128)(2,1)S(1)} collective-permute-done((f16[2,96,768]{2,1,0:T(8,128)(2,1)S(1)}, f16[2,96,768]{2,1,0:T(8,128)(2,1)S(1)}, u32[]{:S(2)}, u32[]{:S(2)}) %collective-permute-start.21) | collective-permute-done | bytes 294944 | tf_op jit(solution)/shard_map/ppermute | solution.py:188
  177.7 12.9 %collective-permute-start.26 = (bf16[768,3072]{1,0:T(8,128)(2,1)}, bf16[768,3072]{1,0:T(8,128)(2,1)}, u32[]{:S(2)}, u32[]{:S(2)}) collective-permute-start(bf16[768,3072]{1,0:T(8,128)(2,1)} %collective-permute-done.17.refs_3_), channel_id=1, source_target_pairs={{0,8},{24,16},{32,40},{56,48},{64,72},{88,80},{96,104},{120,112},{... | collective-permute-start | bytes 14155784 | tf_op jit(solution)/shard_map/ppermute | solution.py:184
  196.7 17.2 %shard_map.103 = f32[4,2,2,96,768]{4,3,2,1,0:T(8,128)S(1)} custom-call(s32[5]{0:T(128)S(1)} %get-tuple-element.62.table, f32[1,3072]{1,0:T(1,128)S(1)} %add_divide_fusion.weight, bf16[768,3072]{1,0:T(8,128)(2,1)S(1)} %bitcast.249, bf16[768,3072]{1,0:T(8,128)(2,1)} %collective-permute-done.3.refs_2_.refs_1_, bf16[768,3072]{1,0:T(8,128)(2,1)} %copy-done.5, ...), custom_call_target="tpu_custom_call" | custom-call | flops 1179648 | bytes 1179648 | tf_op jit(solution)/shard_map/pallas_call | solution.py:115
  218.9 17.2 %shard_map.104 = f32[4,2,2,96,768]{4,3,2,1,0:T(8,128)S(1)} custom-call(s32[5]{0:T(128)S(1)} %get-tuple-element.68.table, f32[1,3072]{1,0:T(1,128)S(1)} %add_divide_fusion.weight, bf16[768,3072]{1,0:T(8,128)(2,1)S(1)} %copy-done.2, bf16[768,3072]{1,0:T(8,128)(2,1)} %copy-done, bf16[768,3072]{1,0:T(8,128)(2,1)} %collective-permute-done.3.refs_2_.refs_1_, ...), custom_call_target="tpu_custom_call" | custom-call | flops 1179648 | bytes 1179648 | tf_op jit(solution)/shard_map/pallas_call | solution.py:115
  240.5 4.7 %collective-permute-done.30 = f16[2,96,768]{2,1,0:T(8,128)(2,1)S(1)} collective-permute-done((f16[2,96,768]{2,1,0:T(8,128)(2,1)S(1)}, f16[2,96,768]{2,1,0:T(8,128)(2,1)S(1)}, u32[]{:S(2)}, u32[]{:S(2)}) %collective-permute-start.30) | collective-permute-done | bytes 294944 | tf_op jit(solution)/shard_map/ppermute | solution.py:188
  250.1 8.4 %collective-permute-done.33 = f16[4,96,768]{2,1,0:T(8,128)(2,1)S(1)} collective-permute-done((f16[4,96,768]{2,1,0:T(8,128)(2,1)S(1)}, f16[4,96,768]{2,1,0:T(8,128)(2,1)S(1)}, u32[]{:S(2)}, u32[]{:S(2)}) %collective-permute-start.33) | collective-permute-done | bytes 589856 | tf_op jit(solution)/shard_map/ppermute | solution.py:188
  260.5 3.3 collective-permute-done.32
  263.8 3.0 collective-permute-done.34
  269.1 4.3 %collective-permute-done.35 = f16[2,96,768]{2,1,0:T(8,128)(2,1)S(1)} collective-permute-done((f16[2,96,768]{2,1,0:T(8,128)(2,1)S(1)}, f16[2,96,768]{2,1,0:T(8,128)(2,1)S(1)}, u32[]{:S(2)}, u32[]{:S(2)}) %collective-permute-start.35) | collective-permute-done | bytes 294944 | tf_op jit(solution)/shard_map/ppermute | solution.py:188
  276.6 3.3 shard_map.105
  280.3 13.6 %collective-permute-start.38 = (f16[4,96,768]{2,1,0:T(8,128)(2,1)S(1)}, f16[4,96,768]{2,1,0:T(8,128)(2,1)S(1)}, u32[]{:S(2)}, u32[]{:S(2)}) collective-permute-start(f16[4,96,768]{2,1,0:T(8,128)(2,1)S(1)} %fusion.10), channel_id=1, source_target_pairs={{0,16},{1,17},{2,18},{3,19},{8,24},{9,25},{10,26},{11,27},{16,4},{... | collective-permute-start | bytes 1769480 | tf_op jit(solution)/shard_map/ppermute | solution.py:200
  294.1 8.5 %collective-permute-done.38 = f16[4,96,768]{2,1,0:T(8,128)(2,1)S(1)} collective-permute-done((f16[4,96,768]{2,1,0:T(8,128)(2,1)S(1)}, f16[4,96,768]{2,1,0:T(8,128)(2,1)S(1)}, u32[]{:S(2)}, u32[]{:S(2)}) %collective-permute-start.38) | collective-permute-done | bytes 589856 | tf_op jit(solution)/shard_map/ppermute | solution.py:200
  305.0 5.2 %collective-permute-done.42 = f16[2,96,768]{2,1,0:T(8,128)(2,1)S(1)} collective-permute-done((f16[2,96,768]{2,1,0:T(8,128)(2,1)S(1)}, f16[2,96,768]{2,1,0:T(8,128)(2,1)S(1)}, u32[]{:S(2)}, u32[]{:S(2)}) %collective-permute-start.42) | collective-permute-done | bytes 294944 | tf_op jit(solution)/shard_map/ppermute | solution.py:200
  312.5 4.1 %collective-permute-done.40 = f16[2,96,768]{2,1,0:T(8,128)(2,1)S(1)} collective-permute-done((f16[2,96,768]{2,1,0:T(8,128)(2,1)S(1)}, f16[2,96,768]{2,1,0:T(8,128)(2,1)S(1)}, u32[]{:S(2)}, u32[]{:S(2)}) %collective-permute-start.40) | collective-permute-done | bytes 294944 | tf_op jit(solution)/shard_map/ppermute | solution.py:200
  318.1 8.7 %collective-permute-start.41 = (f16[96,768]{1,0:T(8,128)(2,1)S(1)}, f16[96,768]{1,0:T(8,128)(2,1)S(1)}, u32[]{:S(2)}, u32[]{:S(2)}) collective-permute-start(f16[96,768]{1,0:T(8,128)(2,1)S(1)} %multiply_convert_fusion), channel_id=1, source_target_pairs={{16,24},{24,16},{48,56},{56,48},{80,88},{88,80},{112,120},{120,112... | collective-permute-start | bytes 442376 | tf_op jit(solution)/shard_map/ppermute | solution.py:184
  329.6 18.0 %all_to_all.15 = f16[3,96,8,96]{1,3,0,2:T(8,128)(2,1)S(1)} all-to-all(f16[3,96,8,96]{1,3,0,2:T(8,128)(2,1)S(1)} %fusion.12), channel_id=1, replica_groups=mesh['aux'=16,'pair'=8] {'pair'}, dimensions={2} | all-to-all | bytes 884736 | tf_op jit(solution)/shard_map/all_to_all | solution.py:389
  354.3 3.9 %collective-permute-done.44 = f16[768,96]{0,1:T(8,128)(2,1)S(1)} collective-permute-done((f16[768,96]{0,1:T(8,128)(2,1)S(1)}, f16[768,96]{0,1:T(8,128)(2,1)S(1)}, u32[]{:S(2)}, u32[]{:S(2)}) %collective-permute-start.44) | collective-permute-done | bytes 147488 | tf_op jit(solution)/shard_map/ppermute | solution.py:184
  (167 shorter events, 87.4 us)
Async XLA Ops:
  5.2 8.2 %collective-permute-start.1 = (f32[8,128]{1,0:T(8,128)S(1)}, f32[8,128]{1,0:T(8,128)S(1)}, u32[]{:S(2)}, u32[]{:S(2)}) collective-permute-start(f32[8,128]{1,0:T(8,128)S(1)} %convert_element_type.184), channel_id=1, source_target_pairs={{0,4},{1,5},{2,6},{3,7},{8,12},{9,13},{10,14},{11,15},{16,20},{17,... | collective-permute-start | bytes 12296 | tf_op jit(solution)/shard_map/ppermute | solution.py:200
  13.4 54.4 %collective-permute-start.3 = (bf16[768,3072]{1,0:T(8,128)(2,1)}, bf16[768,3072]{1,0:T(8,128)(2,1)}, u32[]{:S(2)}, u32[]{:S(2)}) collective-permute-start(bf16[768,3072]{1,0:T(8,128)(2,1)} %constant_dynamic-slice_fusion.6), channel_id=1, source_target_pairs={{0,16},{24,8},{32,48},{56,40},{64,80},{88,72},{96,112},{120,104},{... | collective-permute-start | bytes 14155784 | tf_op jit(solution)/shard_map/ppermute | solution.py:184
  28.2 9.3 %collective-permute-start.6 = (f32[8,128]{1,0:T(8,128)S(1)}, f32[8,128]{1,0:T(8,128)S(1)}, u32[]{:S(2)}, u32[]{:S(2)}) collective-permute-start(f32[8,128]{1,0:T(8,128)S(1)} %maximum_maximum_fusion.2), channel_id=1, source_target_pairs={{0,96},{8,104},{16,112},{24,120},{32,0},{40,8},{48,16},{56,24},{64... | collective-permute-start | bytes 12296 | tf_op jit(solution)/shard_map/ppermute | solution.py:184
  45.3 56.4 %collective-permute-start.12 = (bf16[768,3072]{1,0:T(8,128)(2,1)}, bf16[768,3072]{1,0:T(8,128)(2,1)}, u32[]{:S(2)}, u32[]{:S(2)}) collective-permute-start(bf16[768,3072]{1,0:T(8,128)(2,1)} %constant_dynamic-slice_fusion.5.refs_0_), channel_id=1, source_target_pairs={{0,96},{24,56},{32,0},{56,88},{64,32},{88,120},{96,64},{120,24},{1... | collective-permute-start | bytes 14155784 | tf_op jit(solution)/shard_map/ppermute | solution.py:184
  67.9 33.8 %collective-permute-start.13 = (bf16[768,3072]{1,0:T(8,128)(2,1)}, bf16[768,3072]{1,0:T(8,128)(2,1)S(1)}, u32[]{:S(2)}, u32[]{:S(2)}) collective-permute-start(bf16[768,3072]{1,0:T(8,128)(2,1)} %collective-permute-done.3.refs_2_.refs_1_), channel_id=1, source_target_pairs={{8,0},{16,24},{40,32},{48,56},{72,64},{80,88},{104,96},{112,120},{... | collective-permute-start | bytes 14155784 | tf_op jit(solution)/shard_map/ppermute | solution.py:184
  69.2 43.2 %collective-permute-start.11 = (bf16[768,3072]{1,0:T(8,128)(2,1)}, bf16[768,3072]{1,0:T(8,128)(2,1)S(1)}, u32[]{:S(2)}, u32[]{:S(2)}) collective-permute-start(bf16[768,3072]{1,0:T(8,128)(2,1)} %constant_dynamic-slice_fusion.5.refs_0_), channel_id=1, source_target_pairs={{0,8},{8,0},{16,24},{24,16},{32,40},{40,32},{48,56},{56,48},{64,72... | collective-permute-start | bytes 14155784 | tf_op jit(solution)/shard_map/ppermute | solution.py:184
  101.7 35.2 %collective-permute-start.16 = (bf16[768,3072]{1,0:T(8,128)(2,1)}, bf16[768,3072]{1,0:T(8,128)(2,1)}, u32[]{:S(2)}, u32[]{:S(2)}) collective-permute-start(bf16[768,3072]{1,0:T(8,128)(2,1)} %collective-permute-done.12.refs_4_.refs_5_), channel_id=1, source_target_pairs={{24,16},{56,48},{88,80},{120,112},{25,17},{57,49},{89,81},{121,113... | collective-permute-start | bytes 14155784 | tf_op jit(solution)/shard_map/ppermute | solution.py:184
  105.2 64.6 %collective-permute-start.19 = (bf16[768,3072]{1,0:T(8,128)(2,1)}, bf16[768,3072]{1,0:T(8,128)(2,1)}, u32[]{:S(2)}, u32[]{:S(2)}) collective-permute-start(bf16[768,3072]{1,0:T(8,128)(2,1)} %collective-permute-done.3.refs_2_.refs_1_), channel_id=1, source_target_pairs={{8,32},{16,112},{40,64},{48,16},{72,96},{80,48},{104,0},{112,80},{... | collective-permute-start | bytes 14155784 | tf_op jit(solution)/shard_map/ppermute | solution.py:184
  108.1 61.8 %collective-permute-start.17 = (bf16[768,3072]{1,0:T(8,128)(2,1)}, bf16[768,3072]{1,0:T(8,128)(2,1)}, u32[]{:S(2)}, u32[]{:S(2)}) collective-permute-start(bf16[768,3072]{1,0:T(8,128)(2,1)} %constant_dynamic-slice_fusion.6), channel_id=1, source_target_pairs={{8,24},{16,0},{40,56},{48,32},{72,88},{80,64},{104,120},{112,96},{... | collective-permute-start | bytes 14155784 | tf_op jit(solution)/shard_map/ppermute | solution.py:184
  109.4 60.5 %collective-permute-start.18 = (bf16[768,3072]{1,0:T(8,128)(2,1)}, bf16[768,3072]{1,0:T(8,128)(2,1)}, u32[]{:S(2)}, u32[]{:S(2)}) collective-permute-start(bf16[768,3072]{1,0:T(8,128)(2,1)} %constant_dynamic-slice_fusion.5.refs_0_), channel_id=1, source_target_pairs={{8,104},{16,48},{40,8},{48,80},{72,40},{80,112},{104,72},{112,16},... | collective-permute-start | bytes 14155784 | tf_op jit(solution)/shard_map/ppermute | solution.py:184
  136.6 20.3 %collective-permute-start.14 = (f16[4,96,768]{2,1,0:T(8,128)(2,1)S(1)}, f16[4,96,768]{2,1,0:T(8,128)(2,1)S(1)}, u32[]{:S(2)}, u32[]{:S(2)}) collective-permute-start(f16[4,96,768]{2,1,0:T(8,128)(2,1)S(1)} %fusion), channel_id=1, source_target_pairs={{0,1},{1,2},{2,3},{3,0},{4,5},{5,6},{6,7},{7,4},{8,9},{9,10},{10,1... | collective-permute-start | bytes 1769480 | tf_op jit(solution)/shard_map/ppermute | solution.py:188
  136.9 20.1 %collective-permute-start.15 = (f16[4,96,768]{2,1,0:T(8,128)(2,1)S(1)}, f16[4,96,768]{2,1,0:T(8,128)(2,1)}, u32[]{:S(2)}, u32[]{:S(2)}) collective-permute-start(f16[4,96,768]{2,1,0:T(8,128)(2,1)S(1)} %fusion.1), channel_id=1, source_target_pairs={{0,3},{1,0},{2,1},{3,2},{4,7},{5,4},{6,5},{7,6},{8,11},{9,8},{10,9... | collective-permute-start | bytes 1769480 | tf_op jit(solution)/shard_map/ppermute | solution.py:188
  157.0 10.4 %collective-permute-start.22 = (f16[4,96,768]{2,1,0:T(8,128)(2,1)S(1)}, f16[4,96,768]{2,1,0:T(8,128)(2,1)S(1)}, u32[]{:S(2)}, u32[]{:S(2)}) collective-permute-start(f16[4,96,768]{2,1,0:T(8,128)(2,1)S(1)} %fusion.2), channel_id=1, source_target_pairs={{0,1},{1,2},{2,3},{3,0},{4,5},{5,6},{6,7},{7,4},{8,9},{9,10},{10,1... | collective-permute-start | bytes 1769480 | tf_op jit(solution)/shard_map/ppermute | solution.py:188
  157.0 10.3 %collective-permute-start.23 = (f16[4,96,768]{2,1,0:T(8,128)(2,1)S(1)}, f16[4,96,768]{2,1,0:T(8,128)(2,1)S(1)}, u32[]{:S(2)}, u32[]{:S(2)}) collective-permute-start(f16[4,96,768]{2,1,0:T(8,128)(2,1)S(1)} %fusion.3), channel_id=1, source_target_pairs={{0,3},{1,0},{2,1},{3,2},{4,7},{5,4},{6,5},{7,6},{8,11},{9,8},{10,9... | collective-permute-start | bytes 1769480 | tf_op jit(solution)/shard_map/ppermute | solution.py:188
  167.4 9.1 %collective-permute-start.21 = (f16[2,96,768]{2,1,0:T(8,128)(2,1)S(1)}, f16[2,96,768]{2,1,0:T(8,128)(2,1)S(1)}, u32[]{:S(2)}, u32[]{:S(2)}) collective-permute-start(f16[2,96,768]{2,1,0:T(8,128)(2,1)S(1)} %get-tuple-element.100), channel_id=1, source_target_pairs={{0,3},{1,0},{2,1},{3,2},{4,7},{5,4},{6,5},{7,6},{8,11},{9,8},{10,9... | collective-permute-start | bytes 884744 | tf_op jit(solution)/shard_map/ppermute | solution.py:188
  167.4 10.3 %collective-permute-start.20 = (f16[2,96,768]{2,1,0:T(8,128)(2,1)S(1)}, f16[2,96,768]{2,1,0:T(8,128)(2,1)S(1)}, u32[]{:S(2)}, u32[]{:S(2)}) collective-permute-start(f16[2,96,768]{2,1,0:T(8,128)(2,1)S(1)} %get-tuple-element.101), channel_id=1, source_target_pairs={{0,1},{1,2},{2,3},{3,0},{4,5},{5,6},{6,7},{7,4},{8,9},{9,10},{10,1... | collective-permute-start | bytes 884744 | tf_op jit(solution)/shard_map/ppermute | solution.py:188
  177.7 19.0 %collective-permute-start.26 = (bf16[768,3072]{1,0:T(8,128)(2,1)}, bf16[768,3072]{1,0:T(8,128)(2,1)}, u32[]{:S(2)}, u32[]{:S(2)}) collective-permute-start(bf16[768,3072]{1,0:T(8,128)(2,1)} %collective-permute-done.17.refs_3_), channel_id=1, source_target_pairs={{0,8},{24,16},{32,40},{56,48},{64,72},{88,80},{96,104},{120,112},{... | collective-permute-start | bytes 14155784 | tf_op jit(solution)/shard_map/ppermute | solution.py:184
  190.6 28.3 %collective-permute-start.29 = (bf16[768,3072]{1,0:T(8,128)(2,1)}, bf16[768,3072]{1,0:T(8,128)(2,1)}, u32[]{:S(2)}, u32[]{:S(2)}) collective-permute-start(bf16[768,3072]{1,0:T(8,128)(2,1)} %collective-permute-done.18.refs_6_), channel_id=1, source_target_pairs={{16,24},{48,56},{80,88},{112,120},{17,25},{49,57},{81,89},{113,121... | collective-permute-start | bytes 14155784 | tf_op jit(solution)/shard_map/ppermute | solution.py:184
  191.8 27.0 %collective-permute-start.25 = (f16[2,96,768]{2,1,0:T(8,128)(2,1)}, f16[2,96,768]{2,1,0:T(8,128)(2,1)}, u32[]{:S(2)}, u32[]{:S(2)}) collective-permute-start(f16[2,96,768]{2,1,0:T(8,128)(2,1)} %get-tuple-element.98), channel_id=1, source_target_pairs={{0,3},{1,0},{2,1},{3,2},{4,7},{5,4},{6,5},{7,6},{8,11},{9,8},{10,9... | collective-permute-start | bytes 884744 | tf_op jit(solution)/shard_map/ppermute | solution.py:188
  193.3 25.6 %collective-permute-start.24 = (f16[2,96,768]{2,1,0:T(8,128)(2,1)}, f16[2,96,768]{2,1,0:T(8,128)(2,1)}, u32[]{:S(2)}, u32[]{:S(2)}) collective-permute-start(f16[2,96,768]{2,1,0:T(8,128)(2,1)} %get-tuple-element.99), channel_id=1, source_target_pairs={{0,1},{1,2},{2,3},{3,0},{4,5},{5,6},{6,7},{7,4},{8,9},{9,10},{10,1... | collective-permute-start | bytes 884744 | tf_op jit(solution)/shard_map/ppermute | solution.py:188
  215.1 23.2 %collective-permute-start.27 = (f16[4,96,768]{2,1,0:T(8,128)(2,1)}, f16[4,96,768]{2,1,0:T(8,128)(2,1)S(1)}, u32[]{:S(2)}, u32[]{:S(2)}) collective-permute-start(f16[4,96,768]{2,1,0:T(8,128)(2,1)} %fusion.4), channel_id=1, source_target_pairs={{0,1},{1,2},{2,3},{3,0},{4,5},{5,6},{6,7},{7,4},{8,9},{9,10},{10,1... | collective-permute-start | bytes 1769480 | tf_op jit(solution)/shard_map/ppermute | solution.py:188
  216.6 21.7 %collective-permute-start.28 = (f16[4,96,768]{2,1,0:T(8,128)(2,1)}, f16[4,96,768]{2,1,0:T(8,128)(2,1)}, u32[]{:S(2)}, u32[]{:S(2)}) collective-permute-start(f16[4,96,768]{2,1,0:T(8,128)(2,1)} %fusion.5), channel_id=1, source_target_pairs={{0,3},{1,0},{2,1},{3,2},{4,7},{5,4},{6,5},{7,6},{8,11},{9,8},{10,9... | collective-permute-start | bytes 1769480 | tf_op jit(solution)/shard_map/ppermute | solution.py:188
  247.4 11.1 %collective-permute-start.33 = (f16[4,96,768]{2,1,0:T(8,128)(2,1)S(1)}, f16[4,96,768]{2,1,0:T(8,128)(2,1)S(1)}, u32[]{:S(2)}, u32[]{:S(2)}) collective-permute-start(f16[4,96,768]{2,1,0:T(8,128)(2,1)S(1)} %fusion.6), channel_id=1, source_target_pairs={{0,1},{1,2},{2,3},{3,0},{4,5},{5,6},{6,7},{7,4},{8,9},{9,10},{10,1... | collective-permute-start | bytes 1769480 | tf_op jit(solution)/shard_map/ppermute | solution.py:188
  247.4 12.2 %collective-permute-start.31 = (f16[2,96,768]{2,1,0:T(8,128)(2,1)S(1)}, f16[2,96,768]{2,1,0:T(8,128)(2,1)S(1)}, u32[]{:S(2)}, u32[]{:S(2)}) collective-permute-start(f16[2,96,768]{2,1,0:T(8,128)(2,1)S(1)} %get-tuple-element.85), channel_id=1, source_target_pairs={{0,3},{1,0},{2,1},{3,2},{4,7},{5,4},{6,5},{7,6},{8,11},{9,8},{10,9... | collective-permute-start | bytes 884744 | tf_op jit(solution)/shard_map/ppermute | solution.py:188
  250.1 13.8 %collective-permute-start.32 = (f16[4,96,768]{2,1,0:T(8,128)(2,1)S(1)}, f16[4,96,768]{2,1,0:T(8,128)(2,1)S(1)}, u32[]{:S(2)}, u32[]{:S(2)}) collective-permute-start(f16[4,96,768]{2,1,0:T(8,128)(2,1)S(1)} %fusion.7), channel_id=1, source_target_pairs={{0,3},{1,0},{2,1},{3,2},{4,7},{5,4},{6,5},{7,6},{8,11},{9,8},{10,9... | collective-permute-start | bytes 1769480 | tf_op jit(solution)/shard_map/ppermute | solution.py:188
  258.7 8.2 %collective-permute-start.34 = (f16[2,96,768]{2,1,0:T(8,128)(2,1)S(1)}, f16[2,96,768]{2,1,0:T(8,128)(2,1)S(1)}, u32[]{:S(2)}, u32[]{:S(2)}) collective-permute-start(f16[2,96,768]{2,1,0:T(8,128)(2,1)S(1)} %fusion.31), channel_id=1, source_target_pairs={{0,1},{1,2},{2,3},{3,0},{4,5},{5,6},{6,7},{7,4},{8,9},{9,10},{10,1... | collective-permute-start | bytes 884744 | tf_op jit(solution)/shard_map/ppermute | solution.py:188
  258.8 15.6 %collective-permute-start.36 = (f16[4,96,768]{2,1,0:T(8,128)(2,1)S(1)}, f16[4,96,768]{2,1,0:T(8,128)(2,1)S(1)}, u32[]{:S(2)}, u32[]{:S(2)}) collective-permute-start(f16[4,96,768]{2,1,0:T(8,128)(2,1)S(1)} %fusion.8), channel_id=1, source_target_pairs={{0,32},{32,64},{64,96},{96,0},{1,33},{33,65},{65,97},{97,1},{2,34}... | collective-permute-start | bytes 1769480 | tf_op jit(solution)/shard_map/ppermute | solution.py:184
  280.3 22.4 %collective-permute-start.38 = (f16[4,96,768]{2,1,0:T(8,128)(2,1)S(1)}, f16[4,96,768]{2,1,0:T(8,128)(2,1)S(1)}, u32[]{:S(2)}, u32[]{:S(2)}) collective-permute-start(f16[4,96,768]{2,1,0:T(8,128)(2,1)S(1)} %fusion.10), channel_id=1, source_target_pairs={{0,16},{1,17},{2,18},{3,19},{8,24},{9,25},{10,26},{11,27},{16,4},{... | collective-permute-start | bytes 1769480 | tf_op jit(solution)/shard_map/ppermute | solution.py:200
  294.0 11.0 %collective-permute-start.39 = (f16[4,96,768]{2,1,0:T(8,128)(2,1)S(1)}, f16[4,96,768]{2,1,0:T(8,128)(2,1)S(1)}, u32[]{:S(2)}, u32[]{:S(2)}) collective-permute-start(f16[4,96,768]{2,1,0:T(8,128)(2,1)S(1)} %fusion.11), channel_id=1, source_target_pairs={{0,20},{1,21},{2,22},{3,23},{8,28},{9,29},{10,30},{11,31},{16,0},{... | collective-permute-start | bytes 1769480 | tf_op jit(solution)/shard_map/ppermute | solution.py:200
  302.7 7.5 %collective-permute-start.42 = (f16[2,96,768]{2,1,0:T(8,128)(2,1)S(1)}, f16[2,96,768]{2,1,0:T(8,128)(2,1)S(1)}, u32[]{:S(2)}, u32[]{:S(2)}) collective-permute-start(f16[2,96,768]{2,1,0:T(8,128)(2,1)S(1)} %fusion.15), channel_id=1, source_target_pairs={{0,16},{1,17},{2,18},{3,19},{8,24},{9,25},{10,26},{11,27},{16,4},{... | collective-permute-start | bytes 884744 | tf_op jit(solution)/shard_map/ppermute | solution.py:200
  318.1 9.7 %collective-permute-start.41 = (f16[96,768]{1,0:T(8,128)(2,1)S(1)}, f16[96,768]{1,0:T(8,128)(2,1)S(1)}, u32[]{:S(2)}, u32[]{:S(2)}) collective-permute-start(f16[96,768]{1,0:T(8,128)(2,1)S(1)} %multiply_convert_fusion), channel_id=1, source_target_pairs={{16,24},{24,16},{48,56},{56,48},{80,88},{88,80},{112,120},{120,112... | collective-permute-start | bytes 442376 | tf_op jit(solution)/shard_map/ppermute | solution.py:184
  350.8 9.4 %collective-permute-start.45 = (f16[768,96]{0,1:T(8,128)(2,1)S(1)}, f16[768,96]{0,1:T(8,128)(2,1)S(1)}, u32[]{:S(2)}, u32[]{:S(2)}) collective-permute-start(f16[768,96]{0,1:T(8,128)(2,1)S(1)} %squeeze.198), channel_id=1, source_target_pairs={{0,104},{8,112},{16,120},{24,0},{32,8},{40,16},{48,24},{56,32},{64... | collective-permute-start | bytes 442376 | tf_op jit(solution)/shard_map/ppermute | solution.py:184
  (27 other events, 277.2 us)

commit v2 on v1

v2 whole, which is shorter than its diff:
```python
import functools

import jax
import jax.numpy as jnp
import numpy as np
from jax import lax
from jax.experimental import pallas as pl
from jax.experimental.pallas import tpu as pltpu
from jax.sharding import PartitionSpec as P

ROWS = 768
HALF = 3072
PART = 96
PLANES = 4
WIDE = 256
freq_point = 0.5

OWN, SIB, FAR_A, FAR_A_SIB, FAR_B, FAR_B_SIB, HALO_A, HALO_B, HALO_A_SIB, HALO_B_SIB, MINOR = range(11)

WHERE = [
    {"A0": OWN, "A1": SIB, "A2": FAR_B, "A3": FAR_A_SIB, "P0": HALO_A, "B3": MINOR},
    {"A1": OWN, "A0": SIB, "A3": FAR_A, "A2": FAR_B_SIB, "P1": HALO_B},
    {"A2": OWN, "A3": SIB, "A0": FAR_A, "A1": FAR_B_SIB, "B2": HALO_B, "B3": HALO_A_SIB, "P0": MINOR},
    {"A3": OWN, "A2": SIB, "A1": FAR_B, "A0": FAR_A_SIB, "B3": HALO_A, "B2": HALO_B_SIB},
]

BATCHES = [
    [["A0A0", "P0A1"],
     ["A1A0", "A1A1"],
     ["A2A2", "A0A0"],
     ["A3A2", "A3A3"]],
    [["A3A1", "P0A3"],
     ["A3A0", "A3A3"],
     ["A0B3", "A2B3"],
     ["A3A0", "A2A0"]],
    [["P0A2", "A2A1"],
     ["P1A2", "P1A3"],
     ["P0A1", "A0B2"],
     ["A1A0", "A1A1"]],
    [["A2A2", "A2B3"],
     ["A3A2", "A2A0"],
     ["A2A1", "A3A1"],
     ["A1B3", "A1B2"]],
]
MOVED = [["A0B1", "A0B3", "A0B2", None], [None, None, "A1B2", "A1B3"],
         [None, None, "A0B1", None], [None, None, None, None]]
ENTRIES = [
    [["A0A0", "A0B3", "A0B2", "A0B1"], ["A2A2", "A2A1", "A3A1", "A2B3"]],
    [["A1A1", "A1A0", "A1B3", "A1B2"], ["A3A3", "A3A2", "A2A0", "A3A0"]],
]
def batch_tables(batch, sources):
    held_most = 0
    plans = []
    for role, tiles in enumerate(batch):
        held = []
        first = []
        for step, tile in enumerate(tiles):
            for block in (tile[:2], tile[2:]):
                if block not in held:
                    held.append(block)
                    first.append(step)
        plans.append((held, first))
        held_most = max(held_most, len(held))
    rows = []
    for role, tiles in enumerate(batch):
        held, first = plans[role]
        left = [held.index(tile[:2]) for tile in tiles]
        right = [held.index(tile[2:]) for tile in tiles]
        fresh = [int(i == 0 or left[i] != left[i - 1]) for i in range(len(tiles))]
        pad = held_most - len(held)
        source = [sources.index(WHERE[role][block]) for block in held] + [-1] * pad
        rows.append(left + right + fresh + source + first + [-1] * pad)
    return np.array(rows, np.int32), held_most


def tiles_kernel(count, held_most, sources, table, weight, *refs):
    source_refs = refs[:sources]
    out, held, scaled, sems = refs[sources:]
    step = pl.program_id(0)
    source_at = 3 * count
    first_at = source_at + held_most

    @pl.when(step == 0)
    def _():
        for j in range(held_most):
            for k in range(sources):
                @pl.when(table[source_at + j] == k)
                def _():
                    pltpu.make_async_copy(source_refs[k], held.at[j], sems.at[j]).start()

    def wait(block):
        for j in range(held_most):
            @pl.when((table[first_at + j] == step) & (block == j))
            def _():
                pltpu.make_async_copy(source_refs[0], held.at[j], sems.at[j]).wait()

    left = table[step]
    right = table[count + step]
    wait(left)

    @pl.when(table[2 * count + step] == 1)
    def _():
        @pl.loop(0, ROWS // 32)
        def _(i):
            rows = pl.ds(pl.multiple_of(i * 32, 32), 32)
            scaled[rows, :] = (held[left, rows, :].astype(jnp.float32) * weight[...]).astype(jnp.bfloat16)

    @pl.when(left != right)
    def _():
        wait(right)

    here = table[first_at + held_most]
    for n in range(ROWS // WIDE):
        columns = slice(n * WIDE, (n + 1) * WIDE)
        acc = lax.dot_general(
            scaled[...], held[right, columns, :],
            (((1,), (1,)), ((), ())), preferred_element_type=jnp.float32)
        for y in range(4):
            at = lax.rem(y + 4 - here, 4)
            for h in range(2):
                first = (h * 4 + y) * PART
                out[at, h, 0, :, columns] = acc[first:first + PART]


def tile_batch(batch, table_row, held_most, weight, sources):
    count = len(batch[0])
    return pl.pallas_call(
        functools.partial(tiles_kernel, count, held_most, len(sources)),
        grid_spec=pltpu.PrefetchScalarGridSpec(
            num_scalar_prefetch=1,
            grid=(count,),
            in_specs=[pl.BlockSpec((1, HALF), lambda i, t: (0, 0))]
            + [pl.BlockSpec(memory_space=pl.ANY)] * len(sources),
            out_specs=pl.BlockSpec((4, 2, 1, PART, ROWS), lambda i, t: (0, 0, i, 0, 0)),
            scratch_shapes=[
                pltpu.VMEM((held_most, ROWS, HALF), jnp.bfloat16),
                pltpu.VMEM((ROWS, HALF), jnp.bfloat16),
                pltpu.SemaphoreType.DMA((held_most,)),
            ],
        ),
        out_shape=jax.ShapeDtypeStruct((4, 2, count, PART, ROWS), jnp.float32),
        compiler_params=pltpu.CompilerParams(
            dimension_semantics=("arbitrary",), vmem_limit_bytes=56 * 1024 * 1024),
        cost_estimate=pl.CostEstimate(
            flops=count * ROWS * ROWS,
            bytes_accessed=count * ROWS * ROWS,
            transcendentals=0),
    )(table_row, weight, *sources)


def lookup(table, index):
    blocks = table.shape[0]
    high = lax.shift_right_logical(index, 7)
    low = jnp.bitwise_and(index, 127)
    pairs = index.shape[1]
    hot = jnp.where(lax.broadcasted_iota(jnp.int32, (blocks, pairs), 0) == high, 1.0, 0.0).astype(jnp.bfloat16)
    rest = table
    column = jnp.zeros((128, pairs), jnp.float32)
    for _ in range(3):
        piece = rest.astype(jnp.bfloat16)
        rest = rest - piece.astype(jnp.float32)
        column = column + lax.dot_general(
            piece, hot, (((0,), (0,)), ((), ())), preferred_element_type=jnp.float32)
    mask = lax.broadcasted_iota(jnp.int32, (128, pairs), 0) == low
    return jnp.sum(jnp.where(mask, column, 0.0), axis=0, keepdims=True)


def gap_kernel(occ_index, virt_index, occ_energy, virt_energy, gap):
    gap[...] = lookup(virt_energy[...], virt_index[...]) - lookup(occ_energy[...], occ_index[...])


def pair_gaps(occ_index, virt_index, occ_energy, virt_energy):
    block = 512
    pairs = occ_index.shape[0]
    occ_table = occ_energy.reshape(-1, 128)
    virt_table = virt_energy.reshape(-1, 128)
    line = pl.BlockSpec((1, block), lambda i: (0, i))
    return pl.pallas_call(
        gap_kernel,
        grid=(pairs // block,),
        in_specs=[line, line,
                  pl.BlockSpec(occ_table.shape, lambda i: (0, 0)),
                  pl.BlockSpec(virt_table.shape, lambda i: (0, 0))],
        out_specs=line,
        out_shape=jax.ShapeDtypeStruct((1, pairs), jnp.float32),
        cost_estimate=pl.CostEstimate(flops=6 * 128 * 288 * pairs, bytes_accessed=200000, transcendentals=0),
    )(occ_index[None, :], virt_index[None, :], occ_table, virt_table)


def halves_kernel(x_lo, coeffs, mine, other, largest):
    for low in range(2):
        @pl.when(x_lo[0] == low)
        def _():
            mine[...] = coeffs[:, low * HALF:(low + 1) * HALF]
            other[...] = coeffs[:, (1 - low) * HALF:(2 - low) * HALF]

    @pl.when(pl.program_id(0) == 0)
    def _():
        largest[...] = jnp.zeros_like(largest)

    top = jnp.zeros((coeffs.shape[0], 128), jnp.float32)
    for c in range(coeffs.shape[1] // 128):
        top = jnp.maximum(top, jnp.abs(coeffs[:, c * 128:(c + 1) * 128].astype(jnp.float32)))
    largest[...] = jnp.maximum(largest[...], jnp.max(top.reshape(-1, 8, 128), axis=0))


def cut_in_halves(x_lo, coeffs):
    half = jax.ShapeDtypeStruct((ROWS, HALF), jnp.bfloat16)
    block = pl.BlockSpec((PART, HALF), lambda i, t: (i, 0))
    return pl.pallas_call(
        halves_kernel,
        grid_spec=pltpu.PrefetchScalarGridSpec(
            num_scalar_prefetch=1,
            grid=(ROWS // PART,),
            in_specs=[pl.BlockSpec((PART, 2 * HALF), lambda i, t: (i, 0))],
            out_specs=[block, block, pl.BlockSpec((8, 128), lambda i, t: (0, 0))],
        ),
        out_shape=[half, half, jax.ShapeDtypeStruct((8, 128), jnp.float32)],
        compiler_params=pltpu.CompilerParams(vmem_limit_bytes=24 * 1024 * 1024),
        cost_estimate=pl.CostEstimate(flops=0, bytes_accessed=PART * ROWS, transcendentals=0),
    )(x_lo[None], coeffs)


def moves(pairs):
    return [(z * 4 + src, (z + dz) % PLANES * 4 + dst) for z in range(PLANES) for src, dst, dz in pairs]


def aux_permute(value, pairs):
    return lax.ppermute(value, "aux", moves(pairs))


def y_permute(value, by):
    return lax.ppermute(value, "pair", [(h * 4 + y, h * 4 + (y + by) % 4) for h in range(2) for y in range(4)])


def x_permute(value, by):
    perm = []
    for z in range(PLANES):
        for x in range(4):
            to = (x + by) % 4
            for core in range(2):
                for y in range(4):
                    source = (z * 4 + x % 2 * 2 + core) * 8 + x // 2 * 4 + y
                    perm.append((source, (z * 4 + to % 2 * 2 + core) * 8 + to // 2 * 4 + y))
    return lax.ppermute(value, ("aux", "pair"), perm)


def both_ways(permute, up, down):
    return lax.optimization_barrier((permute(up, 1), permute(down, -1)))


def ring_sum(part, permute, scales):
    count = part(0, 0).shape[0]
    up, down = both_ways(permute, narrow(jnp.concatenate([part(2, 0), part(1, 1)]), scales),
                         narrow(jnp.concatenate([part(2, 1), part(3, 0)]), scales))
    up_more, down_more = both_ways(permute, narrow(part(1, 0) + wide(up[:count], scales), scales),
                                   narrow(part(3, 1) + wide(down[:count], scales), scales))
    zero = part(0, 0) + wide(down[count:], scales) + wide(up_more, scales)
    one = part(0, 1) + wide(up[count:], scales) + wide(down_more, scales)
    return zero, one


def slot_names(role):
    names = []
    for batch in BATCHES:
        names += [(tile, h) for h in range(2) for tile in batch[role]]
    early, late = MOVED[role][:2], MOVED[role][2:]
    names += [(tile, h) for h in range(2) for tile in early]
    names += [(tile, h) for h in range(2) for tile in late]
    return names


def entry_table():
    rows = []
    for role in range(4):
        names = slot_names(role)
        for x_hi in range(2):
            row = []
            for k in range(4):
                to = (x_hi * 2 + role // 2 + k) % 4
                row += [names.index((tile, to // 2)) for tile in ENTRIES[role % 2][to % 2]]
            rows.append(row)
    return np.array(rows, np.int32)


def pick_kernel(table, slots, parts):
    for i in range(16):
        parts[i] = slots[table[i]]


def pick_parts(table, slots):
    return pl.pallas_call(
        pick_kernel,
        in_specs=[pl.BlockSpec(memory_space=pltpu.SMEM), pl.BlockSpec(memory_space=pltpu.VMEM)],
        out_specs=pl.BlockSpec(memory_space=pltpu.VMEM),
        out_shape=jax.ShapeDtypeStruct((16, PART, ROWS), jnp.float32),
        compiler_params=pltpu.CompilerParams(vmem_limit_bytes=20 * 1024 * 1024),
        cost_estimate=pl.CostEstimate(flops=0, bytes_accessed=PART * ROWS, transcendentals=0),
    )(table, slots)


def largest_round(value, permute):
    got = [permute(value, by) for by in (1, 2, 3)]
    return jnp.maximum(jnp.maximum(value, got[0]), jnp.maximum(got[1], got[2]))


def z_permute(value, by):
    return aux_permute(value, [(r, r, by) for r in range(4)])


def scales_of(largest):
    bound = 8.0 * HALF * 4 * largest * largest * 4.0
    scale = 32768.0 / jnp.maximum(bound, 1e-30)
    return scale, 1.0 / scale


def narrow(value, scales):
    return (value * scales[0]).astype(jnp.float16)


def wide(value, scales):
    return value.astype(jnp.float32) * scales[1]


def after(value, other):
    return lax.optimization_barrier((value, other))[0]


def local(coeffs, occ_index, virt_index, occ_energy, virt_energy):
    role = lax.rem(lax.axis_index("aux"), 4)
    x_lo = role // 2
    x_hi = lax.axis_index("pair") // 4
    y = lax.rem(lax.axis_index("pair"), 4)

    mine, other, largest = cut_in_halves(x_lo.astype(jnp.int32), coeffs)
    side = [(0, 2, 0), (1, 3, 0), (2, 0, 0), (3, 1, 0)]
    near = [aux_permute(largest, side), z_permute(largest, 1), z_permute(largest, -1)]
    mine, other, near = lax.optimization_barrier((mine, other, near))
    halo_a = aux_permute(mine, [(0, 0, -1), (3, 3, 1)])
    far_a = aux_permute(other, [(0, 2, 0), (3, 1, 0)])
    sib = aux_permute(mine, [(0, 1, 0), (1, 0, 0), (2, 3, 0), (3, 2, 0)])

    largest = jnp.maximum(jnp.maximum(largest, near[0]), jnp.maximum(near[1], near[2]))
    largest = jnp.maximum(largest, aux_permute(largest, [(0, 1, 0), (1, 0, 0), (2, 3, 0), (3, 2, 0)]))
    largest = largest_round(largest, y_permute)
    early = scales_of(jnp.max(largest))

    occ_index, virt_index = after([occ_index, virt_index], mine)
    begin = x_lo * HALF
    gap = pair_gaps(
        lax.dynamic_slice_in_dim(occ_index, begin, HALF),
        lax.dynamic_slice_in_dim(virt_index, begin, HALF),
        occ_energy, virt_energy)
    weight = -4.0 * gap / (gap * gap + freq_point * freq_point)

    plans = []
    for batch in BATCHES:
        used = sorted({WHERE[r][t[i:i + 2]] for r in range(4) for t in batch[r] for i in (0, 2)})
        table, held_most = batch_tables(batch, used)
        row = lax.dynamic_index_in_dim(jnp.asarray(table), role, axis=0, keepdims=False)
        row = jnp.concatenate([row, y[None].astype(jnp.int32)])
        plans.append([used, row, held_most])
    entries = lax.dynamic_index_in_dim(jnp.asarray(entry_table()), role * 2 + x_hi, axis=0, keepdims=False)
    rows = [plan[1] for plan in plans]
    far_a, halo_a, sib, early, largest, weight, entries, rows = lax.optimization_barrier(
        (far_a, halo_a, sib, early, largest, weight, entries, rows))

    far_b = aux_permute(after(other, far_a), [(1, 3, 0), (2, 0, 0)])
    halo_b = aux_permute(after(mine, halo_a), [(1, 1, -1), (2, 2, 1)])
    far_a_sib = aux_permute(far_a, [(1, 0, 0), (2, 3, 0)])
    halo_a_sib = aux_permute(halo_a, [(3, 2, 0)])
    minor = aux_permute(far_a, [(1, 0, 1), (2, 2, -1)])

    held = {OWN: mine, SIB: sib, FAR_A: far_a, HALO_A: halo_a}

    def tiles(number):
        used, _, held_most = plans[number]
        return tile_batch(BATCHES[number], rows[number], held_most, weight, [held[s] for s in used])

    def first_sends(partial, scales):
        return [narrow(jnp.concatenate([partial[2, 0], partial[1, 1]]), scales),
                narrow(jnp.concatenate([partial[2, 1], partial[3, 0]]), scales)]

    def first_round(sends):
        return [y_permute(sends[0], 1), y_permute(sends[1], -1)]

    def second_sends(partial, got, scales):
        return [narrow(partial[1, 0] + wide(got[0][:2], scales), scales),
                narrow(partial[3, 1] + wide(got[1][:2], scales), scales)]

    def finish(partial, got, more, scales):
        zero = partial[0, 0] + wide(got[1][2:], scales) + wide(more[0], scales)
        one = partial[0, 1] + wide(got[0][2:], scales) + wide(more[1], scales)
        return [zero, one]

    partial0 = tiles(0)
    sends0 = first_sends(partial0, early)
    held[FAR_A_SIB], held[HALO_A_SIB] = after([far_a_sib, halo_a_sib], sends0)
    got0 = first_round(sends0)
    partial1 = tiles(1)
    sends1 = first_sends(partial1, early)
    got0, sends1 = lax.optimization_barrier((got0, sends1))
    got1 = first_round(sends1)
    sends0 = second_sends(partial0, got0, early)
    more0 = first_round(sends0)
    far_b, halo_b, minor, got1, largest = lax.optimization_barrier(
        (far_b, halo_b, minor, got1, largest, sends0))[:5]
    more1 = first_round(second_sends(partial1, got1, early))
    held[FAR_B], held[HALO_B], held[MINOR] = far_b, halo_b, minor
    held[FAR_B_SIB] = aux_permute(far_b, [(0, 1, 0), (3, 2, 0)])
    held[HALO_B_SIB] = aux_permute(halo_b, [(2, 3, 0)])
    largest = jnp.maximum(largest, x_permute(largest, 2))
    largest = jnp.maximum(largest, z_permute(largest, 2))
    largest = jnp.maximum(largest, aux_permute(largest, side))
    late = scales_of(jnp.max(largest))
    partial2 = tiles(2)
    sends2 = first_sends(partial2, late)
    more0, more1 = after([more0, more1], sends2)
    got2 = first_round(sends2)
    rows[3], more0 = lax.optimization_barrier((rows[3], more0, sends2))[:2]
    partial3 = tiles(3)
    total0 = finish(partial0, got0, more0, early)
    total1 = finish(partial1, got1, more1, early)
    moved0 = jnp.stack([total0[0][1], total1[0][1], total0[1][1], total1[1][1]])
    moved0 = wide(aux_permute(narrow(moved0, late), [(0, 0, 1)]), late)
    sends3 = first_sends(partial3, late)
    got2 = after(got2, partial3)
    sends2 = second_sends(partial2, got2, late)
    more2 = first_round(sends2)
    sends3 = after(sends3, sends2)
    got3 = first_round(sends3)
    more2 = after(more2, sends3)
    total2 = finish(partial2, got2, more2, late)
    moved2 = aux_permute(narrow(jnp.concatenate(total2), late), [(0, 0, 1), (1, 1, 1), (2, 2, 1)])
    moved2 = wide(moved2, late)
    more3 = both_ways(y_permute, *second_sends(partial3, got3, late))
    total3 = finish(partial3, got3, more3, late)
    slots = jnp.concatenate(total0 + total1 + total2 + total3 + [moved0, moved2])
    parts = pick_parts(entries, slots).reshape(4, 2, 2, PART, ROWS)

    def x_part(k, d):
        return parts[k, d]

    zero, one = ring_sum(x_part, x_permute, late)
    final = [zero[0], zero[1], one[0], one[1]]

    crossed = narrow(jnp.stack(final[1:]), late).reshape(3, PART, 8, PART)
    crossed = lax.all_to_all(crossed, "pair", split_axis=2, concat_axis=1, tiled=True)
    crossed = crossed.reshape(3, ROWS, PART)

    swapped = aux_permute(after(narrow(one[0], late), crossed), [(2, 3, 0), (3, 2, 0)])
    lower = [final[0], final[1], jnp.where(x_lo == 1, wide(swapped, late), final[2]), final[3]]

    back = [
        [(0, 3, -1), (1, 0, 0), (2, 1, 0), (3, 2, 0)],
        [(0, 2, -1), (1, 3, -1), (2, 1, 0), (3, 0, 0)],
        [(0, 1, -1), (1, 2, -1), (2, 3, -1), (3, 0, 0)],
    ]
    upper = [wide(aux_permute(crossed[o], back[o]), late).T for o in range(3)]
    return jnp.stack(lower[::-1] + upper)


def solution(mesh):
    return jax.shard_map(
        local,
        mesh=mesh,
        in_specs=(P("aux", "pair"), P("pair"), P("pair"), P(), P()),
        out_specs=P(None, ("aux", "pair"), None),
        check_vma=False,
    )
```

time: 368 us -> 314 us (0.85); the launches traced: 361 us -> 313 us
  waiting for transfers between devices: 111 us -> 77.8 us
  other arithmetic: 30.1 us -> 20.6 us
  starting transfers between devices: 97.6 us -> 106 us
  Pallas kernels: 76.4 us -> 69.5 us
  local copies, waits for them, and re-layouts: 25.8 us -> 19.6 us
    ppermute x19, waiting for transfers between devices: 40.9 us -> 13.7 us  [y_permute(): lax.ppermute(value, 'pair', [(h * 4 + y, h * 4 + (y + by) % 4) for h in r...]
    dynamic_slice x2 -> x0, local copies, waits for them, and re-layouts: 9.62 us -> none  [the longest x1 4.83 us: local(): other = lax.dynamic_slice_in_dim(coeffs, (1 - x_lo) * HALF, HALF, axis=1)]
    ppermute x20 -> x22, starting transfers between devices: 56.9 us -> 65.8 us  [aux_permute(): return lax.ppermute(value, 'aux', moves(pairs))]
    ppermute x7 -> x5, starting transfers between devices: 21.4 us -> 14.8 us  [x_permute(): return lax.ppermute(value, ('aux', 'pair'), perm)]
    squeeze x4, local copies, waits for them, and re-layouts: 0.7 us -> 7.07 us  [first_sends(): partial[2, 1]]
    unnamed x13 -> x14, other arithmetic: 13.4 us -> 7.25 us
    ppermute x19, starting transfers between devices: 19.2 us -> 24.9 us  [y_permute(): lax.ppermute(value, 'pair', [(h * 4 + y, h * 4 + (y + by) % 4) for h in r...]
    ppermute x20 -> x22, waiting for transfers between devices: 52.4 us -> 46.7 us  [aux_permute(): return lax.ppermute(value, 'aux', moves(pairs))]
where the time goes in v2:
time: 314 us; the launch traced here: 313 us
  starting transfers between devices  106 us (34%)
  waiting for transfers between devices  77.8 us (25%)
  Pallas kernels  69.5 us (22%)
  other arithmetic  20.6 us (7%)
  local copies, waits for them, and re-layouts  19.6 us (6%)
  blocking collectives  16.5 us (5%)
  between operations  3.25 us (1%)
    ppermute x22, starting transfers between devices, aux_permute(): return lax.ppermute(value, 'aux', moves(pairs))  65.8 us
    pallas_call x4, Pallas kernels, tile_batch(): pl.pallas_call(functools.partial(tiles_kernel, count, held_most, len(sour...  58.9 us
    ppermute x22, waiting for transfers between devices, aux_permute(): return lax.ppermute(value, 'aux', moves(pairs))  46.7 us
    ppermute x19, starting transfers between devices, y_permute(): lax.ppermute(value, 'pair', [(h * 4 + y, h * 4 + (y + by) % 4) for h in r...  24.9 us
    ppermute x5, waiting for transfers between devices, x_permute(): return lax.ppermute(value, ('aux', 'pair'), perm)  17.4 us
    all_to_all x1, blocking collectives, local(): lax.all_to_all(crossed, 'pair', split_axis=2, concat_axis=1, tiled=True)  16.5 us
    ppermute x5, starting transfers between devices, x_permute(): return lax.ppermute(value, ('aux', 'pair'), perm)  14.8 us
    ppermute x19, waiting for transfers between devices, y_permute(): lax.ppermute(value, 'pair', [(h * 4 + y, h * 4 + (y + by) % 4) for h in r...  13.7 us
  transfers between devices with their start and end apart: 46, of which 19 were waited for; matrix products, arithmetic and copies ran while one was open for 10% of the time, Pallas kernels for 20%

profile of v2, /device:TPU:3, one launch (start us, length us, event | category | flops | bytes accessed | tf_op | source)
XLA Modules:
  0.0 312.8 jit_solution(12230115397438269745)
XLA Ops:
  0.0 3.7 %copy-done.1 = bf16[768,6144]{1,0:T(8,128)(2,1)S(1)} copy-done((bf16[768,6144]{1,0:T(8,128)(2,1)S(1)}, bf16[768,6144]{1,0:T(8,128)(2,1)}, u32[]{:S(2)}) %copy-start.1) | copy-done | bytes 9437208
  3.7 4.9 %shard_map.100 = (bf16[768,3072]{1,0:T(8,128)(2,1)}, bf16[768,3072]{1,0:T(8,128)(2,1)}, f32[8,128]{1,0:T(8,128)S(1)}) custom-call(s32[1]{0:T(128)} %bitcast.x_lo, bf16[768,6144]{1,0:T(8,128)(2,1)S(1)} %copy-done.1), custom_call_target="tpu_custom_call" | custom-call | bytes 73728 | tf_op jit(solution)/shard_map/pallas_call | solution.py:210
  13.7 5.3 %collective-permute-start.3 = (bf16[768,3072]{1,0:T(8,128)(2,1)}, bf16[768,3072]{1,0:T(8,128)(2,1)}, u32[]{:S(2)}, u32[]{:S(2)}) collective-permute-start(bf16[768,3072]{1,0:T(8,128)(2,1)} %get-tuple-element.84), channel_id=1, source_target_pairs={{0,16},{24,8},{32,48},{56,40},{64,80},{88,72},{96,112},{120,104},{... | collective-permute-start | bytes 14155784 | tf_op jit(solution)/shard_map/ppermute | solution.py:229
  19.0 2.9 collective-permute-start.4
  31.2 4.8 %shard_map.101 = f32[1,3072]{1,0:T(1,128)} custom-call(s32[1,3072]{1,0:T(1,128)} %bitcast.252, s32[1,3072]{1,0:T(1,128)} %bitcast.253, f32[32,128]{1,0:T(8,128)} %bitcast.255, f32[256,128]{1,0:T(8,128)} %bitcast.254), custom_call_target="tpu_custom_call" | custom-call | flops 679477248 | bytes 200000 | tf_op jit(solution)/shard_map/pallas_call | solution.py:178
  36.0 2.6 collective-permute-start.8
  43.4 24.7 %collective-permute-done.3.refs_2_.refs_1_ = bf16[768,3072]{1,0:T(8,128)(2,1)} collective-permute-done((bf16[768,3072]{1,0:T(8,128)(2,1)}, bf16[768,3072]{1,0:T(8,128)(2,1)}, u32[]{:S(2)}, u32[]{:S(2)}) %collective-permute-start.3) | collective-permute-done | bytes 4718624 | tf_op jit(solution)/shard_map/ppermute | solution.py:229
  68.1 7.2 %collective-permute-done.4.refs_3_.refs_4_.refs_5_ = bf16[768,3072]{1,0:T(8,128)(2,1)} collective-permute-done((bf16[768,3072]{1,0:T(8,128)(2,1)}, bf16[768,3072]{1,0:T(8,128)(2,1)}, u32[]{:S(2)}, u32[]{:S(2)}) %collective-permute-start.4) | collective-permute-done | bytes 4718624 | tf_op jit(solution)/shard_map/ppermute | solution.py:229
  76.6 5.6 %collective-permute-start.13 = (bf16[768,3072]{1,0:T(8,128)(2,1)}, bf16[768,3072]{1,0:T(8,128)(2,1)}, u32[]{:S(2)}, u32[]{:S(2)}) collective-permute-start(bf16[768,3072]{1,0:T(8,128)(2,1)} %collective-permute-done.4.refs_3_.refs_4_.refs_5_), channel_id=1, source_target_pairs={{24,16},{56,48},{88,80},{120,112},{25,17},{57,49},{89,81},{121,113... | collective-permute-start | bytes 14155784 | tf_op jit(solution)/shard_map/ppermute | solution.py:229
  83.5 2.8 collective-permute-start.17
  86.3 2.9 collective-permute-start.18
  89.2 14.5 %shard_map.102 = f32[4,2,2,96,768]{4,3,2,1,0:T(8,128)} custom-call(s32[13]{0:T(128)} %get-tuple-element.71.table, f32[1,3072]{1,0:T(1,128)} %add_divide_fusion.weight, bf16[768,3072]{1,0:T(8,128)(2,1)} %get-tuple-element.85.refs_0_, bf16[768,3072]{1,0:T(8,128)(2,1)} %collective-permute-done.5.refs_1_.refs_0_, ...), custom_call_target="tpu_custom_call" | custom-call | flops 1179648 | bytes 1179648 | tf_op jit(solution)/shard_map/pallas_call | solution.py:127
  105.7 2.8 collective-permute-start.11
  108.5 15.4 %shard_map.103 = f32[4,2,2,96,768]{4,3,2,1,0:T(8,128)} custom-call(s32[13]{0:T(128)} %get-tuple-element.77.table, f32[1,3072]{1,0:T(1,128)} %add_divide_fusion.weight, bf16[768,3072]{1,0:T(8,128)(2,1)} %get-tuple-element.85.refs_0_, bf16[768,3072]{1,0:T(8,128)(2,1)} %collective-permute-done.5.refs_1_.refs_0_, ...), custom_call_target="tpu_custom_call" | custom-call | flops 1179648 | bytes 1179648 | tf_op jit(solution)/shard_map/pallas_call | solution.py:127
  131.0 6.7 %collective-permute-done.16.refs_3_ = bf16[768,3072]{1,0:T(8,128)(2,1)} collective-permute-done((bf16[768,3072]{1,0:T(8,128)(2,1)}, bf16[768,3072]{1,0:T(8,128)(2,1)}, u32[]{:S(2)}, u32[]{:S(2)}) %collective-permute-start.16) | collective-permute-done | bytes 4718624 | tf_op jit(solution)/shard_map/ppermute | solution.py:229
  137.7 12.7 %collective-permute-start.23 = (bf16[768,3072]{1,0:T(8,128)(2,1)}, bf16[768,3072]{1,0:T(8,128)(2,1)}, u32[]{:S(2)}, u32[]{:S(2)}) collective-permute-start(bf16[768,3072]{1,0:T(8,128)(2,1)} %collective-permute-done.16.refs_3_), channel_id=1, source_target_pairs={{0,8},{24,16},{32,40},{56,48},{64,72},{88,80},{96,104},{120,112},{... | collective-permute-start | bytes 14155784 | tf_op jit(solution)/shard_map/ppermute | solution.py:229
  155.9 3.7 %collective-permute-start.25 = (f32[8,128]{1,0:T(8,128)S(1)}, f32[8,128]{1,0:T(8,128)S(1)}, u32[]{:S(2)}, u32[]{:S(2)}) collective-permute-start(f32[8,128]{1,0:T(8,128)S(1)} %max.44), channel_id=1, source_target_pairs={{0,64},{8,72},{16,80},{24,88},{32,96},{40,104},{48,112},{56,120},{... | collective-permute-start | bytes 12296 | tf_op jit(solution)/shard_map/ppermute | solution.py:229
  162.4 2.3 fusion.53
  167.0 2.7 collective-permute-start.22
  169.7 14.5 %shard_map.104 = f32[4,2,2,96,768]{4,3,2,1,0:T(8,128)} custom-call(s32[15]{0:T(128)} %pad_add_fusion.2.table, f32[1,3072]{1,0:T(1,128)} %add_divide_fusion.weight, bf16[768,3072]{1,0:T(8,128)(2,1)} %collective-permute-done.5.refs_1_.refs_0_, bf16[768,3072]{1,0:T(8,128)(2,1)} %collective-permute-done.3.refs_2_.refs_1_, bf16[768,3072]{1,0:T(8,128)(2,1)} %copy-done.2, ...), custom_call_target="tpu_custom_call" | custom-call | flops 1179648 | bytes 1179648 | tf_op jit(solution)/shard_map/pallas_call | solution.py:127
  187.8 14.5 %shard_map.105 = f32[4,2,2,96,768]{4,3,2,1,0:T(8,128)} custom-call(s32[13]{0:T(128)} %pad_add_fusion.3.table, f32[1,3072]{1,0:T(1,128)} %add_divide_fusion.weight, bf16[768,3072]{1,0:T(8,128)(2,1)} %get-tuple-element.85.refs_0_, bf16[768,3072]{1,0:T(8,128)(2,1)} %collective-permute-done.5.refs_1_.refs_0_, ...), custom_call_target="tpu_custom_call" | custom-call | flops 1179648 | bytes 1179648 | tf_op jit(solution)/shard_map/pallas_call | solution.py:127
  208.6 2.7 collective-permute-start.31
  215.5 5.8 %collective-permute-done.32 = f16[4,96,768]{2,1,0:T(8,128)(2,1)S(1)} collective-permute-done((f16[4,96,768]{2,1,0:T(8,128)(2,1)S(1)}, f16[4,96,768]{2,1,0:T(8,128)(2,1)S(1)}, u32[]{:S(2)}, u32[]{:S(2)}) %collective-permute-start.32) | collective-permute-done | bytes 589856 | tf_op jit(solution)/shard_map/ppermute | solution.py:233
  225.9 6.5 %collective-permute-done.34 = f16[2,96,768]{2,1,0:T(8,128)(2,1)S(1)} collective-permute-done((f16[2,96,768]{2,1,0:T(8,128)(2,1)S(1)}, f16[2,96,768]{2,1,0:T(8,128)(2,1)S(1)}, u32[]{:S(2)}, u32[]{:S(2)}) %collective-permute-start.34) | collective-permute-done | bytes 294944 | tf_op jit(solution)/shard_map/ppermute | solution.py:233
  234.1 9.5 %collective-permute-start.39 = (f16[4,96,768]{2,1,0:T(8,128)(2,1)S(1)}, f16[4,96,768]{2,1,0:T(8,128)(2,1)S(1)}, u32[]{:S(2)}, u32[]{:S(2)}) collective-permute-start(f16[4,96,768]{2,1,0:T(8,128)(2,1)S(1)} %fusion.11), channel_id=1, source_target_pairs={{0,20},{1,21},{2,22},{3,23},{8,28},{9,29},{10,30},{11,31},{16,0},{... | collective-permute-start | bytes 1769480 | tf_op jit(solution)/shard_map/ppermute | solution.py:245
  245.0 7.4 %collective-permute-done.39 = f16[4,96,768]{2,1,0:T(8,128)(2,1)S(1)} collective-permute-done((f16[4,96,768]{2,1,0:T(8,128)(2,1)S(1)}, f16[4,96,768]{2,1,0:T(8,128)(2,1)S(1)}, u32[]{:S(2)}, u32[]{:S(2)}) %collective-permute-start.39) | collective-permute-done | bytes 589856 | tf_op jit(solution)/shard_map/ppermute | solution.py:245
  254.7 4.3 %collective-permute-done.40 = f16[2,96,768]{2,1,0:T(8,128)(2,1)S(1)} collective-permute-done((f16[2,96,768]{2,1,0:T(8,128)(2,1)S(1)}, f16[2,96,768]{2,1,0:T(8,128)(2,1)S(1)}, u32[]{:S(2)}, u32[]{:S(2)}) %collective-permute-start.40) | collective-permute-done | bytes 294944 | tf_op jit(solution)/shard_map/ppermute | solution.py:245
  259.0 3.6 %collective-permute-done.41 = f16[2,96,768]{2,1,0:T(8,128)(2,1)S(1)} collective-permute-done((f16[2,96,768]{2,1,0:T(8,128)(2,1)S(1)}, f16[2,96,768]{2,1,0:T(8,128)(2,1)S(1)}, u32[]{:S(2)}, u32[]{:S(2)}) %collective-permute-start.41) | collective-permute-done | bytes 294944 | tf_op jit(solution)/shard_map/ppermute | solution.py:245
  264.6 15.3 %collective-permute-start.42 = (f16[96,768]{1,0:T(8,128)(2,1)S(1)}, f16[96,768]{1,0:T(8,128)(2,1)S(1)}, u32[]{:S(2)}, u32[]{:S(2)}) collective-permute-start(f16[96,768]{1,0:T(8,128)(2,1)S(1)} %multiply_convert_fusion), channel_id=1, source_target_pairs={{16,24},{24,16},{48,56},{56,48},{80,88},{88,80},{112,120},{120,112... | collective-permute-start | bytes 442376 | tf_op jit(solution)/shard_map/ppermute | solution.py:229
  282.6 16.5 %all_to_all.15 = f16[3,96,8,96]{1,3,0,2:T(8,128)(2,1)S(1)} all-to-all(f16[3,96,8,96]{1,3,0,2:T(8,128)(2,1)S(1)} %fusion.12), channel_id=1, replica_groups=mesh['aux'=16,'pair'=8] {'pair'}, dimensions={2} | all-to-all | bytes 884736 | tf_op jit(solution)/shard_map/all_to_all | solution.py:448
  306.2 2.5 collective-permute-done.44
  309.5 2.5 collective-permute-done.45
  (163 shorter events, 75.6 us)
Async XLA Ops:
  13.7 54.5 %collective-permute-start.3 = (bf16[768,3072]{1,0:T(8,128)(2,1)}, bf16[768,3072]{1,0:T(8,128)(2,1)}, u32[]{:S(2)}, u32[]{:S(2)}) collective-permute-start(bf16[768,3072]{1,0:T(8,128)(2,1)} %get-tuple-element.84), channel_id=1, source_target_pairs={{0,16},{24,8},{32,48},{56,40},{64,80},{88,72},{96,112},{120,104},{... | collective-permute-start | bytes 14155784 | tf_op jit(solution)/shard_map/ppermute | solution.py:229
  19.0 56.4 %collective-permute-start.4 = (bf16[768,3072]{1,0:T(8,128)(2,1)}, bf16[768,3072]{1,0:T(8,128)(2,1)}, u32[]{:S(2)}, u32[]{:S(2)}) collective-permute-start(bf16[768,3072]{1,0:T(8,128)(2,1)} %get-tuple-element.85.refs_0_), channel_id=1, source_target_pairs={{0,96},{24,56},{32,0},{56,88},{64,32},{88,120},{96,64},{120,24},{1... | collective-permute-start | bytes 14155784 | tf_op jit(solution)/shard_map/ppermute | solution.py:229
  21.9 53.4 %collective-permute-start.5 = (bf16[768,3072]{1,0:T(8,128)(2,1)}, bf16[768,3072]{1,0:T(8,128)(2,1)}, u32[]{:S(2)}, u32[]{:S(2)}) collective-permute-start(bf16[768,3072]{1,0:T(8,128)(2,1)} %get-tuple-element.85.refs_0_), channel_id=1, source_target_pairs={{0,8},{8,0},{16,24},{24,16},{32,40},{40,32},{48,56},{56,48},{64,72... | collective-permute-start | bytes 14155784 | tf_op jit(solution)/shard_map/ppermute | solution.py:229
  29.9 8.7 %collective-permute-start.7 = (f32[8,128]{1,0:T(8,128)S(1)}, f32[8,128]{1,0:T(8,128)S(1)}, u32[]{:S(2)}, u32[]{:S(2)}) collective-permute-start(f32[8,128]{1,0:T(8,128)S(1)} %max.39), channel_id=1, source_target_pairs={{0,1},{1,2},{2,3},{3,0},{4,5},{5,6},{6,7},{7,4},{8,9},{9,10},{10,1... | collective-permute-start | bytes 12296 | tf_op jit(solution)/shard_map/ppermute | solution.py:233
  75.4 30.3 %collective-permute-start.12 = (bf16[768,3072]{1,0:T(8,128)(2,1)}, bf16[768,3072]{1,0:T(8,128)(2,1)S(1)}, u32[]{:S(2)}, u32[]{:S(2)}) collective-permute-start(bf16[768,3072]{1,0:T(8,128)(2,1)} %collective-permute-done.3.refs_2_.refs_1_), channel_id=1, source_target_pairs={{8,0},{16,24},{40,32},{48,56},{72,64},{80,88},{104,96},{112,120},{... | collective-permute-start | bytes 14155784 | tf_op jit(solution)/shard_map/ppermute | solution.py:229
  76.6 31.9 %collective-permute-start.13 = (bf16[768,3072]{1,0:T(8,128)(2,1)}, bf16[768,3072]{1,0:T(8,128)(2,1)}, u32[]{:S(2)}, u32[]{:S(2)}) collective-permute-start(bf16[768,3072]{1,0:T(8,128)(2,1)} %collective-permute-done.4.refs_3_.refs_4_.refs_5_), channel_id=1, source_target_pairs={{24,16},{56,48},{88,80},{120,112},{25,17},{57,49},{89,81},{121,113... | collective-permute-start | bytes 14155784 | tf_op jit(solution)/shard_map/ppermute | solution.py:229
  82.2 55.5 %collective-permute-start.16 = (bf16[768,3072]{1,0:T(8,128)(2,1)}, bf16[768,3072]{1,0:T(8,128)(2,1)}, u32[]{:S(2)}, u32[]{:S(2)}) collective-permute-start(bf16[768,3072]{1,0:T(8,128)(2,1)} %get-tuple-element.84), channel_id=1, source_target_pairs={{8,24},{16,0},{40,56},{48,32},{72,88},{80,64},{104,120},{112,96},{... | collective-permute-start | bytes 14155784 | tf_op jit(solution)/shard_map/ppermute | solution.py:229
  83.5 54.2 %collective-permute-start.17 = (bf16[768,3072]{1,0:T(8,128)(2,1)}, bf16[768,3072]{1,0:T(8,128)(2,1)}, u32[]{:S(2)}, u32[]{:S(2)}) collective-permute-start(bf16[768,3072]{1,0:T(8,128)(2,1)} %get-tuple-element.85.refs_0_), channel_id=1, source_target_pairs={{8,104},{16,48},{40,8},{48,80},{72,40},{80,112},{104,72},{112,16},... | collective-permute-start | bytes 14155784 | tf_op jit(solution)/shard_map/ppermute | solution.py:229
  86.3 51.4 %collective-permute-start.18 = (bf16[768,3072]{1,0:T(8,128)(2,1)}, bf16[768,3072]{1,0:T(8,128)(2,1)}, u32[]{:S(2)}, u32[]{:S(2)}) collective-permute-start(bf16[768,3072]{1,0:T(8,128)(2,1)} %collective-permute-done.3.refs_2_.refs_1_), channel_id=1, source_target_pairs={{8,32},{16,112},{40,64},{48,16},{72,96},{80,48},{104,0},{112,80},{... | collective-permute-start | bytes 14155784 | tf_op jit(solution)/shard_map/ppermute | solution.py:229
  105.7 20.2 %collective-permute-start.11 = (f16[4,96,768]{2,1,0:T(8,128)(2,1)S(1)}, f16[4,96,768]{2,1,0:T(8,128)(2,1)S(1)}, u32[]{:S(2)}, u32[]{:S(2)}) collective-permute-start(f16[4,96,768]{2,1,0:T(8,128)(2,1)S(1)} %fusion.1), channel_id=1, source_target_pairs={{0,3},{1,0},{2,1},{3,2},{4,7},{5,4},{6,5},{7,6},{8,11},{9,8},{10,9... | collective-permute-start | bytes 1769480 | tf_op jit(solution)/shard_map/ppermute | solution.py:233
  108.5 17.4 %collective-permute-start.10 = (f16[4,96,768]{2,1,0:T(8,128)(2,1)S(1)}, f16[4,96,768]{2,1,0:T(8,128)(2,1)S(1)}, u32[]{:S(2)}, u32[]{:S(2)}) collective-permute-start(f16[4,96,768]{2,1,0:T(8,128)(2,1)S(1)} %fusion), channel_id=1, source_target_pairs={{0,1},{1,2},{2,3},{3,0},{4,5},{5,6},{6,7},{7,4},{8,9},{9,10},{10,1... | collective-permute-start | bytes 1769480 | tf_op jit(solution)/shard_map/ppermute | solution.py:233
  126.0 11.7 %collective-permute-start.19 = (f16[4,96,768]{2,1,0:T(8,128)(2,1)S(1)}, f16[4,96,768]{2,1,0:T(8,128)(2,1)S(1)}, u32[]{:S(2)}, u32[]{:S(2)}) collective-permute-start(f16[4,96,768]{2,1,0:T(8,128)(2,1)S(1)} %fusion.2), channel_id=1, source_target_pairs={{0,1},{1,2},{2,3},{3,0},{4,5},{5,6},{6,7},{7,4},{8,9},{9,10},{10,1... | collective-permute-start | bytes 1769480 | tf_op jit(solution)/shard_map/ppermute | solution.py:233
  126.6 11.1 %collective-permute-start.20 = (f16[4,96,768]{2,1,0:T(8,128)(2,1)S(1)}, f16[4,96,768]{2,1,0:T(8,128)(2,1)S(1)}, u32[]{:S(2)}, u32[]{:S(2)}) collective-permute-start(f16[4,96,768]{2,1,0:T(8,128)(2,1)S(1)} %fusion.3), channel_id=1, source_target_pairs={{0,3},{1,0},{2,1},{3,2},{4,7},{5,4},{6,5},{7,6},{8,11},{9,8},{10,9... | collective-permute-start | bytes 1769480 | tf_op jit(solution)/shard_map/ppermute | solution.py:233
  137.7 29.3 %collective-permute-start.23 = (bf16[768,3072]{1,0:T(8,128)(2,1)}, bf16[768,3072]{1,0:T(8,128)(2,1)}, u32[]{:S(2)}, u32[]{:S(2)}) collective-permute-start(bf16[768,3072]{1,0:T(8,128)(2,1)} %collective-permute-done.16.refs_3_), channel_id=1, source_target_pairs={{0,8},{24,16},{32,40},{56,48},{64,72},{88,80},{96,104},{120,112},{... | collective-permute-start | bytes 14155784 | tf_op jit(solution)/shard_map/ppermute | solution.py:229
  150.4 37.3 %collective-permute-start.29 = (bf16[768,3072]{1,0:T(8,128)(2,1)}, bf16[768,3072]{1,0:T(8,128)(2,1)}, u32[]{:S(2)}, u32[]{:S(2)}) collective-permute-start(bf16[768,3072]{1,0:T(8,128)(2,1)} %collective-permute-done.17.refs_6_), channel_id=1, source_target_pairs={{16,24},{48,56},{80,88},{112,120},{17,25},{49,57},{81,89},{113,121... | collective-permute-start | bytes 14155784 | tf_op jit(solution)/shard_map/ppermute | solution.py:229
  159.6 26.6 %collective-permute-start.14 = (f16[2,96,768]{2,1,0:T(8,128)(2,1)}, f16[2,96,768]{2,1,0:T(8,128)(2,1)S(1)}, u32[]{:S(2)}, u32[]{:S(2)}) collective-permute-start(f16[2,96,768]{2,1,0:T(8,128)(2,1)} %get-tuple-element.152), channel_id=1, source_target_pairs={{0,1},{1,2},{2,3},{3,0},{4,5},{5,6},{6,7},{7,4},{8,9},{9,10},{10,1... | collective-permute-start | bytes 884744 | tf_op jit(solution)/shard_map/ppermute | solution.py:233
  160.9 25.4 %collective-permute-start.15 = (f16[2,96,768]{2,1,0:T(8,128)(2,1)S(1)}, f16[2,96,768]{2,1,0:T(8,128)(2,1)S(1)}, u32[]{:S(2)}, u32[]{:S(2)}) collective-permute-start(f16[2,96,768]{2,1,0:T(8,128)(2,1)S(1)} %get-tuple-element.151), channel_id=1, source_target_pairs={{0,3},{1,0},{2,1},{3,2},{4,7},{5,4},{6,5},{7,6},{8,11},{9,8},{10,9... | collective-permute-start | bytes 884744 | tf_op jit(solution)/shard_map/ppermute | solution.py:233
  165.1 22.7 %collective-permute-start.21 = (f16[2,96,768]{2,1,0:T(8,128)(2,1)}, f16[2,96,768]{2,1,0:T(8,128)(2,1)S(1)}, u32[]{:S(2)}, u32[]{:S(2)}) collective-permute-start(f16[2,96,768]{2,1,0:T(8,128)(2,1)} %get-tuple-element.150), channel_id=1, source_target_pairs={{0,1},{1,2},{2,3},{3,0},{4,5},{5,6},{6,7},{7,4},{8,9},{9,10},{10,1... | collective-permute-start | bytes 884744 | tf_op jit(solution)/shard_map/ppermute | solution.py:233
  167.0 20.7 %collective-permute-start.22 = (f16[2,96,768]{2,1,0:T(8,128)(2,1)}, f16[2,96,768]{2,1,0:T(8,128)(2,1)S(1)}, u32[]{:S(2)}, u32[]{:S(2)}) collective-permute-start(f16[2,96,768]{2,1,0:T(8,128)(2,1)} %get-tuple-element.149), channel_id=1, source_target_pairs={{0,3},{1,0},{2,1},{3,2},{4,7},{5,4},{6,5},{7,6},{8,11},{9,8},{10,9... | collective-permute-start | bytes 884744 | tf_op jit(solution)/shard_map/ppermute | solution.py:233
  186.2 22.1 %collective-permute-start.28 = (f16[4,96,768]{2,1,0:T(8,128)(2,1)S(1)}, f16[4,96,768]{2,1,0:T(8,128)(2,1)S(1)}, u32[]{:S(2)}, u32[]{:S(2)}) collective-permute-start(f16[4,96,768]{2,1,0:T(8,128)(2,1)S(1)} %fusion.5), channel_id=1, source_target_pairs={{0,3},{1,0},{2,1},{3,2},{4,7},{5,4},{6,5},{7,6},{8,11},{9,8},{10,9... | collective-permute-start | bytes 1769480 | tf_op jit(solution)/shard_map/ppermute | solution.py:233
  186.3 22.0 %collective-permute-start.27 = (f16[4,96,768]{2,1,0:T(8,128)(2,1)S(1)}, f16[4,96,768]{2,1,0:T(8,128)(2,1)S(1)}, u32[]{:S(2)}, u32[]{:S(2)}) collective-permute-start(f16[4,96,768]{2,1,0:T(8,128)(2,1)S(1)} %fusion.4), channel_id=1, source_target_pairs={{0,1},{1,2},{2,3},{3,0},{4,5},{5,6},{6,7},{7,4},{8,9},{9,10},{10,1... | collective-permute-start | bytes 1769480 | tf_op jit(solution)/shard_map/ppermute | solution.py:233
  211.3 10.0 %collective-permute-start.32 = (f16[4,96,768]{2,1,0:T(8,128)(2,1)S(1)}, f16[4,96,768]{2,1,0:T(8,128)(2,1)S(1)}, u32[]{:S(2)}, u32[]{:S(2)}) collective-permute-start(f16[4,96,768]{2,1,0:T(8,128)(2,1)S(1)} %fusion.7), channel_id=1, source_target_pairs={{0,3},{1,0},{2,1},{3,2},{4,7},{5,4},{6,5},{7,6},{8,11},{9,8},{10,9... | collective-permute-start | bytes 1769480 | tf_op jit(solution)/shard_map/ppermute | solution.py:233
  211.4 10.3 %collective-permute-start.33 = (f16[4,96,768]{2,1,0:T(8,128)(2,1)S(1)}, f16[4,96,768]{2,1,0:T(8,128)(2,1)S(1)}, u32[]{:S(2)}, u32[]{:S(2)}) collective-permute-start(f16[4,96,768]{2,1,0:T(8,128)(2,1)S(1)} %fusion.6), channel_id=1, source_target_pairs={{0,1},{1,2},{2,3},{3,0},{4,5},{5,6},{6,7},{7,4},{8,9},{9,10},{10,1... | collective-permute-start | bytes 1769480 | tf_op jit(solution)/shard_map/ppermute | solution.py:233
  214.2 18.5 %collective-permute-start.36 = (f16[4,96,768]{2,1,0:T(8,128)(2,1)S(1)}, f16[4,96,768]{2,1,0:T(8,128)(2,1)S(1)}, u32[]{:S(2)}, u32[]{:S(2)}) collective-permute-start(f16[4,96,768]{2,1,0:T(8,128)(2,1)S(1)} %fusion.8), channel_id=1, source_target_pairs={{0,32},{32,64},{64,96},{96,0},{1,33},{33,65},{65,97},{97,1},{2,34}... | collective-permute-start | bytes 1769480 | tf_op jit(solution)/shard_map/ppermute | solution.py:229
  221.9 10.6 %collective-permute-start.34 = (f16[2,96,768]{2,1,0:T(8,128)(2,1)S(1)}, f16[2,96,768]{2,1,0:T(8,128)(2,1)S(1)}, u32[]{:S(2)}, u32[]{:S(2)}) collective-permute-start(f16[2,96,768]{2,1,0:T(8,128)(2,1)S(1)} %get-tuple-element.138), channel_id=1, source_target_pairs={{0,1},{1,2},{2,3},{3,0},{4,5},{5,6},{6,7},{7,4},{8,9},{9,10},{10,1... | collective-permute-start | bytes 884744 | tf_op jit(solution)/shard_map/ppermute | solution.py:233
  223.5 9.1 %collective-permute-start.35 = (f16[2,96,768]{2,1,0:T(8,128)(2,1)S(1)}, f16[2,96,768]{2,1,0:T(8,128)(2,1)S(1)}, u32[]{:S(2)}, u32[]{:S(2)}) collective-permute-start(f16[2,96,768]{2,1,0:T(8,128)(2,1)S(1)} %get-tuple-element.137), channel_id=1, source_target_pairs={{0,3},{1,0},{2,1},{3,2},{4,7},{5,4},{6,5},{7,6},{8,11},{9,8},{10,9... | collective-permute-start | bytes 884744 | tf_op jit(solution)/shard_map/ppermute | solution.py:233
  225.2 7.7 %collective-permute-start.37 = (f16[4,96,768]{2,1,0:T(8,128)(2,1)S(1)}, f16[4,96,768]{2,1,0:T(8,128)(2,1)S(1)}, u32[]{:S(2)}, u32[]{:S(2)}) collective-permute-start(f16[4,96,768]{2,1,0:T(8,128)(2,1)S(1)} %fusion.9), channel_id=1, source_target_pairs={{0,32},{8,40},{16,48},{32,64},{40,72},{48,80},{64,96},{72,104},{80... | collective-permute-start | bytes 1769480 | tf_op jit(solution)/shard_map/ppermute | solution.py:229
  234.1 18.2 %collective-permute-start.39 = (f16[4,96,768]{2,1,0:T(8,128)(2,1)S(1)}, f16[4,96,768]{2,1,0:T(8,128)(2,1)S(1)}, u32[]{:S(2)}, u32[]{:S(2)}) collective-permute-start(f16[4,96,768]{2,1,0:T(8,128)(2,1)S(1)} %fusion.11), channel_id=1, source_target_pairs={{0,20},{1,21},{2,22},{3,23},{8,28},{9,29},{10,30},{11,31},{16,0},{... | collective-permute-start | bytes 1769480 | tf_op jit(solution)/shard_map/ppermute | solution.py:245
  243.8 8.8 %collective-permute-start.38 = (f16[4,96,768]{2,1,0:T(8,128)(2,1)S(1)}, f16[4,96,768]{2,1,0:T(8,128)(2,1)S(1)}, u32[]{:S(2)}, u32[]{:S(2)}) collective-permute-start(f16[4,96,768]{2,1,0:T(8,128)(2,1)S(1)} %fusion.10), channel_id=1, source_target_pairs={{0,16},{1,17},{2,18},{3,19},{8,24},{9,25},{10,26},{11,27},{16,4},{... | collective-permute-start | bytes 1769480 | tf_op jit(solution)/shard_map/ppermute | solution.py:245
  254.0 8.6 %collective-permute-start.41 = (f16[2,96,768]{2,1,0:T(8,128)(2,1)S(1)}, f16[2,96,768]{2,1,0:T(8,128)(2,1)S(1)}, u32[]{:S(2)}, u32[]{:S(2)}) collective-permute-start(f16[2,96,768]{2,1,0:T(8,128)(2,1)S(1)} %get-tuple-element.131), channel_id=1, source_target_pairs={{0,20},{1,21},{2,22},{3,23},{8,28},{9,29},{10,30},{11,31},{16,0},{... | collective-permute-start | bytes 884744 | tf_op jit(solution)/shard_map/ppermute | solution.py:245
  264.6 16.3 %collective-permute-start.42 = (f16[96,768]{1,0:T(8,128)(2,1)S(1)}, f16[96,768]{1,0:T(8,128)(2,1)S(1)}, u32[]{:S(2)}, u32[]{:S(2)}) collective-permute-start(f16[96,768]{1,0:T(8,128)(2,1)S(1)} %multiply_convert_fusion), channel_id=1, source_target_pairs={{16,24},{24,16},{48,56},{56,48},{80,88},{88,80},{112,120},{120,112... | collective-permute-start | bytes 442376 | tf_op jit(solution)/shard_map/ppermute | solution.py:229
  303.8 8.2 %collective-permute-start.45 = (f16[768,96]{0,1:T(8,128)(2,1)S(1)}, f16[768,96]{0,1:T(8,128)(2,1)S(1)}, u32[]{:S(2)}, u32[]{:S(2)}) collective-permute-start(f16[768,96]{0,1:T(8,128)(2,1)S(1)} %squeeze.199), channel_id=1, source_target_pairs={{0,104},{8,112},{16,120},{24,0},{32,8},{40,16},{48,24},{56,32},{64... | collective-permute-start | bytes 442376 | tf_op jit(solution)/shard_map/ppermute | solution.py:229
  (24 other events, 176.9 us)

commit v3 on v2

--- a/solution.py
+++ b/solution.py
@@ -233,12 +233,14 @@
     return lax.ppermute(value, "pair", [(h * 4 + y, h * 4 + (y + by) % 4) for h in range(2) for y in range(4)])
 
 
-def x_permute(value, by):
+def x_permute(value, by, roles=range(4)):
     perm = []
     for z in range(PLANES):
         for x in range(4):
             to = (x + by) % 4
             for core in range(2):
+                if x % 2 * 2 + core not in roles:
+                    continue
                 for y in range(4):
                     source = (z * 4 + x % 2 * 2 + core) * 8 + x // 2 * 4 + y
                     perm.append((source, (z * 4 + to % 2 * 2 + core) * 8 + to // 2 * 4 + y))
@@ -304,10 +306,6 @@
     return jnp.maximum(jnp.maximum(value, got[0]), jnp.maximum(got[1], got[2]))
 
 
-def z_permute(value, by):
-    return aux_permute(value, [(r, r, by) for r in range(4)])
-
-
 def scales_of(largest):
     bound = 8.0 * HALF * 4 * largest * largest * 4.0
     scale = 32768.0 / jnp.maximum(bound, 1e-30)
@@ -333,17 +331,18 @@
     y = lax.rem(lax.axis_index("pair"), 4)
 
     mine, other, largest = cut_in_halves(x_lo.astype(jnp.int32), coeffs)
-    side = [(0, 2, 0), (1, 3, 0), (2, 0, 0), (3, 1, 0)]
-    near = [aux_permute(largest, side), z_permute(largest, 1), z_permute(largest, -1)]
-    mine, other, near = lax.optimization_barrier((mine, other, near))
     halo_a = aux_permute(mine, [(0, 0, -1), (3, 3, 1)])
     far_a = aux_permute(other, [(0, 2, 0), (3, 1, 0)])
     sib = aux_permute(mine, [(0, 1, 0), (1, 0, 0), (2, 3, 0), (3, 2, 0)])
 
-    largest = jnp.maximum(jnp.maximum(largest, near[0]), jnp.maximum(near[1], near[2]))
     largest = jnp.maximum(largest, aux_permute(largest, [(0, 1, 0), (1, 0, 0), (2, 3, 0), (3, 2, 0)]))
     largest = largest_round(largest, y_permute)
-    early = scales_of(jnp.max(largest))
+    largest = jnp.maximum(largest, x_permute(largest, 2, (1, 2)))
+    largest = jnp.maximum(largest, aux_permute(largest, [(1, 2, 0), (2, 1, 0)]))
+    largest = jnp.maximum(largest, aux_permute(largest, [(1, 1, 2), (2, 2, 2)]))
+    largest = jnp.maximum(largest, aux_permute(largest, [(1, 1, 1), (2, 2, 1)]))
+    largest = jnp.maximum(largest, aux_permute(largest, [(1, 0, 0), (2, 3, 0)]))
+    scales = scales_of(jnp.max(largest))
 
     occ_index, virt_index = after([occ_index, virt_index], mine)
     begin = x_lo * HALF
@@ -362,8 +361,8 @@
         plans.append([used, row, held_most])
     entries = lax.dynamic_index_in_dim(jnp.asarray(entry_table()), role * 2 + x_hi, axis=0, keepdims=False)
     rows = [plan[1] for plan in plans]
-    far_a, halo_a, sib, early, largest, weight, entries, rows = lax.optimization_barrier(
-        (far_a, halo_a, sib, early, largest, weight, entries, rows))
+    far_a, halo_a, sib, scales, weight, entries, rows = lax.optimization_barrier(
+        (far_a, halo_a, sib, scales, weight, entries, rows))
 
     far_b = aux_permute(after(other, far_a), [(1, 3, 0), (2, 0, 0)])
     halo_b = aux_permute(after(mine, halo_a), [(1, 1, -1), (2, 2, 1)])
@@ -394,69 +393,66 @@
         return [zero, one]
 
     partial0 = tiles(0)
-    sends0 = first_sends(partial0, early)
+    sends0 = first_sends(partial0, scales)
     held[FAR_A_SIB], held[HALO_A_SIB] = after([far_a_sib, halo_a_sib], sends0)
     got0 = first_round(sends0)
     partial1 = tiles(1)
-    sends1 = first_sends(partial1, early)
+    sends1 = first_sends(partial1, scales)
     got0, sends1 = lax.optimization_barrier((got0, sends1))
     got1 = first_round(sends1)
-    sends0 = second_sends(partial0, got0, early)
+    sends0 = second_sends(partial0, got0, scales)
     more0 = first_round(sends0)
-    far_b, halo_b, minor, got1, largest = lax.optimization_barrier(
-        (far_b, halo_b, minor, got1, largest, sends0))[:5]
-    more1 = first_round(second_sends(partial1, got1, early))
+    far_b, halo_b, minor, got1 = lax.optimization_barrier((far_b, halo_b, minor, got1, sends0))[:4]
+    more1 = first_round(second_sends(partial1, got1, scales))
     held[FAR_B], held[HALO_B], held[MINOR] = far_b, halo_b, minor
     held[FAR_B_SIB] = aux_permute(far_b, [(0, 1, 0), (3, 2, 0)])
     held[HALO_B_SIB] = aux_permute(halo_b, [(2, 3, 0)])
-    largest = jnp.maximum(largest, x_permute(largest, 2))
-    largest = jnp.maximum(largest, z_permute(largest, 2))
-    largest = jnp.maximum(largest, aux_permute(largest, side))
-    late = scales_of(jnp.max(largest))
     partial2 = tiles(2)
-    sends2 = first_sends(partial2, late)
-    more0, more1 = after([more0, more1], sends2)
+    sends2 = first_sends(partial2, scales)
     got2 = first_round(sends2)
     rows[3], more0 = lax.optimization_barrier((rows[3], more0, sends2))[:2]
     partial3 = tiles(3)
-    total0 = finish(partial0, got0, more0, early)
-    total1 = finish(partial1, got1, more1, early)
+    more0, more1 = after([more0, more1], partial3)
+    total0 = finish(partial0, got0, more0, scales)
+    total1 = finish(partial1, got1, more1, scales)
     moved0 = jnp.stack([total0[0][1], total1[0][1], total0[1][1], total1[1][1]])
-    moved0 = wide(aux_permute(narrow(moved0, late), [(0, 0, 1)]), late)
-    sends3 = first_sends(partial3, late)
+    moved0 = aux_permute(narrow(moved0, scales), [(0, 0, 1)])
+    sends3 = first_sends(partial3, scales)
     got2 = after(got2, partial3)
-    sends2 = second_sends(partial2, got2, late)
+    sends2 = second_sends(partial2, got2, scales)
     more2 = first_round(sends2)
     sends3 = after(sends3, sends2)
     got3 = first_round(sends3)
     more2 = after(more2, sends3)
-    total2 = finish(partial2, got2, more2, late)
-    moved2 = aux_permute(narrow(jnp.concatenate(total2), late), [(0, 0, 1), (1, 1, 1), (2, 2, 1)])
-    moved2 = wide(moved2, late)
-    more3 = both_ways(y_permute, *second_sends(partial3, got3, late))
-    total3 = finish(partial3, got3, more3, late)
+    total2 = finish(partial2, got2, more2, scales)
+    moved2 = narrow(jnp.concatenate(total2), scales)
+    moved2 = aux_permute(moved2, [(0, 0, 1), (1, 1, 1), (2, 2, 1)])
+    got3, moved2, moved0 = lax.optimization_barrier((got3, moved2, moved0))
+    more3 = both_ways(y_permute, *second_sends(partial3, got3, scales))
+    moved0, moved2 = wide(moved0, scales), wide(moved2, scales)
+    total3 = finish(partial3, got3, more3, scales)
     slots = jnp.concatenate(total0 + total1 + total2 + total3 + [moved0, moved2])
     parts = pick_parts(entries, slots).reshape(4, 2, 2, PART, ROWS)
 
     def x_part(k, d):
         return parts[k, d]
 
-    zero, one = ring_sum(x_part, x_permute, late)
+    zero, one = ring_sum(x_part, x_permute, scales)
     final = [zero[0], zero[1], one[0], one[1]]
 
-    crossed = narrow(jnp.stack(final[1:]), late).reshape(3, PART, 8, PART)
+    crossed = narrow(jnp.stack(final[1:]), scales).reshape(3, PART, 8, PART)
     crossed = lax.all_to_all(crossed, "pair", split_axis=2, concat_axis=1, tiled=True)
     crossed = crossed.reshape(3, ROWS, PART)
 
-    swapped = aux_permute(after(narrow(one[0], late), crossed), [(2, 3, 0), (3, 2, 0)])
-    lower = [final[0], final[1], jnp.where(x_lo == 1, wide(swapped, late), final[2]), final[3]]
+    swapped = aux_permute(after(narrow(one[0], scales), crossed), [(2, 3, 0), (3, 2, 0)])
+    lower = [final[0], final[1], jnp.where(x_lo == 1, wide(swapped, scales), final[2]), final[3]]
 
     back = [
         [(0, 3, -1), (1, 0, 0), (2, 1, 0), (3, 2, 0)],
         [(0, 2, -1), (1, 3, -1), (2, 1, 0), (3, 0, 0)],
         [(0, 1, -1), (1, 2, -1), (2, 3, -1), (3, 0, 0)],
     ]
-    upper = [wide(aux_permute(crossed[o], back[o]), late).T for o in range(3)]
+    upper = [wide(aux_permute(crossed[o], back[o]), scales).T for o in range(3)]
     return jnp.stack(lower[::-1] + upper)
 
 

time: 314 us -> 299 us (0.952)
  starting transfers between devices: 106 us -> 87.1 us
  blocking collectives: 16.5 us -> 20.7 us
    ppermute x22 -> x21, starting transfers between devices: 65.8 us -> 49.5 us  [aux_permute(): return lax.ppermute(value, 'aux', moves(pairs))]
    ppermute x19, waiting for transfers between devices: 13.7 us -> 19.8 us  [y_permute(): lax.ppermute(value, 'pair', [(h * 4 + y, h * 4 + (y + by) % 4) for h in r...]
    ppermute x22 -> x21, waiting for transfers between devices: 46.7 us -> 41.7 us  [aux_permute(): return lax.ppermute(value, 'aux', moves(pairs))]
    all_to_all x1, blocking collectives: 16.5 us -> 20.7 us  [local(): lax.all_to_all(crossed, 'pair', split_axis=2, concat_axis=1, tiled=True)]
    ppermute x5, starting transfers between devices: 14.8 us -> 11.3 us  [x_permute(): return lax.ppermute(value, ('aux', 'pair'), perm)]
    unnamed x14 -> x13, other arithmetic: 7.25 us -> 7.26 us
  transfers between devices with their start and end apart: 46 -> 45, of which waited for: 19 -> 15; matrix products, arithmetic and copies ran while one was open for 10% -> 9% of each run, Pallas kernels for 20% -> 21%
where the time goes in v3:
time: 299 us; the launch traced here: 298 us
  starting transfers between devices  87.1 us (29%)
  waiting for transfers between devices  77.2 us (26%)
  Pallas kernels  69.4 us (23%)
  local copies, waits for them, and re-layouts  21.1 us (7%)
  blocking collectives  20.7 us (7%)
  other arithmetic  20 us (7%)
    pallas_call x4, Pallas kernels, tile_batch(): pl.pallas_call(functools.partial(tiles_kernel, count, held_most, len(sour...  58.8 us
    ppermute x21, starting transfers between devices, aux_permute(): return lax.ppermute(value, 'aux', moves(pairs))  49.5 us
    ppermute x21, waiting for transfers between devices, aux_permute(): return lax.ppermute(value, 'aux', moves(pairs))  41.7 us
    ppermute x19, starting transfers between devices, y_permute(): lax.ppermute(value, 'pair', [(h * 4 + y, h * 4 + (y + by) % 4) for h in r...  26.3 us
    all_to_all x1, blocking collectives, local(): lax.all_to_all(crossed, 'pair', split_axis=2, concat_axis=1, tiled=True)  20.7 us
    ppermute x19, waiting for transfers between devices, y_permute(): lax.ppermute(value, 'pair', [(h * 4 + y, h * 4 + (y + by) % 4) for h in r...  19.8 us
    ppermute x5, waiting for transfers between devices, x_permute(): return lax.ppermute(value, ('aux', 'pair'), perm)  15.8 us
    ppermute x5, starting transfers between devices, x_permute(): return lax.ppermute(value, ('aux', 'pair'), perm)  11.3 us
  transfers between devices with their start and end apart: 45, of which 15 were waited for; matrix products, arithmetic and copies ran while one was open for 9% of the time, Pallas kernels for 21%

profile of v3, /device:TPU:3, one launch (start us, length us, event | category | flops | bytes accessed | tf_op | source)
XLA Modules:
  0.0 297.6 jit_solution(5113819020982240181)
XLA Ops:
  0.0 3.7 %copy-done.1 = bf16[768,6144]{1,0:T(8,128)(2,1)S(1)} copy-done((bf16[768,6144]{1,0:T(8,128)(2,1)S(1)}, bf16[768,6144]{1,0:T(8,128)(2,1)}, u32[]{:S(2)}) %copy-start.1) | copy-done | bytes 9437208
  3.7 5.0 %shard_map.100 = (bf16[768,3072]{1,0:T(8,128)(2,1)}, bf16[768,3072]{1,0:T(8,128)(2,1)}, f32[8,128]{1,0:T(8,128)S(1)}) custom-call(s32[1]{0:T(128)} %bitcast.x_lo, bf16[768,6144]{1,0:T(8,128)(2,1)S(1)} %copy-done.1), custom_call_target="tpu_custom_call" | custom-call | bytes 73728 | tf_op jit(solution)/shard_map/pallas_call | solution.py:210
  8.6 3.6 %collective-permute-start = (bf16[768,3072]{1,0:T(8,128)(2,1)}, bf16[768,3072]{1,0:T(8,128)(2,1)}, u32[]{:S(2)}, u32[]{:S(2)}) collective-permute-start(bf16[768,3072]{1,0:T(8,128)(2,1)} %get-tuple-element.77), channel_id=1, source_target_pairs={{0,16},{24,8},{32,48},{56,40},{64,80},{88,72},{96,112},{120,104},{... | collective-permute-start | bytes 14155784 | tf_op jit(solution)/shard_map/ppermute | solution.py:229
  12.2 4.4 %collective-permute-start.1 = (bf16[768,3072]{1,0:T(8,128)(2,1)}, bf16[768,3072]{1,0:T(8,128)(2,1)}, u32[]{:S(2)}, u32[]{:S(2)}) collective-permute-start(bf16[768,3072]{1,0:T(8,128)(2,1)} %get-tuple-element.78.refs_0_), channel_id=1, source_target_pairs={{0,96},{24,56},{32,0},{56,88},{64,32},{88,120},{96,64},{120,24},{1... | collective-permute-start | bytes 14155784 | tf_op jit(solution)/shard_map/ppermute | solution.py:229
  18.4 4.8 %shard_map.101 = f32[1,3072]{1,0:T(1,128)} custom-call(s32[1,3072]{1,0:T(1,128)} %bitcast.250, s32[1,3072]{1,0:T(1,128)} %bitcast.251, f32[32,128]{1,0:T(8,128)} %bitcast.253, f32[256,128]{1,0:T(8,128)} %bitcast.252), custom_call_target="tpu_custom_call" | custom-call | flops 679477248 | bytes 200000 | tf_op jit(solution)/shard_map/pallas_call | solution.py:178
  27.3 2.6 collective-permute-start.5
  40.1 22.3 %collective-permute-done.11 = f32[8,128]{1,0:T(8,128)S(1)} collective-permute-done((f32[8,128]{1,0:T(8,128)S(1)}, f32[8,128]{1,0:T(8,128)S(1)}, u32[]{:S(2)}, u32[]{:S(2)}) %collective-permute-start.11) | collective-permute-done | bytes 4128 | tf_op jit(solution)/shard_map/ppermute | solution.py:229
  64.3 6.3 %collective-permute-done.1.refs_3_.refs_4_.refs_5_ = bf16[768,3072]{1,0:T(8,128)(2,1)} collective-permute-done((bf16[768,3072]{1,0:T(8,128)(2,1)}, bf16[768,3072]{1,0:T(8,128)(2,1)}, u32[]{:S(2)}, u32[]{:S(2)}) %collective-permute-start.1) | collective-permute-done | bytes 4718624 | tf_op jit(solution)/shard_map/ppermute | solution.py:229
  71.9 7.4 %collective-permute-start.15 = (bf16[768,3072]{1,0:T(8,128)(2,1)}, bf16[768,3072]{1,0:T(8,128)(2,1)}, u32[]{:S(2)}, u32[]{:S(2)}) collective-permute-start(bf16[768,3072]{1,0:T(8,128)(2,1)} %collective-permute-done.1.refs_3_.refs_4_.refs_5_), channel_id=1, source_target_pairs={{24,16},{56,48},{88,80},{120,112},{25,17},{57,49},{89,81},{121,113... | collective-permute-start | bytes 14155784 | tf_op jit(solution)/shard_map/ppermute | solution.py:229
  80.6 2.8 collective-permute-start.19
  83.4 2.8 collective-permute-start.20
  86.2 14.5 %shard_map.102 = f32[4,2,2,96,768]{4,3,2,1,0:T(8,128)} custom-call(s32[13]{0:T(128)} %get-tuple-element.63.table, f32[1,3072]{1,0:T(1,128)} %add_divide_fusion.weight, bf16[768,3072]{1,0:T(8,128)(2,1)} %get-tuple-element.78.refs_0_, bf16[768,3072]{1,0:T(8,128)(2,1)} %collective-permute-done.2.refs_1_.refs_0_, ...), custom_call_target="tpu_custom_call" | custom-call | flops 1179648 | bytes 1179648 | tf_op jit(solution)/shard_map/pallas_call | solution.py:127
  102.6 2.8 collective-permute-start.13
  105.5 15.4 %shard_map.103 = f32[4,2,2,96,768]{4,3,2,1,0:T(8,128)} custom-call(s32[13]{0:T(128)} %get-tuple-element.69.table, f32[1,3072]{1,0:T(1,128)} %add_divide_fusion.weight, bf16[768,3072]{1,0:T(8,128)(2,1)} %get-tuple-element.78.refs_0_, bf16[768,3072]{1,0:T(8,128)(2,1)} %collective-permute-done.2.refs_1_.refs_0_, ...), custom_call_target="tpu_custom_call" | custom-call | flops 1179648 | bytes 1179648 | tf_op jit(solution)/shard_map/pallas_call | solution.py:127
  122.9 2.7 collective-permute-start.22
  128.0 6.8 %collective-permute-done.18.refs_3_ = bf16[768,3072]{1,0:T(8,128)(2,1)S(1)} collective-permute-done((bf16[768,3072]{1,0:T(8,128)(2,1)}, bf16[768,3072]{1,0:T(8,128)(2,1)S(1)}, u32[]{:S(2)}, u32[]{:S(2)}) %collective-permute-start.18) | collective-permute-done | bytes 4718624 | tf_op jit(solution)/shard_map/ppermute | solution.py:229
  137.2 4.9 %collective-permute-start.23 = (bf16[768,3072]{1,0:T(8,128)(2,1)S(1)}, bf16[768,3072]{1,0:T(8,128)(2,1)S(1)}, u32[]{:S(2)}, u32[]{:S(2)}) collective-permute-start(bf16[768,3072]{1,0:T(8,128)(2,1)S(1)} %collective-permute-done.18.refs_3_), channel_id=1, source_target_pairs={{0,8},{24,16},{32,40},{56,48},{64,72},{88,80},{96,104},{120,112},{... | collective-permute-start | bytes 14155784 | tf_op jit(solution)/shard_map/ppermute | solution.py:229
  151.4 2.7 collective-permute-start.25
  154.2 14.5 %shard_map.104 = f32[4,2,2,96,768]{4,3,2,1,0:T(8,128)} custom-call(s32[15]{0:T(128)} %pad_add_fusion.2.table, f32[1,3072]{1,0:T(1,128)} %add_divide_fusion.weight, bf16[768,3072]{1,0:T(8,128)(2,1)} %collective-permute-done.2.refs_1_.refs_0_, bf16[768,3072]{1,0:T(8,128)(2,1)} %collective-permute-done.refs_2_.refs_1_, ...), custom_call_target="tpu_custom_call" | custom-call | flops 1179648 | bytes 1179648 | tf_op jit(solution)/shard_map/pallas_call | solution.py:127
  172.2 14.4 %shard_map.105 = f32[4,2,2,96,768]{4,3,2,1,0:T(8,128)} custom-call(s32[13]{0:T(128)} %pad_add_fusion.3.table, f32[1,3072]{1,0:T(1,128)} %add_divide_fusion.weight, bf16[768,3072]{1,0:T(8,128)(2,1)} %get-tuple-element.78.refs_0_, bf16[768,3072]{1,0:T(8,128)(2,1)} %collective-permute-done.2.refs_1_.refs_0_, ...), custom_call_target="tpu_custom_call" | custom-call | flops 1179648 | bytes 1179648 | tf_op jit(solution)/shard_map/pallas_call | solution.py:127
  193.5 2.7 collective-permute-start.30
  197.3 2.7 collective-permute-start.32
  201.4 10.0 %collective-permute-done.31 = f16[4,96,768]{2,1,0:T(8,128)(2,1)S(1)} collective-permute-done((f16[4,96,768]{2,1,0:T(8,128)(2,1)S(1)}, f16[4,96,768]{2,1,0:T(8,128)(2,1)S(1)}, u32[]{:S(2)}, u32[]{:S(2)}) %collective-permute-start.31) | collective-permute-done | bytes 589856 | tf_op jit(solution)/shard_map/ppermute | solution.py:233
  211.7 2.7 collective-permute-start.36
  214.4 5.8 %collective-permute-done.35 = f16[2,96,768]{2,1,0:T(8,128)(2,1)S(1)} collective-permute-done((f16[2,96,768]{2,1,0:T(8,128)(2,1)S(1)}, f16[2,96,768]{2,1,0:T(8,128)(2,1)S(1)}, u32[]{:S(2)}, u32[]{:S(2)}) %collective-permute-start.35) | collective-permute-done | bytes 294944 | tf_op jit(solution)/shard_map/ppermute | solution.py:233
  221.8 8.3 %collective-permute-start.38 = (f16[4,96,768]{2,1,0:T(8,128)(2,1)S(1)}, f16[4,96,768]{2,1,0:T(8,128)(2,1)S(1)}, u32[]{:S(2)}, u32[]{:S(2)}) collective-permute-start(f16[4,96,768]{2,1,0:T(8,128)(2,1)S(1)} %fusion.11), channel_id=1, source_target_pairs={{0,20},{1,21},{2,22},{3,23},{8,28},{9,29},{10,30},{11,31},{16,0},{... | collective-permute-start | bytes 1769480 | tf_op jit(solution)/shard_map/ppermute | solution.py:247
  230.9 8.3 %collective-permute-done.38 = f16[4,96,768]{2,1,0:T(8,128)(2,1)S(1)} collective-permute-done((f16[4,96,768]{2,1,0:T(8,128)(2,1)S(1)}, f16[4,96,768]{2,1,0:T(8,128)(2,1)S(1)}, u32[]{:S(2)}, u32[]{:S(2)}) %collective-permute-start.38) | collective-permute-done | bytes 589856 | tf_op jit(solution)/shard_map/ppermute | solution.py:247
  241.4 7.1 %collective-permute-done.39 = f16[2,96,768]{2,1,0:T(8,128)(2,1)S(1)} collective-permute-done((f16[2,96,768]{2,1,0:T(8,128)(2,1)S(1)}, f16[2,96,768]{2,1,0:T(8,128)(2,1)S(1)}, u32[]{:S(2)}, u32[]{:S(2)}) %collective-permute-start.39) | collective-permute-done | bytes 294944 | tf_op jit(solution)/shard_map/ppermute | solution.py:247
  250.3 10.1 %collective-permute-start.41 = (f16[96,768]{1,0:T(8,128)(2,1)S(1)}, f16[96,768]{1,0:T(8,128)(2,1)S(1)}, u32[]{:S(2)}, u32[]{:S(2)}) collective-permute-start(f16[96,768]{1,0:T(8,128)(2,1)S(1)} %multiply_convert_fusion), channel_id=1, source_target_pairs={{16,24},{24,16},{48,56},{56,48},{80,88},{88,80},{112,120},{120,112... | collective-permute-start | bytes 442376 | tf_op jit(solution)/shard_map/ppermute | solution.py:229
  263.2 20.7 %all_to_all.15 = f16[3,96,8,96]{1,3,0,2:T(8,128)(2,1)S(1)} all-to-all(f16[3,96,8,96]{1,3,0,2:T(8,128)(2,1)S(1)} %fusion.12), channel_id=1, replica_groups=mesh['aux'=16,'pair'=8] {'pair'}, dimensions={2} | all-to-all | bytes 884736 | tf_op jit(solution)/shard_map/all_to_all | solution.py:444
  291.0 2.6 collective-permute-done.43
  294.3 2.5 collective-permute-done.44
  (161 shorter events, 67.8 us)
Async XLA Ops:
  8.6 55.7 %collective-permute-start = (bf16[768,3072]{1,0:T(8,128)(2,1)}, bf16[768,3072]{1,0:T(8,128)(2,1)}, u32[]{:S(2)}, u32[]{:S(2)}) collective-permute-start(bf16[768,3072]{1,0:T(8,128)(2,1)} %get-tuple-element.77), channel_id=1, source_target_pairs={{0,16},{24,8},{32,48},{56,40},{64,80},{88,72},{96,112},{120,104},{... | collective-permute-start | bytes 14155784 | tf_op jit(solution)/shard_map/ppermute | solution.py:229
  12.2 58.4 %collective-permute-start.1 = (bf16[768,3072]{1,0:T(8,128)(2,1)}, bf16[768,3072]{1,0:T(8,128)(2,1)}, u32[]{:S(2)}, u32[]{:S(2)}) collective-permute-start(bf16[768,3072]{1,0:T(8,128)(2,1)} %get-tuple-element.78.refs_0_), channel_id=1, source_target_pairs={{0,96},{24,56},{32,0},{56,88},{64,32},{88,120},{96,64},{120,24},{1... | collective-permute-start | bytes 14155784 | tf_op jit(solution)/shard_map/ppermute | solution.py:229
  16.6 54.0 %collective-permute-start.2 = (bf16[768,3072]{1,0:T(8,128)(2,1)}, bf16[768,3072]{1,0:T(8,128)(2,1)}, u32[]{:S(2)}, u32[]{:S(2)}) collective-permute-start(bf16[768,3072]{1,0:T(8,128)(2,1)} %get-tuple-element.78.refs_0_), channel_id=1, source_target_pairs={{0,8},{8,0},{16,24},{24,16},{32,40},{40,32},{48,56},{56,48},{64,72... | collective-permute-start | bytes 14155784 | tf_op jit(solution)/shard_map/ppermute | solution.py:229
  16.7 8.5 %collective-permute-start.3 = (f32[8,128]{1,0:T(8,128)S(1)}, f32[8,128]{1,0:T(8,128)S(1)}, u32[]{:S(2)}, u32[]{:S(2)}) collective-permute-start(f32[8,128]{1,0:T(8,128)S(1)} %get-tuple-element.59), channel_id=1, source_target_pairs={{0,8},{8,0},{16,24},{24,16},{32,40},{40,32},{48,56},{56,48},{64,72... | collective-permute-start | bytes 12296 | tf_op jit(solution)/shard_map/ppermute | solution.py:229
  38.1 24.3 %collective-permute-start.11 = (f32[8,128]{1,0:T(8,128)S(1)}, f32[8,128]{1,0:T(8,128)S(1)}, u32[]{:S(2)}, u32[]{:S(2)}) collective-permute-start(f32[8,128]{1,0:T(8,128)S(1)} %max.37), channel_id=1, source_target_pairs={{8,0},{16,24},{40,32},{48,56},{72,64},{80,88},{104,96},{112,120},{... | collective-permute-start | bytes 12296 | tf_op jit(solution)/shard_map/ppermute | solution.py:229
  70.6 32.0 %collective-permute-start.14 = (bf16[768,3072]{1,0:T(8,128)(2,1)}, bf16[768,3072]{1,0:T(8,128)(2,1)}, u32[]{:S(2)}, u32[]{:S(2)}) collective-permute-start(bf16[768,3072]{1,0:T(8,128)(2,1)} %collective-permute-done.refs_2_.refs_1_), channel_id=1, source_target_pairs={{8,0},{16,24},{40,32},{48,56},{72,64},{80,88},{104,96},{112,120},{... | collective-permute-start | bytes 14155784 | tf_op jit(solution)/shard_map/ppermute | solution.py:229
  71.9 33.5 %collective-permute-start.15 = (bf16[768,3072]{1,0:T(8,128)(2,1)}, bf16[768,3072]{1,0:T(8,128)(2,1)}, u32[]{:S(2)}, u32[]{:S(2)}) collective-permute-start(bf16[768,3072]{1,0:T(8,128)(2,1)} %collective-permute-done.1.refs_3_.refs_4_.refs_5_), channel_id=1, source_target_pairs={{24,16},{56,48},{88,80},{120,112},{25,17},{57,49},{89,81},{121,113... | collective-permute-start | bytes 14155784 | tf_op jit(solution)/shard_map/ppermute | solution.py:229
  79.3 55.5 %collective-permute-start.18 = (bf16[768,3072]{1,0:T(8,128)(2,1)}, bf16[768,3072]{1,0:T(8,128)(2,1)S(1)}, u32[]{:S(2)}, u32[]{:S(2)}) collective-permute-start(bf16[768,3072]{1,0:T(8,128)(2,1)} %get-tuple-element.77), channel_id=1, source_target_pairs={{8,24},{16,0},{40,56},{48,32},{72,88},{80,64},{104,120},{112,96},{... | collective-permute-start | bytes 14155784 | tf_op jit(solution)/shard_map/ppermute | solution.py:229
  80.6 54.2 %collective-permute-start.19 = (bf16[768,3072]{1,0:T(8,128)(2,1)}, bf16[768,3072]{1,0:T(8,128)(2,1)}, u32[]{:S(2)}, u32[]{:S(2)}) collective-permute-start(bf16[768,3072]{1,0:T(8,128)(2,1)} %get-tuple-element.78.refs_0_), channel_id=1, source_target_pairs={{8,104},{16,48},{40,8},{48,80},{72,40},{80,112},{104,72},{112,16},... | collective-permute-start | bytes 14155784 | tf_op jit(solution)/shard_map/ppermute | solution.py:229
  83.4 51.4 %collective-permute-start.20 = (bf16[768,3072]{1,0:T(8,128)(2,1)}, bf16[768,3072]{1,0:T(8,128)(2,1)}, u32[]{:S(2)}, u32[]{:S(2)}) collective-permute-start(bf16[768,3072]{1,0:T(8,128)(2,1)} %collective-permute-done.refs_2_.refs_1_), channel_id=1, source_target_pairs={{8,32},{16,112},{40,64},{48,16},{72,96},{80,48},{104,0},{112,80},{... | collective-permute-start | bytes 14155784 | tf_op jit(solution)/shard_map/ppermute | solution.py:229
  102.6 20.2 %collective-permute-start.13 = (f16[4,96,768]{2,1,0:T(8,128)(2,1)S(1)}, f16[4,96,768]{2,1,0:T(8,128)(2,1)S(1)}, u32[]{:S(2)}, u32[]{:S(2)}) collective-permute-start(f16[4,96,768]{2,1,0:T(8,128)(2,1)S(1)} %fusion.1), channel_id=1, source_target_pairs={{0,3},{1,0},{2,1},{3,2},{4,7},{5,4},{6,5},{7,6},{8,11},{9,8},{10,9... | collective-permute-start | bytes 1769480 | tf_op jit(solution)/shard_map/ppermute | solution.py:233
  105.5 17.4 %collective-permute-start.12 = (f16[4,96,768]{2,1,0:T(8,128)(2,1)S(1)}, f16[4,96,768]{2,1,0:T(8,128)(2,1)S(1)}, u32[]{:S(2)}, u32[]{:S(2)}) collective-permute-start(f16[4,96,768]{2,1,0:T(8,128)(2,1)S(1)} %fusion), channel_id=1, source_target_pairs={{0,1},{1,2},{2,3},{3,0},{4,5},{5,6},{6,7},{7,4},{8,9},{9,10},{10,1... | collective-permute-start | bytes 1769480 | tf_op jit(solution)/shard_map/ppermute | solution.py:233
  122.8 14.4 %collective-permute-start.21 = (f16[4,96,768]{2,1,0:T(8,128)(2,1)S(1)}, f16[4,96,768]{2,1,0:T(8,128)(2,1)S(1)}, u32[]{:S(2)}, u32[]{:S(2)}) collective-permute-start(f16[4,96,768]{2,1,0:T(8,128)(2,1)S(1)} %fusion.2), channel_id=1, source_target_pairs={{0,1},{1,2},{2,3},{3,0},{4,5},{5,6},{6,7},{7,4},{8,9},{9,10},{10,1... | collective-permute-start | bytes 1769480 | tf_op jit(solution)/shard_map/ppermute | solution.py:233
  122.9 14.3 %collective-permute-start.22 = (f16[4,96,768]{2,1,0:T(8,128)(2,1)S(1)}, f16[4,96,768]{2,1,0:T(8,128)(2,1)S(1)}, u32[]{:S(2)}, u32[]{:S(2)}) collective-permute-start(f16[4,96,768]{2,1,0:T(8,128)(2,1)S(1)} %fusion.3), channel_id=1, source_target_pairs={{0,3},{1,0},{2,1},{3,2},{4,7},{5,4},{6,5},{7,6},{8,11},{9,8},{10,9... | collective-permute-start | bytes 1769480 | tf_op jit(solution)/shard_map/ppermute | solution.py:233
  137.2 12.1 %collective-permute-start.23 = (bf16[768,3072]{1,0:T(8,128)(2,1)S(1)}, bf16[768,3072]{1,0:T(8,128)(2,1)S(1)}, u32[]{:S(2)}, u32[]{:S(2)}) collective-permute-start(bf16[768,3072]{1,0:T(8,128)(2,1)S(1)} %collective-permute-done.18.refs_3_), channel_id=1, source_target_pairs={{0,8},{24,16},{32,40},{56,48},{64,72},{88,80},{96,104},{120,112},{... | collective-permute-start | bytes 14155784 | tf_op jit(solution)/shard_map/ppermute | solution.py:229
  142.1 30.1 %collective-permute-start.26 = (bf16[768,3072]{1,0:T(8,128)(2,1)}, bf16[768,3072]{1,0:T(8,128)(2,1)}, u32[]{:S(2)}, u32[]{:S(2)}) collective-permute-start(bf16[768,3072]{1,0:T(8,128)(2,1)} %collective-permute-done.19.refs_6_), channel_id=1, source_target_pairs={{16,24},{48,56},{80,88},{112,120},{17,25},{49,57},{81,89},{113,121... | collective-permute-start | bytes 14155784 | tf_op jit(solution)/shard_map/ppermute | solution.py:229
  143.4 27.2 %collective-permute-start.16 = (f16[2,96,768]{2,1,0:T(8,128)(2,1)}, f16[2,96,768]{2,1,0:T(8,128)(2,1)S(1)}, u32[]{:S(2)}, u32[]{:S(2)}) collective-permute-start(f16[2,96,768]{2,1,0:T(8,128)(2,1)} %get-tuple-element.144), channel_id=1, source_target_pairs={{0,1},{1,2},{2,3},{3,0},{4,5},{5,6},{6,7},{7,4},{8,9},{9,10},{10,1... | collective-permute-start | bytes 884744 | tf_op jit(solution)/shard_map/ppermute | solution.py:233
  144.5 26.4 %collective-permute-start.17 = (f16[2,96,768]{2,1,0:T(8,128)(2,1)}, f16[2,96,768]{2,1,0:T(8,128)(2,1)S(1)}, u32[]{:S(2)}, u32[]{:S(2)}) collective-permute-start(f16[2,96,768]{2,1,0:T(8,128)(2,1)} %get-tuple-element.143), channel_id=1, source_target_pairs={{0,3},{1,0},{2,1},{3,2},{4,7},{5,4},{6,5},{7,6},{8,11},{9,8},{10,9... | collective-permute-start | bytes 884744 | tf_op jit(solution)/shard_map/ppermute | solution.py:233
  148.8 37.9 %collective-permute-start.24 = (f16[2,96,768]{2,1,0:T(8,128)(2,1)}, f16[2,96,768]{2,1,0:T(8,128)(2,1)S(1)}, u32[]{:S(2)}, u32[]{:S(2)}) collective-permute-start(f16[2,96,768]{2,1,0:T(8,128)(2,1)} %get-tuple-element.138), channel_id=1, source_target_pairs={{0,1},{1,2},{2,3},{3,0},{4,5},{5,6},{6,7},{7,4},{8,9},{9,10},{10,1... | collective-permute-start | bytes 884744 | tf_op jit(solution)/shard_map/ppermute | solution.py:233
  151.4 35.2 %collective-permute-start.25 = (f16[2,96,768]{2,1,0:T(8,128)(2,1)}, f16[2,96,768]{2,1,0:T(8,128)(2,1)S(1)}, u32[]{:S(2)}, u32[]{:S(2)}) collective-permute-start(f16[2,96,768]{2,1,0:T(8,128)(2,1)} %get-tuple-element.137), channel_id=1, source_target_pairs={{0,3},{1,0},{2,1},{3,2},{4,7},{5,4},{6,5},{7,6},{8,11},{9,8},{10,9... | collective-permute-start | bytes 884744 | tf_op jit(solution)/shard_map/ppermute | solution.py:233
  170.6 22.5 %collective-permute-start.28 = (f16[4,96,768]{2,1,0:T(8,128)(2,1)S(1)}, f16[4,96,768]{2,1,0:T(8,128)(2,1)S(1)}, u32[]{:S(2)}, u32[]{:S(2)}) collective-permute-start(f16[4,96,768]{2,1,0:T(8,128)(2,1)S(1)} %fusion.5), channel_id=1, source_target_pairs={{0,3},{1,0},{2,1},{3,2},{4,7},{5,4},{6,5},{7,6},{8,11},{9,8},{10,9... | collective-permute-start | bytes 1769480 | tf_op jit(solution)/shard_map/ppermute | solution.py:233
  170.9 22.3 %collective-permute-start.27 = (f16[4,96,768]{2,1,0:T(8,128)(2,1)S(1)}, f16[4,96,768]{2,1,0:T(8,128)(2,1)S(1)}, u32[]{:S(2)}, u32[]{:S(2)}) collective-permute-start(f16[4,96,768]{2,1,0:T(8,128)(2,1)S(1)} %fusion.4), channel_id=1, source_target_pairs={{0,1},{1,2},{2,3},{3,0},{4,5},{5,6},{6,7},{7,4},{8,9},{9,10},{10,1... | collective-permute-start | bytes 1769480 | tf_op jit(solution)/shard_map/ppermute | solution.py:233
  197.2 14.1 %collective-permute-start.31 = (f16[4,96,768]{2,1,0:T(8,128)(2,1)S(1)}, f16[4,96,768]{2,1,0:T(8,128)(2,1)S(1)}, u32[]{:S(2)}, u32[]{:S(2)}) collective-permute-start(f16[4,96,768]{2,1,0:T(8,128)(2,1)S(1)} %fusion.6), channel_id=1, source_target_pairs={{0,1},{1,2},{2,3},{3,0},{4,5},{5,6},{6,7},{7,4},{8,9},{9,10},{10,1... | collective-permute-start | bytes 1769480 | tf_op jit(solution)/shard_map/ppermute | solution.py:233
  197.3 14.1 %collective-permute-start.32 = (f16[4,96,768]{2,1,0:T(8,128)(2,1)S(1)}, f16[4,96,768]{2,1,0:T(8,128)(2,1)S(1)}, u32[]{:S(2)}, u32[]{:S(2)}) collective-permute-start(f16[4,96,768]{2,1,0:T(8,128)(2,1)S(1)} %fusion.7), channel_id=1, source_target_pairs={{0,3},{1,0},{2,1},{3,2},{4,7},{5,4},{6,5},{7,6},{8,11},{9,8},{10,9... | collective-permute-start | bytes 1769480 | tf_op jit(solution)/shard_map/ppermute | solution.py:233
  200.7 10.7 %collective-permute-start.33 = (f16[4,96,768]{2,1,0:T(8,128)(2,1)S(1)}, f16[4,96,768]{2,1,0:T(8,128)(2,1)S(1)}, u32[]{:S(2)}, u32[]{:S(2)}) collective-permute-start(f16[4,96,768]{2,1,0:T(8,128)(2,1)S(1)} %fusion.8), channel_id=1, source_target_pairs={{0,32},{8,40},{16,48},{32,64},{40,72},{48,80},{64,96},{72,104},{80... | collective-permute-start | bytes 1769480 | tf_op jit(solution)/shard_map/ppermute | solution.py:229
  211.6 8.6 %collective-permute-start.35 = (f16[2,96,768]{2,1,0:T(8,128)(2,1)S(1)}, f16[2,96,768]{2,1,0:T(8,128)(2,1)S(1)}, u32[]{:S(2)}, u32[]{:S(2)}) collective-permute-start(f16[2,96,768]{2,1,0:T(8,128)(2,1)S(1)} %get-tuple-element.130), channel_id=1, source_target_pairs={{0,1},{1,2},{2,3},{3,0},{4,5},{5,6},{6,7},{7,4},{8,9},{9,10},{10,1... | collective-permute-start | bytes 884744 | tf_op jit(solution)/shard_map/ppermute | solution.py:233
  211.7 8.5 %collective-permute-start.36 = (f16[2,96,768]{2,1,0:T(8,128)(2,1)S(1)}, f16[2,96,768]{2,1,0:T(8,128)(2,1)S(1)}, u32[]{:S(2)}, u32[]{:S(2)}) collective-permute-start(f16[2,96,768]{2,1,0:T(8,128)(2,1)S(1)} %get-tuple-element.129), channel_id=1, source_target_pairs={{0,3},{1,0},{2,1},{3,2},{4,7},{5,4},{6,5},{7,6},{8,11},{9,8},{10,9... | collective-permute-start | bytes 884744 | tf_op jit(solution)/shard_map/ppermute | solution.py:233
  221.8 17.5 %collective-permute-start.38 = (f16[4,96,768]{2,1,0:T(8,128)(2,1)S(1)}, f16[4,96,768]{2,1,0:T(8,128)(2,1)S(1)}, u32[]{:S(2)}, u32[]{:S(2)}) collective-permute-start(f16[4,96,768]{2,1,0:T(8,128)(2,1)S(1)} %fusion.11), channel_id=1, source_target_pairs={{0,20},{1,21},{2,22},{3,23},{8,28},{9,29},{10,30},{11,31},{16,0},{... | collective-permute-start | bytes 1769480 | tf_op jit(solution)/shard_map/ppermute | solution.py:247
  230.1 9.5 %collective-permute-start.37 = (f16[4,96,768]{2,1,0:T(8,128)(2,1)S(1)}, f16[4,96,768]{2,1,0:T(8,128)(2,1)S(1)}, u32[]{:S(2)}, u32[]{:S(2)}) collective-permute-start(f16[4,96,768]{2,1,0:T(8,128)(2,1)S(1)} %fusion.10), channel_id=1, source_target_pairs={{0,16},{1,17},{2,18},{3,19},{8,24},{9,25},{10,26},{11,27},{16,4},{... | collective-permute-start | bytes 1769480 | tf_op jit(solution)/shard_map/ppermute | solution.py:247
  239.8 8.6 %collective-permute-start.39 = (f16[2,96,768]{2,1,0:T(8,128)(2,1)S(1)}, f16[2,96,768]{2,1,0:T(8,128)(2,1)S(1)}, u32[]{:S(2)}, u32[]{:S(2)}) collective-permute-start(f16[2,96,768]{2,1,0:T(8,128)(2,1)S(1)} %get-tuple-element.124), channel_id=1, source_target_pairs={{0,16},{1,17},{2,18},{3,19},{8,24},{9,25},{10,26},{11,27},{16,4},{... | collective-permute-start | bytes 884744 | tf_op jit(solution)/shard_map/ppermute | solution.py:247
  250.3 11.1 %collective-permute-start.41 = (f16[96,768]{1,0:T(8,128)(2,1)S(1)}, f16[96,768]{1,0:T(8,128)(2,1)S(1)}, u32[]{:S(2)}, u32[]{:S(2)}) collective-permute-start(f16[96,768]{1,0:T(8,128)(2,1)S(1)} %multiply_convert_fusion), channel_id=1, source_target_pairs={{16,24},{24,16},{48,56},{56,48},{80,88},{88,80},{112,120},{120,112... | collective-permute-start | bytes 442376 | tf_op jit(solution)/shard_map/ppermute | solution.py:229
  288.6 8.2 %collective-permute-start.44 = (f16[768,96]{0,1:T(8,128)(2,1)S(1)}, f16[768,96]{0,1:T(8,128)(2,1)S(1)}, u32[]{:S(2)}, u32[]{:S(2)}) collective-permute-start(f16[768,96]{0,1:T(8,128)(2,1)S(1)} %squeeze.199), channel_id=1, source_target_pairs={{0,104},{8,112},{16,120},{24,0},{32,8},{40,16},{48,24},{56,32},{64... | collective-permute-start | bytes 442376 | tf_op jit(solution)/shard_map/ppermute | solution.py:229
  (23 other events, 139.8 us)

commit v4 on v3

--- a/solution.py
+++ b/solution.py
@@ -25,14 +25,18 @@
 ]
 
 BATCHES = [
-    [["A0A0", "P0A1"],
-     ["A1A0", "A1A1"],
-     ["A2A2", "A0A0"],
-     ["A3A2", "A3A3"]],
-    [["A3A1", "P0A3"],
-     ["A3A0", "A3A3"],
-     ["A0B3", "A2B3"],
-     ["A3A0", "A2A0"]],
+    [["A0A0"],
+     ["A1A1"],
+     ["A2A2"],
+     ["A3A3"]],
+    [["P0A1", "P0A3"],
+     ["A1A0", "A3A0"],
+     ["A0A0", "A0B3"],
+     ["A3A2", "A3A0"]],
+    [["A3A1"],
+     ["A3A3"],
+     ["A2B3"],
+     ["A2A0"]],
     [["P0A2", "A2A1"],
      ["P1A2", "P1A3"],
      ["P0A1", "A0B2"],
@@ -187,38 +191,34 @@
     )(occ_index[None, :], virt_index[None, :], occ_table, virt_table)
 
 
-def halves_kernel(x_lo, coeffs, mine, other, largest):
-    for low in range(2):
-        @pl.when(x_lo[0] == low)
-        def _():
-            mine[...] = coeffs[:, low * HALF:(low + 1) * HALF]
-            other[...] = coeffs[:, (1 - low) * HALF:(2 - low) * HALF]
+def half_kernel(which, coeffs, half, largest):
+    half[...] = coeffs[...]
 
     @pl.when(pl.program_id(0) == 0)
     def _():
         largest[...] = jnp.zeros_like(largest)
 
     top = jnp.zeros((coeffs.shape[0], 128), jnp.float32)
-    for c in range(coeffs.shape[1] // 128):
+    for c in range(HALF // 128):
         top = jnp.maximum(top, jnp.abs(coeffs[:, c * 128:(c + 1) * 128].astype(jnp.float32)))
     largest[...] = jnp.maximum(largest[...], jnp.max(top.reshape(-1, 8, 128), axis=0))
 
 
-def cut_in_halves(x_lo, coeffs):
-    half = jax.ShapeDtypeStruct((ROWS, HALF), jnp.bfloat16)
-    block = pl.BlockSpec((PART, HALF), lambda i, t: (i, 0))
+def cut_half(which, coeffs):
     return pl.pallas_call(
-        halves_kernel,
+        half_kernel,
         grid_spec=pltpu.PrefetchScalarGridSpec(
             num_scalar_prefetch=1,
             grid=(ROWS // PART,),
-            in_specs=[pl.BlockSpec((PART, 2 * HALF), lambda i, t: (i, 0))],
-            out_specs=[block, block, pl.BlockSpec((8, 128), lambda i, t: (0, 0))],
+            in_specs=[pl.BlockSpec((PART, HALF), lambda i, t: (i, t[0]))],
+            out_specs=[pl.BlockSpec((PART, HALF), lambda i, t: (i, 0)),
+                       pl.BlockSpec((8, 128), lambda i, t: (0, 0))],
         ),
-        out_shape=[half, half, jax.ShapeDtypeStruct((8, 128), jnp.float32)],
-        compiler_params=pltpu.CompilerParams(vmem_limit_bytes=24 * 1024 * 1024),
+        out_shape=[jax.ShapeDtypeStruct((ROWS, HALF), jnp.bfloat16),
+                   jax.ShapeDtypeStruct((8, 128), jnp.float32)],
+        compiler_params=pltpu.CompilerParams(vmem_limit_bytes=60 * 1024 * 1024),
         cost_estimate=pl.CostEstimate(flops=0, bytes_accessed=PART * ROWS, transcendentals=0),
-    )(x_lo[None], coeffs)
+    )(which[None], coeffs)
 
 
 def moves(pairs):
@@ -264,8 +264,9 @@
 
 def slot_names(role):
     names = []
-    for batch in BATCHES:
-        names += [(tile, h) for h in range(2) for tile in batch[role]]
+    first, second, *rest = [batch[role] for batch in BATCHES]
+    for tiles in [first + second] + rest:
+        names += [(tile, h) for h in range(2) for tile in tiles]
     early, late = MOVED[role][:2], MOVED[role][2:]
     names += [(tile, h) for h in range(2) for tile in early]
     names += [(tile, h) for h in range(2) for tile in late]
@@ -330,7 +331,11 @@
     x_hi = lax.axis_index("pair") // 4
     y = lax.rem(lax.axis_index("pair"), 4)
 
-    mine, other, largest = cut_in_halves(x_lo.astype(jnp.int32), coeffs)
+    which = x_lo.astype(jnp.int32)
+    mine, largest = cut_half(which, coeffs)
+    which, mine, largest = lax.optimization_barrier((which, mine, largest))
+    other, larger = cut_half(1 - which, coeffs)
+    largest = jnp.maximum(largest, larger)
     halo_a = aux_permute(mine, [(0, 0, -1), (3, 3, 1)])
     far_a = aux_permute(other, [(0, 2, 0), (3, 1, 0)])
     sib = aux_permute(mine, [(0, 1, 0), (1, 0, 0), (2, 3, 0), (3, 2, 0)])
@@ -344,7 +349,7 @@
     largest = jnp.maximum(largest, aux_permute(largest, [(1, 0, 0), (2, 3, 0)]))
     scales = scales_of(jnp.max(largest))
 
-    occ_index, virt_index = after([occ_index, virt_index], mine)
+    occ_index, virt_index = after([occ_index, virt_index], largest)
     begin = x_lo * HALF
     gap = pair_gaps(
         lax.dynamic_slice_in_dim(occ_index, begin, HALF),
@@ -361,76 +366,81 @@
         plans.append([used, row, held_most])
     entries = lax.dynamic_index_in_dim(jnp.asarray(entry_table()), role * 2 + x_hi, axis=0, keepdims=False)
     rows = [plan[1] for plan in plans]
-    far_a, halo_a, sib, scales, weight, entries, rows = lax.optimization_barrier(
-        (far_a, halo_a, sib, scales, weight, entries, rows))
-
-    far_b = aux_permute(after(other, far_a), [(1, 3, 0), (2, 0, 0)])
-    halo_b = aux_permute(after(mine, halo_a), [(1, 1, -1), (2, 2, 1)])
-    far_a_sib = aux_permute(far_a, [(1, 0, 0), (2, 3, 0)])
-    halo_a_sib = aux_permute(halo_a, [(3, 2, 0)])
-    minor = aux_permute(far_a, [(1, 0, 1), (2, 2, -1)])
-
-    held = {OWN: mine, SIB: sib, FAR_A: far_a, HALO_A: halo_a}
+    held = {OWN: mine}
 
     def tiles(number):
         used, _, held_most = plans[number]
         return tile_batch(BATCHES[number], rows[number], held_most, weight, [held[s] for s in used])
 
-    def first_sends(partial, scales):
-        return [narrow(jnp.concatenate([partial[2, 0], partial[1, 1]]), scales),
-                narrow(jnp.concatenate([partial[2, 1], partial[3, 0]]), scales)]
+    def part(partials, k, d):
+        return jnp.concatenate([partial[k, d] for partial in partials])
+
+    def first_sends(partials):
+        return [narrow(jnp.concatenate([part(partials, 2, 0), part(partials, 1, 1)]), scales),
+                narrow(jnp.concatenate([part(partials, 2, 1), part(partials, 3, 0)]), scales)]
 
     def first_round(sends):
         return [y_permute(sends[0], 1), y_permute(sends[1], -1)]
 
-    def second_sends(partial, got, scales):
-        return [narrow(partial[1, 0] + wide(got[0][:2], scales), scales),
-                narrow(partial[3, 1] + wide(got[1][:2], scales), scales)]
-
-    def finish(partial, got, more, scales):
-        zero = partial[0, 0] + wide(got[1][2:], scales) + wide(more[0], scales)
-        one = partial[0, 1] + wide(got[0][2:], scales) + wide(more[1], scales)
+    def second_sends(partials, got):
+        count = got[0].shape[0] // 2
+        return [narrow(part(partials, 1, 0) + wide(got[0][:count], scales), scales),
+                narrow(part(partials, 3, 1) + wide(got[1][:count], scales), scales)]
+
+    def finish(partials, got, more):
+        count = more[0].shape[0]
+        zero = part(partials, 0, 0) + wide(got[1][count:], scales) + wide(more[0], scales)
+        one = part(partials, 0, 1) + wide(got[0][count:], scales) + wide(more[1], scales)
         return [zero, one]
 
-    partial0 = tiles(0)
-    sends0 = first_sends(partial0, scales)
-    held[FAR_A_SIB], held[HALO_A_SIB] = after([far_a_sib, halo_a_sib], sends0)
+    alone = tiles(0)
+    far_a, sib, scales, weight, entries, rows, alone = lax.optimization_barrier(
+        (far_a, sib, scales, weight, entries, rows, alone))
+
+    far_b = aux_permute(after(other, far_a), [(1, 3, 0), (2, 0, 0)])
+    minor = aux_permute(far_a, [(1, 0, 1), (2, 2, -1)])
+    far_a_sib = aux_permute(far_a, [(1, 0, 0), (2, 3, 0)])
+    halo_b = aux_permute(after(mine, halo_a), [(1, 1, -1), (2, 2, 1)])
+    halo_a_sib = aux_permute(halo_a, [(3, 2, 0)])
+    held.update({SIB: sib, FAR_A: far_a, FAR_A_SIB: far_a_sib, HALO_A: halo_a, HALO_A_SIB: halo_a_sib})
+
+    partial0 = [alone, tiles(1)]
+    sends0 = first_sends(partial0)
     got0 = first_round(sends0)
-    partial1 = tiles(1)
-    sends1 = first_sends(partial1, scales)
-    got0, sends1 = lax.optimization_barrier((got0, sends1))
-    got1 = first_round(sends1)
-    sends0 = second_sends(partial0, got0, scales)
-    more0 = first_round(sends0)
-    far_b, halo_b, minor, got1 = lax.optimization_barrier((far_b, halo_b, minor, got1, sends0))[:4]
-    more1 = first_round(second_sends(partial1, got1, scales))
+    far_b, minor, rows = lax.optimization_barrier((far_b, minor, rows, got0))[:3]
     held[FAR_B], held[HALO_B], held[MINOR] = far_b, halo_b, minor
     held[FAR_B_SIB] = aux_permute(far_b, [(0, 1, 0), (3, 2, 0)])
     held[HALO_B_SIB] = aux_permute(halo_b, [(2, 3, 0)])
-    partial2 = tiles(2)
-    sends2 = first_sends(partial2, scales)
+    partial1 = [tiles(2)]
+    sends1 = first_sends(partial1)
+    got0, sends1 = lax.optimization_barrier((got0, sends1))
+    got1 = first_round(sends1)
+    more0 = first_round(second_sends(partial0, got0))
+    more1 = first_round(second_sends(partial1, got1))
+    partial2 = [tiles(3)]
+    sends2 = first_sends(partial2)
     got2 = first_round(sends2)
-    rows[3], more0 = lax.optimization_barrier((rows[3], more0, sends2))[:2]
-    partial3 = tiles(3)
-    more0, more1 = after([more0, more1], partial3)
-    total0 = finish(partial0, got0, more0, scales)
-    total1 = finish(partial1, got1, more1, scales)
-    moved0 = jnp.stack([total0[0][1], total1[0][1], total0[1][1], total1[1][1]])
-    moved0 = aux_permute(narrow(moved0, scales), [(0, 0, 1)])
-    sends3 = first_sends(partial3, scales)
+    rows[4], more0 = lax.optimization_barrier((rows[4], more0, sends2))[:2]
+    partial3 = [tiles(4)]
+    sends3 = first_sends(partial3)
     got2 = after(got2, partial3)
-    sends2 = second_sends(partial2, got2, scales)
+    sends2 = second_sends(partial2, got2)
     more2 = first_round(sends2)
     sends3 = after(sends3, sends2)
     got3 = first_round(sends3)
+    more0, more1 = after([more0, more1], sends3)
+    total0 = finish(partial0, got0, more0)
+    total1 = finish(partial1, got1, more1)
+    moved0 = narrow(jnp.concatenate([total0[0][1:], total0[1][1:]]), scales)
+    moved0 = aux_permute(moved0, [(0, 0, 1)])
     more2 = after(more2, sends3)
-    total2 = finish(partial2, got2, more2, scales)
+    total2 = finish(partial2, got2, more2)
     moved2 = narrow(jnp.concatenate(total2), scales)
     moved2 = aux_permute(moved2, [(0, 0, 1), (1, 1, 1), (2, 2, 1)])
     got3, moved2, moved0 = lax.optimization_barrier((got3, moved2, moved0))
-    more3 = both_ways(y_permute, *second_sends(partial3, got3, scales))
+    more3 = both_ways(y_permute, *second_sends(partial3, got3))
     moved0, moved2 = wide(moved0, scales), wide(moved2, scales)
-    total3 = finish(partial3, got3, more3, scales)
+    total3 = finish(partial3, got3, more3)
     slots = jnp.concatenate(total0 + total1 + total2 + total3 + [moved0, moved2])
     parts = pick_parts(entries, slots).reshape(4, 2, 2, PART, ROWS)
 

time: 299 us -> 328 us (1.097)
  Pallas kernels: 69.4 us -> 83.6 us
  waiting for transfers between devices: 77.2 us -> 87.1 us
  starting transfers between devices: 87.1 us -> 92.7 us
    ppermute x21, waiting for transfers between devices: 41.7 us -> 58.3 us  [aux_permute(): return lax.ppermute(value, 'aux', moves(pairs))]
    ppermute x5, starting transfers between devices: 11.3 us -> 20.9 us  [x_permute(): return lax.ppermute(value, ('aux', 'pair'), perm)]
    pallas_call x1 -> x2, Pallas kernels: 4.96 us -> 13.7 us  [cut_half(): pl.pallas_call(half_kernel, grid_spec=pltpu.PrefetchScalarGridSpec(num_sc...]
    ppermute x19, waiting for transfers between devices: 19.8 us -> 11.7 us  [y_permute(): lax.ppermute(value, 'pair', [(h * 4 + y, h * 4 + (y + by) % 4) for h in r...]
    pallas_call x4 -> x5, Pallas kernels: 58.8 us -> 64.2 us  [tile_batch(): pl.pallas_call(functools.partial(tiles_kernel, count, held_most, len(sour...]
    unnamed x22 -> x56, local copies, waits for them, and re-layouts: 8.9 us -> 3.77 us
    squeeze x4 -> x5, local copies, waits for them, and re-layouts: 5.42 us -> 10.2 us  [part(): return jnp.concatenate([partial[k, d] for partial in partials])]
    convert_element_type x19 -> x20, other arithmetic: 6.61 us -> 6.02 us  [narrow(): return (value * scales[0]).astype(jnp.float16)]
  transfers between devices with their start and end apart: 45 -> 45, of which waited for: 15 -> 15; matrix products, arithmetic and copies ran while one was open for 9% -> 11% of each run, Pallas kernels for 21% -> 21%
where the time goes in v4:
time: 328 us; the launch traced here: 326 us
  starting transfers between devices  92.7 us (28%)
  waiting for transfers between devices  87.1 us (27%)
  Pallas kernels  83.6 us (25%)
  local copies, waits for them, and re-layouts  21.5 us (7%)
  other arithmetic  21.3 us (6%)
  blocking collectives  17.9 us (5%)
    pallas_call x5, Pallas kernels, tile_batch(): pl.pallas_call(functools.partial(tiles_kernel, count, held_most, len(sour...  64.2 us
    ppermute x21, waiting for transfers between devices, aux_permute(): return lax.ppermute(value, 'aux', moves(pairs))  58.3 us
    ppermute x21, starting transfers between devices, aux_permute(): return lax.ppermute(value, 'aux', moves(pairs))  47.3 us
    ppermute x19, starting transfers between devices, y_permute(): lax.ppermute(value, 'pair', [(h * 4 + y, h * 4 + (y + by) % 4) for h in r...  24.5 us
    ppermute x5, starting transfers between devices, x_permute(): return lax.ppermute(value, ('aux', 'pair'), perm)  20.9 us
    all_to_all x1, blocking collectives, local(): lax.all_to_all(crossed, 'pair', split_axis=2, concat_axis=1, tiled=True)  17.9 us
    ppermute x5, waiting for transfers between devices, x_permute(): return lax.ppermute(value, ('aux', 'pair'), perm)  17.2 us
    pallas_call x2, Pallas kernels, cut_half(): pl.pallas_call(half_kernel, grid_spec=pltpu.PrefetchScalarGridSpec(num_sc...  13.7 us
  transfers between devices with their start and end apart: 45, of which 15 were waited for; matrix products, arithmetic and copies ran while one was open for 11% of the time, Pallas kernels for 21%

profile of v4, /device:TPU:3, one launch (start us, length us, event | category | flops | bytes accessed | tf_op | source)
XLA Modules:
  0.0 326.4 jit_solution(14936756812549546023)
XLA Ops:
  0.0 6.8 %shard_map.109 = (bf16[768,3072]{1,0:T(8,128)(2,1)}, f32[8,128]{1,0:T(8,128)}) custom-call(s32[1]{0:T(128)} %bitcast.which, bf16[768,6144]{1,0:T(8,128)(2,1)} %coeffs.3), custom_call_target="tpu_custom_call" | custom-call | bytes 73728 | tf_op jit(solution)/shard_map/pallas_call | solution.py:208
  6.9 6.9 %shard_map.110 = (bf16[768,3072]{1,0:T(8,128)(2,1)}, f32[8,128]{1,0:T(8,128)}) custom-call(s32[1]{0:T(128)} %bitcast.1.which, bf16[768,6144]{1,0:T(8,128)(2,1)} %coeffs.3), custom_call_target="tpu_custom_call" | custom-call | bytes 73728 | tf_op jit(solution)/shard_map/pallas_call | solution.py:208
  13.8 3.5 %collective-permute-start = (bf16[768,3072]{1,0:T(8,128)(2,1)}, bf16[768,3072]{1,0:T(8,128)(2,1)}, u32[]{:S(2)}, u32[]{:S(2)}) collective-permute-start(bf16[768,3072]{1,0:T(8,128)(2,1)} %get-tuple-element.75), channel_id=1, source_target_pairs={{0,16},{24,8},{32,48},{56,40},{64,80},{88,72},{96,112},{120,104},{... | collective-permute-start | bytes 14155784 | tf_op jit(solution)/shard_map/ppermute | solution.py:229
  17.3 4.4 %collective-permute-start.12 = (bf16[768,3072]{1,0:T(8,128)(2,1)}, bf16[768,3072]{1,0:T(8,128)(2,1)}, u32[]{:S(2)}, u32[]{:S(2)}) collective-permute-start(bf16[768,3072]{1,0:T(8,128)(2,1)} %get-tuple-element.86.refs_0_), channel_id=1, source_target_pairs={{0,96},{24,56},{32,0},{56,88},{64,32},{88,120},{96,64},{120,24},{1... | collective-permute-start | bytes 14155784 | tf_op jit(solution)/shard_map/ppermute | solution.py:229
  25.2 3.7 %collective-permute-start.4 = (f32[8,128]{1,0:T(8,128)S(1)}, f32[8,128]{1,0:T(8,128)S(1)}, u32[]{:S(2)}, u32[]{:S(2)}) collective-permute-start(f32[8,128]{1,0:T(8,128)S(1)} %max.34), channel_id=1, source_target_pairs={{0,2},{1,3},{2,0},{3,1},{4,6},{5,7},{6,4},{7,5},{8,10},{9,11},{10,... | collective-permute-start | bytes 12296 | tf_op jit(solution)/shard_map/ppermute | solution.py:233
  41.5 23.3 %collective-permute-done.10 = f32[8,128]{1,0:T(8,128)S(1)} collective-permute-done((f32[8,128]{1,0:T(8,128)S(1)}, f32[8,128]{1,0:T(8,128)S(1)}, u32[]{:S(2)}, u32[]{:S(2)}) %collective-permute-start.10) | collective-permute-done | bytes 4128 | tf_op jit(solution)/shard_map/ppermute | solution.py:229
  68.0 4.8 %shard_map.111 = f32[1,3072]{1,0:T(1,128)} custom-call(s32[1,3072]{1,0:T(1,128)} %bitcast.251, s32[1,3072]{1,0:T(1,128)} %bitcast.252, f32[32,128]{1,0:T(8,128)} %bitcast.254, f32[256,128]{1,0:T(8,128)} %bitcast.253), custom_call_target="tpu_custom_call" | custom-call | flops 679477248 | bytes 200000 | tf_op jit(solution)/shard_map/pallas_call | solution.py:182
  74.1 10.4 %shard_map.112 = f32[4,2,1,96,768]{4,3,2,1,0:T(8,128)} custom-call(s32[6]{0:T(128)} %pad_add_fusion.table, f32[1,3072]{1,0:T(1,128)} %add_divide_fusion.weight, bf16[768,3072]{1,0:T(8,128)(2,1)} %get-tuple-element.86.refs_0_), custom_call_target="tpu_custom_call" | custom-call | flops 589824 | bytes 589824 | tf_op jit(solution)/shard_map/pallas_call | solution.py:131
  85.8 7.3 %collective-permute-start.13 = (bf16[768,3072]{1,0:T(8,128)(2,1)}, bf16[768,3072]{1,0:T(8,128)(2,1)}, u32[]{:S(2)}, u32[]{:S(2)}) collective-permute-start(bf16[768,3072]{1,0:T(8,128)(2,1)} %collective-permute-done.12.refs_4_.refs_5_), channel_id=1, source_target_pairs={{24,16},{56,48},{88,80},{120,112},{25,17},{57,49},{89,81},{121,113... | collective-permute-start | bytes 14155784 | tf_op jit(solution)/shard_map/ppermute | solution.py:229
  94.4 2.8 collective-permute-start.17
  97.2 2.8 collective-permute-start.21
  100.0 2.7 slice_bitcast_fusion.41
  102.6 14.5 %shard_map.113 = f32[4,2,2,96,768]{4,3,2,1,0:T(8,128)} custom-call(s32[13]{0:T(128)} %get-tuple-element.70.table, f32[1,3072]{1,0:T(1,128)} %add_divide_fusion.weight, bf16[768,3072]{1,0:T(8,128)(2,1)} %get-tuple-element.86.refs_0_, bf16[768,3072]{1,0:T(8,128)(2,1)} %collective-permute-done.1.refs_1_.refs_0_, ...), custom_call_target="tpu_custom_call" | custom-call | flops 1179648 | bytes 1179648 | tf_op jit(solution)/shard_map/pallas_call | solution.py:131
  117.1 2.6 slice_bitcast_fusion.14
  120.2 2.7 collective-permute-start.15
  122.9 25.7 %collective-permute-done.16.refs_3_ = bf16[768,3072]{1,0:T(8,128)(2,1)} collective-permute-done((bf16[768,3072]{1,0:T(8,128)(2,1)}, bf16[768,3072]{1,0:T(8,128)(2,1)}, u32[]{:S(2)}, u32[]{:S(2)}) %collective-permute-start.16) | collective-permute-done | bytes 4718624 | tf_op jit(solution)/shard_map/ppermute | solution.py:229
  148.6 5.5 %collective-permute-start.20 = (bf16[768,3072]{1,0:T(8,128)(2,1)}, bf16[768,3072]{1,0:T(8,128)(2,1)}, u32[]{:S(2)}, u32[]{:S(2)}) collective-permute-start(bf16[768,3072]{1,0:T(8,128)(2,1)} %collective-permute-done.16.refs_3_), channel_id=1, source_target_pairs={{0,8},{24,16},{32,40},{56,48},{64,72},{88,80},{96,104},{120,112},{... | collective-permute-start | bytes 14155784 | tf_op jit(solution)/shard_map/ppermute | solution.py:229
  155.4 10.4 %shard_map.114 = f32[4,2,1,96,768]{4,3,2,1,0:T(8,128)} custom-call(s32[8]{0:T(128)} %pad_add_fusion.2.table, f32[1,3072]{1,0:T(1,128)} %add_divide_fusion.weight, bf16[768,3072]{1,0:T(8,128)(2,1)} %get-tuple-element.86.refs_0_, bf16[768,3072]{1,0:T(8,128)(2,1)} %collective-permute-done.1.refs_1_.refs_0_, ...), custom_call_target="tpu_custom_call" | custom-call | flops 589824 | bytes 589824 | tf_op jit(solution)/shard_map/pallas_call | solution.py:131
  172.2 14.5 %shard_map.115 = f32[4,2,2,96,768]{4,3,2,1,0:T(8,128)} custom-call(s32[15]{0:T(128)} %pad_add_fusion.3.table, f32[1,3072]{1,0:T(1,128)} %add_divide_fusion.weight, bf16[768,3072]{1,0:T(8,128)(2,1)} %collective-permute-done.1.refs_1_.refs_0_, bf16[768,3072]{1,0:T(8,128)(2,1)} %collective-permute-done.refs_2_.refs_1_, ...), custom_call_target="tpu_custom_call" | custom-call | flops 1179648 | bytes 1179648 | tf_op jit(solution)/shard_map/pallas_call | solution.py:131
  190.3 2.7 collective-permute-start.28
  196.6 14.5 %shard_map.116 = f32[4,2,2,96,768]{4,3,2,1,0:T(8,128)} custom-call(s32[13]{0:T(128)} %get-tuple-element.92.table, f32[1,3072]{1,0:T(1,128)} %add_divide_fusion.weight, bf16[768,3072]{1,0:T(8,128)(2,1)} %get-tuple-element.86.refs_0_, bf16[768,3072]{1,0:T(8,128)(2,1)} %collective-permute-done.1.refs_1_.refs_0_, ...), custom_call_target="tpu_custom_call" | custom-call | flops 1179648 | bytes 1179648 | tf_op jit(solution)/shard_map/pallas_call | solution.py:131
  214.6 2.7 collective-permute-start.30
  217.3 2.7 collective-permute-start.32
  230.0 2.7 collective-permute-start.36
  232.6 7.6 %collective-permute-done.35 = f16[2,96,768]{2,1,0:T(8,128)(2,1)S(1)} collective-permute-done((f16[2,96,768]{2,1,0:T(8,128)(2,1)S(1)}, f16[2,96,768]{2,1,0:T(8,128)(2,1)S(1)}, u32[]{:S(2)}, u32[]{:S(2)}) %collective-permute-start.35) | collective-permute-done | bytes 294944 | tf_op jit(solution)/shard_map/ppermute | solution.py:233
  241.8 18.6 %collective-permute-start.37 = (f16[4,96,768]{2,1,0:T(8,128)(2,1)S(1)}, f16[4,96,768]{2,1,0:T(8,128)(2,1)S(1)}, u32[]{:S(2)}, u32[]{:S(2)}) collective-permute-start(f16[4,96,768]{2,1,0:T(8,128)(2,1)S(1)} %fusion.8), channel_id=1, source_target_pairs={{0,16},{1,17},{2,18},{3,19},{8,24},{9,25},{10,26},{11,27},{16,4},{... | collective-permute-start | bytes 1769480 | tf_op jit(solution)/shard_map/ppermute | solution.py:247
  260.6 6.6 %collective-permute-done.37 = f16[4,96,768]{2,1,0:T(8,128)(2,1)S(1)} collective-permute-done((f16[4,96,768]{2,1,0:T(8,128)(2,1)S(1)}, f16[4,96,768]{2,1,0:T(8,128)(2,1)S(1)}, u32[]{:S(2)}, u32[]{:S(2)}) %collective-permute-start.37) | collective-permute-done | bytes 589856 | tf_op jit(solution)/shard_map/ppermute | solution.py:247
  271.4 5.5 %collective-permute-done.39 = f16[2,96,768]{2,1,0:T(8,128)(2,1)S(1)} collective-permute-done((f16[2,96,768]{2,1,0:T(8,128)(2,1)S(1)}, f16[2,96,768]{2,1,0:T(8,128)(2,1)S(1)}, u32[]{:S(2)}, u32[]{:S(2)}) %collective-permute-start.39) | collective-permute-done | bytes 294944 | tf_op jit(solution)/shard_map/ppermute | solution.py:247
  276.9 2.7 collective-permute-done.40
  281.5 10.6 %collective-permute-start.41 = (f16[96,768]{1,0:T(8,128)(2,1)S(1)}, f16[96,768]{1,0:T(8,128)(2,1)S(1)}, u32[]{:S(2)}, u32[]{:S(2)}) collective-permute-start(f16[96,768]{1,0:T(8,128)(2,1)S(1)} %multiply_convert_fusion), channel_id=1, source_target_pairs={{16,24},{24,16},{48,56},{56,48},{80,88},{88,80},{112,120},{120,112... | collective-permute-start | bytes 442376 | tf_op jit(solution)/shard_map/ppermute | solution.py:229
  294.8 17.9 %all_to_all.15 = f16[3,96,8,96]{1,3,0,2:T(8,128)(2,1)S(1)} all-to-all(f16[3,96,8,96]{1,3,0,2:T(8,128)(2,1)S(1)} %fusion.10), channel_id=1, replica_groups=mesh['aux'=16,'pair'=8] {'pair'}, dimensions={2} | all-to-all | bytes 884736 | tf_op jit(solution)/shard_map/all_to_all | solution.py:454
  319.4 3.0 collective-permute-done.43
  (201 shorter events, 71.1 us)
Async XLA Ops:
  13.8 70.7 %collective-permute-start = (bf16[768,3072]{1,0:T(8,128)(2,1)}, bf16[768,3072]{1,0:T(8,128)(2,1)}, u32[]{:S(2)}, u32[]{:S(2)}) collective-permute-start(bf16[768,3072]{1,0:T(8,128)(2,1)} %get-tuple-element.75), channel_id=1, source_target_pairs={{0,16},{24,8},{32,48},{56,40},{64,80},{88,72},{96,112},{120,104},{... | collective-permute-start | bytes 14155784 | tf_op jit(solution)/shard_map/ppermute | solution.py:229
  17.3 67.2 %collective-permute-start.1 = (bf16[768,3072]{1,0:T(8,128)(2,1)}, bf16[768,3072]{1,0:T(8,128)(2,1)}, u32[]{:S(2)}, u32[]{:S(2)}) collective-permute-start(bf16[768,3072]{1,0:T(8,128)(2,1)} %get-tuple-element.86.refs_0_), channel_id=1, source_target_pairs={{0,8},{8,0},{16,24},{24,16},{32,40},{40,32},{48,56},{56,48},{64,72... | collective-permute-start | bytes 14155784 | tf_op jit(solution)/shard_map/ppermute | solution.py:229
  17.3 68.5 %collective-permute-start.12 = (bf16[768,3072]{1,0:T(8,128)(2,1)}, bf16[768,3072]{1,0:T(8,128)(2,1)}, u32[]{:S(2)}, u32[]{:S(2)}) collective-permute-start(bf16[768,3072]{1,0:T(8,128)(2,1)} %get-tuple-element.86.refs_0_), channel_id=1, source_target_pairs={{0,96},{24,56},{32,0},{56,88},{64,32},{88,120},{96,64},{120,24},{1... | collective-permute-start | bytes 14155784 | tf_op jit(solution)/shard_map/ppermute | solution.py:229
  39.5 25.3 %collective-permute-start.10 = (f32[8,128]{1,0:T(8,128)S(1)}, f32[8,128]{1,0:T(8,128)S(1)}, u32[]{:S(2)}, u32[]{:S(2)}) collective-permute-start(f32[8,128]{1,0:T(8,128)S(1)} %max.41), channel_id=1, source_target_pairs={{8,0},{16,24},{40,32},{48,56},{72,64},{80,88},{104,96},{112,120},{... | collective-permute-start | bytes 12296 | tf_op jit(solution)/shard_map/ppermute | solution.py:229
  84.5 18.2 %collective-permute-start.11 = (bf16[768,3072]{1,0:T(8,128)(2,1)}, bf16[768,3072]{1,0:T(8,128)(2,1)}, u32[]{:S(2)}, u32[]{:S(2)}) collective-permute-start(bf16[768,3072]{1,0:T(8,128)(2,1)} %collective-permute-done.refs_2_.refs_1_), channel_id=1, source_target_pairs={{8,0},{16,24},{40,32},{48,56},{72,64},{80,88},{104,96},{112,120},{... | collective-permute-start | bytes 14155784 | tf_op jit(solution)/shard_map/ppermute | solution.py:229
  85.8 16.9 %collective-permute-start.13 = (bf16[768,3072]{1,0:T(8,128)(2,1)}, bf16[768,3072]{1,0:T(8,128)(2,1)}, u32[]{:S(2)}, u32[]{:S(2)}) collective-permute-start(bf16[768,3072]{1,0:T(8,128)(2,1)} %collective-permute-done.12.refs_4_.refs_5_), channel_id=1, source_target_pairs={{24,16},{56,48},{88,80},{120,112},{25,17},{57,49},{89,81},{121,113... | collective-permute-start | bytes 14155784 | tf_op jit(solution)/shard_map/ppermute | solution.py:229
  93.1 55.5 %collective-permute-start.16 = (bf16[768,3072]{1,0:T(8,128)(2,1)}, bf16[768,3072]{1,0:T(8,128)(2,1)}, u32[]{:S(2)}, u32[]{:S(2)}) collective-permute-start(bf16[768,3072]{1,0:T(8,128)(2,1)} %get-tuple-element.75), channel_id=1, source_target_pairs={{8,24},{16,0},{40,56},{48,32},{72,88},{80,64},{104,120},{112,96},{... | collective-permute-start | bytes 14155784 | tf_op jit(solution)/shard_map/ppermute | solution.py:229
  94.4 54.2 %collective-permute-start.17 = (bf16[768,3072]{1,0:T(8,128)(2,1)}, bf16[768,3072]{1,0:T(8,128)(2,1)}, u32[]{:S(2)}, u32[]{:S(2)}) collective-permute-start(bf16[768,3072]{1,0:T(8,128)(2,1)} %collective-permute-done.refs_2_.refs_1_), channel_id=1, source_target_pairs={{8,32},{16,112},{40,64},{48,16},{72,96},{80,48},{104,0},{112,80},{... | collective-permute-start | bytes 14155784 | tf_op jit(solution)/shard_map/ppermute | solution.py:229
  97.2 56.9 %collective-permute-start.21 = (bf16[768,3072]{1,0:T(8,128)(2,1)S(1)}, bf16[768,3072]{1,0:T(8,128)(2,1)}, u32[]{:S(2)}, u32[]{:S(2)}) collective-permute-start(bf16[768,3072]{1,0:T(8,128)(2,1)S(1)} %copy-done.1), channel_id=1, source_target_pairs={{8,104},{16,48},{40,8},{48,80},{72,40},{80,112},{104,72},{112,16},... | collective-permute-start | bytes 14155784 | tf_op jit(solution)/shard_map/ppermute | solution.py:229
  119.9 28.7 %collective-permute-start.14 = (f16[6,96,768]{2,1,0:T(8,128)(2,1)S(1)}, f16[6,96,768]{2,1,0:T(8,128)(2,1)S(1)}, u32[]{:S(2)}, u32[]{:S(2)}) collective-permute-start(f16[6,96,768]{2,1,0:T(8,128)(2,1)S(1)} %fusion), channel_id=1, source_target_pairs={{0,1},{1,2},{2,3},{3,0},{4,5},{5,6},{6,7},{7,4},{8,9},{9,10},{10,1... | collective-permute-start | bytes 2654216 | tf_op jit(solution)/shard_map/ppermute | solution.py:233
  120.2 28.4 %collective-permute-start.15 = (f16[6,96,768]{2,1,0:T(8,128)(2,1)S(1)}, f16[6,96,768]{2,1,0:T(8,128)(2,1)S(1)}, u32[]{:S(2)}, u32[]{:S(2)}) collective-permute-start(f16[6,96,768]{2,1,0:T(8,128)(2,1)S(1)} %fusion.1), channel_id=1, source_target_pairs={{0,3},{1,0},{2,1},{3,2},{4,7},{5,4},{6,5},{7,6},{8,11},{9,8},{10,9... | collective-permute-start | bytes 2654216 | tf_op jit(solution)/shard_map/ppermute | solution.py:233
  148.6 22.4 %collective-permute-start.20 = (bf16[768,3072]{1,0:T(8,128)(2,1)}, bf16[768,3072]{1,0:T(8,128)(2,1)}, u32[]{:S(2)}, u32[]{:S(2)}) collective-permute-start(bf16[768,3072]{1,0:T(8,128)(2,1)} %collective-permute-done.16.refs_3_), channel_id=1, source_target_pairs={{0,8},{24,16},{32,40},{56,48},{64,72},{88,80},{96,104},{120,112},{... | collective-permute-start | bytes 14155784 | tf_op jit(solution)/shard_map/ppermute | solution.py:229
  154.1 42.5 %collective-permute-start.26 = (bf16[768,3072]{1,0:T(8,128)(2,1)}, bf16[768,3072]{1,0:T(8,128)(2,1)}, u32[]{:S(2)}, u32[]{:S(2)}) collective-permute-start(bf16[768,3072]{1,0:T(8,128)(2,1)} %collective-permute-done.21.refs_6_), channel_id=1, source_target_pairs={{16,24},{48,56},{80,88},{112,120},{17,25},{49,57},{81,89},{113,121... | collective-permute-start | bytes 14155784 | tf_op jit(solution)/shard_map/ppermute | solution.py:229
  167.7 26.1 %collective-permute-start.18 = (f16[3,96,768]{2,1,0:T(8,128)(2,1)S(1)}, f16[3,96,768]{2,1,0:T(8,128)(2,1)S(1)}, u32[]{:S(2)}, u32[]{:S(2)}) collective-permute-start(f16[3,96,768]{2,1,0:T(8,128)(2,1)S(1)} %fusion.13), channel_id=1, source_target_pairs={{0,1},{1,2},{2,3},{3,0},{4,5},{5,6},{6,7},{7,4},{8,9},{9,10},{10,1... | collective-permute-start | bytes 1327112 | tf_op jit(solution)/shard_map/ppermute | solution.py:233
  168.8 25.8 %collective-permute-start.19 = (f16[3,96,768]{2,1,0:T(8,128)(2,1)S(1)}, f16[3,96,768]{2,1,0:T(8,128)(2,1)}, u32[]{:S(2)}, u32[]{:S(2)}) collective-permute-start(f16[3,96,768]{2,1,0:T(8,128)(2,1)S(1)} %fusion.15), channel_id=1, source_target_pairs={{0,3},{1,0},{2,1},{3,2},{4,7},{5,4},{6,5},{7,6},{8,11},{9,8},{10,9... | collective-permute-start | bytes 1327112 | tf_op jit(solution)/shard_map/ppermute | solution.py:233
  170.7 19.6 %collective-permute-start.24 = (f16[2,96,768]{2,1,0:T(8,128)(2,1)S(1)}, f16[2,96,768]{2,1,0:T(8,128)(2,1)S(1)}, u32[]{:S(2)}, u32[]{:S(2)}) collective-permute-start(f16[2,96,768]{2,1,0:T(8,128)(2,1)S(1)} %fusion.50), channel_id=1, source_target_pairs={{0,3},{1,0},{2,1},{3,2},{4,7},{5,4},{6,5},{7,6},{8,11},{9,8},{10,9... | collective-permute-start | bytes 884744 | tf_op jit(solution)/shard_map/ppermute | solution.py:233
  171.0 19.3 %collective-permute-start.22 = (f16[2,96,768]{2,1,0:T(8,128)(2,1)S(1)}, f16[2,96,768]{2,1,0:T(8,128)(2,1)S(1)}, u32[]{:S(2)}, u32[]{:S(2)}) collective-permute-start(f16[2,96,768]{2,1,0:T(8,128)(2,1)S(1)} %fusion.49), channel_id=1, source_target_pairs={{0,1},{1,2},{2,3},{3,0},{4,5},{5,6},{6,7},{7,4},{8,9},{9,10},{10,1... | collective-permute-start | bytes 884744 | tf_op jit(solution)/shard_map/ppermute | solution.py:233
  190.3 22.8 %collective-permute-start.27 = (f16[4,96,768]{2,1,0:T(8,128)(2,1)}, f16[4,96,768]{2,1,0:T(8,128)(2,1)}, u32[]{:S(2)}, u32[]{:S(2)}) collective-permute-start(f16[4,96,768]{2,1,0:T(8,128)(2,1)} %fusion.2), channel_id=1, source_target_pairs={{0,1},{1,2},{2,3},{3,0},{4,5},{5,6},{6,7},{7,4},{8,9},{9,10},{10,1... | collective-permute-start | bytes 1769480 | tf_op jit(solution)/shard_map/ppermute | solution.py:233
  190.3 22.8 %collective-permute-start.28 = (f16[4,96,768]{2,1,0:T(8,128)(2,1)}, f16[4,96,768]{2,1,0:T(8,128)(2,1)}, u32[]{:S(2)}, u32[]{:S(2)}) collective-permute-start(f16[4,96,768]{2,1,0:T(8,128)(2,1)} %fusion.3), channel_id=1, source_target_pairs={{0,3},{1,0},{2,1},{3,2},{4,7},{5,4},{6,5},{7,6},{8,11},{9,8},{10,9... | collective-permute-start | bytes 1769480 | tf_op jit(solution)/shard_map/ppermute | solution.py:233
  193.8 23.4 %collective-permute-start.23 = (f16[1,96,768]{2,1,0:T(8,128)(2,1)}, f16[1,96,768]{2,1,0:T(8,128)(2,1)}, u32[]{:S(2)}, u32[]{:S(2)}) collective-permute-start(f16[1,96,768]{2,1,0:T(8,128)(2,1)} %get-tuple-element.160), channel_id=1, source_target_pairs={{0,1},{1,2},{2,3},{3,0},{4,5},{5,6},{6,7},{7,4},{8,9},{9,10},{10,1... | collective-permute-start | bytes 442376 | tf_op jit(solution)/shard_map/ppermute | solution.py:233
  194.6 25.3 %collective-permute-start.25 = (f16[1,96,768]{2,1,0:T(8,128)(2,1)}, f16[1,96,768]{2,1,0:T(8,128)(2,1)}, u32[]{:S(2)}, u32[]{:S(2)}) collective-permute-start(f16[1,96,768]{2,1,0:T(8,128)(2,1)} %get-tuple-element.159), channel_id=1, source_target_pairs={{0,3},{1,0},{2,1},{3,2},{4,7},{5,4},{6,5},{7,6},{8,11},{9,8},{10,9... | collective-permute-start | bytes 442376 | tf_op jit(solution)/shard_map/ppermute | solution.py:233
  214.5 10.3 %collective-permute-start.29 = (f16[2,96,768]{2,1,0:T(8,128)(2,1)S(1)}, f16[2,96,768]{2,1,0:T(8,128)(2,1)S(1)}, u32[]{:S(2)}, u32[]{:S(2)}) collective-permute-start(f16[2,96,768]{2,1,0:T(8,128)(2,1)S(1)} %get-tuple-element.142), channel_id=1, source_target_pairs={{0,1},{1,2},{2,3},{3,0},{4,5},{5,6},{6,7},{7,4},{8,9},{9,10},{10,1... | collective-permute-start | bytes 884744 | tf_op jit(solution)/shard_map/ppermute | solution.py:233
  214.6 10.2 %collective-permute-start.30 = (f16[2,96,768]{2,1,0:T(8,128)(2,1)S(1)}, f16[2,96,768]{2,1,0:T(8,128)(2,1)S(1)}, u32[]{:S(2)}, u32[]{:S(2)}) collective-permute-start(f16[2,96,768]{2,1,0:T(8,128)(2,1)S(1)} %get-tuple-element.141), channel_id=1, source_target_pairs={{0,3},{1,0},{2,1},{3,2},{4,7},{5,4},{6,5},{7,6},{8,11},{9,8},{10,9... | collective-permute-start | bytes 884744 | tf_op jit(solution)/shard_map/ppermute | solution.py:233
  217.3 12.4 %collective-permute-start.31 = (f16[4,96,768]{2,1,0:T(8,128)(2,1)S(1)}, f16[4,96,768]{2,1,0:T(8,128)(2,1)S(1)}, u32[]{:S(2)}, u32[]{:S(2)}) collective-permute-start(f16[4,96,768]{2,1,0:T(8,128)(2,1)S(1)} %fusion.4), channel_id=1, source_target_pairs={{0,1},{1,2},{2,3},{3,0},{4,5},{5,6},{6,7},{7,4},{8,9},{9,10},{10,1... | collective-permute-start | bytes 1769480 | tf_op jit(solution)/shard_map/ppermute | solution.py:233
  217.3 12.3 %collective-permute-start.32 = (f16[4,96,768]{2,1,0:T(8,128)(2,1)S(1)}, f16[4,96,768]{2,1,0:T(8,128)(2,1)S(1)}, u32[]{:S(2)}, u32[]{:S(2)}) collective-permute-start(f16[4,96,768]{2,1,0:T(8,128)(2,1)S(1)} %fusion.5), channel_id=1, source_target_pairs={{0,3},{1,0},{2,1},{3,2},{4,7},{5,4},{6,5},{7,6},{8,11},{9,8},{10,9... | collective-permute-start | bytes 1769480 | tf_op jit(solution)/shard_map/ppermute | solution.py:233
  229.9 10.4 %collective-permute-start.35 = (f16[2,96,768]{2,1,0:T(8,128)(2,1)S(1)}, f16[2,96,768]{2,1,0:T(8,128)(2,1)S(1)}, u32[]{:S(2)}, u32[]{:S(2)}) collective-permute-start(f16[2,96,768]{2,1,0:T(8,128)(2,1)S(1)} %get-tuple-element.132), channel_id=1, source_target_pairs={{0,1},{1,2},{2,3},{3,0},{4,5},{5,6},{6,7},{7,4},{8,9},{9,10},{10,1... | collective-permute-start | bytes 884744 | tf_op jit(solution)/shard_map/ppermute | solution.py:233
  230.0 10.3 %collective-permute-start.36 = (f16[2,96,768]{2,1,0:T(8,128)(2,1)S(1)}, f16[2,96,768]{2,1,0:T(8,128)(2,1)S(1)}, u32[]{:S(2)}, u32[]{:S(2)}) collective-permute-start(f16[2,96,768]{2,1,0:T(8,128)(2,1)S(1)} %get-tuple-element.131), channel_id=1, source_target_pairs={{0,3},{1,0},{2,1},{3,2},{4,7},{5,4},{6,5},{7,6},{8,11},{9,8},{10,9... | collective-permute-start | bytes 884744 | tf_op jit(solution)/shard_map/ppermute | solution.py:233
  241.8 25.5 %collective-permute-start.37 = (f16[4,96,768]{2,1,0:T(8,128)(2,1)S(1)}, f16[4,96,768]{2,1,0:T(8,128)(2,1)S(1)}, u32[]{:S(2)}, u32[]{:S(2)}) collective-permute-start(f16[4,96,768]{2,1,0:T(8,128)(2,1)S(1)} %fusion.8), channel_id=1, source_target_pairs={{0,16},{1,17},{2,18},{3,19},{8,24},{9,25},{10,26},{11,27},{16,4},{... | collective-permute-start | bytes 1769480 | tf_op jit(solution)/shard_map/ppermute | solution.py:247
  260.6 9.1 %collective-permute-start.38 = (f16[4,96,768]{2,1,0:T(8,128)(2,1)S(1)}, f16[4,96,768]{2,1,0:T(8,128)(2,1)S(1)}, u32[]{:S(2)}, u32[]{:S(2)}) collective-permute-start(f16[4,96,768]{2,1,0:T(8,128)(2,1)S(1)} %fusion.9), channel_id=1, source_target_pairs={{0,20},{1,21},{2,22},{3,23},{8,28},{9,29},{10,30},{11,31},{16,0},{... | collective-permute-start | bytes 1769480 | tf_op jit(solution)/shard_map/ppermute | solution.py:247
  270.0 9.6 %collective-permute-start.40 = (f16[2,96,768]{2,1,0:T(8,128)(2,1)S(1)}, f16[2,96,768]{2,1,0:T(8,128)(2,1)S(1)}, u32[]{:S(2)}, u32[]{:S(2)}) collective-permute-start(f16[2,96,768]{2,1,0:T(8,128)(2,1)S(1)} %get-tuple-element.125), channel_id=1, source_target_pairs={{0,20},{1,21},{2,22},{3,23},{8,28},{9,29},{10,30},{11,31},{16,0},{... | collective-permute-start | bytes 884744 | tf_op jit(solution)/shard_map/ppermute | solution.py:247
  281.5 11.6 %collective-permute-start.41 = (f16[96,768]{1,0:T(8,128)(2,1)S(1)}, f16[96,768]{1,0:T(8,128)(2,1)S(1)}, u32[]{:S(2)}, u32[]{:S(2)}) collective-permute-start(f16[96,768]{1,0:T(8,128)(2,1)S(1)} %multiply_convert_fusion), channel_id=1, source_target_pairs={{16,24},{24,16},{48,56},{56,48},{80,88},{88,80},{112,120},{120,112... | collective-permute-start | bytes 442376 | tf_op jit(solution)/shard_map/ppermute | solution.py:229
  316.3 9.3 %collective-permute-start.44 = (f16[768,96]{0,1:T(8,128)(2,1)S(1)}, f16[768,96]{0,1:T(8,128)(2,1)S(1)}, u32[]{:S(2)}, u32[]{:S(2)}) collective-permute-start(f16[768,96]{0,1:T(8,128)(2,1)S(1)} %squeeze.237), channel_id=1, source_target_pairs={{0,104},{8,112},{16,120},{24,0},{32,8},{40,16},{48,24},{56,32},{64... | collective-permute-start | bytes 442376 | tf_op jit(solution)/shard_map/ppermute | solution.py:229
  (40 other events, 356.4 us)

commit v5 on v3

--- a/solution.py
+++ b/solution.py
@@ -48,6 +48,10 @@
     [["A0A0", "A0B3", "A0B2", "A0B1"], ["A2A2", "A2A1", "A3A1", "A2B3"]],
     [["A1A1", "A1A0", "A1B3", "A1B2"], ["A3A3", "A3A2", "A2A0", "A3A0"]],
 ]
+ORDER = [(2, 0), (1, 1), (2, 1), (3, 0), (0, 0), (0, 1), (1, 0), (3, 1)]
+ROW_ORDER = np.array([[ORDER.index(((rows % 4 - y) % 4, rows // 4)) for rows in range(8)] for y in range(4)], np.int32)
+
+
 def batch_tables(batch, sources):
     held_most = 0
     plans = []
@@ -80,13 +84,16 @@
     source_at = 3 * count
     first_at = source_at + held_most
 
+    def fetch(of_first):
+        for j in range(held_most):
+            for k in range(sources):
+                @pl.when((table[source_at + j] == k) & ((table[first_at + j] == 0) == of_first))
+                def _():
+                    pltpu.make_async_copy(source_refs[k], held.at[j], sems.at[j]).start()
+
     @pl.when(step == 0)
     def _():
-        for j in range(held_most):
-            for k in range(sources):
-                @pl.when(table[source_at + j] == k)
-                def _():
-                    pltpu.make_async_copy(source_refs[k], held.at[j], sems.at[j]).start()
+        fetch(True)
 
     def wait(block):
         for j in range(held_most):
@@ -109,17 +116,18 @@
     def _():
         wait(right)
 
-    here = table[first_at + held_most]
+    @pl.when(step == 0)
+    def _():
+        fetch(False)
+
+    order_at = first_at + held_most
     for n in range(ROWS // WIDE):
         columns = slice(n * WIDE, (n + 1) * WIDE)
         acc = lax.dot_general(
             scaled[...], held[right, columns, :],
             (((1,), (1,)), ((), ())), preferred_element_type=jnp.float32)
-        for y in range(4):
-            at = lax.rem(y + 4 - here, 4)
-            for h in range(2):
-                first = (h * 4 + y) * PART
-                out[at, h, 0, :, columns] = acc[first:first + PART]
+        for rows in range(8):
+            out[table[order_at + rows], 0, :, columns] = acc[rows * PART:(rows + 1) * PART]
 
 
 def tile_batch(batch, table_row, held_most, weight, sources):
@@ -131,14 +139,14 @@
             grid=(count,),
             in_specs=[pl.BlockSpec((1, HALF), lambda i, t: (0, 0))]
             + [pl.BlockSpec(memory_space=pl.ANY)] * len(sources),
-            out_specs=pl.BlockSpec((4, 2, 1, PART, ROWS), lambda i, t: (0, 0, i, 0, 0)),
+            out_specs=pl.BlockSpec((8, 1, PART, ROWS), lambda i, t: (0, i, 0, 0)),
             scratch_shapes=[
                 pltpu.VMEM((held_most, ROWS, HALF), jnp.bfloat16),
                 pltpu.VMEM((ROWS, HALF), jnp.bfloat16),
                 pltpu.SemaphoreType.DMA((held_most,)),
             ],
         ),
-        out_shape=jax.ShapeDtypeStruct((4, 2, count, PART, ROWS), jnp.float32),
+        out_shape=jax.ShapeDtypeStruct((8, count, PART, ROWS), jnp.float32),
         compiler_params=pltpu.CompilerParams(
             dimension_semantics=("arbitrary",), vmem_limit_bytes=56 * 1024 * 1024),
         cost_estimate=pl.CostEstimate(
@@ -251,15 +259,19 @@
     return lax.optimization_barrier((permute(up, 1), permute(down, -1)))
 
 
-def ring_sum(part, permute, scales):
-    count = part(0, 0).shape[0]
-    up, down = both_ways(permute, narrow(jnp.concatenate([part(2, 0), part(1, 1)]), scales),
-                         narrow(jnp.concatenate([part(2, 1), part(3, 0)]), scales))
-    up_more, down_more = both_ways(permute, narrow(part(1, 0) + wide(up[:count], scales), scales),
-                                   narrow(part(3, 1) + wide(down[:count], scales), scales))
-    zero = part(0, 0) + wide(down[count:], scales) + wide(up_more, scales)
-    one = part(0, 1) + wide(up[count:], scales) + wide(down_more, scales)
-    return zero, one
+def first_sends(terms, scales):
+    return [narrow(terms[0:2], scales), narrow(terms[2:4], scales)]
+
+
+def second_sends(terms, got, scales):
+    return [narrow(terms[6] + wide(got[0][0], scales), scales),
+            narrow(terms[7] + wide(got[1][0], scales), scales)]
+
+
+def finish(terms, got, more, scales, slots=slice(None)):
+    zero = terms[4][slots] + wide(got[1][1][slots], scales) + wide(more[0][slots], scales)
+    one = terms[5][slots] + wide(got[0][1][slots], scales) + wide(more[1][slots], scales)
+    return [zero, one]
 
 
 def slot_names(role):
@@ -278,9 +290,9 @@
         names = slot_names(role)
         for x_hi in range(2):
             row = []
-            for k in range(4):
+            for k, d in ORDER:
                 to = (x_hi * 2 + role // 2 + k) % 4
-                row += [names.index((tile, to // 2)) for tile in ENTRIES[role % 2][to % 2]]
+                row += [names.index((tile, to // 2)) for tile in ENTRIES[role % 2][to % 2][2 * d:2 * d + 2]]
             rows.append(row)
     return np.array(rows, np.int32)
 
@@ -357,12 +369,12 @@
         used = sorted({WHERE[r][t[i:i + 2]] for r in range(4) for t in batch[r] for i in (0, 2)})
         table, held_most = batch_tables(batch, used)
         row = lax.dynamic_index_in_dim(jnp.asarray(table), role, axis=0, keepdims=False)
-        row = jnp.concatenate([row, y[None].astype(jnp.int32)])
+        row = jnp.concatenate([row, lax.dynamic_index_in_dim(jnp.asarray(ROW_ORDER), y, axis=0, keepdims=False)])
         plans.append([used, row, held_most])
     entries = lax.dynamic_index_in_dim(jnp.asarray(entry_table()), role * 2 + x_hi, axis=0, keepdims=False)
     rows = [plan[1] for plan in plans]
-    far_a, halo_a, sib, scales, weight, entries, rows = lax.optimization_barrier(
-        (far_a, halo_a, sib, scales, weight, entries, rows))
+    halo_a, far_a, sib, scales, weight, entries, rows = lax.optimization_barrier(
+        (halo_a, far_a, sib, scales, weight, entries, rows))
 
     far_b = aux_permute(after(other, far_a), [(1, 3, 0), (2, 0, 0)])
     halo_b = aux_permute(after(mine, halo_a), [(1, 1, -1), (2, 2, 1)])
@@ -376,21 +388,8 @@
         used, _, held_most = plans[number]
         return tile_batch(BATCHES[number], rows[number], held_most, weight, [held[s] for s in used])
 
-    def first_sends(partial, scales):
-        return [narrow(jnp.concatenate([partial[2, 0], partial[1, 1]]), scales),
-                narrow(jnp.concatenate([partial[2, 1], partial[3, 0]]), scales)]
-
     def first_round(sends):
         return [y_permute(sends[0], 1), y_permute(sends[1], -1)]
-
-    def second_sends(partial, got, scales):
-        return [narrow(partial[1, 0] + wide(got[0][:2], scales), scales),
-                narrow(partial[3, 1] + wide(got[1][:2], scales), scales)]
-
-    def finish(partial, got, more, scales):
-        zero = partial[0, 0] + wide(got[1][2:], scales) + wide(more[0], scales)
-        one = partial[0, 1] + wide(got[0][2:], scales) + wide(more[1], scales)
-        return [zero, one]
 
     partial0 = tiles(0)
     sends0 = first_sends(partial0, scales)
@@ -400,23 +399,23 @@
     sends1 = first_sends(partial1, scales)
     got0, sends1 = lax.optimization_barrier((got0, sends1))
     got1 = first_round(sends1)
-    sends0 = second_sends(partial0, got0, scales)
-    more0 = first_round(sends0)
-    far_b, halo_b, minor, got1 = lax.optimization_barrier((far_b, halo_b, minor, got1, sends0))[:4]
-    more1 = first_round(second_sends(partial1, got1, scales))
+    more = second_sends(partial0, got0, scales)
+    minor, far_b, halo_b, got1, more = lax.optimization_barrier((minor, far_b, halo_b, got1, more))
     held[FAR_B], held[HALO_B], held[MINOR] = far_b, halo_b, minor
     held[FAR_B_SIB] = aux_permute(far_b, [(0, 1, 0), (3, 2, 0)])
     held[HALO_B_SIB] = aux_permute(halo_b, [(2, 3, 0)])
+    more = [jnp.concatenate(pair) for pair in zip(more, second_sends(partial1, got1, scales))]
+    more = first_round(more)
     partial2 = tiles(2)
     sends2 = first_sends(partial2, scales)
     got2 = first_round(sends2)
-    rows[3], more0 = lax.optimization_barrier((rows[3], more0, sends2))[:2]
+    more = after(more, sends2)
+    more0, more1 = [m[:2] for m in more], [m[2:] for m in more]
+    moved0 = [finish(partial0, got0, more0, scales, slice(1, 2)), finish(partial1, got1, more1, scales, slice(1, 2))]
+    moved0 = narrow(jnp.concatenate([tile[h] for h in range(2) for tile in moved0]), scales)
+    rows[3], moved0 = lax.optimization_barrier((rows[3], moved0, sends2))[:2]
+    moved0 = aux_permute(moved0, [(0, 0, 1)])
     partial3 = tiles(3)
-    more0, more1 = after([more0, more1], partial3)
-    total0 = finish(partial0, got0, more0, scales)
-    total1 = finish(partial1, got1, more1, scales)
-    moved0 = jnp.stack([total0[0][1], total1[0][1], total0[1][1], total1[1][1]])
-    moved0 = aux_permute(narrow(moved0, scales), [(0, 0, 1)])
     sends3 = first_sends(partial3, scales)
     got2 = after(got2, partial3)
     sends2 = second_sends(partial2, got2, scales)
@@ -426,18 +425,18 @@
     more2 = after(more2, sends3)
     total2 = finish(partial2, got2, more2, scales)
     moved2 = narrow(jnp.concatenate(total2), scales)
+    more0, more1 = after([more0, more1], moved2)
+    total0 = finish(partial0, got0, more0, scales)
+    total1 = finish(partial1, got1, more1, scales)
     moved2 = aux_permute(moved2, [(0, 0, 1), (1, 1, 1), (2, 2, 1)])
     got3, moved2, moved0 = lax.optimization_barrier((got3, moved2, moved0))
     more3 = both_ways(y_permute, *second_sends(partial3, got3, scales))
     moved0, moved2 = wide(moved0, scales), wide(moved2, scales)
     total3 = finish(partial3, got3, more3, scales)
     slots = jnp.concatenate(total0 + total1 + total2 + total3 + [moved0, moved2])
-    parts = pick_parts(entries, slots).reshape(4, 2, 2, PART, ROWS)
-
-    def x_part(k, d):
-        return parts[k, d]
-
-    zero, one = ring_sum(x_part, x_permute, scales)
+    terms = pick_parts(entries, slots).reshape(8, 2, PART, ROWS)
+    got = both_ways(x_permute, *first_sends(terms, scales))
+    zero, one = finish(terms, got, both_ways(x_permute, *second_sends(terms, got, scales)), scales)
     final = [zero[0], zero[1], one[0], one[1]]
 
     crossed = narrow(jnp.stack(final[1:]), scales).reshape(3, PART, 8, PART)

time: 299 us -> 296 us (0.990)
  local copies, waits for them, and re-layouts: 21.1 us -> 12.6 us
  other arithmetic: 20 us -> 27.4 us
  starting transfers between devices: 87.1 us -> 91.5 us
  waiting for transfers between devices: 77.2 us -> 73.8 us
    ppermute x21, starting transfers between devices: 49.5 us -> 55.9 us  [aux_permute(): return lax.ppermute(value, 'aux', moves(pairs))]
    ppermute x19 -> x17, waiting for transfers between devices: 19.8 us -> 14.1 us  [y_permute(): lax.ppermute(value, 'pair', [(h * 4 + y, h * 4 + (y + by) % 4) for h in r...]
    squeeze x5 -> x1, local copies, waits for them, and re-layouts: 5.57 us -> 0.69 us  [local(): lax.dynamic_index_in_dim(jnp.asarray(ROW_ORDER), y, axis=0, keepdims=False)]
    mul x0 -> x4, other arithmetic: none -> 3.74 us  [narrow(): return (value * scales[0]).astype(jnp.float16)]
    unnamed x22 -> x20, local copies, waits for them, and re-layouts: 8.9 us -> 5.84 us
    add x1 -> x3, other arithmetic: 1.48 us -> 4.5 us  [finish(): terms[4][slots] + wide(got[1][1][slots], scales)]
    unnamed x13 -> x11, other arithmetic: 7.26 us -> 4.56 us
    ppermute x19 -> x17, starting transfers between devices: 26.3 us -> 23.9 us  [y_permute(): lax.ppermute(value, 'pair', [(h * 4 + y, h * 4 + (y + by) % 4) for h in r...]
  transfers between devices with their start and end apart: 45 -> 43, of which waited for: 15 -> 16; matrix products, arithmetic and copies ran while one was open for 9% -> 10% of each run, Pallas kernels for 21% -> 22%
where the time goes in v5:
time: 296 us; the launch traced here: 295 us
  starting transfers between devices  91.5 us (31%)
  waiting for transfers between devices  73.8 us (25%)
  Pallas kernels  69.5 us (23%)
  other arithmetic  27.4 us (9%)
  blocking collectives  17.9 us (6%)
  local copies, waits for them, and re-layouts  12.6 us (4%)
    pallas_call x4, Pallas kernels, tile_batch(): pl.pallas_call(functools.partial(tiles_kernel, count, held_most, len(sour...  58.9 us
    ppermute x21, starting transfers between devices, aux_permute(): return lax.ppermute(value, 'aux', moves(pairs))  55.9 us
    ppermute x21, waiting for transfers between devices, aux_permute(): return lax.ppermute(value, 'aux', moves(pairs))  42.2 us
    ppermute x17, starting transfers between devices, y_permute(): lax.ppermute(value, 'pair', [(h * 4 + y, h * 4 + (y + by) % 4) for h in r...  23.9 us
    all_to_all x1, blocking collectives, local(): lax.all_to_all(crossed, 'pair', split_axis=2, concat_axis=1, tiled=True)  17.9 us
    ppermute x5, waiting for transfers between devices, x_permute(): return lax.ppermute(value, ('aux', 'pair'), perm)  17.5 us
    ppermute x17, waiting for transfers between devices, y_permute(): lax.ppermute(value, 'pair', [(h * 4 + y, h * 4 + (y + by) % 4) for h in r...  14.1 us
    ppermute x5, starting transfers between devices, x_permute(): return lax.ppermute(value, ('aux', 'pair'), perm)  11.7 us
  transfers between devices with their start and end apart: 43, of which 16 were waited for; matrix products, arithmetic and copies ran while one was open for 10% of the time, Pallas kernels for 22%

profile of v5, /device:TPU:3, one launch (start us, length us, event | category | flops | bytes accessed | tf_op | source)
XLA Modules:
  0.0 294.5 jit_solution(6372137547628809651)
XLA Ops:
  0.0 3.7 %copy-done.1 = bf16[768,6144]{1,0:T(8,128)(2,1)S(1)} copy-done((bf16[768,6144]{1,0:T(8,128)(2,1)S(1)}, bf16[768,6144]{1,0:T(8,128)(2,1)}, u32[]{:S(2)}) %copy-start.1) | copy-done | bytes 9437208
  3.7 4.9 %shard_map.109 = (bf16[768,3072]{1,0:T(8,128)(2,1)}, bf16[768,3072]{1,0:T(8,128)(2,1)}, f32[8,128]{1,0:T(8,128)S(1)}) custom-call(s32[1]{0:T(128)} %bitcast.x_lo, bf16[768,6144]{1,0:T(8,128)(2,1)S(1)} %copy-done.1), custom_call_target="tpu_custom_call" | custom-call | bytes 73728 | tf_op jit(solution)/shard_map/pallas_call | solution.py:218
  8.6 3.5 %collective-permute-start = (bf16[768,3072]{1,0:T(8,128)(2,1)}, bf16[768,3072]{1,0:T(8,128)(2,1)}, u32[]{:S(2)}, u32[]{:S(2)}) collective-permute-start(bf16[768,3072]{1,0:T(8,128)(2,1)} %get-tuple-element.78.refs_0_), channel_id=1, source_target_pairs={{0,96},{24,56},{32,0},{56,88},{64,32},{88,120},{96,64},{120,24},{1... | collective-permute-start | bytes 14155784 | tf_op jit(solution)/shard_map/ppermute | solution.py:237
  12.1 3.5 %collective-permute-start.1 = (bf16[768,3072]{1,0:T(8,128)(2,1)}, bf16[768,3072]{1,0:T(8,128)(2,1)}, u32[]{:S(2)}, u32[]{:S(2)}) collective-permute-start(bf16[768,3072]{1,0:T(8,128)(2,1)} %get-tuple-element.77), channel_id=1, source_target_pairs={{0,16},{24,8},{32,48},{56,40},{64,80},{88,72},{96,112},{120,104},{... | collective-permute-start | bytes 14155784 | tf_op jit(solution)/shard_map/ppermute | solution.py:237
  17.3 4.8 %shard_map.110 = f32[1,3072]{1,0:T(1,128)} custom-call(s32[1,3072]{1,0:T(1,128)} %bitcast.145, s32[1,3072]{1,0:T(1,128)} %bitcast.146, f32[32,128]{1,0:T(8,128)} %bitcast.148, f32[256,128]{1,0:T(8,128)} %bitcast.147), custom_call_target="tpu_custom_call" | custom-call | flops 679477248 | bytes 200000 | tf_op jit(solution)/shard_map/pallas_call | solution.py:186
  23.5 3.0 %collective-permute-start.5 = (f32[8,128]{1,0:T(8,128)S(1)}, f32[8,128]{1,0:T(8,128)S(1)}, u32[]{:S(2)}, u32[]{:S(2)}) collective-permute-start(f32[8,128]{1,0:T(8,128)S(1)} %max.30), channel_id=1, source_target_pairs={{0,2},{1,3},{2,0},{3,1},{4,6},{5,7},{6,4},{7,5},{8,10},{9,11},{10,... | collective-permute-start | bytes 12296 | tf_op jit(solution)/shard_map/ppermute | solution.py:241
  39.0 23.2 %collective-permute-done.11 = f32[8,128]{1,0:T(8,128)S(1)} collective-permute-done((f32[8,128]{1,0:T(8,128)S(1)}, f32[8,128]{1,0:T(8,128)S(1)}, u32[]{:S(2)}, u32[]{:S(2)}) %collective-permute-start.11) | collective-permute-done | bytes 4128 | tf_op jit(solution)/shard_map/ppermute | solution.py:237
  67.4 9.6 %collective-permute-start.15 = (bf16[768,3072]{1,0:T(8,128)(2,1)}, bf16[768,3072]{1,0:T(8,128)(2,1)}, u32[]{:S(2)}, u32[]{:S(2)}) collective-permute-start(bf16[768,3072]{1,0:T(8,128)(2,1)} %collective-permute-done.refs_3_.refs_4_.refs_5_), channel_id=1, source_target_pairs={{24,16},{56,48},{88,80},{120,112},{25,17},{57,49},{89,81},{121,113... | collective-permute-start | bytes 14155784 | tf_op jit(solution)/shard_map/ppermute | solution.py:237
  77.0 2.8 collective-permute-start.16
  81.0 2.8 collective-permute-start.18
  83.8 14.6 %shard_map.111 = f32[8,2,96,768]{3,2,1,0:T(8,128)} custom-call(s32[20]{0:T(128)} %get-tuple-element.66.table, f32[1,3072]{1,0:T(1,128)} %add_divide_fusion.weight, bf16[768,3072]{1,0:T(8,128)(2,1)} %get-tuple-element.78.refs_0_, bf16[768,3072]{1,0:T(8,128)(2,1)} %collective-permute-done.2.refs_1_.refs_0_, ...), custom_call_target="tpu_custom_call" | custom-call | flops 1179648 | bytes 1179648 | tf_op jit(solution)/shard_map/pallas_call | solution.py:135
  103.3 15.4 %shard_map.112 = f32[8,2,96,768]{3,2,1,0:T(8,128)} custom-call(s32[20]{0:T(128)} %get-tuple-element.72.table, f32[1,3072]{1,0:T(1,128)} %add_divide_fusion.weight, bf16[768,3072]{1,0:T(8,128)(2,1)} %get-tuple-element.78.refs_0_, bf16[768,3072]{1,0:T(8,128)(2,1)} %collective-permute-done.2.refs_1_.refs_0_, ...), custom_call_target="tpu_custom_call" | custom-call | flops 1179648 | bytes 1179648 | tf_op jit(solution)/shard_map/pallas_call | solution.py:135
  120.6 2.7 collective-permute-start.20
  123.6 11.7 %collective-permute-done.17.refs_3_ = bf16[768,3072]{1,0:T(8,128)(2,1)} collective-permute-done((bf16[768,3072]{1,0:T(8,128)(2,1)}, bf16[768,3072]{1,0:T(8,128)(2,1)}, u32[]{:S(2)}, u32[]{:S(2)}) %collective-permute-start.17) | collective-permute-done | bytes 4718624 | tf_op jit(solution)/shard_map/ppermute | solution.py:237
  135.3 8.8 %collective-permute-start.23 = (bf16[768,3072]{1,0:T(8,128)(2,1)}, bf16[768,3072]{1,0:T(8,128)(2,1)}, u32[]{:S(2)}, u32[]{:S(2)}) collective-permute-start(bf16[768,3072]{1,0:T(8,128)(2,1)} %collective-permute-done.17.refs_3_), channel_id=1, source_target_pairs={{0,8},{24,16},{32,40},{56,48},{64,72},{88,80},{96,104},{120,112},{... | collective-permute-start | bytes 14155784 | tf_op jit(solution)/shard_map/ppermute | solution.py:237
  151.5 14.5 %shard_map.113 = f32[8,2,96,768]{3,2,1,0:T(8,128)} custom-call(s32[22]{0:T(128)} %pad_add_fusion.2.table, f32[1,3072]{1,0:T(1,128)} %add_divide_fusion.weight, bf16[768,3072]{1,0:T(8,128)(2,1)} %collective-permute-done.2.refs_1_.refs_0_, bf16[768,3072]{1,0:T(8,128)(2,1)} %collective-permute-done.1.refs_2_.refs_1_, ...), custom_call_target="tpu_custom_call" | custom-call | flops 1179648 | bytes 1179648 | tf_op jit(solution)/shard_map/pallas_call | solution.py:135
  166.0 2.9 fusion.4
  168.9 2.6 collective-permute-start.25
  173.8 14.5 %shard_map.114 = f32[8,2,96,768]{3,2,1,0:T(8,128)} custom-call(s32[20]{0:T(128)} %get-tuple-element.93.table, f32[1,3072]{1,0:T(1,128)} %add_divide_fusion.weight, bf16[768,3072]{1,0:T(8,128)(2,1)} %get-tuple-element.78.refs_0_, bf16[768,3072]{1,0:T(8,128)(2,1)} %collective-permute-done.2.refs_1_.refs_0_, ...), custom_call_target="tpu_custom_call" | custom-call | flops 1179648 | bytes 1179648 | tf_op jit(solution)/shard_map/pallas_call | solution.py:135
  190.3 2.7 collective-permute-start.28
  194.1 2.7 collective-permute-start.30
  201.1 6.6 %collective-permute-done.29 = f16[2,2,96,768]{3,2,1,0:T(8,128)(2,1)S(1)} collective-permute-done((f16[2,2,96,768]{3,2,1,0:T(8,128)(2,1)S(1)}, f16[2,2,96,768]{3,2,1,0:T(8,128)(2,1)S(1)}, u32[]{:S(2)}, u32[]{:S(2)}) %collective-permute-start.29) | collective-permute-done | bytes 589856 | tf_op jit(solution)/shard_map/ppermute | solution.py:241
  208.0 2.7 collective-permute-start.34
  212.0 5.0 %collective-permute-done.33 = f16[2,96,768]{2,1,0:T(8,128)(2,1)S(1)} collective-permute-done((f16[2,96,768]{2,1,0:T(8,128)(2,1)S(1)}, f16[2,96,768]{2,1,0:T(8,128)(2,1)S(1)}, u32[]{:S(2)}, u32[]{:S(2)}) %collective-permute-start.33) | collective-permute-done | bytes 294944 | tf_op jit(solution)/shard_map/ppermute | solution.py:241
  218.5 9.6 %collective-permute-start.35 = (f16[2,2,96,768]{3,2,1,0:T(8,128)(2,1)S(1)}, f16[2,2,96,768]{3,2,1,0:T(8,128)(2,1)S(1)}, u32[]{:S(2)}, u32[]{:S(2)}) collective-permute-start(f16[2,2,96,768]{3,2,1,0:T(8,128)(2,1)S(1)} %bitcast.144), channel_id=1, source_target_pairs={{0,16},{1,17},{2,18},{3,19},{8,24},{9,25},{10,26},{11,27},{16,4},{... | collective-permute-start | bytes 1769480 | tf_op jit(solution)/shard_map/ppermute | solution.py:255
  228.1 6.8 %collective-permute-done.35 = f16[2,2,96,768]{3,2,1,0:T(8,128)(2,1)S(1)} collective-permute-done((f16[2,2,96,768]{3,2,1,0:T(8,128)(2,1)S(1)}, f16[2,2,96,768]{3,2,1,0:T(8,128)(2,1)S(1)}, u32[]{:S(2)}, u32[]{:S(2)}) %collective-permute-start.35) | collective-permute-done | bytes 589856 | tf_op jit(solution)/shard_map/ppermute | solution.py:255
  234.9 2.2 collective-permute-done.36
  238.9 6.2 %collective-permute-done.37 = f16[2,96,768]{2,1,0:T(8,128)(2,1)S(1)} collective-permute-done((f16[2,96,768]{2,1,0:T(8,128)(2,1)S(1)}, f16[2,96,768]{2,1,0:T(8,128)(2,1)S(1)}, u32[]{:S(2)}, u32[]{:S(2)}) %collective-permute-start.37) | collective-permute-done | bytes 294944 | tf_op jit(solution)/shard_map/ppermute | solution.py:255
  245.1 2.3 collective-permute-done.38
  249.3 10.9 %collective-permute-start.39 = (f16[96,768]{1,0:T(8,128)(2,1)S(1)}, f16[96,768]{1,0:T(8,128)(2,1)S(1)}, u32[]{:S(2)}, u32[]{:S(2)}) collective-permute-start(f16[96,768]{1,0:T(8,128)(2,1)S(1)} %multiply_convert_fusion), channel_id=1, source_target_pairs={{16,24},{24,16},{48,56},{56,48},{80,88},{88,80},{112,120},{120,112... | collective-permute-start | bytes 442376 | tf_op jit(solution)/shard_map/ppermute | solution.py:237
  263.0 17.9 %all_to_all.15 = f16[3,96,8,96]{1,3,0,2:T(8,128)(2,1)S(1)} all-to-all(f16[3,96,8,96]{1,3,0,2:T(8,128)(2,1)S(1)} %fusion.12), channel_id=1, replica_groups=mesh['aux'=16,'pair'=8] {'pair'}, dimensions={2} | all-to-all | bytes 884736 | tf_op jit(solution)/shard_map/all_to_all | solution.py:443
  291.3 2.5 collective-permute-done.42
  (144 shorter events, 65.4 us)
Async XLA Ops:
  8.6 57.6 %collective-permute-start = (bf16[768,3072]{1,0:T(8,128)(2,1)}, bf16[768,3072]{1,0:T(8,128)(2,1)}, u32[]{:S(2)}, u32[]{:S(2)}) collective-permute-start(bf16[768,3072]{1,0:T(8,128)(2,1)} %get-tuple-element.78.refs_0_), channel_id=1, source_target_pairs={{0,96},{24,56},{32,0},{56,88},{64,32},{88,120},{96,64},{120,24},{1... | collective-permute-start | bytes 14155784 | tf_op jit(solution)/shard_map/ppermute | solution.py:237
  12.1 54.0 %collective-permute-start.1 = (bf16[768,3072]{1,0:T(8,128)(2,1)}, bf16[768,3072]{1,0:T(8,128)(2,1)}, u32[]{:S(2)}, u32[]{:S(2)}) collective-permute-start(bf16[768,3072]{1,0:T(8,128)(2,1)} %get-tuple-element.77), channel_id=1, source_target_pairs={{0,16},{24,8},{32,48},{56,40},{64,80},{88,72},{96,112},{120,104},{... | collective-permute-start | bytes 14155784 | tf_op jit(solution)/shard_map/ppermute | solution.py:237
  15.6 50.5 %collective-permute-start.2 = (bf16[768,3072]{1,0:T(8,128)(2,1)}, bf16[768,3072]{1,0:T(8,128)(2,1)}, u32[]{:S(2)}, u32[]{:S(2)}) collective-permute-start(bf16[768,3072]{1,0:T(8,128)(2,1)} %get-tuple-element.78.refs_0_), channel_id=1, source_target_pairs={{0,8},{8,0},{16,24},{24,16},{32,40},{40,32},{48,56},{56,48},{64,72... | collective-permute-start | bytes 14155784 | tf_op jit(solution)/shard_map/ppermute | solution.py:237
  15.6 7.9 %collective-permute-start.3 = (f32[8,128]{1,0:T(8,128)S(1)}, f32[8,128]{1,0:T(8,128)S(1)}, u32[]{:S(2)}, u32[]{:S(2)}) collective-permute-start(f32[8,128]{1,0:T(8,128)S(1)} %get-tuple-element.62), channel_id=1, source_target_pairs={{0,8},{8,0},{16,24},{24,16},{32,40},{40,32},{48,56},{56,48},{64,72... | collective-permute-start | bytes 12296 | tf_op jit(solution)/shard_map/ppermute | solution.py:237
  37.0 25.2 %collective-permute-start.11 = (f32[8,128]{1,0:T(8,128)S(1)}, f32[8,128]{1,0:T(8,128)S(1)}, u32[]{:S(2)}, u32[]{:S(2)}) collective-permute-start(f32[8,128]{1,0:T(8,128)S(1)} %max.37), channel_id=1, source_target_pairs={{8,0},{16,24},{40,32},{48,56},{72,64},{80,88},{104,96},{112,120},{... | collective-permute-start | bytes 12296 | tf_op jit(solution)/shard_map/ppermute | solution.py:237
  66.1 34.3 %collective-permute-start.14 = (bf16[768,3072]{1,0:T(8,128)(2,1)}, bf16[768,3072]{1,0:T(8,128)(2,1)}, u32[]{:S(2)}, u32[]{:S(2)}) collective-permute-start(bf16[768,3072]{1,0:T(8,128)(2,1)} %collective-permute-done.1.refs_2_.refs_1_), channel_id=1, source_target_pairs={{8,0},{16,24},{40,32},{48,56},{72,64},{80,88},{104,96},{112,120},{... | collective-permute-start | bytes 14155784 | tf_op jit(solution)/shard_map/ppermute | solution.py:237
  67.4 34.3 %collective-permute-start.15 = (bf16[768,3072]{1,0:T(8,128)(2,1)}, bf16[768,3072]{1,0:T(8,128)(2,1)}, u32[]{:S(2)}, u32[]{:S(2)}) collective-permute-start(bf16[768,3072]{1,0:T(8,128)(2,1)} %collective-permute-done.refs_3_.refs_4_.refs_5_), channel_id=1, source_target_pairs={{24,16},{56,48},{88,80},{120,112},{25,17},{57,49},{89,81},{121,113... | collective-permute-start | bytes 14155784 | tf_op jit(solution)/shard_map/ppermute | solution.py:237
  77.0 46.6 %collective-permute-start.16 = (bf16[768,3072]{1,0:T(8,128)(2,1)}, bf16[768,3072]{1,0:T(8,128)(2,1)}, u32[]{:S(2)}, u32[]{:S(2)}) collective-permute-start(bf16[768,3072]{1,0:T(8,128)(2,1)} %collective-permute-done.1.refs_2_.refs_1_), channel_id=1, source_target_pairs={{8,32},{16,112},{40,64},{48,16},{72,96},{80,48},{104,0},{112,80},{... | collective-permute-start | bytes 14155784 | tf_op jit(solution)/shard_map/ppermute | solution.py:237
  79.8 55.5 %collective-permute-start.17 = (bf16[768,3072]{1,0:T(8,128)(2,1)}, bf16[768,3072]{1,0:T(8,128)(2,1)}, u32[]{:S(2)}, u32[]{:S(2)}) collective-permute-start(bf16[768,3072]{1,0:T(8,128)(2,1)} %get-tuple-element.77), channel_id=1, source_target_pairs={{8,24},{16,0},{40,56},{48,32},{72,88},{80,64},{104,120},{112,96},{... | collective-permute-start | bytes 14155784 | tf_op jit(solution)/shard_map/ppermute | solution.py:237
  81.0 54.2 %collective-permute-start.18 = (bf16[768,3072]{1,0:T(8,128)(2,1)}, bf16[768,3072]{1,0:T(8,128)(2,1)}, u32[]{:S(2)}, u32[]{:S(2)}) collective-permute-start(bf16[768,3072]{1,0:T(8,128)(2,1)} %get-tuple-element.78.refs_0_), channel_id=1, source_target_pairs={{8,104},{16,48},{40,8},{48,80},{72,40},{80,112},{104,72},{112,16},... | collective-permute-start | bytes 14155784 | tf_op jit(solution)/shard_map/ppermute | solution.py:237
  100.4 20.1 %collective-permute-start.12 = (f16[2,2,96,768]{3,2,1,0:T(8,128)(2,1)S(1)}, f16[2,2,96,768]{3,2,1,0:T(8,128)(2,1)S(1)}, u32[]{:S(2)}, u32[]{:S(2)}) collective-permute-start(f16[2,2,96,768]{3,2,1,0:T(8,128)(2,1)S(1)} %get-tuple-element.142), channel_id=1, source_target_pairs={{0,1},{1,2},{2,3},{3,0},{4,5},{5,6},{6,7},{7,4},{8,9},{9,10},{10,1... | collective-permute-start | bytes 1769480 | tf_op jit(solution)/shard_map/ppermute | solution.py:241
  101.8 18.8 %collective-permute-start.13 = (f16[2,2,96,768]{3,2,1,0:T(8,128)(2,1)S(1)}, f16[2,2,96,768]{3,2,1,0:T(8,128)(2,1)S(1)}, u32[]{:S(2)}, u32[]{:S(2)}) collective-permute-start(f16[2,2,96,768]{3,2,1,0:T(8,128)(2,1)S(1)} %get-tuple-element.141), channel_id=1, source_target_pairs={{0,3},{1,0},{2,1},{3,2},{4,7},{5,4},{6,5},{7,6},{8,11},{9,8},{10,9... | collective-permute-start | bytes 1769480 | tf_op jit(solution)/shard_map/ppermute | solution.py:241
  120.5 14.7 %collective-permute-start.19 = (f16[2,2,96,768]{3,2,1,0:T(8,128)(2,1)S(1)}, f16[2,2,96,768]{3,2,1,0:T(8,128)(2,1)S(1)}, u32[]{:S(2)}, u32[]{:S(2)}) collective-permute-start(f16[2,2,96,768]{3,2,1,0:T(8,128)(2,1)S(1)} %get-tuple-element.79), channel_id=1, source_target_pairs={{0,1},{1,2},{2,3},{3,0},{4,5},{5,6},{6,7},{7,4},{8,9},{9,10},{10,1... | collective-permute-start | bytes 1769480 | tf_op jit(solution)/shard_map/ppermute | solution.py:241
  120.6 14.7 %collective-permute-start.20 = (f16[2,2,96,768]{3,2,1,0:T(8,128)(2,1)S(1)}, f16[2,2,96,768]{3,2,1,0:T(8,128)(2,1)S(1)}, u32[]{:S(2)}, u32[]{:S(2)}) collective-permute-start(f16[2,2,96,768]{3,2,1,0:T(8,128)(2,1)S(1)} %get-tuple-element.80), channel_id=1, source_target_pairs={{0,3},{1,0},{2,1},{3,2},{4,7},{5,4},{6,5},{7,6},{8,11},{9,8},{10,9... | collective-permute-start | bytes 1769480 | tf_op jit(solution)/shard_map/ppermute | solution.py:241
  135.3 16.2 %collective-permute-start.23 = (bf16[768,3072]{1,0:T(8,128)(2,1)}, bf16[768,3072]{1,0:T(8,128)(2,1)}, u32[]{:S(2)}, u32[]{:S(2)}) collective-permute-start(bf16[768,3072]{1,0:T(8,128)(2,1)} %collective-permute-done.17.refs_3_), channel_id=1, source_target_pairs={{0,8},{24,16},{32,40},{56,48},{64,72},{88,80},{96,104},{120,112},{... | collective-permute-start | bytes 14155784 | tf_op jit(solution)/shard_map/ppermute | solution.py:237
  144.1 29.7 %collective-permute-start.26 = (bf16[768,3072]{1,0:T(8,128)(2,1)}, bf16[768,3072]{1,0:T(8,128)(2,1)}, u32[]{:S(2)}, u32[]{:S(2)}) collective-permute-start(bf16[768,3072]{1,0:T(8,128)(2,1)} %collective-permute-done.18.refs_6_), channel_id=1, source_target_pairs={{16,24},{48,56},{80,88},{112,120},{17,25},{49,57},{81,89},{113,121... | collective-permute-start | bytes 14155784 | tf_op jit(solution)/shard_map/ppermute | solution.py:237
  147.8 23.7 %collective-permute-start.21 = (f16[4,96,768]{2,1,0:T(8,128)(2,1)}, f16[4,96,768]{2,1,0:T(8,128)(2,1)S(1)}, u32[]{:S(2)}, u32[]{:S(2)}) collective-permute-start(f16[4,96,768]{2,1,0:T(8,128)(2,1)} %pad_maximum_fusion), channel_id=1, source_target_pairs={{0,1},{1,2},{2,3},{3,0},{4,5},{5,6},{6,7},{7,4},{8,9},{9,10},{10,1... | collective-permute-start | bytes 1769480 | tf_op jit(solution)/shard_map/ppermute | solution.py:241
  150.1 21.5 %collective-permute-start.22 = (f16[4,96,768]{2,1,0:T(8,128)(2,1)}, f16[4,96,768]{2,1,0:T(8,128)(2,1)S(1)}, u32[]{:S(2)}, u32[]{:S(2)}) collective-permute-start(f16[4,96,768]{2,1,0:T(8,128)(2,1)} %pad_maximum_fusion.1), channel_id=1, source_target_pairs={{0,3},{1,0},{2,1},{3,2},{4,7},{5,4},{6,5},{7,6},{8,11},{9,8},{10,9... | collective-permute-start | bytes 1769480 | tf_op jit(solution)/shard_map/ppermute | solution.py:241
  168.9 19.6 %collective-permute-start.24 = (f16[2,2,96,768]{3,2,1,0:T(8,128)(2,1)}, f16[2,2,96,768]{3,2,1,0:T(8,128)(2,1)}, u32[]{:S(2)}, u32[]{:S(2)}) collective-permute-start(f16[2,2,96,768]{3,2,1,0:T(8,128)(2,1)} %get-tuple-element.134), channel_id=1, source_target_pairs={{0,1},{1,2},{2,3},{3,0},{4,5},{5,6},{6,7},{7,4},{8,9},{9,10},{10,1... | collective-permute-start | bytes 1769480 | tf_op jit(solution)/shard_map/ppermute | solution.py:241
  168.9 19.5 %collective-permute-start.25 = (f16[2,2,96,768]{3,2,1,0:T(8,128)(2,1)}, f16[2,2,96,768]{3,2,1,0:T(8,128)(2,1)}, u32[]{:S(2)}, u32[]{:S(2)}) collective-permute-start(f16[2,2,96,768]{3,2,1,0:T(8,128)(2,1)} %get-tuple-element.133), channel_id=1, source_target_pairs={{0,3},{1,0},{2,1},{3,2},{4,7},{5,4},{6,5},{7,6},{8,11},{9,8},{10,9... | collective-permute-start | bytes 1769480 | tf_op jit(solution)/shard_map/ppermute | solution.py:241
  193.1 8.0 %collective-permute-start.32 = (f16[4,96,768]{2,1,0:T(8,128)(2,1)}, f16[4,96,768]{2,1,0:T(8,128)(2,1)S(1)}, u32[]{:S(2)}, u32[]{:S(2)}) collective-permute-start(f16[4,96,768]{2,1,0:T(8,128)(2,1)} %fusion.10), channel_id=1, source_target_pairs={{0,32},{32,64},{64,96},{96,0},{1,33},{33,65},{65,97},{97,1},{2,34}... | collective-permute-start | bytes 1769480 | tf_op jit(solution)/shard_map/ppermute | solution.py:237
  194.0 13.7 %collective-permute-start.29 = (f16[2,2,96,768]{3,2,1,0:T(8,128)(2,1)S(1)}, f16[2,2,96,768]{3,2,1,0:T(8,128)(2,1)S(1)}, u32[]{:S(2)}, u32[]{:S(2)}) collective-permute-start(f16[2,2,96,768]{3,2,1,0:T(8,128)(2,1)S(1)} %get-tuple-element.96), channel_id=1, source_target_pairs={{0,1},{1,2},{2,3},{3,0},{4,5},{5,6},{6,7},{7,4},{8,9},{9,10},{10,1... | collective-permute-start | bytes 1769480 | tf_op jit(solution)/shard_map/ppermute | solution.py:241
  194.1 13.6 %collective-permute-start.30 = (f16[2,2,96,768]{3,2,1,0:T(8,128)(2,1)S(1)}, f16[2,2,96,768]{3,2,1,0:T(8,128)(2,1)S(1)}, u32[]{:S(2)}, u32[]{:S(2)}) collective-permute-start(f16[2,2,96,768]{3,2,1,0:T(8,128)(2,1)S(1)} %get-tuple-element.97), channel_id=1, source_target_pairs={{0,3},{1,0},{2,1},{3,2},{4,7},{5,4},{6,5},{7,6},{8,11},{9,8},{10,9... | collective-permute-start | bytes 1769480 | tf_op jit(solution)/shard_map/ppermute | solution.py:241
  198.9 8.8 %collective-permute-start.31 = (f16[4,96,768]{2,1,0:T(8,128)(2,1)S(1)}, f16[4,96,768]{2,1,0:T(8,128)(2,1)S(1)}, u32[]{:S(2)}, u32[]{:S(2)}) collective-permute-start(f16[4,96,768]{2,1,0:T(8,128)(2,1)S(1)} %fusion.11), channel_id=1, source_target_pairs={{0,32},{8,40},{16,48},{32,64},{40,72},{48,80},{64,96},{72,104},{80... | collective-permute-start | bytes 1769480 | tf_op jit(solution)/shard_map/ppermute | solution.py:237
  207.9 9.0 %collective-permute-start.33 = (f16[2,96,768]{2,1,0:T(8,128)(2,1)S(1)}, f16[2,96,768]{2,1,0:T(8,128)(2,1)S(1)}, u32[]{:S(2)}, u32[]{:S(2)}) collective-permute-start(f16[2,96,768]{2,1,0:T(8,128)(2,1)S(1)} %get-tuple-element.122), channel_id=1, source_target_pairs={{0,1},{1,2},{2,3},{3,0},{4,5},{5,6},{6,7},{7,4},{8,9},{9,10},{10,1... | collective-permute-start | bytes 884744 | tf_op jit(solution)/shard_map/ppermute | solution.py:241
  208.0 9.0 %collective-permute-start.34 = (f16[2,96,768]{2,1,0:T(8,128)(2,1)S(1)}, f16[2,96,768]{2,1,0:T(8,128)(2,1)S(1)}, u32[]{:S(2)}, u32[]{:S(2)}) collective-permute-start(f16[2,96,768]{2,1,0:T(8,128)(2,1)S(1)} %get-tuple-element.121), channel_id=1, source_target_pairs={{0,3},{1,0},{2,1},{3,2},{4,7},{5,4},{6,5},{7,6},{8,11},{9,8},{10,9... | collective-permute-start | bytes 884744 | tf_op jit(solution)/shard_map/ppermute | solution.py:241
  218.5 16.4 %collective-permute-start.35 = (f16[2,2,96,768]{3,2,1,0:T(8,128)(2,1)S(1)}, f16[2,2,96,768]{3,2,1,0:T(8,128)(2,1)S(1)}, u32[]{:S(2)}, u32[]{:S(2)}) collective-permute-start(f16[2,2,96,768]{3,2,1,0:T(8,128)(2,1)S(1)} %bitcast.144), channel_id=1, source_target_pairs={{0,16},{1,17},{2,18},{3,19},{8,24},{9,25},{10,26},{11,27},{16,4},{... | collective-permute-start | bytes 1769480 | tf_op jit(solution)/shard_map/ppermute | solution.py:255
  228.1 9.0 %collective-permute-start.36 = (f16[2,2,96,768]{3,2,1,0:T(8,128)(2,1)S(1)}, f16[2,2,96,768]{3,2,1,0:T(8,128)(2,1)S(1)}, u32[]{:S(2)}, u32[]{:S(2)}) collective-permute-start(f16[2,2,96,768]{3,2,1,0:T(8,128)(2,1)S(1)} %bitcast.143), channel_id=1, source_target_pairs={{0,20},{1,21},{2,22},{3,23},{8,28},{9,29},{10,30},{11,31},{16,0},{... | collective-permute-start | bytes 1769480 | tf_op jit(solution)/shard_map/ppermute | solution.py:255
  237.4 7.8 %collective-permute-start.37 = (f16[2,96,768]{2,1,0:T(8,128)(2,1)S(1)}, f16[2,96,768]{2,1,0:T(8,128)(2,1)S(1)}, u32[]{:S(2)}, u32[]{:S(2)}) collective-permute-start(f16[2,96,768]{2,1,0:T(8,128)(2,1)S(1)} %get-tuple-element.118), channel_id=1, source_target_pairs={{0,16},{1,17},{2,18},{3,19},{8,24},{9,25},{10,26},{11,27},{16,4},{... | collective-permute-start | bytes 884744 | tf_op jit(solution)/shard_map/ppermute | solution.py:255
  237.5 9.9 %collective-permute-start.38 = (f16[2,96,768]{2,1,0:T(8,128)(2,1)S(1)}, f16[2,96,768]{2,1,0:T(8,128)(2,1)S(1)}, u32[]{:S(2)}, u32[]{:S(2)}) collective-permute-start(f16[2,96,768]{2,1,0:T(8,128)(2,1)S(1)} %get-tuple-element.117), channel_id=1, source_target_pairs={{0,20},{1,21},{2,22},{3,23},{8,28},{9,29},{10,30},{11,31},{16,0},{... | collective-permute-start | bytes 884744 | tf_op jit(solution)/shard_map/ppermute | solution.py:255
  249.3 11.9 %collective-permute-start.39 = (f16[96,768]{1,0:T(8,128)(2,1)S(1)}, f16[96,768]{1,0:T(8,128)(2,1)S(1)}, u32[]{:S(2)}, u32[]{:S(2)}) collective-permute-start(f16[96,768]{1,0:T(8,128)(2,1)S(1)} %multiply_convert_fusion), channel_id=1, source_target_pairs={{16,24},{24,16},{48,56},{56,48},{80,88},{88,80},{112,120},{120,112... | collective-permute-start | bytes 442376 | tf_op jit(solution)/shard_map/ppermute | solution.py:237
  286.0 7.8 %collective-permute-start.42 = (f16[768,96]{0,1:T(8,128)(2,1)S(1)}, f16[768,96]{0,1:T(8,128)(2,1)S(1)}, u32[]{:S(2)}, u32[]{:S(2)}) collective-permute-start(f16[768,96]{0,1:T(8,128)(2,1)S(1)} %squeeze.42), channel_id=1, source_target_pairs={{0,104},{8,112},{16,120},{24,0},{32,8},{40,16},{48,24},{56,32},{64... | collective-permute-start | bytes 442376 | tf_op jit(solution)/shard_map/ppermute | solution.py:237
  (19 other events, 144.3 us)

commit v6 on v5

--- a/solution.py
+++ b/solution.py
@@ -148,7 +148,7 @@
         ),
         out_shape=jax.ShapeDtypeStruct((8, count, PART, ROWS), jnp.float32),
         compiler_params=pltpu.CompilerParams(
-            dimension_semantics=("arbitrary",), vmem_limit_bytes=56 * 1024 * 1024),
+            dimension_semantics=("arbitrary",), vmem_limit_bytes=36 * 1024 * 1024),
         cost_estimate=pl.CostEstimate(
             flops=count * ROWS * ROWS,
             bytes_accessed=count * ROWS * ROWS,
@@ -400,7 +400,7 @@
     got0, sends1 = lax.optimization_barrier((got0, sends1))
     got1 = first_round(sends1)
     more = second_sends(partial0, got0, scales)
-    minor, far_b, halo_b, got1, more = lax.optimization_barrier((minor, far_b, halo_b, got1, more))
+    far_b, halo_b, minor, got1, more = lax.optimization_barrier((far_b, halo_b, minor, got1, more))
     held[FAR_B], held[HALO_B], held[MINOR] = far_b, halo_b, minor
     held[FAR_B_SIB] = aux_permute(far_b, [(0, 1, 0), (3, 2, 0)])
     held[HALO_B_SIB] = aux_permute(halo_b, [(2, 3, 0)])
@@ -417,7 +417,7 @@
     moved0 = aux_permute(moved0, [(0, 0, 1)])
     partial3 = tiles(3)
     sends3 = first_sends(partial3, scales)
-    got2 = after(got2, partial3)
+    got2, moved0 = lax.optimization_barrier((got2, moved0, partial3))[:2]
     sends2 = second_sends(partial2, got2, scales)
     more2 = first_round(sends2)
     sends3 = after(sends3, sends2)
@@ -429,7 +429,7 @@
     total0 = finish(partial0, got0, more0, scales)
     total1 = finish(partial1, got1, more1, scales)
     moved2 = aux_permute(moved2, [(0, 0, 1), (1, 1, 1), (2, 2, 1)])
-    got3, moved2, moved0 = lax.optimization_barrier((got3, moved2, moved0))
+    got3, moved2 = lax.optimization_barrier((got3, moved2))
     more3 = both_ways(y_permute, *second_sends(partial3, got3, scales))
     moved0, moved2 = wide(moved0, scales), wide(moved2, scales)
     total3 = finish(partial3, got3, more3, scales)

time: 296 us -> 283 us (0.956)
  other arithmetic: 27.4 us -> 16 us
  Pallas kernels: 69.5 us -> 61.7 us
  waiting for transfers between devices: 73.8 us -> 80.2 us
    pallas_call x4, Pallas kernels: 58.9 us -> 51.1 us  [tile_batch(): pl.pallas_call(functools.partial(tiles_kernel, count, held_most, len(sour...]
    convert_element_type x10, other arithmetic: 8.61 us -> 3.49 us  [narrow(): return (value * scales[0]).astype(jnp.float16)]
    ppermute x21, waiting for transfers between devices: 42.2 us -> 47.2 us  [aux_permute(): return lax.ppermute(value, 'aux', moves(pairs))]
    ppermute x5, starting transfers between devices: 11.7 us -> 7.57 us  [x_permute(): return lax.ppermute(value, ('aux', 'pair'), perm)]
    unnamed x20 -> x34, local copies, waits for them, and re-layouts: 5.84 us -> 6.17 us
  transfers between devices with their start and end apart: 43 -> 43, of which waited for: 16 -> 15; matrix products, arithmetic and copies ran while one was open for 10% -> 6% of each run, Pallas kernels for 22% -> 20%
where the time goes in v6:
time: 283 us; the launch traced here: 282 us
  starting transfers between devices  90 us (32%)
  waiting for transfers between devices  80.2 us (28%)
  Pallas kernels  61.7 us (22%)
  blocking collectives  17.7 us (6%)
  other arithmetic  16 us (6%)
  local copies, waits for them, and re-layouts  14.7 us (5%)
    ppermute x21, starting transfers between devices, aux_permute(): return lax.ppermute(value, 'aux', moves(pairs))  56.9 us
    pallas_call x4, Pallas kernels, tile_batch(): pl.pallas_call(functools.partial(tiles_kernel, count, held_most, len(sour...  51.1 us
    ppermute x21, waiting for transfers between devices, aux_permute(): return lax.ppermute(value, 'aux', moves(pairs))  47.2 us
    ppermute x17, starting transfers between devices, y_permute(): lax.ppermute(value, 'pair', [(h * 4 + y, h * 4 + (y + by) % 4) for h in r...  25.5 us
    all_to_all x1, blocking collectives, local(): lax.all_to_all(crossed, 'pair', split_axis=2, concat_axis=1, tiled=True)  17.7 us
    ppermute x17, waiting for transfers between devices, y_permute(): lax.ppermute(value, 'pair', [(h * 4 + y, h * 4 + (y + by) % 4) for h in r...  16.5 us
    ppermute x5, waiting for transfers between devices, x_permute(): return lax.ppermute(value, ('aux', 'pair'), perm)  16.4 us
    ppermute x5, starting transfers between devices, x_permute(): return lax.ppermute(value, ('aux', 'pair'), perm)  7.57 us
  transfers between devices with their start and end apart: 43, of which 15 were waited for; matrix products, arithmetic and copies ran while one was open for 6% of the time, Pallas kernels for 20%

profile of v6, /device:TPU:3, one launch (start us, length us, event | category | flops | bytes accessed | tf_op | source)
XLA Modules:
  0.0 282.2 jit_solution(9396657725848979463)
XLA Ops:
  0.0 3.7 %copy-done.1 = bf16[768,6144]{1,0:T(8,128)(2,1)S(1)} copy-done((bf16[768,6144]{1,0:T(8,128)(2,1)S(1)}, bf16[768,6144]{1,0:T(8,128)(2,1)}, u32[]{:S(2)}) %copy-start.1) | copy-done | bytes 9437208
  3.7 4.9 %shard_map.109 = (bf16[768,3072]{1,0:T(8,128)(2,1)}, bf16[768,3072]{1,0:T(8,128)(2,1)}, f32[8,128]{1,0:T(8,128)S(1)}) custom-call(s32[1]{0:T(128)} %bitcast.x_lo, bf16[768,6144]{1,0:T(8,128)(2,1)S(1)} %copy-done.1), custom_call_target="tpu_custom_call" | custom-call | bytes 73728 | tf_op jit(solution)/shard_map/pallas_call | solution.py:218
  8.6 3.5 %collective-permute-start = (bf16[768,3072]{1,0:T(8,128)(2,1)}, bf16[768,3072]{1,0:T(8,128)(2,1)}, u32[]{:S(2)}, u32[]{:S(2)}) collective-permute-start(bf16[768,3072]{1,0:T(8,128)(2,1)} %get-tuple-element.78.refs_0_), channel_id=1, source_target_pairs={{0,96},{24,56},{32,0},{56,88},{64,32},{88,120},{96,64},{120,24},{1... | collective-permute-start | bytes 14155784 | tf_op jit(solution)/shard_map/ppermute | solution.py:237
  12.1 3.5 %collective-permute-start.1 = (bf16[768,3072]{1,0:T(8,128)(2,1)}, bf16[768,3072]{1,0:T(8,128)(2,1)}, u32[]{:S(2)}, u32[]{:S(2)}) collective-permute-start(bf16[768,3072]{1,0:T(8,128)(2,1)} %get-tuple-element.77), channel_id=1, source_target_pairs={{0,16},{24,8},{32,48},{56,40},{64,80},{88,72},{96,112},{120,104},{... | collective-permute-start | bytes 14155784 | tf_op jit(solution)/shard_map/ppermute | solution.py:237
  17.4 4.8 %shard_map.110 = f32[1,3072]{1,0:T(1,128)} custom-call(s32[1,3072]{1,0:T(1,128)} %bitcast.143, s32[1,3072]{1,0:T(1,128)} %bitcast.144, f32[32,128]{1,0:T(8,128)} %bitcast.146, f32[256,128]{1,0:T(8,128)} %bitcast.145), custom_call_target="tpu_custom_call" | custom-call | flops 679477248 | bytes 200000 | tf_op jit(solution)/shard_map/pallas_call | solution.py:186
  22.9 3.1 %collective-permute-start.5 = (f32[8,128]{1,0:T(8,128)S(1)}, f32[8,128]{1,0:T(8,128)S(1)}, u32[]{:S(2)}, u32[]{:S(2)}) collective-permute-start(f32[8,128]{1,0:T(8,128)S(1)} %max.30), channel_id=1, source_target_pairs={{0,2},{1,3},{2,0},{3,1},{4,6},{5,7},{6,4},{7,5},{8,10},{9,11},{10,... | collective-permute-start | bytes 12296 | tf_op jit(solution)/shard_map/ppermute | solution.py:241
  37.4 24.3 %collective-permute-done.11 = f32[8,128]{1,0:T(8,128)S(1)} collective-permute-done((f32[8,128]{1,0:T(8,128)S(1)}, f32[8,128]{1,0:T(8,128)S(1)}, u32[]{:S(2)}, u32[]{:S(2)}) %collective-permute-start.11) | collective-permute-done | bytes 4128 | tf_op jit(solution)/shard_map/ppermute | solution.py:237
  63.6 2.5 collective-permute-done.refs_3_.refs_4_.refs_5_
  67.4 7.8 %collective-permute-start.15 = (bf16[768,3072]{1,0:T(8,128)(2,1)}, bf16[768,3072]{1,0:T(8,128)(2,1)}, u32[]{:S(2)}, u32[]{:S(2)}) collective-permute-start(bf16[768,3072]{1,0:T(8,128)(2,1)} %collective-permute-done.refs_3_.refs_4_.refs_5_), channel_id=1, source_target_pairs={{24,16},{56,48},{88,80},{120,112},{25,17},{57,49},{89,81},{121,113... | collective-permute-start | bytes 14155784 | tf_op jit(solution)/shard_map/ppermute | solution.py:237
  76.6 2.8 collective-permute-start.17
  79.4 2.8 collective-permute-start.18
  82.1 12.6 %shard_map.111 = f32[8,2,96,768]{3,2,1,0:T(8,128)S(1)} custom-call(s32[20]{0:T(128)S(1)} %get-tuple-element.66.table, f32[1,3072]{1,0:T(1,128)S(1)} %add_divide_fusion.weight, bf16[768,3072]{1,0:T(8,128)(2,1)} %get-tuple-element.78.refs_0_, bf16[768,3072]{1,0:T(8,128)(2,1)} %collective-permute-done.2.refs_1_.refs_0_, ...), custom_call_target="tpu_custom_call" | custom-call | flops 1179648 | bytes 1179648 | tf_op jit(solution)/shard_map/pallas_call | solution.py:135
  97.2 2.7 collective-permute-start.13
  99.9 13.4 %shard_map.112 = f32[8,2,96,768]{3,2,1,0:T(8,128)S(1)} custom-call(s32[20]{0:T(128)S(1)} %get-tuple-element.72.table, f32[1,3072]{1,0:T(1,128)S(1)} %add_divide_fusion.weight, bf16[768,3072]{1,0:T(8,128)(2,1)} %get-tuple-element.78.refs_0_, bf16[768,3072]{1,0:T(8,128)(2,1)} %collective-permute-done.2.refs_1_.refs_0_, ...), custom_call_target="tpu_custom_call" | custom-call | flops 1179648 | bytes 1179648 | tf_op jit(solution)/shard_map/pallas_call | solution.py:135
  113.7 2.7 collective-permute-start.20
  116.6 14.1 %collective-permute-done.16.refs_3_ = bf16[768,3072]{1,0:T(8,128)(2,1)S(1)} collective-permute-done((bf16[768,3072]{1,0:T(8,128)(2,1)}, bf16[768,3072]{1,0:T(8,128)(2,1)S(1)}, u32[]{:S(2)}, u32[]{:S(2)}) %collective-permute-start.16) | collective-permute-done | bytes 4718624 | tf_op jit(solution)/shard_map/ppermute | solution.py:237
  130.8 7.9 %collective-permute-start.23 = (bf16[768,3072]{1,0:T(8,128)(2,1)S(1)}, bf16[768,3072]{1,0:T(8,128)(2,1)}, u32[]{:S(2)}, u32[]{:S(2)}) collective-permute-start(bf16[768,3072]{1,0:T(8,128)(2,1)S(1)} %collective-permute-done.16.refs_3_), channel_id=1, source_target_pairs={{0,8},{24,16},{32,40},{56,48},{64,72},{88,80},{96,104},{120,112},{... | collective-permute-start | bytes 14155784 | tf_op jit(solution)/shard_map/ppermute | solution.py:237
  144.3 12.6 %shard_map.113 = f32[8,2,96,768]{3,2,1,0:T(8,128)S(1)} custom-call(s32[22]{0:T(128)S(1)} %pad_add_fusion.2.table, f32[1,3072]{1,0:T(1,128)S(1)} %add_divide_fusion.weight, bf16[768,3072]{1,0:T(8,128)(2,1)} %collective-permute-done.2.refs_1_.refs_0_, bf16[768,3072]{1,0:T(8,128)(2,1)} %collective-permute-done.1.refs_2_.refs_1_, bf16[768,3072]{1,0:T(8,128)(2,1)} %copy-done.3, ...), custom_call_target="tpu_custom_call" | custom-call | flops 1179648 | bytes 1179648 | tf_op jit(solution)/shard_map/pallas_call | solution.py:135
  163.6 12.5 %shard_map.114 = f32[8,2,96,768]{3,2,1,0:T(8,128)S(1)} custom-call(s32[20]{0:T(128)S(1)} %get-tuple-element.94.table, f32[1,3072]{1,0:T(1,128)S(1)} %add_divide_fusion.weight, bf16[768,3072]{1,0:T(8,128)(2,1)} %get-tuple-element.78.refs_0_, bf16[768,3072]{1,0:T(8,128)(2,1)} %collective-permute-done.2.refs_1_.refs_0_, ...), custom_call_target="tpu_custom_call" | custom-call | flops 1179648 | bytes 1179648 | tf_op jit(solution)/shard_map/pallas_call | solution.py:135
  178.7 2.7 collective-permute-start.29
  181.8 2.7 collective-permute-start.31
  188.2 6.8 %collective-permute-done.30 = f16[2,2,96,768]{3,2,1,0:T(8,128)(2,1)S(1)} collective-permute-done((f16[2,2,96,768]{3,2,1,0:T(8,128)(2,1)S(1)}, f16[2,2,96,768]{3,2,1,0:T(8,128)(2,1)S(1)}, u32[]{:S(2)}, u32[]{:S(2)}) %collective-permute-start.30) | collective-permute-done | bytes 589856 | tf_op jit(solution)/shard_map/ppermute | solution.py:241
  195.9 2.0 collective-permute-start.34
  198.1 6.6 %collective-permute-done.33 = f16[2,96,768]{2,1,0:T(8,128)(2,1)S(1)} collective-permute-done((f16[2,96,768]{2,1,0:T(8,128)(2,1)S(1)}, f16[2,96,768]{2,1,0:T(8,128)(2,1)S(1)}, u32[]{:S(2)}, u32[]{:S(2)}) %collective-permute-start.33) | collective-permute-done | bytes 294944 | tf_op jit(solution)/shard_map/ppermute | solution.py:241
  207.3 5.4 %collective-permute-start.35 = (f16[2,2,96,768]{3,2,1,0:T(8,128)(2,1)S(1)}, f16[2,2,96,768]{3,2,1,0:T(8,128)(2,1)S(1)}, u32[]{:S(2)}, u32[]{:S(2)}) collective-permute-start(f16[2,2,96,768]{3,2,1,0:T(8,128)(2,1)S(1)} %bitcast.142), channel_id=1, source_target_pairs={{0,16},{1,17},{2,18},{3,19},{8,24},{9,25},{10,26},{11,27},{16,4},{... | collective-permute-start | bytes 1769480 | tf_op jit(solution)/shard_map/ppermute | solution.py:255
  212.7 6.8 %collective-permute-done.35 = f16[2,2,96,768]{3,2,1,0:T(8,128)(2,1)S(1)} collective-permute-done((f16[2,2,96,768]{3,2,1,0:T(8,128)(2,1)S(1)}, f16[2,2,96,768]{3,2,1,0:T(8,128)(2,1)S(1)}, u32[]{:S(2)}, u32[]{:S(2)}) %collective-permute-start.35) | collective-permute-done | bytes 589856 | tf_op jit(solution)/shard_map/ppermute | solution.py:255
  219.5 1.9 collective-permute-done.36
  223.2 7.3 %collective-permute-done.37 = f16[2,96,768]{2,1,0:T(8,128)(2,1)S(1)} collective-permute-done((f16[2,96,768]{2,1,0:T(8,128)(2,1)S(1)}, f16[2,96,768]{2,1,0:T(8,128)(2,1)S(1)}, u32[]{:S(2)}, u32[]{:S(2)}) %collective-permute-start.37) | collective-permute-done | bytes 294944 | tf_op jit(solution)/shard_map/ppermute | solution.py:255
  232.8 15.3 %collective-permute-start.39 = (f16[96,768]{1,0:T(8,128)(2,1)S(1)}, f16[96,768]{1,0:T(8,128)(2,1)S(1)}, u32[]{:S(2)}, u32[]{:S(2)}) collective-permute-start(f16[96,768]{1,0:T(8,128)(2,1)S(1)} %multiply_convert_fusion), channel_id=1, source_target_pairs={{16,24},{24,16},{48,56},{56,48},{80,88},{88,80},{112,120},{120,112... | collective-permute-start | bytes 442376 | tf_op jit(solution)/shard_map/ppermute | solution.py:237
  251.0 17.7 %all_to_all.15 = f16[3,96,8,96]{1,3,0,2:T(8,128)(2,1)S(1)} all-to-all(f16[3,96,8,96]{1,3,0,2:T(8,128)(2,1)S(1)} %fusion.12), channel_id=1, replica_groups=mesh['aux'=16,'pair'=8] {'pair'}, dimensions={2} | all-to-all | bytes 884736 | tf_op jit(solution)/shard_map/all_to_all | solution.py:443
  275.3 2.9 %collective-permute-done.41 = f16[768,96]{0,1:T(8,128)(2,1)S(1)} collective-permute-done((f16[768,96]{0,1:T(8,128)(2,1)S(1)}, f16[768,96]{0,1:T(8,128)(2,1)S(1)}, u32[]{:S(2)}, u32[]{:S(2)}) %collective-permute-start.41) | collective-permute-done | bytes 147488 | tf_op jit(solution)/shard_map/ppermute | solution.py:237
  279.0 2.5 collective-permute-done.42
  (157 shorter events, 57.5 us)
Async XLA Ops:
  8.6 57.6 %collective-permute-start = (bf16[768,3072]{1,0:T(8,128)(2,1)}, bf16[768,3072]{1,0:T(8,128)(2,1)}, u32[]{:S(2)}, u32[]{:S(2)}) collective-permute-start(bf16[768,3072]{1,0:T(8,128)(2,1)} %get-tuple-element.78.refs_0_), channel_id=1, source_target_pairs={{0,96},{24,56},{32,0},{56,88},{64,32},{88,120},{96,64},{120,24},{1... | collective-permute-start | bytes 14155784 | tf_op jit(solution)/shard_map/ppermute | solution.py:237
  12.1 54.0 %collective-permute-start.1 = (bf16[768,3072]{1,0:T(8,128)(2,1)}, bf16[768,3072]{1,0:T(8,128)(2,1)}, u32[]{:S(2)}, u32[]{:S(2)}) collective-permute-start(bf16[768,3072]{1,0:T(8,128)(2,1)} %get-tuple-element.77), channel_id=1, source_target_pairs={{0,16},{24,8},{32,48},{56,40},{64,80},{88,72},{96,112},{120,104},{... | collective-permute-start | bytes 14155784 | tf_op jit(solution)/shard_map/ppermute | solution.py:237
  15.6 50.5 %collective-permute-start.2 = (bf16[768,3072]{1,0:T(8,128)(2,1)}, bf16[768,3072]{1,0:T(8,128)(2,1)}, u32[]{:S(2)}, u32[]{:S(2)}) collective-permute-start(bf16[768,3072]{1,0:T(8,128)(2,1)} %get-tuple-element.78.refs_0_), channel_id=1, source_target_pairs={{0,8},{8,0},{16,24},{24,16},{32,40},{40,32},{48,56},{56,48},{64,72... | collective-permute-start | bytes 14155784 | tf_op jit(solution)/shard_map/ppermute | solution.py:237
  15.6 7.2 %collective-permute-start.3 = (f32[8,128]{1,0:T(8,128)S(1)}, f32[8,128]{1,0:T(8,128)S(1)}, u32[]{:S(2)}, u32[]{:S(2)}) collective-permute-start(f32[8,128]{1,0:T(8,128)S(1)} %get-tuple-element.62), channel_id=1, source_target_pairs={{0,8},{8,0},{16,24},{24,16},{32,40},{40,32},{48,56},{56,48},{64,72... | collective-permute-start | bytes 12296 | tf_op jit(solution)/shard_map/ppermute | solution.py:237
  35.4 26.3 %collective-permute-start.11 = (f32[8,128]{1,0:T(8,128)S(1)}, f32[8,128]{1,0:T(8,128)S(1)}, u32[]{:S(2)}, u32[]{:S(2)}) collective-permute-start(f32[8,128]{1,0:T(8,128)S(1)} %max.37), channel_id=1, source_target_pairs={{8,0},{16,24},{40,32},{48,56},{72,64},{80,88},{104,96},{112,120},{... | collective-permute-start | bytes 12296 | tf_op jit(solution)/shard_map/ppermute | solution.py:237
  66.2 28.8 %collective-permute-start.14 = (bf16[768,3072]{1,0:T(8,128)(2,1)}, bf16[768,3072]{1,0:T(8,128)(2,1)S(1)}, u32[]{:S(2)}, u32[]{:S(2)}) collective-permute-start(bf16[768,3072]{1,0:T(8,128)(2,1)} %collective-permute-done.1.refs_2_.refs_1_), channel_id=1, source_target_pairs={{8,0},{16,24},{40,32},{48,56},{72,64},{80,88},{104,96},{112,120},{... | collective-permute-start | bytes 14155784 | tf_op jit(solution)/shard_map/ppermute | solution.py:237
  67.4 28.9 %collective-permute-start.15 = (bf16[768,3072]{1,0:T(8,128)(2,1)}, bf16[768,3072]{1,0:T(8,128)(2,1)}, u32[]{:S(2)}, u32[]{:S(2)}) collective-permute-start(bf16[768,3072]{1,0:T(8,128)(2,1)} %collective-permute-done.refs_3_.refs_4_.refs_5_), channel_id=1, source_target_pairs={{24,16},{56,48},{88,80},{120,112},{25,17},{57,49},{89,81},{121,113... | collective-permute-start | bytes 14155784 | tf_op jit(solution)/shard_map/ppermute | solution.py:237
  75.3 55.5 %collective-permute-start.16 = (bf16[768,3072]{1,0:T(8,128)(2,1)}, bf16[768,3072]{1,0:T(8,128)(2,1)S(1)}, u32[]{:S(2)}, u32[]{:S(2)}) collective-permute-start(bf16[768,3072]{1,0:T(8,128)(2,1)} %get-tuple-element.77), channel_id=1, source_target_pairs={{8,24},{16,0},{40,56},{48,32},{72,88},{80,64},{104,120},{112,96},{... | collective-permute-start | bytes 14155784 | tf_op jit(solution)/shard_map/ppermute | solution.py:237
  76.6 54.2 %collective-permute-start.17 = (bf16[768,3072]{1,0:T(8,128)(2,1)}, bf16[768,3072]{1,0:T(8,128)(2,1)}, u32[]{:S(2)}, u32[]{:S(2)}) collective-permute-start(bf16[768,3072]{1,0:T(8,128)(2,1)} %get-tuple-element.78.refs_0_), channel_id=1, source_target_pairs={{8,104},{16,48},{40,8},{48,80},{72,40},{80,112},{104,72},{112,16},... | collective-permute-start | bytes 14155784 | tf_op jit(solution)/shard_map/ppermute | solution.py:237
  79.4 51.4 %collective-permute-start.18 = (bf16[768,3072]{1,0:T(8,128)(2,1)}, bf16[768,3072]{1,0:T(8,128)(2,1)}, u32[]{:S(2)}, u32[]{:S(2)}) collective-permute-start(bf16[768,3072]{1,0:T(8,128)(2,1)} %collective-permute-done.1.refs_2_.refs_1_), channel_id=1, source_target_pairs={{8,32},{16,112},{40,64},{48,16},{72,96},{80,48},{104,0},{112,80},{... | collective-permute-start | bytes 14155784 | tf_op jit(solution)/shard_map/ppermute | solution.py:237
  94.9 18.6 %collective-permute-start.12 = (f16[2,2,96,768]{3,2,1,0:T(8,128)(2,1)S(1)}, f16[2,2,96,768]{3,2,1,0:T(8,128)(2,1)S(1)}, u32[]{:S(2)}, u32[]{:S(2)}) collective-permute-start(f16[2,2,96,768]{3,2,1,0:T(8,128)(2,1)S(1)} %get-tuple-element.142), channel_id=1, source_target_pairs={{0,1},{1,2},{2,3},{3,0},{4,5},{5,6},{6,7},{7,4},{8,9},{9,10},{10,1... | collective-permute-start | bytes 1769480 | tf_op jit(solution)/shard_map/ppermute | solution.py:241
  97.2 16.4 %collective-permute-start.13 = (f16[2,2,96,768]{3,2,1,0:T(8,128)(2,1)S(1)}, f16[2,2,96,768]{3,2,1,0:T(8,128)(2,1)S(1)}, u32[]{:S(2)}, u32[]{:S(2)}) collective-permute-start(f16[2,2,96,768]{3,2,1,0:T(8,128)(2,1)S(1)} %get-tuple-element.141), channel_id=1, source_target_pairs={{0,3},{1,0},{2,1},{3,2},{4,7},{5,4},{6,5},{7,6},{8,11},{9,8},{10,9... | collective-permute-start | bytes 1769480 | tf_op jit(solution)/shard_map/ppermute | solution.py:241
  113.6 17.1 %collective-permute-start.19 = (f16[2,2,96,768]{3,2,1,0:T(8,128)(2,1)S(1)}, f16[2,2,96,768]{3,2,1,0:T(8,128)(2,1)S(1)}, u32[]{:S(2)}, u32[]{:S(2)}) collective-permute-start(f16[2,2,96,768]{3,2,1,0:T(8,128)(2,1)S(1)} %get-tuple-element.79), channel_id=1, source_target_pairs={{0,1},{1,2},{2,3},{3,0},{4,5},{5,6},{6,7},{7,4},{8,9},{9,10},{10,1... | collective-permute-start | bytes 1769480 | tf_op jit(solution)/shard_map/ppermute | solution.py:241
  113.7 17.1 %collective-permute-start.20 = (f16[2,2,96,768]{3,2,1,0:T(8,128)(2,1)S(1)}, f16[2,2,96,768]{3,2,1,0:T(8,128)(2,1)S(1)}, u32[]{:S(2)}, u32[]{:S(2)}) collective-permute-start(f16[2,2,96,768]{3,2,1,0:T(8,128)(2,1)S(1)} %get-tuple-element.80), channel_id=1, source_target_pairs={{0,3},{1,0},{2,1},{3,2},{4,7},{5,4},{6,5},{7,6},{8,11},{9,8},{10,9... | collective-permute-start | bytes 1769480 | tf_op jit(solution)/shard_map/ppermute | solution.py:241
  130.8 13.5 %collective-permute-start.23 = (bf16[768,3072]{1,0:T(8,128)(2,1)S(1)}, bf16[768,3072]{1,0:T(8,128)(2,1)}, u32[]{:S(2)}, u32[]{:S(2)}) collective-permute-start(bf16[768,3072]{1,0:T(8,128)(2,1)S(1)} %collective-permute-done.16.refs_3_), channel_id=1, source_target_pairs={{0,8},{24,16},{32,40},{56,48},{64,72},{88,80},{96,104},{120,112},{... | collective-permute-start | bytes 14155784 | tf_op jit(solution)/shard_map/ppermute | solution.py:237
  138.7 24.9 %collective-permute-start.27 = (bf16[768,3072]{1,0:T(8,128)(2,1)}, bf16[768,3072]{1,0:T(8,128)(2,1)}, u32[]{:S(2)}, u32[]{:S(2)}) collective-permute-start(bf16[768,3072]{1,0:T(8,128)(2,1)} %collective-permute-done.17.refs_6_), channel_id=1, source_target_pairs={{16,24},{48,56},{80,88},{112,120},{17,25},{49,57},{81,89},{113,121... | collective-permute-start | bytes 14155784 | tf_op jit(solution)/shard_map/ppermute | solution.py:237
  140.4 20.5 %collective-permute-start.21 = (f16[4,96,768]{2,1,0:T(8,128)(2,1)S(1)}, f16[4,96,768]{2,1,0:T(8,128)(2,1)S(1)}, u32[]{:S(2)}, u32[]{:S(2)}) collective-permute-start(f16[4,96,768]{2,1,0:T(8,128)(2,1)S(1)} %pad_maximum_fusion), channel_id=1, source_target_pairs={{0,1},{1,2},{2,3},{3,0},{4,5},{5,6},{6,7},{7,4},{8,9},{9,10},{10,1... | collective-permute-start | bytes 1769480 | tf_op jit(solution)/shard_map/ppermute | solution.py:241
  142.9 18.0 %collective-permute-start.22 = (f16[4,96,768]{2,1,0:T(8,128)(2,1)}, f16[4,96,768]{2,1,0:T(8,128)(2,1)S(1)}, u32[]{:S(2)}, u32[]{:S(2)}) collective-permute-start(f16[4,96,768]{2,1,0:T(8,128)(2,1)} %pad_maximum_fusion.1), channel_id=1, source_target_pairs={{0,3},{1,0},{2,1},{3,2},{4,7},{5,4},{6,5},{7,6},{8,11},{9,8},{10,9... | collective-permute-start | bytes 1769480 | tf_op jit(solution)/shard_map/ppermute | solution.py:241
  158.1 19.2 %collective-permute-start.24 = (f16[2,2,96,768]{3,2,1,0:T(8,128)(2,1)}, f16[2,2,96,768]{3,2,1,0:T(8,128)(2,1)}, u32[]{:S(2)}, u32[]{:S(2)}) collective-permute-start(f16[2,2,96,768]{3,2,1,0:T(8,128)(2,1)} %get-tuple-element.134), channel_id=1, source_target_pairs={{0,1},{1,2},{2,3},{3,0},{4,5},{5,6},{6,7},{7,4},{8,9},{9,10},{10,1... | collective-permute-start | bytes 1769480 | tf_op jit(solution)/shard_map/ppermute | solution.py:241
  159.2 18.1 %collective-permute-start.25 = (f16[2,2,96,768]{3,2,1,0:T(8,128)(2,1)}, f16[2,2,96,768]{3,2,1,0:T(8,128)(2,1)}, u32[]{:S(2)}, u32[]{:S(2)}) collective-permute-start(f16[2,2,96,768]{3,2,1,0:T(8,128)(2,1)} %get-tuple-element.133), channel_id=1, source_target_pairs={{0,3},{1,0},{2,1},{3,2},{4,7},{5,4},{6,5},{7,6},{8,11},{9,8},{10,9... | collective-permute-start | bytes 1769480 | tf_op jit(solution)/shard_map/ppermute | solution.py:241
  162.1 15.3 %collective-permute-start.26 = (f16[4,96,768]{2,1,0:T(8,128)(2,1)}, f16[4,96,768]{2,1,0:T(8,128)(2,1)}, u32[]{:S(2)}, u32[]{:S(2)}) collective-permute-start(f16[4,96,768]{2,1,0:T(8,128)(2,1)} %fusion.10), channel_id=1, source_target_pairs={{0,32},{32,64},{64,96},{96,0},{1,33},{33,65},{65,97},{97,1},{2,34}... | collective-permute-start | bytes 1769480 | tf_op jit(solution)/shard_map/ppermute | solution.py:237
  181.7 13.2 %collective-permute-start.30 = (f16[2,2,96,768]{3,2,1,0:T(8,128)(2,1)S(1)}, f16[2,2,96,768]{3,2,1,0:T(8,128)(2,1)S(1)}, u32[]{:S(2)}, u32[]{:S(2)}) collective-permute-start(f16[2,2,96,768]{3,2,1,0:T(8,128)(2,1)S(1)} %get-tuple-element.97), channel_id=1, source_target_pairs={{0,1},{1,2},{2,3},{3,0},{4,5},{5,6},{6,7},{7,4},{8,9},{9,10},{10,1... | collective-permute-start | bytes 1769480 | tf_op jit(solution)/shard_map/ppermute | solution.py:241
  181.8 13.2 %collective-permute-start.31 = (f16[2,2,96,768]{3,2,1,0:T(8,128)(2,1)S(1)}, f16[2,2,96,768]{3,2,1,0:T(8,128)(2,1)S(1)}, u32[]{:S(2)}, u32[]{:S(2)}) collective-permute-start(f16[2,2,96,768]{3,2,1,0:T(8,128)(2,1)S(1)} %get-tuple-element.98), channel_id=1, source_target_pairs={{0,3},{1,0},{2,1},{3,2},{4,7},{5,4},{6,5},{7,6},{8,11},{9,8},{10,9... | collective-permute-start | bytes 1769480 | tf_op jit(solution)/shard_map/ppermute | solution.py:241
  186.9 8.1 %collective-permute-start.32 = (f16[4,96,768]{2,1,0:T(8,128)(2,1)S(1)}, f16[4,96,768]{2,1,0:T(8,128)(2,1)S(1)}, u32[]{:S(2)}, u32[]{:S(2)}) collective-permute-start(f16[4,96,768]{2,1,0:T(8,128)(2,1)S(1)} %fusion.11), channel_id=1, source_target_pairs={{0,32},{8,40},{16,48},{32,64},{40,72},{48,80},{64,96},{72,104},{80... | collective-permute-start | bytes 1769480 | tf_op jit(solution)/shard_map/ppermute | solution.py:237
  195.2 9.6 %collective-permute-start.33 = (f16[2,96,768]{2,1,0:T(8,128)(2,1)S(1)}, f16[2,96,768]{2,1,0:T(8,128)(2,1)S(1)}, u32[]{:S(2)}, u32[]{:S(2)}) collective-permute-start(f16[2,96,768]{2,1,0:T(8,128)(2,1)S(1)} %get-tuple-element.122), channel_id=1, source_target_pairs={{0,1},{1,2},{2,3},{3,0},{4,5},{5,6},{6,7},{7,4},{8,9},{9,10},{10,1... | collective-permute-start | bytes 884744 | tf_op jit(solution)/shard_map/ppermute | solution.py:241
  195.9 8.8 %collective-permute-start.34 = (f16[2,96,768]{2,1,0:T(8,128)(2,1)S(1)}, f16[2,96,768]{2,1,0:T(8,128)(2,1)S(1)}, u32[]{:S(2)}, u32[]{:S(2)}) collective-permute-start(f16[2,96,768]{2,1,0:T(8,128)(2,1)S(1)} %get-tuple-element.121), channel_id=1, source_target_pairs={{0,3},{1,0},{2,1},{3,2},{4,7},{5,4},{6,5},{7,6},{8,11},{9,8},{10,9... | collective-permute-start | bytes 884744 | tf_op jit(solution)/shard_map/ppermute | solution.py:241
  207.3 12.2 %collective-permute-start.35 = (f16[2,2,96,768]{3,2,1,0:T(8,128)(2,1)S(1)}, f16[2,2,96,768]{3,2,1,0:T(8,128)(2,1)S(1)}, u32[]{:S(2)}, u32[]{:S(2)}) collective-permute-start(f16[2,2,96,768]{3,2,1,0:T(8,128)(2,1)S(1)} %bitcast.142), channel_id=1, source_target_pairs={{0,16},{1,17},{2,18},{3,19},{8,24},{9,25},{10,26},{11,27},{16,4},{... | collective-permute-start | bytes 1769480 | tf_op jit(solution)/shard_map/ppermute | solution.py:255
  212.7 8.7 %collective-permute-start.36 = (f16[2,2,96,768]{3,2,1,0:T(8,128)(2,1)S(1)}, f16[2,2,96,768]{3,2,1,0:T(8,128)(2,1)S(1)}, u32[]{:S(2)}, u32[]{:S(2)}) collective-permute-start(f16[2,2,96,768]{3,2,1,0:T(8,128)(2,1)S(1)} %bitcast.141), channel_id=1, source_target_pairs={{0,20},{1,21},{2,22},{3,23},{8,28},{9,29},{10,30},{11,31},{16,0},{... | collective-permute-start | bytes 1769480 | tf_op jit(solution)/shard_map/ppermute | solution.py:255
  221.7 8.9 %collective-permute-start.37 = (f16[2,96,768]{2,1,0:T(8,128)(2,1)S(1)}, f16[2,96,768]{2,1,0:T(8,128)(2,1)S(1)}, u32[]{:S(2)}, u32[]{:S(2)}) collective-permute-start(f16[2,96,768]{2,1,0:T(8,128)(2,1)S(1)} %get-tuple-element.118), channel_id=1, source_target_pairs={{0,16},{1,17},{2,18},{3,19},{8,24},{9,25},{10,26},{11,27},{16,4},{... | collective-permute-start | bytes 884744 | tf_op jit(solution)/shard_map/ppermute | solution.py:255
  221.8 9.1 %collective-permute-start.38 = (f16[2,96,768]{2,1,0:T(8,128)(2,1)S(1)}, f16[2,96,768]{2,1,0:T(8,128)(2,1)S(1)}, u32[]{:S(2)}, u32[]{:S(2)}) collective-permute-start(f16[2,96,768]{2,1,0:T(8,128)(2,1)S(1)} %get-tuple-element.117), channel_id=1, source_target_pairs={{0,20},{1,21},{2,22},{3,23},{8,28},{9,29},{10,30},{11,31},{16,0},{... | collective-permute-start | bytes 884744 | tf_op jit(solution)/shard_map/ppermute | solution.py:255
  232.8 16.3 %collective-permute-start.39 = (f16[96,768]{1,0:T(8,128)(2,1)S(1)}, f16[96,768]{1,0:T(8,128)(2,1)S(1)}, u32[]{:S(2)}, u32[]{:S(2)}) collective-permute-start(f16[96,768]{1,0:T(8,128)(2,1)S(1)} %multiply_convert_fusion), channel_id=1, source_target_pairs={{16,24},{24,16},{48,56},{56,48},{80,88},{88,80},{112,120},{120,112... | collective-permute-start | bytes 442376 | tf_op jit(solution)/shard_map/ppermute | solution.py:237
  272.2 9.3 %collective-permute-start.42 = (f16[768,96]{0,1:T(8,128)(2,1)S(1)}, f16[768,96]{0,1:T(8,128)(2,1)S(1)}, u32[]{:S(2)}, u32[]{:S(2)}) collective-permute-start(f16[768,96]{0,1:T(8,128)(2,1)S(1)} %squeeze.42), channel_id=1, source_target_pairs={{0,104},{8,112},{16,120},{24,0},{32,8},{40,16},{48,24},{56,32},{64... | collective-permute-start | bytes 442376 | tf_op jit(solution)/shard_map/ppermute | solution.py:237
  (26 other events, 274.7 us)

commit v7 on v6

--- a/solution.py
+++ b/solution.py
@@ -148,7 +148,7 @@
         ),
         out_shape=jax.ShapeDtypeStruct((8, count, PART, ROWS), jnp.float32),
         compiler_params=pltpu.CompilerParams(
-            dimension_semantics=("arbitrary",), vmem_limit_bytes=36 * 1024 * 1024),
+            dimension_semantics=("arbitrary",), vmem_limit_bytes=(held_most + 2) * ROWS * HALF * 2 + 4 * 1024 * 1024),
         cost_estimate=pl.CostEstimate(
             flops=count * ROWS * ROWS,
             bytes_accessed=count * ROWS * ROWS,
@@ -224,7 +224,7 @@
             out_specs=[block, block, pl.BlockSpec((8, 128), lambda i, t: (0, 0))],
         ),
         out_shape=[half, half, jax.ShapeDtypeStruct((8, 128), jnp.float32)],
-        compiler_params=pltpu.CompilerParams(vmem_limit_bytes=24 * 1024 * 1024),
+        compiler_params=pltpu.CompilerParams(vmem_limit_bytes=12 * 1024 * 1024),
         cost_estimate=pl.CostEstimate(flops=0, bytes_accessed=PART * ROWS, transcendentals=0),
     )(x_lo[None], coeffs)
 
@@ -308,7 +308,7 @@
         in_specs=[pl.BlockSpec(memory_space=pltpu.SMEM), pl.BlockSpec(memory_space=pltpu.VMEM)],
         out_specs=pl.BlockSpec(memory_space=pltpu.VMEM),
         out_shape=jax.ShapeDtypeStruct((16, PART, ROWS), jnp.float32),
-        compiler_params=pltpu.CompilerParams(vmem_limit_bytes=20 * 1024 * 1024),
+        compiler_params=pltpu.CompilerParams(vmem_limit_bytes=16 * 1024 * 1024),
         cost_estimate=pl.CostEstimate(flops=0, bytes_accessed=PART * ROWS, transcendentals=0),
     )(table, slots)
 

time: 283 us -> 284 us (level)
  waiting for transfers between devices: 80.2 us -> 75.6 us
  other arithmetic: 16 us -> 20 us
  Pallas kernels: 61.7 us -> 58.2 us
    ppermute x5, starting transfers between devices: 7.57 us -> 16 us  [x_permute(): return lax.ppermute(value, ('aux', 'pair'), perm)]
    ppermute x21, starting transfers between devices: 56.9 us -> 50.6 us  [aux_permute(): return lax.ppermute(value, 'aux', moves(pairs))]
    unnamed x34 -> x42, local copies, waits for them, and re-layouts: 6.17 us -> 9.95 us
    pallas_call x4, Pallas kernels: 51.1 us -> 47.6 us  [tile_batch(): pl.pallas_call(functools.partial(tiles_kernel, count, held_most, len(sour...]
    ppermute x17, waiting for transfers between devices: 16.5 us -> 13.3 us  [y_permute(): lax.ppermute(value, 'pair', [(h * 4 + y, h * 4 + (y + by) % 4) for h in r...]
  transfers between devices with their start and end apart: 43 -> 43, of which waited for: 15 -> 14; matrix products, arithmetic and copies ran while one was open for 6% -> 7% of each run, Pallas kernels for 20% -> 19%
where the time goes in v7:
time: 284 us; the launch traced here: 283 us
  starting transfers between devices  90.6 us (32%)
  waiting for transfers between devices  75.6 us (27%)
  Pallas kernels  58.2 us (20%)
  other arithmetic  20 us (7%)
  blocking collectives  19.3 us (7%)
  local copies, waits for them, and re-layouts  17.5 us (6%)
    ppermute x21, starting transfers between devices, aux_permute(): return lax.ppermute(value, 'aux', moves(pairs))  50.6 us
    pallas_call x4, Pallas kernels, tile_batch(): pl.pallas_call(functools.partial(tiles_kernel, count, held_most, len(sour...  47.6 us
    ppermute x21, waiting for transfers between devices, aux_permute(): return lax.ppermute(value, 'aux', moves(pairs))  45.8 us
    ppermute x17, starting transfers between devices, y_permute(): lax.ppermute(value, 'pair', [(h * 4 + y, h * 4 + (y + by) % 4) for h in r...  24 us
    all_to_all x1, blocking collectives, local(): lax.all_to_all(crossed, 'pair', split_axis=2, concat_axis=1, tiled=True)  19.3 us
    ppermute x5, waiting for transfers between devices, x_permute(): return lax.ppermute(value, ('aux', 'pair'), perm)  16.5 us
    ppermute x5, starting transfers between devices, x_permute(): return lax.ppermute(value, ('aux', 'pair'), perm)  16 us
    ppermute x17, waiting for transfers between devices, y_permute(): lax.ppermute(value, 'pair', [(h * 4 + y, h * 4 + (y + by) % 4) for h in r...  13.3 us
  transfers between devices with their start and end apart: 43, of which 14 were waited for; matrix products, arithmetic and copies ran while one was open for 7% of the time, Pallas kernels for 19%

profile of v7, /device:TPU:3, one launch (start us, length us, event | category | flops | bytes accessed | tf_op | source)
XLA Modules:
  0.0 283.1 jit_solution(16323881345988645088)
XLA Ops:
  0.0 3.7 %copy-done.7 = bf16[768,6144]{1,0:T(8,128)(2,1)S(1)} copy-done((bf16[768,6144]{1,0:T(8,128)(2,1)S(1)}, bf16[768,6144]{1,0:T(8,128)(2,1)}, u32[]{:S(2)}) %copy-start.7) | copy-done | bytes 9437208
  3.7 4.9 %shard_map.109 = (bf16[768,3072]{1,0:T(8,128)(2,1)}, bf16[768,3072]{1,0:T(8,128)(2,1)}, f32[8,128]{1,0:T(8,128)S(1)}) custom-call(s32[1]{0:T(128)} %bitcast.x_lo, bf16[768,6144]{1,0:T(8,128)(2,1)S(1)} %copy-done.7), custom_call_target="tpu_custom_call" | custom-call | bytes 73728 | tf_op jit(solution)/shard_map/pallas_call | solution.py:218
  8.6 3.5 %collective-permute-start = (bf16[768,3072]{1,0:T(8,128)(2,1)}, bf16[768,3072]{1,0:T(8,128)(2,1)}, u32[]{:S(2)}, u32[]{:S(2)}) collective-permute-start(bf16[768,3072]{1,0:T(8,128)(2,1)} %get-tuple-element.78.refs_0_), channel_id=1, source_target_pairs={{0,96},{24,56},{32,0},{56,88},{64,32},{88,120},{96,64},{120,24},{1... | collective-permute-start | bytes 14155784 | tf_op jit(solution)/shard_map/ppermute | solution.py:237
  12.2 3.5 %collective-permute-start.1 = (bf16[768,3072]{1,0:T(8,128)(2,1)}, bf16[768,3072]{1,0:T(8,128)(2,1)}, u32[]{:S(2)}, u32[]{:S(2)}) collective-permute-start(bf16[768,3072]{1,0:T(8,128)(2,1)} %get-tuple-element.77), channel_id=1, source_target_pairs={{0,16},{24,8},{32,48},{56,40},{64,80},{88,72},{96,112},{120,104},{... | collective-permute-start | bytes 14155784 | tf_op jit(solution)/shard_map/ppermute | solution.py:237
  17.4 4.9 %shard_map.110 = f32[1,3072]{1,0:T(1,128)} custom-call(s32[1,3072]{1,0:T(1,128)} %bitcast.143, s32[1,3072]{1,0:T(1,128)} %bitcast.144, f32[32,128]{1,0:T(8,128)} %bitcast.146, f32[256,128]{1,0:T(8,128)} %bitcast.145), custom_call_target="tpu_custom_call" | custom-call | flops 679477248 | bytes 200000 | tf_op jit(solution)/shard_map/pallas_call | solution.py:186
  23.0 3.1 %collective-permute-start.5 = (f32[8,128]{1,0:T(8,128)S(1)}, f32[8,128]{1,0:T(8,128)S(1)}, u32[]{:S(2)}, u32[]{:S(2)}) collective-permute-start(f32[8,128]{1,0:T(8,128)S(1)} %max.30), channel_id=1, source_target_pairs={{0,2},{1,3},{2,0},{3,1},{4,6},{5,7},{6,4},{7,5},{8,10},{9,11},{10,... | collective-permute-start | bytes 12296 | tf_op jit(solution)/shard_map/ppermute | solution.py:241
  37.5 24.3 %collective-permute-done.11 = f32[8,128]{1,0:T(8,128)S(1)} collective-permute-done((f32[8,128]{1,0:T(8,128)S(1)}, f32[8,128]{1,0:T(8,128)S(1)}, u32[]{:S(2)}, u32[]{:S(2)}) %collective-permute-start.11) | collective-permute-done | bytes 4128 | tf_op jit(solution)/shard_map/ppermute | solution.py:237
  63.8 2.4 collective-permute-done.refs_3_.refs_4_.refs_5_
  67.5 5.9 %collective-permute-start.15 = (bf16[768,3072]{1,0:T(8,128)(2,1)}, bf16[768,3072]{1,0:T(8,128)(2,1)S(1)}, u32[]{:S(2)}, u32[]{:S(2)}) collective-permute-start(bf16[768,3072]{1,0:T(8,128)(2,1)} %collective-permute-done.refs_3_.refs_4_.refs_5_), channel_id=1, source_target_pairs={{24,16},{56,48},{88,80},{120,112},{25,17},{57,49},{89,81},{121,113... | collective-permute-start | bytes 14155784 | tf_op jit(solution)/shard_map/ppermute | solution.py:237
  74.7 2.8 collective-permute-start.17
  77.5 2.8 collective-permute-start.18
  80.2 12.6 %shard_map.111 = f32[8,2,96,768]{3,2,1,0:T(8,128)S(1)} custom-call(s32[20]{0:T(128)S(1)} %get-tuple-element.66.table, f32[1,3072]{1,0:T(1,128)S(1)} %add_divide_fusion.weight, bf16[768,3072]{1,0:T(8,128)(2,1)} %get-tuple-element.78.refs_0_, bf16[768,3072]{1,0:T(8,128)(2,1)} %collective-permute-done.2.refs_1_.refs_0_, ...), custom_call_target="tpu_custom_call" | custom-call | flops 1179648 | bytes 1179648 | tf_op jit(solution)/shard_map/pallas_call | solution.py:135
  95.4 2.3 copy-done.8
  99.0 13.0 %shard_map.112 = f32[8,2,96,768]{3,2,1,0:T(8,128)S(1)} custom-call(s32[20]{0:T(128)S(1)} %get-tuple-element.72.table, f32[1,3072]{1,0:T(1,128)S(1)} %add_divide_fusion.weight, bf16[768,3072]{1,0:T(8,128)(2,1)} %get-tuple-element.78.refs_0_, bf16[768,3072]{1,0:T(8,128)(2,1)} %collective-permute-done.2.refs_1_.refs_0_, ...), custom_call_target="tpu_custom_call" | custom-call | flops 1179648 | bytes 1179648 | tf_op jit(solution)/shard_map/pallas_call | solution.py:135
  112.7 2.3 collective-permute-start.20
  115.2 13.7 %collective-permute-done.16.refs_3_ = bf16[768,3072]{1,0:T(8,128)(2,1)S(1)} collective-permute-done((bf16[768,3072]{1,0:T(8,128)(2,1)}, bf16[768,3072]{1,0:T(8,128)(2,1)S(1)}, u32[]{:S(2)}, u32[]{:S(2)}) %collective-permute-start.16) | collective-permute-done | bytes 4718624 | tf_op jit(solution)/shard_map/ppermute | solution.py:237
  128.9 8.5 %collective-permute-start.23 = (bf16[768,3072]{1,0:T(8,128)(2,1)S(1)}, bf16[768,3072]{1,0:T(8,128)(2,1)}, u32[]{:S(2)}, u32[]{:S(2)}) collective-permute-start(bf16[768,3072]{1,0:T(8,128)(2,1)S(1)} %collective-permute-done.16.refs_3_), channel_id=1, source_target_pairs={{0,8},{24,16},{32,40},{56,48},{64,72},{88,80},{96,104},{120,112},{... | collective-permute-start | bytes 14155784 | tf_op jit(solution)/shard_map/ppermute | solution.py:237
  143.9 2.3 copy-done.1
  146.2 10.6 %shard_map.113 = f32[8,2,96,768]{3,2,1,0:T(8,128)S(1)} custom-call(s32[22]{0:T(128)S(1)} %pad_add_fusion.2.table, f32[1,3072]{1,0:T(1,128)S(1)} %add_divide_fusion.weight, bf16[768,3072]{1,0:T(8,128)(2,1)} %collective-permute-done.2.refs_1_.refs_0_, bf16[768,3072]{1,0:T(8,128)(2,1)} %collective-permute-done.1.refs_2_.refs_1_, ...), custom_call_target="tpu_custom_call" | custom-call | flops 1179648 | bytes 1179648 | tf_op jit(solution)/shard_map/pallas_call | solution.py:135
  164.6 11.4 %shard_map.114 = f32[8,2,96,768]{3,2,1,0:T(8,128)S(1)} custom-call(s32[20]{0:T(128)S(1)} %get-tuple-element.94.table, f32[1,3072]{1,0:T(1,128)S(1)} %add_divide_fusion.weight, bf16[768,3072]{1,0:T(8,128)(2,1)} %get-tuple-element.78.refs_0_, bf16[768,3072]{1,0:T(8,128)(2,1)} %collective-permute-done.2.refs_1_.refs_0_, ...), custom_call_target="tpu_custom_call" | custom-call | flops 1179648 | bytes 1179648 | tf_op jit(solution)/shard_map/pallas_call | solution.py:135
  177.9 2.7 collective-permute-start.29
  181.0 2.7 collective-permute-start.31
  187.9 3.2 %collective-permute-done.30 = f16[2,2,96,768]{3,2,1,0:T(8,128)(2,1)S(1)} collective-permute-done((f16[2,2,96,768]{3,2,1,0:T(8,128)(2,1)S(1)}, f16[2,2,96,768]{3,2,1,0:T(8,128)(2,1)S(1)}, u32[]{:S(2)}, u32[]{:S(2)}) %collective-permute-start.30) | collective-permute-done | bytes 589856 | tf_op jit(solution)/shard_map/ppermute | solution.py:241
  191.3 3.0 %collective-permute-start.34 = (f16[2,96,768]{2,1,0:T(8,128)(2,1)S(1)}, f16[2,96,768]{2,1,0:T(8,128)(2,1)S(1)}, u32[]{:S(2)}, u32[]{:S(2)}) collective-permute-start(f16[2,96,768]{2,1,0:T(8,128)(2,1)S(1)} %get-tuple-element.121), channel_id=1, source_target_pairs={{0,3},{1,0},{2,1},{3,2},{4,7},{5,4},{6,5},{7,6},{8,11},{9,8},{10,9... | collective-permute-start | bytes 884744 | tf_op jit(solution)/shard_map/ppermute | solution.py:241
  194.6 7.0 %collective-permute-done.33 = f16[2,96,768]{2,1,0:T(8,128)(2,1)S(1)} collective-permute-done((f16[2,96,768]{2,1,0:T(8,128)(2,1)S(1)}, f16[2,96,768]{2,1,0:T(8,128)(2,1)S(1)}, u32[]{:S(2)}, u32[]{:S(2)}) %collective-permute-start.33) | collective-permute-done | bytes 294944 | tf_op jit(solution)/shard_map/ppermute | solution.py:241
  204.2 13.8 %collective-permute-start.35 = (f16[2,2,96,768]{3,2,1,0:T(8,128)(2,1)S(1)}, f16[2,2,96,768]{3,2,1,0:T(8,128)(2,1)S(1)}, u32[]{:S(2)}, u32[]{:S(2)}) collective-permute-start(f16[2,2,96,768]{3,2,1,0:T(8,128)(2,1)S(1)} %bitcast.142), channel_id=1, source_target_pairs={{0,16},{1,17},{2,18},{3,19},{8,24},{9,25},{10,26},{11,27},{16,4},{... | collective-permute-start | bytes 1769480 | tf_op jit(solution)/shard_map/ppermute | solution.py:255
  218.0 7.7 %collective-permute-done.35 = f16[2,2,96,768]{3,2,1,0:T(8,128)(2,1)S(1)} collective-permute-done((f16[2,2,96,768]{3,2,1,0:T(8,128)(2,1)S(1)}, f16[2,2,96,768]{3,2,1,0:T(8,128)(2,1)S(1)}, u32[]{:S(2)}, u32[]{:S(2)}) %collective-permute-start.35) | collective-permute-done | bytes 589856 | tf_op jit(solution)/shard_map/ppermute | solution.py:255
  229.3 5.3 %collective-permute-done.37 = f16[2,96,768]{2,1,0:T(8,128)(2,1)S(1)} collective-permute-done((f16[2,96,768]{2,1,0:T(8,128)(2,1)S(1)}, f16[2,96,768]{2,1,0:T(8,128)(2,1)S(1)}, u32[]{:S(2)}, u32[]{:S(2)}) %collective-permute-start.37) | collective-permute-done | bytes 294944 | tf_op jit(solution)/shard_map/ppermute | solution.py:255
  238.1 9.2 %collective-permute-start.39 = (f16[96,768]{1,0:T(8,128)(2,1)S(1)}, f16[96,768]{1,0:T(8,128)(2,1)S(1)}, u32[]{:S(2)}, u32[]{:S(2)}) collective-permute-start(f16[96,768]{1,0:T(8,128)(2,1)S(1)} %multiply_convert_fusion), channel_id=1, source_target_pairs={{16,24},{24,16},{48,56},{56,48},{80,88},{88,80},{112,120},{120,112... | collective-permute-start | bytes 442376 | tf_op jit(solution)/shard_map/ppermute | solution.py:237
  250.3 19.3 %all_to_all.15 = f16[3,96,8,96]{1,3,0,2:T(8,128)(2,1)S(1)} all-to-all(f16[3,96,8,96]{1,3,0,2:T(8,128)(2,1)S(1)} %fusion.12), channel_id=1, replica_groups=mesh['aux'=16,'pair'=8] {'pair'}, dimensions={2} | all-to-all | bytes 884736 | tf_op jit(solution)/shard_map/all_to_all | solution.py:443
  276.2 2.9 %collective-permute-done.41 = f16[768,96]{0,1:T(8,128)(2,1)S(1)} collective-permute-done((f16[768,96]{0,1:T(8,128)(2,1)S(1)}, f16[768,96]{0,1:T(8,128)(2,1)S(1)}, u32[]{:S(2)}, u32[]{:S(2)}) %collective-permute-start.41) | collective-permute-done | bytes 147488 | tf_op jit(solution)/shard_map/ppermute | solution.py:237
  279.9 2.5 collective-permute-done.42
  (165 shorter events, 63.5 us)
Async XLA Ops:
  8.6 57.6 %collective-permute-start = (bf16[768,3072]{1,0:T(8,128)(2,1)}, bf16[768,3072]{1,0:T(8,128)(2,1)}, u32[]{:S(2)}, u32[]{:S(2)}) collective-permute-start(bf16[768,3072]{1,0:T(8,128)(2,1)} %get-tuple-element.78.refs_0_), channel_id=1, source_target_pairs={{0,96},{24,56},{32,0},{56,88},{64,32},{88,120},{96,64},{120,24},{1... | collective-permute-start | bytes 14155784 | tf_op jit(solution)/shard_map/ppermute | solution.py:237
  12.2 54.0 %collective-permute-start.1 = (bf16[768,3072]{1,0:T(8,128)(2,1)}, bf16[768,3072]{1,0:T(8,128)(2,1)}, u32[]{:S(2)}, u32[]{:S(2)}) collective-permute-start(bf16[768,3072]{1,0:T(8,128)(2,1)} %get-tuple-element.77), channel_id=1, source_target_pairs={{0,16},{24,8},{32,48},{56,40},{64,80},{88,72},{96,112},{120,104},{... | collective-permute-start | bytes 14155784 | tf_op jit(solution)/shard_map/ppermute | solution.py:237
  15.7 50.5 %collective-permute-start.2 = (bf16[768,3072]{1,0:T(8,128)(2,1)}, bf16[768,3072]{1,0:T(8,128)(2,1)}, u32[]{:S(2)}, u32[]{:S(2)}) collective-permute-start(bf16[768,3072]{1,0:T(8,128)(2,1)} %get-tuple-element.78.refs_0_), channel_id=1, source_target_pairs={{0,8},{8,0},{16,24},{24,16},{32,40},{40,32},{48,56},{56,48},{64,72... | collective-permute-start | bytes 14155784 | tf_op jit(solution)/shard_map/ppermute | solution.py:237
  15.7 7.3 %collective-permute-start.3 = (f32[8,128]{1,0:T(8,128)S(1)}, f32[8,128]{1,0:T(8,128)S(1)}, u32[]{:S(2)}, u32[]{:S(2)}) collective-permute-start(f32[8,128]{1,0:T(8,128)S(1)} %get-tuple-element.62), channel_id=1, source_target_pairs={{0,8},{8,0},{16,24},{24,16},{32,40},{40,32},{48,56},{56,48},{64,72... | collective-permute-start | bytes 12296 | tf_op jit(solution)/shard_map/ppermute | solution.py:237
  35.5 26.3 %collective-permute-start.11 = (f32[8,128]{1,0:T(8,128)S(1)}, f32[8,128]{1,0:T(8,128)S(1)}, u32[]{:S(2)}, u32[]{:S(2)}) collective-permute-start(f32[8,128]{1,0:T(8,128)S(1)} %max.37), channel_id=1, source_target_pairs={{8,0},{16,24},{40,32},{48,56},{72,64},{80,88},{104,96},{112,120},{... | collective-permute-start | bytes 12296 | tf_op jit(solution)/shard_map/ppermute | solution.py:237
  66.2 27.9 %collective-permute-start.14 = (bf16[768,3072]{1,0:T(8,128)(2,1)}, bf16[768,3072]{1,0:T(8,128)(2,1)S(1)}, u32[]{:S(2)}, u32[]{:S(2)}) collective-permute-start(bf16[768,3072]{1,0:T(8,128)(2,1)} %collective-permute-done.1.refs_2_.refs_1_), channel_id=1, source_target_pairs={{8,0},{16,24},{40,32},{48,56},{72,64},{80,88},{104,96},{112,120},{... | collective-permute-start | bytes 14155784 | tf_op jit(solution)/shard_map/ppermute | solution.py:237
  67.5 27.9 %collective-permute-start.15 = (bf16[768,3072]{1,0:T(8,128)(2,1)}, bf16[768,3072]{1,0:T(8,128)(2,1)S(1)}, u32[]{:S(2)}, u32[]{:S(2)}) collective-permute-start(bf16[768,3072]{1,0:T(8,128)(2,1)} %collective-permute-done.refs_3_.refs_4_.refs_5_), channel_id=1, source_target_pairs={{24,16},{56,48},{88,80},{120,112},{25,17},{57,49},{89,81},{121,113... | collective-permute-start | bytes 14155784 | tf_op jit(solution)/shard_map/ppermute | solution.py:237
  73.4 55.5 %collective-permute-start.16 = (bf16[768,3072]{1,0:T(8,128)(2,1)}, bf16[768,3072]{1,0:T(8,128)(2,1)S(1)}, u32[]{:S(2)}, u32[]{:S(2)}) collective-permute-start(bf16[768,3072]{1,0:T(8,128)(2,1)} %get-tuple-element.77), channel_id=1, source_target_pairs={{8,24},{16,0},{40,56},{48,32},{72,88},{80,64},{104,120},{112,96},{... | collective-permute-start | bytes 14155784 | tf_op jit(solution)/shard_map/ppermute | solution.py:237
  74.7 54.2 %collective-permute-start.17 = (bf16[768,3072]{1,0:T(8,128)(2,1)}, bf16[768,3072]{1,0:T(8,128)(2,1)}, u32[]{:S(2)}, u32[]{:S(2)}) collective-permute-start(bf16[768,3072]{1,0:T(8,128)(2,1)} %get-tuple-element.78.refs_0_), channel_id=1, source_target_pairs={{8,104},{16,48},{40,8},{48,80},{72,40},{80,112},{104,72},{112,16},... | collective-permute-start | bytes 14155784 | tf_op jit(solution)/shard_map/ppermute | solution.py:237
  77.5 51.4 %collective-permute-start.18 = (bf16[768,3072]{1,0:T(8,128)(2,1)}, bf16[768,3072]{1,0:T(8,128)(2,1)}, u32[]{:S(2)}, u32[]{:S(2)}) collective-permute-start(bf16[768,3072]{1,0:T(8,128)(2,1)} %collective-permute-done.1.refs_2_.refs_1_), channel_id=1, source_target_pairs={{8,32},{16,112},{40,64},{48,16},{72,96},{80,48},{104,0},{112,80},{... | collective-permute-start | bytes 14155784 | tf_op jit(solution)/shard_map/ppermute | solution.py:237
  94.1 18.1 %collective-permute-start.12 = (f16[2,2,96,768]{3,2,1,0:T(8,128)(2,1)}, f16[2,2,96,768]{3,2,1,0:T(8,128)(2,1)S(1)}, u32[]{:S(2)}, u32[]{:S(2)}) collective-permute-start(f16[2,2,96,768]{3,2,1,0:T(8,128)(2,1)} %get-tuple-element.142), channel_id=1, source_target_pairs={{0,1},{1,2},{2,3},{3,0},{4,5},{5,6},{6,7},{7,4},{8,9},{9,10},{10,1... | collective-permute-start | bytes 1769480 | tf_op jit(solution)/shard_map/ppermute | solution.py:241
  97.7 14.5 %collective-permute-start.13 = (f16[2,2,96,768]{3,2,1,0:T(8,128)(2,1)}, f16[2,2,96,768]{3,2,1,0:T(8,128)(2,1)S(1)}, u32[]{:S(2)}, u32[]{:S(2)}) collective-permute-start(f16[2,2,96,768]{3,2,1,0:T(8,128)(2,1)} %get-tuple-element.141), channel_id=1, source_target_pairs={{0,3},{1,0},{2,1},{3,2},{4,7},{5,4},{6,5},{7,6},{8,11},{9,8},{10,9... | collective-permute-start | bytes 1769480 | tf_op jit(solution)/shard_map/ppermute | solution.py:241
  112.2 16.6 %collective-permute-start.19 = (f16[2,2,96,768]{3,2,1,0:T(8,128)(2,1)S(1)}, f16[2,2,96,768]{3,2,1,0:T(8,128)(2,1)S(1)}, u32[]{:S(2)}, u32[]{:S(2)}) collective-permute-start(f16[2,2,96,768]{3,2,1,0:T(8,128)(2,1)S(1)} %get-tuple-element.79), channel_id=1, source_target_pairs={{0,1},{1,2},{2,3},{3,0},{4,5},{5,6},{6,7},{7,4},{8,9},{9,10},{10,1... | collective-permute-start | bytes 1769480 | tf_op jit(solution)/shard_map/ppermute | solution.py:241
  112.7 16.2 %collective-permute-start.20 = (f16[2,2,96,768]{3,2,1,0:T(8,128)(2,1)S(1)}, f16[2,2,96,768]{3,2,1,0:T(8,128)(2,1)S(1)}, u32[]{:S(2)}, u32[]{:S(2)}) collective-permute-start(f16[2,2,96,768]{3,2,1,0:T(8,128)(2,1)S(1)} %get-tuple-element.80), channel_id=1, source_target_pairs={{0,3},{1,0},{2,1},{3,2},{4,7},{5,4},{6,5},{7,6},{8,11},{9,8},{10,9... | collective-permute-start | bytes 1769480 | tf_op jit(solution)/shard_map/ppermute | solution.py:241
  128.9 14.9 %collective-permute-start.23 = (bf16[768,3072]{1,0:T(8,128)(2,1)S(1)}, bf16[768,3072]{1,0:T(8,128)(2,1)}, u32[]{:S(2)}, u32[]{:S(2)}) collective-permute-start(bf16[768,3072]{1,0:T(8,128)(2,1)S(1)} %collective-permute-done.16.refs_3_), channel_id=1, source_target_pairs={{0,8},{24,16},{32,40},{56,48},{64,72},{88,80},{96,104},{120,112},{... | collective-permute-start | bytes 14155784 | tf_op jit(solution)/shard_map/ppermute | solution.py:237
  137.5 27.1 %collective-permute-start.27 = (bf16[768,3072]{1,0:T(8,128)(2,1)}, bf16[768,3072]{1,0:T(8,128)(2,1)}, u32[]{:S(2)}, u32[]{:S(2)}) collective-permute-start(bf16[768,3072]{1,0:T(8,128)(2,1)} %collective-permute-done.17.refs_6_), channel_id=1, source_target_pairs={{16,24},{48,56},{80,88},{112,120},{17,25},{49,57},{81,89},{113,121... | collective-permute-start | bytes 14155784 | tf_op jit(solution)/shard_map/ppermute | solution.py:237
  140.1 20.7 %collective-permute-start.21 = (f16[4,96,768]{2,1,0:T(8,128)(2,1)}, f16[4,96,768]{2,1,0:T(8,128)(2,1)S(1)}, u32[]{:S(2)}, u32[]{:S(2)}) collective-permute-start(f16[4,96,768]{2,1,0:T(8,128)(2,1)} %pad_maximum_fusion), channel_id=1, source_target_pairs={{0,1},{1,2},{2,3},{3,0},{4,5},{5,6},{6,7},{7,4},{8,9},{9,10},{10,1... | collective-permute-start | bytes 1769480 | tf_op jit(solution)/shard_map/ppermute | solution.py:241
  142.4 18.5 %collective-permute-start.22 = (f16[4,96,768]{2,1,0:T(8,128)(2,1)}, f16[4,96,768]{2,1,0:T(8,128)(2,1)S(1)}, u32[]{:S(2)}, u32[]{:S(2)}) collective-permute-start(f16[4,96,768]{2,1,0:T(8,128)(2,1)} %pad_maximum_fusion.1), channel_id=1, source_target_pairs={{0,3},{1,0},{2,1},{3,2},{4,7},{5,4},{6,5},{7,6},{8,11},{9,8},{10,9... | collective-permute-start | bytes 1769480 | tf_op jit(solution)/shard_map/ppermute | solution.py:241
  158.2 18.0 %collective-permute-start.24 = (f16[2,2,96,768]{3,2,1,0:T(8,128)(2,1)}, f16[2,2,96,768]{3,2,1,0:T(8,128)(2,1)}, u32[]{:S(2)}, u32[]{:S(2)}) collective-permute-start(f16[2,2,96,768]{3,2,1,0:T(8,128)(2,1)} %get-tuple-element.134), channel_id=1, source_target_pairs={{0,1},{1,2},{2,3},{3,0},{4,5},{5,6},{6,7},{7,4},{8,9},{9,10},{10,1... | collective-permute-start | bytes 1769480 | tf_op jit(solution)/shard_map/ppermute | solution.py:241
  158.6 17.6 %collective-permute-start.25 = (f16[2,2,96,768]{3,2,1,0:T(8,128)(2,1)}, f16[2,2,96,768]{3,2,1,0:T(8,128)(2,1)}, u32[]{:S(2)}, u32[]{:S(2)}) collective-permute-start(f16[2,2,96,768]{3,2,1,0:T(8,128)(2,1)} %get-tuple-element.133), channel_id=1, source_target_pairs={{0,3},{1,0},{2,1},{3,2},{4,7},{5,4},{6,5},{7,6},{8,11},{9,8},{10,9... | collective-permute-start | bytes 1769480 | tf_op jit(solution)/shard_map/ppermute | solution.py:241
  163.1 13.1 %collective-permute-start.26 = (f16[4,96,768]{2,1,0:T(8,128)(2,1)}, f16[4,96,768]{2,1,0:T(8,128)(2,1)}, u32[]{:S(2)}, u32[]{:S(2)}) collective-permute-start(f16[4,96,768]{2,1,0:T(8,128)(2,1)} %fusion.10), channel_id=1, source_target_pairs={{0,32},{32,64},{64,96},{96,0},{1,33},{33,65},{65,97},{97,1},{2,34}... | collective-permute-start | bytes 1769480 | tf_op jit(solution)/shard_map/ppermute | solution.py:237
  177.8 6.9 %collective-permute-start.28 = (f16[2,96,768]{2,1,0:T(8,128)(2,1)S(1)}, f16[2,96,768]{2,1,0:T(8,128)(2,1)S(1)}, u32[]{:S(2)}, u32[]{:S(2)}) collective-permute-start(f16[2,96,768]{2,1,0:T(8,128)(2,1)S(1)} %get-tuple-element.128), channel_id=1, source_target_pairs={{0,1},{1,2},{2,3},{3,0},{4,5},{5,6},{6,7},{7,4},{8,9},{9,10},{10,1... | collective-permute-start | bytes 884744 | tf_op jit(solution)/shard_map/ppermute | solution.py:241
  180.9 10.1 %collective-permute-start.30 = (f16[2,2,96,768]{3,2,1,0:T(8,128)(2,1)S(1)}, f16[2,2,96,768]{3,2,1,0:T(8,128)(2,1)S(1)}, u32[]{:S(2)}, u32[]{:S(2)}) collective-permute-start(f16[2,2,96,768]{3,2,1,0:T(8,128)(2,1)S(1)} %get-tuple-element.97), channel_id=1, source_target_pairs={{0,1},{1,2},{2,3},{3,0},{4,5},{5,6},{6,7},{7,4},{8,9},{9,10},{10,1... | collective-permute-start | bytes 1769480 | tf_op jit(solution)/shard_map/ppermute | solution.py:241
  181.0 10.0 %collective-permute-start.31 = (f16[2,2,96,768]{3,2,1,0:T(8,128)(2,1)S(1)}, f16[2,2,96,768]{3,2,1,0:T(8,128)(2,1)S(1)}, u32[]{:S(2)}, u32[]{:S(2)}) collective-permute-start(f16[2,2,96,768]{3,2,1,0:T(8,128)(2,1)S(1)} %get-tuple-element.98), channel_id=1, source_target_pairs={{0,3},{1,0},{2,1},{3,2},{4,7},{5,4},{6,5},{7,6},{8,11},{9,8},{10,9... | collective-permute-start | bytes 1769480 | tf_op jit(solution)/shard_map/ppermute | solution.py:241
  191.3 10.3 %collective-permute-start.33 = (f16[2,96,768]{2,1,0:T(8,128)(2,1)S(1)}, f16[2,96,768]{2,1,0:T(8,128)(2,1)S(1)}, u32[]{:S(2)}, u32[]{:S(2)}) collective-permute-start(f16[2,96,768]{2,1,0:T(8,128)(2,1)S(1)} %get-tuple-element.122), channel_id=1, source_target_pairs={{0,1},{1,2},{2,3},{3,0},{4,5},{5,6},{6,7},{7,4},{8,9},{9,10},{10,1... | collective-permute-start | bytes 884744 | tf_op jit(solution)/shard_map/ppermute | solution.py:241
  191.3 10.2 %collective-permute-start.34 = (f16[2,96,768]{2,1,0:T(8,128)(2,1)S(1)}, f16[2,96,768]{2,1,0:T(8,128)(2,1)S(1)}, u32[]{:S(2)}, u32[]{:S(2)}) collective-permute-start(f16[2,96,768]{2,1,0:T(8,128)(2,1)S(1)} %get-tuple-element.121), channel_id=1, source_target_pairs={{0,3},{1,0},{2,1},{3,2},{4,7},{5,4},{6,5},{7,6},{8,11},{9,8},{10,9... | collective-permute-start | bytes 884744 | tf_op jit(solution)/shard_map/ppermute | solution.py:241
  204.2 21.6 %collective-permute-start.35 = (f16[2,2,96,768]{3,2,1,0:T(8,128)(2,1)S(1)}, f16[2,2,96,768]{3,2,1,0:T(8,128)(2,1)S(1)}, u32[]{:S(2)}, u32[]{:S(2)}) collective-permute-start(f16[2,2,96,768]{3,2,1,0:T(8,128)(2,1)S(1)} %bitcast.142), channel_id=1, source_target_pairs={{0,16},{1,17},{2,18},{3,19},{8,24},{9,25},{10,26},{11,27},{16,4},{... | collective-permute-start | bytes 1769480 | tf_op jit(solution)/shard_map/ppermute | solution.py:255
  218.0 9.5 %collective-permute-start.36 = (f16[2,2,96,768]{3,2,1,0:T(8,128)(2,1)S(1)}, f16[2,2,96,768]{3,2,1,0:T(8,128)(2,1)S(1)}, u32[]{:S(2)}, u32[]{:S(2)}) collective-permute-start(f16[2,2,96,768]{3,2,1,0:T(8,128)(2,1)S(1)} %bitcast.141), channel_id=1, source_target_pairs={{0,20},{1,21},{2,22},{3,23},{8,28},{9,29},{10,30},{11,31},{16,0},{... | collective-permute-start | bytes 1769480 | tf_op jit(solution)/shard_map/ppermute | solution.py:255
  227.8 6.8 %collective-permute-start.37 = (f16[2,96,768]{2,1,0:T(8,128)(2,1)S(1)}, f16[2,96,768]{2,1,0:T(8,128)(2,1)S(1)}, u32[]{:S(2)}, u32[]{:S(2)}) collective-permute-start(f16[2,96,768]{2,1,0:T(8,128)(2,1)S(1)} %get-tuple-element.118), channel_id=1, source_target_pairs={{0,16},{1,17},{2,18},{3,19},{8,24},{9,25},{10,26},{11,27},{16,4},{... | collective-permute-start | bytes 884744 | tf_op jit(solution)/shard_map/ppermute | solution.py:255
  228.1 8.1 %collective-permute-start.38 = (f16[2,96,768]{2,1,0:T(8,128)(2,1)S(1)}, f16[2,96,768]{2,1,0:T(8,128)(2,1)S(1)}, u32[]{:S(2)}, u32[]{:S(2)}) collective-permute-start(f16[2,96,768]{2,1,0:T(8,128)(2,1)S(1)} %get-tuple-element.117), channel_id=1, source_target_pairs={{0,20},{1,21},{2,22},{3,23},{8,28},{9,29},{10,30},{11,31},{16,0},{... | collective-permute-start | bytes 884744 | tf_op jit(solution)/shard_map/ppermute | solution.py:255
  238.1 10.3 %collective-permute-start.39 = (f16[96,768]{1,0:T(8,128)(2,1)S(1)}, f16[96,768]{1,0:T(8,128)(2,1)S(1)}, u32[]{:S(2)}, u32[]{:S(2)}) collective-permute-start(f16[96,768]{1,0:T(8,128)(2,1)S(1)} %multiply_convert_fusion), channel_id=1, source_target_pairs={{16,24},{24,16},{48,56},{56,48},{80,88},{88,80},{112,120},{120,112... | collective-permute-start | bytes 442376 | tf_op jit(solution)/shard_map/ppermute | solution.py:237
  273.9 8.5 %collective-permute-start.42 = (f16[768,96]{0,1:T(8,128)(2,1)S(1)}, f16[768,96]{0,1:T(8,128)(2,1)S(1)}, u32[]{:S(2)}, u32[]{:S(2)}) collective-permute-start(f16[768,96]{0,1:T(8,128)(2,1)S(1)} %squeeze.42), channel_id=1, source_target_pairs={{0,104},{8,112},{16,120},{24,0},{32,8},{40,16},{48,24},{56,32},{64... | collective-permute-start | bytes 442376 | tf_op jit(solution)/shard_map/ppermute | solution.py:237
  (30 other events, 251.7 us)

commit v8 on v6

--- a/solution.py
+++ b/solution.py
@@ -280,7 +280,7 @@
         names += [(tile, h) for h in range(2) for tile in batch[role]]
     early, late = MOVED[role][:2], MOVED[role][2:]
     names += [(tile, h) for h in range(2) for tile in early]
-    names += [(tile, h) for h in range(2) for tile in late]
+    names += [(tile, h) for tile in late for h in range(2)]
     return names
 
 
@@ -424,14 +424,14 @@
     got3 = first_round(sends3)
     more2 = after(more2, sends3)
     total2 = finish(partial2, got2, more2, scales)
-    moved2 = narrow(jnp.concatenate(total2), scales)
+    moved2 = [narrow(jnp.stack([total2[0][i], total2[1][i]]), scales) for i in range(2)]
     more0, more1 = after([more0, more1], moved2)
     total0 = finish(partial0, got0, more0, scales)
     total1 = finish(partial1, got1, more1, scales)
-    moved2 = aux_permute(moved2, [(0, 0, 1), (1, 1, 1), (2, 2, 1)])
+    moved2 = [aux_permute(moved2[0], [(0, 0, 1), (1, 1, 1), (2, 2, 1)]), aux_permute(moved2[1], [(1, 1, 1)])]
     got3, moved2 = lax.optimization_barrier((got3, moved2))
     more3 = both_ways(y_permute, *second_sends(partial3, got3, scales))
-    moved0, moved2 = wide(moved0, scales), wide(moved2, scales)
+    moved0, moved2 = wide(moved0, scales), wide(jnp.concatenate(moved2), scales)
     total3 = finish(partial3, got3, more3, scales)
     slots = jnp.concatenate(total0 + total1 + total2 + total3 + [moved0, moved2])
     terms = pick_parts(entries, slots).reshape(8, 2, PART, ROWS)

time: 283 us -> 281 us (level)
    ppermute x21 -> x22, starting transfers between devices: 56.9 us -> 54.6 us  [aux_permute(): return lax.ppermute(value, 'aux', moves(pairs))]
    ppermute x21 -> x22, waiting for transfers between devices: 47.2 us -> 46.5 us  [aux_permute(): return lax.ppermute(value, 'aux', moves(pairs))]
  transfers between devices with their start and end apart: 43 -> 44, of which waited for: 15 -> 15; matrix products, arithmetic and copies ran while one was open for 6% -> 6% of each run, Pallas kernels for 20% -> 20%
where the time goes in v8:
time: 281 us; the launch traced here: 280 us
  starting transfers between devices  87.5 us (31%)
  waiting for transfers between devices  79.8 us (28%)
  Pallas kernels  61.8 us (22%)
  blocking collectives  18.3 us (7%)
  other arithmetic  16.1 us (6%)
  local copies, waits for them, and re-layouts  14.8 us (5%)
    ppermute x22, starting transfers between devices, aux_permute(): return lax.ppermute(value, 'aux', moves(pairs))  54.6 us
    pallas_call x4, Pallas kernels, tile_batch(): pl.pallas_call(functools.partial(tiles_kernel, count, held_most, len(sour...  51.2 us
    ppermute x22, waiting for transfers between devices, aux_permute(): return lax.ppermute(value, 'aux', moves(pairs))  46.5 us
    ppermute x17, starting transfers between devices, y_permute(): lax.ppermute(value, 'pair', [(h * 4 + y, h * 4 + (y + by) % 4) for h in r...  25.5 us
    all_to_all x1, blocking collectives, local(): lax.all_to_all(crossed, 'pair', split_axis=2, concat_axis=1, tiled=True)  18.3 us
    ppermute x5, waiting for transfers between devices, x_permute(): return lax.ppermute(value, ('aux', 'pair'), perm)  17.5 us
    ppermute x17, waiting for transfers between devices, y_permute(): lax.ppermute(value, 'pair', [(h * 4 + y, h * 4 + (y + by) % 4) for h in r...  15.8 us
    ppermute x5, starting transfers between devices, x_permute(): return lax.ppermute(value, ('aux', 'pair'), perm)  7.45 us
  transfers between devices with their start and end apart: 44, of which 15 were waited for; matrix products, arithmetic and copies ran while one was open for 6% of the time, Pallas kernels for 20%

profile of v8, /device:TPU:3, one launch (start us, length us, event | category | flops | bytes accessed | tf_op | source)
XLA Modules:
  0.0 280.2 jit_solution(10325589216596658751)
XLA Ops:
  0.0 3.7 %copy-done.1 = bf16[768,6144]{1,0:T(8,128)(2,1)S(1)} copy-done((bf16[768,6144]{1,0:T(8,128)(2,1)S(1)}, bf16[768,6144]{1,0:T(8,128)(2,1)}, u32[]{:S(2)}) %copy-start.1) | copy-done | bytes 9437208
  3.7 4.9 %shard_map.109 = (bf16[768,3072]{1,0:T(8,128)(2,1)}, bf16[768,3072]{1,0:T(8,128)(2,1)}, f32[8,128]{1,0:T(8,128)S(1)}) custom-call(s32[1]{0:T(128)} %bitcast.x_lo, bf16[768,6144]{1,0:T(8,128)(2,1)S(1)} %copy-done.1), custom_call_target="tpu_custom_call" | custom-call | bytes 73728 | tf_op jit(solution)/shard_map/pallas_call | solution.py:218
  8.6 3.5 %collective-permute-start = (bf16[768,3072]{1,0:T(8,128)(2,1)}, bf16[768,3072]{1,0:T(8,128)(2,1)}, u32[]{:S(2)}, u32[]{:S(2)}) collective-permute-start(bf16[768,3072]{1,0:T(8,128)(2,1)} %get-tuple-element.79.refs_0_), channel_id=1, source_target_pairs={{0,96},{24,56},{32,0},{56,88},{64,32},{88,120},{96,64},{120,24},{1... | collective-permute-start | bytes 14155784 | tf_op jit(solution)/shard_map/ppermute | solution.py:237
  12.2 3.5 %collective-permute-start.1 = (bf16[768,3072]{1,0:T(8,128)(2,1)}, bf16[768,3072]{1,0:T(8,128)(2,1)}, u32[]{:S(2)}, u32[]{:S(2)}) collective-permute-start(bf16[768,3072]{1,0:T(8,128)(2,1)} %get-tuple-element.78), channel_id=1, source_target_pairs={{0,16},{24,8},{32,48},{56,40},{64,80},{88,72},{96,112},{120,104},{... | collective-permute-start | bytes 14155784 | tf_op jit(solution)/shard_map/ppermute | solution.py:237
  17.4 4.8 %shard_map.110 = f32[1,3072]{1,0:T(1,128)} custom-call(s32[1,3072]{1,0:T(1,128)} %bitcast.143, s32[1,3072]{1,0:T(1,128)} %bitcast.144, f32[32,128]{1,0:T(8,128)} %bitcast.146, f32[256,128]{1,0:T(8,128)} %bitcast.145), custom_call_target="tpu_custom_call" | custom-call | flops 679477248 | bytes 200000 | tf_op jit(solution)/shard_map/pallas_call | solution.py:186
  23.0 3.1 %collective-permute-start.5 = (f32[8,128]{1,0:T(8,128)S(1)}, f32[8,128]{1,0:T(8,128)S(1)}, u32[]{:S(2)}, u32[]{:S(2)}) collective-permute-start(f32[8,128]{1,0:T(8,128)S(1)} %max.30), channel_id=1, source_target_pairs={{0,2},{1,3},{2,0},{3,1},{4,6},{5,7},{6,4},{7,5},{8,10},{9,11},{10,... | collective-permute-start | bytes 12296 | tf_op jit(solution)/shard_map/ppermute | solution.py:241
  37.4 24.3 %collective-permute-done.11 = f32[8,128]{1,0:T(8,128)S(1)} collective-permute-done((f32[8,128]{1,0:T(8,128)S(1)}, f32[8,128]{1,0:T(8,128)S(1)}, u32[]{:S(2)}, u32[]{:S(2)}) %collective-permute-start.11) | collective-permute-done | bytes 4128 | tf_op jit(solution)/shard_map/ppermute | solution.py:237
  63.7 2.5 collective-permute-done.refs_3_.refs_4_.refs_5_
  67.5 7.8 %collective-permute-start.15 = (bf16[768,3072]{1,0:T(8,128)(2,1)}, bf16[768,3072]{1,0:T(8,128)(2,1)}, u32[]{:S(2)}, u32[]{:S(2)}) collective-permute-start(bf16[768,3072]{1,0:T(8,128)(2,1)} %collective-permute-done.refs_3_.refs_4_.refs_5_), channel_id=1, source_target_pairs={{24,16},{56,48},{88,80},{120,112},{25,17},{57,49},{89,81},{121,113... | collective-permute-start | bytes 14155784 | tf_op jit(solution)/shard_map/ppermute | solution.py:237
  76.6 2.8 collective-permute-start.17
  79.4 2.8 collective-permute-start.18
  82.2 12.6 %shard_map.111 = f32[8,2,96,768]{3,2,1,0:T(8,128)S(1)} custom-call(s32[20]{0:T(128)S(1)} %get-tuple-element.67.table, f32[1,3072]{1,0:T(1,128)S(1)} %add_divide_fusion.weight, bf16[768,3072]{1,0:T(8,128)(2,1)} %get-tuple-element.79.refs_0_, bf16[768,3072]{1,0:T(8,128)(2,1)} %collective-permute-done.2.refs_1_.refs_0_, ...), custom_call_target="tpu_custom_call" | custom-call | flops 1179648 | bytes 1179648 | tf_op jit(solution)/shard_map/pallas_call | solution.py:135
  97.2 2.7 collective-permute-start.13
  100.0 13.4 %shard_map.112 = f32[8,2,96,768]{3,2,1,0:T(8,128)S(1)} custom-call(s32[20]{0:T(128)S(1)} %get-tuple-element.73.table, f32[1,3072]{1,0:T(1,128)S(1)} %add_divide_fusion.weight, bf16[768,3072]{1,0:T(8,128)(2,1)} %get-tuple-element.79.refs_0_, bf16[768,3072]{1,0:T(8,128)(2,1)} %collective-permute-done.2.refs_1_.refs_0_, ...), custom_call_target="tpu_custom_call" | custom-call | flops 1179648 | bytes 1179648 | tf_op jit(solution)/shard_map/pallas_call | solution.py:135
  113.7 2.7 collective-permute-start.20
  116.6 14.1 %collective-permute-done.16.refs_3_ = bf16[768,3072]{1,0:T(8,128)(2,1)S(1)} collective-permute-done((bf16[768,3072]{1,0:T(8,128)(2,1)}, bf16[768,3072]{1,0:T(8,128)(2,1)S(1)}, u32[]{:S(2)}, u32[]{:S(2)}) %collective-permute-start.16) | collective-permute-done | bytes 4718624 | tf_op jit(solution)/shard_map/ppermute | solution.py:237
  130.8 7.9 %collective-permute-start.23 = (bf16[768,3072]{1,0:T(8,128)(2,1)S(1)}, bf16[768,3072]{1,0:T(8,128)(2,1)}, u32[]{:S(2)}, u32[]{:S(2)}) collective-permute-start(bf16[768,3072]{1,0:T(8,128)(2,1)S(1)} %collective-permute-done.16.refs_3_), channel_id=1, source_target_pairs={{0,8},{24,16},{32,40},{56,48},{64,72},{88,80},{96,104},{120,112},{... | collective-permute-start | bytes 14155784 | tf_op jit(solution)/shard_map/ppermute | solution.py:237
  144.4 12.6 %shard_map.113 = f32[8,2,96,768]{3,2,1,0:T(8,128)S(1)} custom-call(s32[22]{0:T(128)S(1)} %pad_add_fusion.2.table, f32[1,3072]{1,0:T(1,128)S(1)} %add_divide_fusion.weight, bf16[768,3072]{1,0:T(8,128)(2,1)} %collective-permute-done.2.refs_1_.refs_0_, bf16[768,3072]{1,0:T(8,128)(2,1)} %collective-permute-done.1.refs_2_.refs_1_, bf16[768,3072]{1,0:T(8,128)(2,1)} %copy-done.3, ...), custom_call_target="tpu_custom_call" | custom-call | flops 1179648 | bytes 1179648 | tf_op jit(solution)/shard_map/pallas_call | solution.py:135
  163.7 12.5 %shard_map.114 = f32[8,2,96,768]{3,2,1,0:T(8,128)S(1)} custom-call(s32[20]{0:T(128)S(1)} %get-tuple-element.95.table, f32[1,3072]{1,0:T(1,128)S(1)} %add_divide_fusion.weight, bf16[768,3072]{1,0:T(8,128)(2,1)} %get-tuple-element.79.refs_0_, bf16[768,3072]{1,0:T(8,128)(2,1)} %collective-permute-done.2.refs_1_.refs_0_, ...), custom_call_target="tpu_custom_call" | custom-call | flops 1179648 | bytes 1179648 | tf_op jit(solution)/shard_map/pallas_call | solution.py:135
  178.8 2.7 collective-permute-start.29
  181.9 2.7 collective-permute-start.31
  189.0 6.1 %collective-permute-done.30 = f16[2,2,96,768]{3,2,1,0:T(8,128)(2,1)S(1)} collective-permute-done((f16[2,2,96,768]{3,2,1,0:T(8,128)(2,1)S(1)}, f16[2,2,96,768]{3,2,1,0:T(8,128)(2,1)S(1)}, u32[]{:S(2)}, u32[]{:S(2)}) %collective-permute-start.30) | collective-permute-done | bytes 589856 | tf_op jit(solution)/shard_map/ppermute | solution.py:241
  196.0 2.1 collective-permute-start.35
  198.3 6.5 %collective-permute-done.34 = f16[2,96,768]{2,1,0:T(8,128)(2,1)S(1)} collective-permute-done((f16[2,96,768]{2,1,0:T(8,128)(2,1)S(1)}, f16[2,96,768]{2,1,0:T(8,128)(2,1)S(1)}, u32[]{:S(2)}, u32[]{:S(2)}) %collective-permute-start.34) | collective-permute-done | bytes 294944 | tf_op jit(solution)/shard_map/ppermute | solution.py:241
  207.5 5.3 %collective-permute-start.36 = (f16[2,2,96,768]{3,2,1,0:T(8,128)(2,1)S(1)}, f16[2,2,96,768]{3,2,1,0:T(8,128)(2,1)S(1)}, u32[]{:S(2)}, u32[]{:S(2)}) collective-permute-start(f16[2,2,96,768]{3,2,1,0:T(8,128)(2,1)S(1)} %bitcast.142), channel_id=1, source_target_pairs={{0,16},{1,17},{2,18},{3,19},{8,24},{9,25},{10,26},{11,27},{16,4},{... | collective-permute-start | bytes 1769480 | tf_op jit(solution)/shard_map/ppermute | solution.py:255
  212.7 6.8 %collective-permute-done.36 = f16[2,2,96,768]{3,2,1,0:T(8,128)(2,1)S(1)} collective-permute-done((f16[2,2,96,768]{3,2,1,0:T(8,128)(2,1)S(1)}, f16[2,2,96,768]{3,2,1,0:T(8,128)(2,1)S(1)}, u32[]{:S(2)}, u32[]{:S(2)}) %collective-permute-start.36) | collective-permute-done | bytes 589856 | tf_op jit(solution)/shard_map/ppermute | solution.py:255
  219.6 2.2 collective-permute-done.37
  223.5 7.6 %collective-permute-done.38 = f16[2,96,768]{2,1,0:T(8,128)(2,1)S(1)} collective-permute-done((f16[2,96,768]{2,1,0:T(8,128)(2,1)S(1)}, f16[2,96,768]{2,1,0:T(8,128)(2,1)S(1)}, u32[]{:S(2)}, u32[]{:S(2)}) %collective-permute-start.38) | collective-permute-done | bytes 294944 | tf_op jit(solution)/shard_map/ppermute | solution.py:255
  233.9 11.6 %collective-permute-start.40 = (f16[96,768]{1,0:T(8,128)(2,1)S(1)}, f16[96,768]{1,0:T(8,128)(2,1)S(1)}, u32[]{:S(2)}, u32[]{:S(2)}) collective-permute-start(f16[96,768]{1,0:T(8,128)(2,1)S(1)} %multiply_convert_fusion), channel_id=1, source_target_pairs={{16,24},{24,16},{48,56},{56,48},{80,88},{88,80},{112,120},{120,112... | collective-permute-start | bytes 442376 | tf_op jit(solution)/shard_map/ppermute | solution.py:237
  248.4 18.3 %all_to_all.15 = f16[3,96,8,96]{1,3,0,2:T(8,128)(2,1)S(1)} all-to-all(f16[3,96,8,96]{1,3,0,2:T(8,128)(2,1)S(1)} %fusion.11), channel_id=1, replica_groups=mesh['aux'=16,'pair'=8] {'pair'}, dimensions={2} | all-to-all | bytes 884736 | tf_op jit(solution)/shard_map/all_to_all | solution.py:443
  273.3 2.9 %collective-permute-done.42 = f16[768,96]{0,1:T(8,128)(2,1)S(1)} collective-permute-done((f16[768,96]{0,1:T(8,128)(2,1)S(1)}, f16[768,96]{0,1:T(8,128)(2,1)S(1)}, u32[]{:S(2)}, u32[]{:S(2)}) %collective-permute-start.42) | collective-permute-done | bytes 147488 | tf_op jit(solution)/shard_map/ppermute | solution.py:237
  277.0 2.5 collective-permute-done.43
  (162 shorter events, 58.6 us)
Async XLA Ops:
  8.6 57.6 %collective-permute-start = (bf16[768,3072]{1,0:T(8,128)(2,1)}, bf16[768,3072]{1,0:T(8,128)(2,1)}, u32[]{:S(2)}, u32[]{:S(2)}) collective-permute-start(bf16[768,3072]{1,0:T(8,128)(2,1)} %get-tuple-element.79.refs_0_), channel_id=1, source_target_pairs={{0,96},{24,56},{32,0},{56,88},{64,32},{88,120},{96,64},{120,24},{1... | collective-permute-start | bytes 14155784 | tf_op jit(solution)/shard_map/ppermute | solution.py:237
  12.2 54.0 %collective-permute-start.1 = (bf16[768,3072]{1,0:T(8,128)(2,1)}, bf16[768,3072]{1,0:T(8,128)(2,1)}, u32[]{:S(2)}, u32[]{:S(2)}) collective-permute-start(bf16[768,3072]{1,0:T(8,128)(2,1)} %get-tuple-element.78), channel_id=1, source_target_pairs={{0,16},{24,8},{32,48},{56,40},{64,80},{88,72},{96,112},{120,104},{... | collective-permute-start | bytes 14155784 | tf_op jit(solution)/shard_map/ppermute | solution.py:237
  15.7 50.5 %collective-permute-start.2 = (bf16[768,3072]{1,0:T(8,128)(2,1)}, bf16[768,3072]{1,0:T(8,128)(2,1)}, u32[]{:S(2)}, u32[]{:S(2)}) collective-permute-start(bf16[768,3072]{1,0:T(8,128)(2,1)} %get-tuple-element.79.refs_0_), channel_id=1, source_target_pairs={{0,8},{8,0},{16,24},{24,16},{32,40},{40,32},{48,56},{56,48},{64,72... | collective-permute-start | bytes 14155784 | tf_op jit(solution)/shard_map/ppermute | solution.py:237
  15.7 7.3 %collective-permute-start.3 = (f32[8,128]{1,0:T(8,128)S(1)}, f32[8,128]{1,0:T(8,128)S(1)}, u32[]{:S(2)}, u32[]{:S(2)}) collective-permute-start(f32[8,128]{1,0:T(8,128)S(1)} %get-tuple-element.63), channel_id=1, source_target_pairs={{0,8},{8,0},{16,24},{24,16},{32,40},{40,32},{48,56},{56,48},{64,72... | collective-permute-start | bytes 12296 | tf_op jit(solution)/shard_map/ppermute | solution.py:237
  35.4 26.3 %collective-permute-start.11 = (f32[8,128]{1,0:T(8,128)S(1)}, f32[8,128]{1,0:T(8,128)S(1)}, u32[]{:S(2)}, u32[]{:S(2)}) collective-permute-start(f32[8,128]{1,0:T(8,128)S(1)} %max.37), channel_id=1, source_target_pairs={{8,0},{16,24},{40,32},{48,56},{72,64},{80,88},{104,96},{112,120},{... | collective-permute-start | bytes 12296 | tf_op jit(solution)/shard_map/ppermute | solution.py:237
  66.2 28.8 %collective-permute-start.14 = (bf16[768,3072]{1,0:T(8,128)(2,1)}, bf16[768,3072]{1,0:T(8,128)(2,1)S(1)}, u32[]{:S(2)}, u32[]{:S(2)}) collective-permute-start(bf16[768,3072]{1,0:T(8,128)(2,1)} %collective-permute-done.1.refs_2_.refs_1_), channel_id=1, source_target_pairs={{8,0},{16,24},{40,32},{48,56},{72,64},{80,88},{104,96},{112,120},{... | collective-permute-start | bytes 14155784 | tf_op jit(solution)/shard_map/ppermute | solution.py:237
  67.5 28.9 %collective-permute-start.15 = (bf16[768,3072]{1,0:T(8,128)(2,1)}, bf16[768,3072]{1,0:T(8,128)(2,1)}, u32[]{:S(2)}, u32[]{:S(2)}) collective-permute-start(bf16[768,3072]{1,0:T(8,128)(2,1)} %collective-permute-done.refs_3_.refs_4_.refs_5_), channel_id=1, source_target_pairs={{24,16},{56,48},{88,80},{120,112},{25,17},{57,49},{89,81},{121,113... | collective-permute-start | bytes 14155784 | tf_op jit(solution)/shard_map/ppermute | solution.py:237
  75.3 55.5 %collective-permute-start.16 = (bf16[768,3072]{1,0:T(8,128)(2,1)}, bf16[768,3072]{1,0:T(8,128)(2,1)S(1)}, u32[]{:S(2)}, u32[]{:S(2)}) collective-permute-start(bf16[768,3072]{1,0:T(8,128)(2,1)} %get-tuple-element.78), channel_id=1, source_target_pairs={{8,24},{16,0},{40,56},{48,32},{72,88},{80,64},{104,120},{112,96},{... | collective-permute-start | bytes 14155784 | tf_op jit(solution)/shard_map/ppermute | solution.py:237
  76.6 54.2 %collective-permute-start.17 = (bf16[768,3072]{1,0:T(8,128)(2,1)}, bf16[768,3072]{1,0:T(8,128)(2,1)}, u32[]{:S(2)}, u32[]{:S(2)}) collective-permute-start(bf16[768,3072]{1,0:T(8,128)(2,1)} %get-tuple-element.79.refs_0_), channel_id=1, source_target_pairs={{8,104},{16,48},{40,8},{48,80},{72,40},{80,112},{104,72},{112,16},... | collective-permute-start | bytes 14155784 | tf_op jit(solution)/shard_map/ppermute | solution.py:237
  79.4 51.4 %collective-permute-start.18 = (bf16[768,3072]{1,0:T(8,128)(2,1)}, bf16[768,3072]{1,0:T(8,128)(2,1)}, u32[]{:S(2)}, u32[]{:S(2)}) collective-permute-start(bf16[768,3072]{1,0:T(8,128)(2,1)} %collective-permute-done.1.refs_2_.refs_1_), channel_id=1, source_target_pairs={{8,32},{16,112},{40,64},{48,16},{72,96},{80,48},{104,0},{112,80},{... | collective-permute-start | bytes 14155784 | tf_op jit(solution)/shard_map/ppermute | solution.py:237
  95.0 18.6 %collective-permute-start.12 = (f16[2,2,96,768]{3,2,1,0:T(8,128)(2,1)S(1)}, f16[2,2,96,768]{3,2,1,0:T(8,128)(2,1)S(1)}, u32[]{:S(2)}, u32[]{:S(2)}) collective-permute-start(f16[2,2,96,768]{3,2,1,0:T(8,128)(2,1)S(1)} %get-tuple-element.144), channel_id=1, source_target_pairs={{0,1},{1,2},{2,3},{3,0},{4,5},{5,6},{6,7},{7,4},{8,9},{9,10},{10,1... | collective-permute-start | bytes 1769480 | tf_op jit(solution)/shard_map/ppermute | solution.py:241
  97.2 16.4 %collective-permute-start.13 = (f16[2,2,96,768]{3,2,1,0:T(8,128)(2,1)S(1)}, f16[2,2,96,768]{3,2,1,0:T(8,128)(2,1)S(1)}, u32[]{:S(2)}, u32[]{:S(2)}) collective-permute-start(f16[2,2,96,768]{3,2,1,0:T(8,128)(2,1)S(1)} %get-tuple-element.143), channel_id=1, source_target_pairs={{0,3},{1,0},{2,1},{3,2},{4,7},{5,4},{6,5},{7,6},{8,11},{9,8},{10,9... | collective-permute-start | bytes 1769480 | tf_op jit(solution)/shard_map/ppermute | solution.py:241
  113.7 17.2 %collective-permute-start.19 = (f16[2,2,96,768]{3,2,1,0:T(8,128)(2,1)S(1)}, f16[2,2,96,768]{3,2,1,0:T(8,128)(2,1)S(1)}, u32[]{:S(2)}, u32[]{:S(2)}) collective-permute-start(f16[2,2,96,768]{3,2,1,0:T(8,128)(2,1)S(1)} %get-tuple-element.80), channel_id=1, source_target_pairs={{0,1},{1,2},{2,3},{3,0},{4,5},{5,6},{6,7},{7,4},{8,9},{9,10},{10,1... | collective-permute-start | bytes 1769480 | tf_op jit(solution)/shard_map/ppermute | solution.py:241
  113.7 17.1 %collective-permute-start.20 = (f16[2,2,96,768]{3,2,1,0:T(8,128)(2,1)S(1)}, f16[2,2,96,768]{3,2,1,0:T(8,128)(2,1)S(1)}, u32[]{:S(2)}, u32[]{:S(2)}) collective-permute-start(f16[2,2,96,768]{3,2,1,0:T(8,128)(2,1)S(1)} %get-tuple-element.81), channel_id=1, source_target_pairs={{0,3},{1,0},{2,1},{3,2},{4,7},{5,4},{6,5},{7,6},{8,11},{9,8},{10,9... | collective-permute-start | bytes 1769480 | tf_op jit(solution)/shard_map/ppermute | solution.py:241
  130.8 13.6 %collective-permute-start.23 = (bf16[768,3072]{1,0:T(8,128)(2,1)S(1)}, bf16[768,3072]{1,0:T(8,128)(2,1)}, u32[]{:S(2)}, u32[]{:S(2)}) collective-permute-start(bf16[768,3072]{1,0:T(8,128)(2,1)S(1)} %collective-permute-done.16.refs_3_), channel_id=1, source_target_pairs={{0,8},{24,16},{32,40},{56,48},{64,72},{88,80},{96,104},{120,112},{... | collective-permute-start | bytes 14155784 | tf_op jit(solution)/shard_map/ppermute | solution.py:237
  138.7 25.0 %collective-permute-start.27 = (bf16[768,3072]{1,0:T(8,128)(2,1)}, bf16[768,3072]{1,0:T(8,128)(2,1)}, u32[]{:S(2)}, u32[]{:S(2)}) collective-permute-start(bf16[768,3072]{1,0:T(8,128)(2,1)} %collective-permute-done.17.refs_6_), channel_id=1, source_target_pairs={{16,24},{48,56},{80,88},{112,120},{17,25},{49,57},{81,89},{113,121... | collective-permute-start | bytes 14155784 | tf_op jit(solution)/shard_map/ppermute | solution.py:237
  140.4 20.5 %collective-permute-start.21 = (f16[4,96,768]{2,1,0:T(8,128)(2,1)S(1)}, f16[4,96,768]{2,1,0:T(8,128)(2,1)S(1)}, u32[]{:S(2)}, u32[]{:S(2)}) collective-permute-start(f16[4,96,768]{2,1,0:T(8,128)(2,1)S(1)} %pad_maximum_fusion), channel_id=1, source_target_pairs={{0,1},{1,2},{2,3},{3,0},{4,5},{5,6},{6,7},{7,4},{8,9},{9,10},{10,1... | collective-permute-start | bytes 1769480 | tf_op jit(solution)/shard_map/ppermute | solution.py:241
  142.9 18.0 %collective-permute-start.22 = (f16[4,96,768]{2,1,0:T(8,128)(2,1)}, f16[4,96,768]{2,1,0:T(8,128)(2,1)S(1)}, u32[]{:S(2)}, u32[]{:S(2)}) collective-permute-start(f16[4,96,768]{2,1,0:T(8,128)(2,1)} %pad_maximum_fusion.1), channel_id=1, source_target_pairs={{0,3},{1,0},{2,1},{3,2},{4,7},{5,4},{6,5},{7,6},{8,11},{9,8},{10,9... | collective-permute-start | bytes 1769480 | tf_op jit(solution)/shard_map/ppermute | solution.py:241
  158.3 19.2 %collective-permute-start.24 = (f16[2,2,96,768]{3,2,1,0:T(8,128)(2,1)}, f16[2,2,96,768]{3,2,1,0:T(8,128)(2,1)}, u32[]{:S(2)}, u32[]{:S(2)}) collective-permute-start(f16[2,2,96,768]{3,2,1,0:T(8,128)(2,1)} %get-tuple-element.136), channel_id=1, source_target_pairs={{0,1},{1,2},{2,3},{3,0},{4,5},{5,6},{6,7},{7,4},{8,9},{9,10},{10,1... | collective-permute-start | bytes 1769480 | tf_op jit(solution)/shard_map/ppermute | solution.py:241
  159.3 18.1 %collective-permute-start.25 = (f16[2,2,96,768]{3,2,1,0:T(8,128)(2,1)}, f16[2,2,96,768]{3,2,1,0:T(8,128)(2,1)}, u32[]{:S(2)}, u32[]{:S(2)}) collective-permute-start(f16[2,2,96,768]{3,2,1,0:T(8,128)(2,1)} %get-tuple-element.135), channel_id=1, source_target_pairs={{0,3},{1,0},{2,1},{3,2},{4,7},{5,4},{6,5},{7,6},{8,11},{9,8},{10,9... | collective-permute-start | bytes 1769480 | tf_op jit(solution)/shard_map/ppermute | solution.py:241
  162.2 15.2 %collective-permute-start.26 = (f16[4,96,768]{2,1,0:T(8,128)(2,1)}, f16[4,96,768]{2,1,0:T(8,128)(2,1)}, u32[]{:S(2)}, u32[]{:S(2)}) collective-permute-start(f16[4,96,768]{2,1,0:T(8,128)(2,1)} %fusion.10), channel_id=1, source_target_pairs={{0,32},{32,64},{64,96},{96,0},{1,33},{33,65},{65,97},{97,1},{2,34}... | collective-permute-start | bytes 1769480 | tf_op jit(solution)/shard_map/ppermute | solution.py:237
  181.8 13.3 %collective-permute-start.30 = (f16[2,2,96,768]{3,2,1,0:T(8,128)(2,1)S(1)}, f16[2,2,96,768]{3,2,1,0:T(8,128)(2,1)S(1)}, u32[]{:S(2)}, u32[]{:S(2)}) collective-permute-start(f16[2,2,96,768]{3,2,1,0:T(8,128)(2,1)S(1)} %get-tuple-element.98), channel_id=1, source_target_pairs={{0,1},{1,2},{2,3},{3,0},{4,5},{5,6},{6,7},{7,4},{8,9},{9,10},{10,1... | collective-permute-start | bytes 1769480 | tf_op jit(solution)/shard_map/ppermute | solution.py:241
  181.9 13.2 %collective-permute-start.31 = (f16[2,2,96,768]{3,2,1,0:T(8,128)(2,1)S(1)}, f16[2,2,96,768]{3,2,1,0:T(8,128)(2,1)S(1)}, u32[]{:S(2)}, u32[]{:S(2)}) collective-permute-start(f16[2,2,96,768]{3,2,1,0:T(8,128)(2,1)S(1)} %get-tuple-element.99), channel_id=1, source_target_pairs={{0,3},{1,0},{2,1},{3,2},{4,7},{5,4},{6,5},{7,6},{8,11},{9,8},{10,9... | collective-permute-start | bytes 1769480 | tf_op jit(solution)/shard_map/ppermute | solution.py:241
  187.0 8.0 %collective-permute-start.32 = (f16[2,96,768]{2,1,0:T(8,128)(2,1)S(1)}, f16[2,96,768]{2,1,0:T(8,128)(2,1)S(1)}, u32[]{:S(2)}, u32[]{:S(2)}) collective-permute-start(f16[2,96,768]{2,1,0:T(8,128)(2,1)S(1)} %fusion.56), channel_id=1, source_target_pairs={{0,32},{8,40},{16,48},{32,64},{40,72},{48,80},{64,96},{72,104},{80... | collective-permute-start | bytes 884744 | tf_op jit(solution)/shard_map/ppermute | solution.py:237
  195.3 9.5 %collective-permute-start.34 = (f16[2,96,768]{2,1,0:T(8,128)(2,1)S(1)}, f16[2,96,768]{2,1,0:T(8,128)(2,1)S(1)}, u32[]{:S(2)}, u32[]{:S(2)}) collective-permute-start(f16[2,96,768]{2,1,0:T(8,128)(2,1)S(1)} %get-tuple-element.124), channel_id=1, source_target_pairs={{0,1},{1,2},{2,3},{3,0},{4,5},{5,6},{6,7},{7,4},{8,9},{9,10},{10,1... | collective-permute-start | bytes 884744 | tf_op jit(solution)/shard_map/ppermute | solution.py:241
  196.0 8.9 %collective-permute-start.35 = (f16[2,96,768]{2,1,0:T(8,128)(2,1)S(1)}, f16[2,96,768]{2,1,0:T(8,128)(2,1)S(1)}, u32[]{:S(2)}, u32[]{:S(2)}) collective-permute-start(f16[2,96,768]{2,1,0:T(8,128)(2,1)S(1)} %get-tuple-element.123), channel_id=1, source_target_pairs={{0,3},{1,0},{2,1},{3,2},{4,7},{5,4},{6,5},{7,6},{8,11},{9,8},{10,9... | collective-permute-start | bytes 884744 | tf_op jit(solution)/shard_map/ppermute | solution.py:241
  207.5 12.1 %collective-permute-start.36 = (f16[2,2,96,768]{3,2,1,0:T(8,128)(2,1)S(1)}, f16[2,2,96,768]{3,2,1,0:T(8,128)(2,1)S(1)}, u32[]{:S(2)}, u32[]{:S(2)}) collective-permute-start(f16[2,2,96,768]{3,2,1,0:T(8,128)(2,1)S(1)} %bitcast.142), channel_id=1, source_target_pairs={{0,16},{1,17},{2,18},{3,19},{8,24},{9,25},{10,26},{11,27},{16,4},{... | collective-permute-start | bytes 1769480 | tf_op jit(solution)/shard_map/ppermute | solution.py:255
  212.7 9.0 %collective-permute-start.37 = (f16[2,2,96,768]{3,2,1,0:T(8,128)(2,1)S(1)}, f16[2,2,96,768]{3,2,1,0:T(8,128)(2,1)S(1)}, u32[]{:S(2)}, u32[]{:S(2)}) collective-permute-start(f16[2,2,96,768]{3,2,1,0:T(8,128)(2,1)S(1)} %bitcast.141), channel_id=1, source_target_pairs={{0,20},{1,21},{2,22},{3,23},{8,28},{9,29},{10,30},{11,31},{16,0},{... | collective-permute-start | bytes 1769480 | tf_op jit(solution)/shard_map/ppermute | solution.py:255
  222.0 9.2 %collective-permute-start.38 = (f16[2,96,768]{2,1,0:T(8,128)(2,1)S(1)}, f16[2,96,768]{2,1,0:T(8,128)(2,1)S(1)}, u32[]{:S(2)}, u32[]{:S(2)}) collective-permute-start(f16[2,96,768]{2,1,0:T(8,128)(2,1)S(1)} %get-tuple-element.120), channel_id=1, source_target_pairs={{0,16},{1,17},{2,18},{3,19},{8,24},{9,25},{10,26},{11,27},{16,4},{... | collective-permute-start | bytes 884744 | tf_op jit(solution)/shard_map/ppermute | solution.py:255
  222.1 9.9 %collective-permute-start.39 = (f16[2,96,768]{2,1,0:T(8,128)(2,1)S(1)}, f16[2,96,768]{2,1,0:T(8,128)(2,1)S(1)}, u32[]{:S(2)}, u32[]{:S(2)}) collective-permute-start(f16[2,96,768]{2,1,0:T(8,128)(2,1)S(1)} %get-tuple-element.119), channel_id=1, source_target_pairs={{0,20},{1,21},{2,22},{3,23},{8,28},{9,29},{10,30},{11,31},{16,0},{... | collective-permute-start | bytes 884744 | tf_op jit(solution)/shard_map/ppermute | solution.py:255
  233.9 12.6 %collective-permute-start.40 = (f16[96,768]{1,0:T(8,128)(2,1)S(1)}, f16[96,768]{1,0:T(8,128)(2,1)S(1)}, u32[]{:S(2)}, u32[]{:S(2)}) collective-permute-start(f16[96,768]{1,0:T(8,128)(2,1)S(1)} %multiply_convert_fusion), channel_id=1, source_target_pairs={{16,24},{24,16},{48,56},{56,48},{80,88},{88,80},{112,120},{120,112... | collective-permute-start | bytes 442376 | tf_op jit(solution)/shard_map/ppermute | solution.py:237
  270.9 8.6 %collective-permute-start.43 = (f16[768,96]{0,1:T(8,128)(2,1)S(1)}, f16[768,96]{0,1:T(8,128)(2,1)S(1)}, u32[]{:S(2)}, u32[]{:S(2)}) collective-permute-start(f16[768,96]{0,1:T(8,128)(2,1)S(1)} %squeeze.42), channel_id=1, source_target_pairs={{0,104},{8,112},{16,120},{24,0},{32,8},{40,16},{48,24},{56,32},{64... | collective-permute-start | bytes 442376 | tf_op jit(solution)/shard_map/ppermute | solution.py:237
  (27 other events, 292.4 us)

commit v9 on v8

--- a/solution.py
+++ b/solution.py
@@ -12,7 +12,7 @@
 HALF = 3072
 PART = 96
 PLANES = 4
-WIDE = 256
+WIDE = 768
 freq_point = 0.5
 
 OWN, SIB, FAR_A, FAR_A_SIB, FAR_B, FAR_B_SIB, HALO_A, HALO_B, HALO_A_SIB, HALO_B_SIB, MINOR = range(11)

time: 281 us -> 281 us (level)
  transfers between devices with their start and end apart: 44 -> 44, of which waited for: 15 -> 14; matrix products, arithmetic and copies ran while one was open for 6% -> 6% of each run, Pallas kernels for 20% -> 20%
where the time goes in v9:
time: 281 us; the launch traced here: 280 us
  starting transfers between devices  87.6 us (31%)
  waiting for transfers between devices  79.8 us (28%)
  Pallas kernels  61.4 us (22%)
  blocking collectives  18.2 us (6%)
  other arithmetic  16.1 us (6%)
  local copies, waits for them, and re-layouts  14.8 us (5%)
    ppermute x22, starting transfers between devices, aux_permute(): return lax.ppermute(value, 'aux', moves(pairs))  54.5 us
    pallas_call x4, Pallas kernels, tile_batch(): pl.pallas_call(functools.partial(tiles_kernel, count, held_most, len(sour...  50.8 us
    ppermute x22, waiting for transfers between devices, aux_permute(): return lax.ppermute(value, 'aux', moves(pairs))  46.5 us
    ppermute x17, starting transfers between devices, y_permute(): lax.ppermute(value, 'pair', [(h * 4 + y, h * 4 + (y + by) % 4) for h in r...  25.3 us
    all_to_all x1, blocking collectives, local(): lax.all_to_all(crossed, 'pair', split_axis=2, concat_axis=1, tiled=True)  18.2 us
    ppermute x5, waiting for transfers between devices, x_permute(): return lax.ppermute(value, ('aux', 'pair'), perm)  17.5 us
    ppermute x17, waiting for transfers between devices, y_permute(): lax.ppermute(value, 'pair', [(h * 4 + y, h * 4 + (y + by) % 4) for h in r...  15.8 us
    ppermute x5, starting transfers between devices, x_permute(): return lax.ppermute(value, ('aux', 'pair'), perm)  7.81 us
  transfers between devices with their start and end apart: 44, of which 14 were waited for; matrix products, arithmetic and copies ran while one was open for 6% of the time, Pallas kernels for 20%

profile of v9, /device:TPU:3, one launch (start us, length us, event | category | flops | bytes accessed | tf_op | source)
XLA Modules:
  0.0 279.9 jit_solution(14358937710662041745)
XLA Ops:
  0.0 3.7 %copy-done.1 = bf16[768,6144]{1,0:T(8,128)(2,1)S(1)} copy-done((bf16[768,6144]{1,0:T(8,128)(2,1)S(1)}, bf16[768,6144]{1,0:T(8,128)(2,1)}, u32[]{:S(2)}) %copy-start.1) | copy-done | bytes 9437208
  3.7 4.9 %shard_map.109 = (bf16[768,3072]{1,0:T(8,128)(2,1)}, bf16[768,3072]{1,0:T(8,128)(2,1)}, f32[8,128]{1,0:T(8,128)S(1)}) custom-call(s32[1]{0:T(128)} %bitcast.x_lo, bf16[768,6144]{1,0:T(8,128)(2,1)S(1)} %copy-done.1), custom_call_target="tpu_custom_call" | custom-call | bytes 73728 | tf_op jit(solution)/shard_map/pallas_call | solution.py:218
  8.6 3.5 %collective-permute-start = (bf16[768,3072]{1,0:T(8,128)(2,1)}, bf16[768,3072]{1,0:T(8,128)(2,1)}, u32[]{:S(2)}, u32[]{:S(2)}) collective-permute-start(bf16[768,3072]{1,0:T(8,128)(2,1)} %get-tuple-element.79.refs_0_), channel_id=1, source_target_pairs={{0,96},{24,56},{32,0},{56,88},{64,32},{88,120},{96,64},{120,24},{1... | collective-permute-start | bytes 14155784 | tf_op jit(solution)/shard_map/ppermute | solution.py:237
  12.2 3.5 %collective-permute-start.1 = (bf16[768,3072]{1,0:T(8,128)(2,1)}, bf16[768,3072]{1,0:T(8,128)(2,1)}, u32[]{:S(2)}, u32[]{:S(2)}) collective-permute-start(bf16[768,3072]{1,0:T(8,128)(2,1)} %get-tuple-element.78), channel_id=1, source_target_pairs={{0,16},{24,8},{32,48},{56,40},{64,80},{88,72},{96,112},{120,104},{... | collective-permute-start | bytes 14155784 | tf_op jit(solution)/shard_map/ppermute | solution.py:237
  17.4 4.8 %shard_map.110 = f32[1,3072]{1,0:T(1,128)} custom-call(s32[1,3072]{1,0:T(1,128)} %bitcast.143, s32[1,3072]{1,0:T(1,128)} %bitcast.144, f32[32,128]{1,0:T(8,128)} %bitcast.146, f32[256,128]{1,0:T(8,128)} %bitcast.145), custom_call_target="tpu_custom_call" | custom-call | flops 679477248 | bytes 200000 | tf_op jit(solution)/shard_map/pallas_call | solution.py:186
  23.0 3.1 %collective-permute-start.5 = (f32[8,128]{1,0:T(8,128)S(1)}, f32[8,128]{1,0:T(8,128)S(1)}, u32[]{:S(2)}, u32[]{:S(2)}) collective-permute-start(f32[8,128]{1,0:T(8,128)S(1)} %max.30), channel_id=1, source_target_pairs={{0,2},{1,3},{2,0},{3,1},{4,6},{5,7},{6,4},{7,5},{8,10},{9,11},{10,... | collective-permute-start | bytes 12296 | tf_op jit(solution)/shard_map/ppermute | solution.py:241
  37.4 24.3 %collective-permute-done.11 = f32[8,128]{1,0:T(8,128)S(1)} collective-permute-done((f32[8,128]{1,0:T(8,128)S(1)}, f32[8,128]{1,0:T(8,128)S(1)}, u32[]{:S(2)}, u32[]{:S(2)}) %collective-permute-start.11) | collective-permute-done | bytes 4128 | tf_op jit(solution)/shard_map/ppermute | solution.py:237
  63.7 2.5 collective-permute-done.refs_3_.refs_4_.refs_5_
  67.5 7.8 %collective-permute-start.15 = (bf16[768,3072]{1,0:T(8,128)(2,1)}, bf16[768,3072]{1,0:T(8,128)(2,1)}, u32[]{:S(2)}, u32[]{:S(2)}) collective-permute-start(bf16[768,3072]{1,0:T(8,128)(2,1)} %collective-permute-done.refs_3_.refs_4_.refs_5_), channel_id=1, source_target_pairs={{24,16},{56,48},{88,80},{120,112},{25,17},{57,49},{89,81},{121,113... | collective-permute-start | bytes 14155784 | tf_op jit(solution)/shard_map/ppermute | solution.py:237
  76.6 2.8 collective-permute-start.17
  79.4 2.8 collective-permute-start.18
  82.2 12.5 %shard_map.111 = f32[8,2,96,768]{3,2,1,0:T(8,128)S(1)} custom-call(s32[20]{0:T(128)S(1)} %get-tuple-element.67.table, f32[1,3072]{1,0:T(1,128)S(1)} %add_divide_fusion.weight, bf16[768,3072]{1,0:T(8,128)(2,1)} %get-tuple-element.79.refs_0_, bf16[768,3072]{1,0:T(8,128)(2,1)} %collective-permute-done.2.refs_1_.refs_0_, ...), custom_call_target="tpu_custom_call" | custom-call | flops 1179648 | bytes 1179648 | tf_op jit(solution)/shard_map/pallas_call | solution.py:135
  97.1 2.7 collective-permute-start.13
  99.9 13.4 %shard_map.112 = f32[8,2,96,768]{3,2,1,0:T(8,128)S(1)} custom-call(s32[20]{0:T(128)S(1)} %get-tuple-element.73.table, f32[1,3072]{1,0:T(1,128)S(1)} %add_divide_fusion.weight, bf16[768,3072]{1,0:T(8,128)(2,1)} %get-tuple-element.79.refs_0_, bf16[768,3072]{1,0:T(8,128)(2,1)} %collective-permute-done.2.refs_1_.refs_0_, ...), custom_call_target="tpu_custom_call" | custom-call | flops 1179648 | bytes 1179648 | tf_op jit(solution)/shard_map/pallas_call | solution.py:135
  113.6 2.7 collective-permute-start.20
  116.5 14.3 %collective-permute-done.16.refs_3_ = bf16[768,3072]{1,0:T(8,128)(2,1)S(1)} collective-permute-done((bf16[768,3072]{1,0:T(8,128)(2,1)}, bf16[768,3072]{1,0:T(8,128)(2,1)S(1)}, u32[]{:S(2)}, u32[]{:S(2)}) %collective-permute-start.16) | collective-permute-done | bytes 4718624 | tf_op jit(solution)/shard_map/ppermute | solution.py:237
  130.8 7.9 %collective-permute-start.23 = (bf16[768,3072]{1,0:T(8,128)(2,1)S(1)}, bf16[768,3072]{1,0:T(8,128)(2,1)}, u32[]{:S(2)}, u32[]{:S(2)}) collective-permute-start(bf16[768,3072]{1,0:T(8,128)(2,1)S(1)} %collective-permute-done.16.refs_3_), channel_id=1, source_target_pairs={{0,8},{24,16},{32,40},{56,48},{64,72},{88,80},{96,104},{120,112},{... | collective-permute-start | bytes 14155784 | tf_op jit(solution)/shard_map/ppermute | solution.py:237
  144.4 12.5 %shard_map.113 = f32[8,2,96,768]{3,2,1,0:T(8,128)S(1)} custom-call(s32[22]{0:T(128)S(1)} %pad_add_fusion.2.table, f32[1,3072]{1,0:T(1,128)S(1)} %add_divide_fusion.weight, bf16[768,3072]{1,0:T(8,128)(2,1)} %collective-permute-done.2.refs_1_.refs_0_, bf16[768,3072]{1,0:T(8,128)(2,1)} %collective-permute-done.1.refs_2_.refs_1_, bf16[768,3072]{1,0:T(8,128)(2,1)} %copy-done.3, ...), custom_call_target="tpu_custom_call" | custom-call | flops 1179648 | bytes 1179648 | tf_op jit(solution)/shard_map/pallas_call | solution.py:135
  163.6 12.5 %shard_map.114 = f32[8,2,96,768]{3,2,1,0:T(8,128)S(1)} custom-call(s32[20]{0:T(128)S(1)} %get-tuple-element.95.table, f32[1,3072]{1,0:T(1,128)S(1)} %add_divide_fusion.weight, bf16[768,3072]{1,0:T(8,128)(2,1)} %get-tuple-element.79.refs_0_, bf16[768,3072]{1,0:T(8,128)(2,1)} %collective-permute-done.2.refs_1_.refs_0_, ...), custom_call_target="tpu_custom_call" | custom-call | flops 1179648 | bytes 1179648 | tf_op jit(solution)/shard_map/pallas_call | solution.py:135
  178.6 2.7 collective-permute-start.29
  181.7 2.7 collective-permute-start.31
  188.8 6.2 %collective-permute-done.30 = f16[2,2,96,768]{3,2,1,0:T(8,128)(2,1)S(1)} collective-permute-done((f16[2,2,96,768]{3,2,1,0:T(8,128)(2,1)S(1)}, f16[2,2,96,768]{3,2,1,0:T(8,128)(2,1)S(1)}, u32[]{:S(2)}, u32[]{:S(2)}) %collective-permute-start.30) | collective-permute-done | bytes 589856 | tf_op jit(solution)/shard_map/ppermute | solution.py:241
  196.0 2.1 collective-permute-start.35
  198.3 6.4 %collective-permute-done.34 = f16[2,96,768]{2,1,0:T(8,128)(2,1)S(1)} collective-permute-done((f16[2,96,768]{2,1,0:T(8,128)(2,1)S(1)}, f16[2,96,768]{2,1,0:T(8,128)(2,1)S(1)}, u32[]{:S(2)}, u32[]{:S(2)}) %collective-permute-start.34) | collective-permute-done | bytes 294944 | tf_op jit(solution)/shard_map/ppermute | solution.py:241
  207.3 5.6 %collective-permute-start.36 = (f16[2,2,96,768]{3,2,1,0:T(8,128)(2,1)S(1)}, f16[2,2,96,768]{3,2,1,0:T(8,128)(2,1)S(1)}, u32[]{:S(2)}, u32[]{:S(2)}) collective-permute-start(f16[2,2,96,768]{3,2,1,0:T(8,128)(2,1)S(1)} %bitcast.142), channel_id=1, source_target_pairs={{0,16},{1,17},{2,18},{3,19},{8,24},{9,25},{10,26},{11,27},{16,4},{... | collective-permute-start | bytes 1769480 | tf_op jit(solution)/shard_map/ppermute | solution.py:255
  212.9 6.8 %collective-permute-done.36 = f16[2,2,96,768]{3,2,1,0:T(8,128)(2,1)S(1)} collective-permute-done((f16[2,2,96,768]{3,2,1,0:T(8,128)(2,1)S(1)}, f16[2,2,96,768]{3,2,1,0:T(8,128)(2,1)S(1)}, u32[]{:S(2)}, u32[]{:S(2)}) %collective-permute-start.36) | collective-permute-done | bytes 589856 | tf_op jit(solution)/shard_map/ppermute | solution.py:255
  219.7 2.2 collective-permute-done.37
  223.7 7.3 %collective-permute-done.38 = f16[2,96,768]{2,1,0:T(8,128)(2,1)S(1)} collective-permute-done((f16[2,96,768]{2,1,0:T(8,128)(2,1)S(1)}, f16[2,96,768]{2,1,0:T(8,128)(2,1)S(1)}, u32[]{:S(2)}, u32[]{:S(2)}) %collective-permute-start.38) | collective-permute-done | bytes 294944 | tf_op jit(solution)/shard_map/ppermute | solution.py:255
  234.1 11.1 %collective-permute-start.40 = (f16[96,768]{1,0:T(8,128)(2,1)S(1)}, f16[96,768]{1,0:T(8,128)(2,1)S(1)}, u32[]{:S(2)}, u32[]{:S(2)}) collective-permute-start(f16[96,768]{1,0:T(8,128)(2,1)S(1)} %multiply_convert_fusion), channel_id=1, source_target_pairs={{16,24},{24,16},{48,56},{56,48},{80,88},{88,80},{112,120},{120,112... | collective-permute-start | bytes 442376 | tf_op jit(solution)/shard_map/ppermute | solution.py:237
  248.1 18.2 %all_to_all.15 = f16[3,96,8,96]{1,3,0,2:T(8,128)(2,1)S(1)} all-to-all(f16[3,96,8,96]{1,3,0,2:T(8,128)(2,1)S(1)} %fusion.11), channel_id=1, replica_groups=mesh['aux'=16,'pair'=8] {'pair'}, dimensions={2} | all-to-all | bytes 884736 | tf_op jit(solution)/shard_map/all_to_all | solution.py:443
  273.1 2.8 %collective-permute-done.42 = f16[768,96]{0,1:T(8,128)(2,1)S(1)} collective-permute-done((f16[768,96]{0,1:T(8,128)(2,1)S(1)}, f16[768,96]{0,1:T(8,128)(2,1)S(1)}, u32[]{:S(2)}, u32[]{:S(2)}) %collective-permute-start.42) | collective-permute-done | bytes 147488 | tf_op jit(solution)/shard_map/ppermute | solution.py:237
  276.7 2.5 collective-permute-done.43
  (162 shorter events, 59.1 us)
Async XLA Ops:
  8.6 57.6 %collective-permute-start = (bf16[768,3072]{1,0:T(8,128)(2,1)}, bf16[768,3072]{1,0:T(8,128)(2,1)}, u32[]{:S(2)}, u32[]{:S(2)}) collective-permute-start(bf16[768,3072]{1,0:T(8,128)(2,1)} %get-tuple-element.79.refs_0_), channel_id=1, source_target_pairs={{0,96},{24,56},{32,0},{56,88},{64,32},{88,120},{96,64},{120,24},{1... | collective-permute-start | bytes 14155784 | tf_op jit(solution)/shard_map/ppermute | solution.py:237
  12.2 54.0 %collective-permute-start.1 = (bf16[768,3072]{1,0:T(8,128)(2,1)}, bf16[768,3072]{1,0:T(8,128)(2,1)}, u32[]{:S(2)}, u32[]{:S(2)}) collective-permute-start(bf16[768,3072]{1,0:T(8,128)(2,1)} %get-tuple-element.78), channel_id=1, source_target_pairs={{0,16},{24,8},{32,48},{56,40},{64,80},{88,72},{96,112},{120,104},{... | collective-permute-start | bytes 14155784 | tf_op jit(solution)/shard_map/ppermute | solution.py:237
  15.7 50.5 %collective-permute-start.2 = (bf16[768,3072]{1,0:T(8,128)(2,1)}, bf16[768,3072]{1,0:T(8,128)(2,1)}, u32[]{:S(2)}, u32[]{:S(2)}) collective-permute-start(bf16[768,3072]{1,0:T(8,128)(2,1)} %get-tuple-element.79.refs_0_), channel_id=1, source_target_pairs={{0,8},{8,0},{16,24},{24,16},{32,40},{40,32},{48,56},{56,48},{64,72... | collective-permute-start | bytes 14155784 | tf_op jit(solution)/shard_map/ppermute | solution.py:237
  35.4 26.3 %collective-permute-start.11 = (f32[8,128]{1,0:T(8,128)S(1)}, f32[8,128]{1,0:T(8,128)S(1)}, u32[]{:S(2)}, u32[]{:S(2)}) collective-permute-start(f32[8,128]{1,0:T(8,128)S(1)} %max.37), channel_id=1, source_target_pairs={{8,0},{16,24},{40,32},{48,56},{72,64},{80,88},{104,96},{112,120},{... | collective-permute-start | bytes 12296 | tf_op jit(solution)/shard_map/ppermute | solution.py:237
  66.2 28.7 %collective-permute-start.14 = (bf16[768,3072]{1,0:T(8,128)(2,1)}, bf16[768,3072]{1,0:T(8,128)(2,1)S(1)}, u32[]{:S(2)}, u32[]{:S(2)}) collective-permute-start(bf16[768,3072]{1,0:T(8,128)(2,1)} %collective-permute-done.1.refs_2_.refs_1_), channel_id=1, source_target_pairs={{8,0},{16,24},{40,32},{48,56},{72,64},{80,88},{104,96},{112,120},{... | collective-permute-start | bytes 14155784 | tf_op jit(solution)/shard_map/ppermute | solution.py:237
  67.5 28.8 %collective-permute-start.15 = (bf16[768,3072]{1,0:T(8,128)(2,1)}, bf16[768,3072]{1,0:T(8,128)(2,1)}, u32[]{:S(2)}, u32[]{:S(2)}) collective-permute-start(bf16[768,3072]{1,0:T(8,128)(2,1)} %collective-permute-done.refs_3_.refs_4_.refs_5_), channel_id=1, source_target_pairs={{24,16},{56,48},{88,80},{120,112},{25,17},{57,49},{89,81},{121,113... | collective-permute-start | bytes 14155784 | tf_op jit(solution)/shard_map/ppermute | solution.py:237
  75.3 55.5 %collective-permute-start.16 = (bf16[768,3072]{1,0:T(8,128)(2,1)}, bf16[768,3072]{1,0:T(8,128)(2,1)S(1)}, u32[]{:S(2)}, u32[]{:S(2)}) collective-permute-start(bf16[768,3072]{1,0:T(8,128)(2,1)} %get-tuple-element.78), channel_id=1, source_target_pairs={{8,24},{16,0},{40,56},{48,32},{72,88},{80,64},{104,120},{112,96},{... | collective-permute-start | bytes 14155784 | tf_op jit(solution)/shard_map/ppermute | solution.py:237
  76.6 54.2 %collective-permute-start.17 = (bf16[768,3072]{1,0:T(8,128)(2,1)}, bf16[768,3072]{1,0:T(8,128)(2,1)}, u32[]{:S(2)}, u32[]{:S(2)}) collective-permute-start(bf16[768,3072]{1,0:T(8,128)(2,1)} %get-tuple-element.79.refs_0_), channel_id=1, source_target_pairs={{8,104},{16,48},{40,8},{48,80},{72,40},{80,112},{104,72},{112,16},... | collective-permute-start | bytes 14155784 | tf_op jit(solution)/shard_map/ppermute | solution.py:237
  79.4 51.4 %collective-permute-start.18 = (bf16[768,3072]{1,0:T(8,128)(2,1)}, bf16[768,3072]{1,0:T(8,128)(2,1)}, u32[]{:S(2)}, u32[]{:S(2)}) collective-permute-start(bf16[768,3072]{1,0:T(8,128)(2,1)} %collective-permute-done.1.refs_2_.refs_1_), channel_id=1, source_target_pairs={{8,32},{16,112},{40,64},{48,16},{72,96},{80,48},{104,0},{112,80},{... | collective-permute-start | bytes 14155784 | tf_op jit(solution)/shard_map/ppermute | solution.py:237
  94.9 18.5 %collective-permute-start.12 = (f16[2,2,96,768]{3,2,1,0:T(8,128)(2,1)S(1)}, f16[2,2,96,768]{3,2,1,0:T(8,128)(2,1)S(1)}, u32[]{:S(2)}, u32[]{:S(2)}) collective-permute-start(f16[2,2,96,768]{3,2,1,0:T(8,128)(2,1)S(1)} %get-tuple-element.144), channel_id=1, source_target_pairs={{0,1},{1,2},{2,3},{3,0},{4,5},{5,6},{6,7},{7,4},{8,9},{9,10},{10,1... | collective-permute-start | bytes 1769480 | tf_op jit(solution)/shard_map/ppermute | solution.py:241
  97.1 16.3 %collective-permute-start.13 = (f16[2,2,96,768]{3,2,1,0:T(8,128)(2,1)S(1)}, f16[2,2,96,768]{3,2,1,0:T(8,128)(2,1)S(1)}, u32[]{:S(2)}, u32[]{:S(2)}) collective-permute-start(f16[2,2,96,768]{3,2,1,0:T(8,128)(2,1)S(1)} %get-tuple-element.143), channel_id=1, source_target_pairs={{0,3},{1,0},{2,1},{3,2},{4,7},{5,4},{6,5},{7,6},{8,11},{9,8},{10,9... | collective-permute-start | bytes 1769480 | tf_op jit(solution)/shard_map/ppermute | solution.py:241
  113.5 17.3 %collective-permute-start.19 = (f16[2,2,96,768]{3,2,1,0:T(8,128)(2,1)S(1)}, f16[2,2,96,768]{3,2,1,0:T(8,128)(2,1)S(1)}, u32[]{:S(2)}, u32[]{:S(2)}) collective-permute-start(f16[2,2,96,768]{3,2,1,0:T(8,128)(2,1)S(1)} %get-tuple-element.80), channel_id=1, source_target_pairs={{0,1},{1,2},{2,3},{3,0},{4,5},{5,6},{6,7},{7,4},{8,9},{9,10},{10,1... | collective-permute-start | bytes 1769480 | tf_op jit(solution)/shard_map/ppermute | solution.py:241
  113.6 17.2 %collective-permute-start.20 = (f16[2,2,96,768]{3,2,1,0:T(8,128)(2,1)S(1)}, f16[2,2,96,768]{3,2,1,0:T(8,128)(2,1)S(1)}, u32[]{:S(2)}, u32[]{:S(2)}) collective-permute-start(f16[2,2,96,768]{3,2,1,0:T(8,128)(2,1)S(1)} %get-tuple-element.81), channel_id=1, source_target_pairs={{0,3},{1,0},{2,1},{3,2},{4,7},{5,4},{6,5},{7,6},{8,11},{9,8},{10,9... | collective-permute-start | bytes 1769480 | tf_op jit(solution)/shard_map/ppermute | solution.py:241
  130.8 13.6 %collective-permute-start.23 = (bf16[768,3072]{1,0:T(8,128)(2,1)S(1)}, bf16[768,3072]{1,0:T(8,128)(2,1)}, u32[]{:S(2)}, u32[]{:S(2)}) collective-permute-start(bf16[768,3072]{1,0:T(8,128)(2,1)S(1)} %collective-permute-done.16.refs_3_), channel_id=1, source_target_pairs={{0,8},{24,16},{32,40},{56,48},{64,72},{88,80},{96,104},{120,112},{... | collective-permute-start | bytes 14155784 | tf_op jit(solution)/shard_map/ppermute | solution.py:237
  138.7 24.9 %collective-permute-start.27 = (bf16[768,3072]{1,0:T(8,128)(2,1)}, bf16[768,3072]{1,0:T(8,128)(2,1)}, u32[]{:S(2)}, u32[]{:S(2)}) collective-permute-start(bf16[768,3072]{1,0:T(8,128)(2,1)} %collective-permute-done.17.refs_6_), channel_id=1, source_target_pairs={{16,24},{48,56},{80,88},{112,120},{17,25},{49,57},{81,89},{113,121... | collective-permute-start | bytes 14155784 | tf_op jit(solution)/shard_map/ppermute | solution.py:237
  140.6 20.2 %collective-permute-start.21 = (f16[4,96,768]{2,1,0:T(8,128)(2,1)S(1)}, f16[4,96,768]{2,1,0:T(8,128)(2,1)S(1)}, u32[]{:S(2)}, u32[]{:S(2)}) collective-permute-start(f16[4,96,768]{2,1,0:T(8,128)(2,1)S(1)} %pad_maximum_fusion), channel_id=1, source_target_pairs={{0,1},{1,2},{2,3},{3,0},{4,5},{5,6},{6,7},{7,4},{8,9},{9,10},{10,1... | collective-permute-start | bytes 1769480 | tf_op jit(solution)/shard_map/ppermute | solution.py:241
  142.9 17.9 %collective-permute-start.22 = (f16[4,96,768]{2,1,0:T(8,128)(2,1)}, f16[4,96,768]{2,1,0:T(8,128)(2,1)S(1)}, u32[]{:S(2)}, u32[]{:S(2)}) collective-permute-start(f16[4,96,768]{2,1,0:T(8,128)(2,1)} %pad_maximum_fusion.1), channel_id=1, source_target_pairs={{0,3},{1,0},{2,1},{3,2},{4,7},{5,4},{6,5},{7,6},{8,11},{9,8},{10,9... | collective-permute-start | bytes 1769480 | tf_op jit(solution)/shard_map/ppermute | solution.py:241
  158.2 19.1 %collective-permute-start.24 = (f16[2,2,96,768]{3,2,1,0:T(8,128)(2,1)}, f16[2,2,96,768]{3,2,1,0:T(8,128)(2,1)}, u32[]{:S(2)}, u32[]{:S(2)}) collective-permute-start(f16[2,2,96,768]{3,2,1,0:T(8,128)(2,1)} %get-tuple-element.136), channel_id=1, source_target_pairs={{0,1},{1,2},{2,3},{3,0},{4,5},{5,6},{6,7},{7,4},{8,9},{9,10},{10,1... | collective-permute-start | bytes 1769480 | tf_op jit(solution)/shard_map/ppermute | solution.py:241
  159.2 18.0 %collective-permute-start.25 = (f16[2,2,96,768]{3,2,1,0:T(8,128)(2,1)}, f16[2,2,96,768]{3,2,1,0:T(8,128)(2,1)}, u32[]{:S(2)}, u32[]{:S(2)}) collective-permute-start(f16[2,2,96,768]{3,2,1,0:T(8,128)(2,1)} %get-tuple-element.135), channel_id=1, source_target_pairs={{0,3},{1,0},{2,1},{3,2},{4,7},{5,4},{6,5},{7,6},{8,11},{9,8},{10,9... | collective-permute-start | bytes 1769480 | tf_op jit(solution)/shard_map/ppermute | solution.py:241
  162.1 15.2 %collective-permute-start.26 = (f16[4,96,768]{2,1,0:T(8,128)(2,1)}, f16[4,96,768]{2,1,0:T(8,128)(2,1)}, u32[]{:S(2)}, u32[]{:S(2)}) collective-permute-start(f16[4,96,768]{2,1,0:T(8,128)(2,1)} %fusion.10), channel_id=1, source_target_pairs={{0,32},{32,64},{64,96},{96,0},{1,33},{33,65},{65,97},{97,1},{2,34}... | collective-permute-start | bytes 1769480 | tf_op jit(solution)/shard_map/ppermute | solution.py:237
  181.6 13.4 %collective-permute-start.30 = (f16[2,2,96,768]{3,2,1,0:T(8,128)(2,1)S(1)}, f16[2,2,96,768]{3,2,1,0:T(8,128)(2,1)S(1)}, u32[]{:S(2)}, u32[]{:S(2)}) collective-permute-start(f16[2,2,96,768]{3,2,1,0:T(8,128)(2,1)S(1)} %get-tuple-element.98), channel_id=1, source_target_pairs={{0,1},{1,2},{2,3},{3,0},{4,5},{5,6},{6,7},{7,4},{8,9},{9,10},{10,1... | collective-permute-start | bytes 1769480 | tf_op jit(solution)/shard_map/ppermute | solution.py:241
  181.7 13.4 %collective-permute-start.31 = (f16[2,2,96,768]{3,2,1,0:T(8,128)(2,1)S(1)}, f16[2,2,96,768]{3,2,1,0:T(8,128)(2,1)S(1)}, u32[]{:S(2)}, u32[]{:S(2)}) collective-permute-start(f16[2,2,96,768]{3,2,1,0:T(8,128)(2,1)S(1)} %get-tuple-element.99), channel_id=1, source_target_pairs={{0,3},{1,0},{2,1},{3,2},{4,7},{5,4},{6,5},{7,6},{8,11},{9,8},{10,9... | collective-permute-start | bytes 1769480 | tf_op jit(solution)/shard_map/ppermute | solution.py:241
  186.8 8.2 %collective-permute-start.32 = (f16[2,96,768]{2,1,0:T(8,128)(2,1)S(1)}, f16[2,96,768]{2,1,0:T(8,128)(2,1)S(1)}, u32[]{:S(2)}, u32[]{:S(2)}) collective-permute-start(f16[2,96,768]{2,1,0:T(8,128)(2,1)S(1)} %fusion.56), channel_id=1, source_target_pairs={{0,32},{8,40},{16,48},{32,64},{40,72},{48,80},{64,96},{72,104},{80... | collective-permute-start | bytes 884744 | tf_op jit(solution)/shard_map/ppermute | solution.py:237
  187.7 7.3 %collective-permute-start.33 = (f16[2,96,768]{2,1,0:T(8,128)(2,1)S(1)}, f16[2,96,768]{2,1,0:T(8,128)(2,1)S(1)}, u32[]{:S(2)}, u32[]{:S(2)}) collective-permute-start(f16[2,96,768]{2,1,0:T(8,128)(2,1)S(1)} %fusion.57), channel_id=1, source_target_pairs={{8,40},{40,72},{72,104},{104,8},{9,41},{41,73},{73,105},{105,9},{1... | collective-permute-start | bytes 884744 | tf_op jit(solution)/shard_map/ppermute | solution.py:237
  195.3 9.3 %collective-permute-start.34 = (f16[2,96,768]{2,1,0:T(8,128)(2,1)S(1)}, f16[2,96,768]{2,1,0:T(8,128)(2,1)S(1)}, u32[]{:S(2)}, u32[]{:S(2)}) collective-permute-start(f16[2,96,768]{2,1,0:T(8,128)(2,1)S(1)} %get-tuple-element.124), channel_id=1, source_target_pairs={{0,1},{1,2},{2,3},{3,0},{4,5},{5,6},{6,7},{7,4},{8,9},{9,10},{10,1... | collective-permute-start | bytes 884744 | tf_op jit(solution)/shard_map/ppermute | solution.py:241
  196.0 8.7 %collective-permute-start.35 = (f16[2,96,768]{2,1,0:T(8,128)(2,1)S(1)}, f16[2,96,768]{2,1,0:T(8,128)(2,1)S(1)}, u32[]{:S(2)}, u32[]{:S(2)}) collective-permute-start(f16[2,96,768]{2,1,0:T(8,128)(2,1)S(1)} %get-tuple-element.123), channel_id=1, source_target_pairs={{0,3},{1,0},{2,1},{3,2},{4,7},{5,4},{6,5},{7,6},{8,11},{9,8},{10,9... | collective-permute-start | bytes 884744 | tf_op jit(solution)/shard_map/ppermute | solution.py:241
  207.3 12.5 %collective-permute-start.36 = (f16[2,2,96,768]{3,2,1,0:T(8,128)(2,1)S(1)}, f16[2,2,96,768]{3,2,1,0:T(8,128)(2,1)S(1)}, u32[]{:S(2)}, u32[]{:S(2)}) collective-permute-start(f16[2,2,96,768]{3,2,1,0:T(8,128)(2,1)S(1)} %bitcast.142), channel_id=1, source_target_pairs={{0,16},{1,17},{2,18},{3,19},{8,24},{9,25},{10,26},{11,27},{16,4},{... | collective-permute-start | bytes 1769480 | tf_op jit(solution)/shard_map/ppermute | solution.py:255
  212.9 9.0 %collective-permute-start.37 = (f16[2,2,96,768]{3,2,1,0:T(8,128)(2,1)S(1)}, f16[2,2,96,768]{3,2,1,0:T(8,128)(2,1)S(1)}, u32[]{:S(2)}, u32[]{:S(2)}) collective-permute-start(f16[2,2,96,768]{3,2,1,0:T(8,128)(2,1)S(1)} %bitcast.141), channel_id=1, source_target_pairs={{0,20},{1,21},{2,22},{3,23},{8,28},{9,29},{10,30},{11,31},{16,0},{... | collective-permute-start | bytes 1769480 | tf_op jit(solution)/shard_map/ppermute | solution.py:255
  222.1 8.8 %collective-permute-start.38 = (f16[2,96,768]{2,1,0:T(8,128)(2,1)S(1)}, f16[2,96,768]{2,1,0:T(8,128)(2,1)S(1)}, u32[]{:S(2)}, u32[]{:S(2)}) collective-permute-start(f16[2,96,768]{2,1,0:T(8,128)(2,1)S(1)} %get-tuple-element.120), channel_id=1, source_target_pairs={{0,16},{1,17},{2,18},{3,19},{8,24},{9,25},{10,26},{11,27},{16,4},{... | collective-permute-start | bytes 884744 | tf_op jit(solution)/shard_map/ppermute | solution.py:255
  222.2 10.0 %collective-permute-start.39 = (f16[2,96,768]{2,1,0:T(8,128)(2,1)S(1)}, f16[2,96,768]{2,1,0:T(8,128)(2,1)S(1)}, u32[]{:S(2)}, u32[]{:S(2)}) collective-permute-start(f16[2,96,768]{2,1,0:T(8,128)(2,1)S(1)} %get-tuple-element.119), channel_id=1, source_target_pairs={{0,20},{1,21},{2,22},{3,23},{8,28},{9,29},{10,30},{11,31},{16,0},{... | collective-permute-start | bytes 884744 | tf_op jit(solution)/shard_map/ppermute | solution.py:255
  234.1 12.2 %collective-permute-start.40 = (f16[96,768]{1,0:T(8,128)(2,1)S(1)}, f16[96,768]{1,0:T(8,128)(2,1)S(1)}, u32[]{:S(2)}, u32[]{:S(2)}) collective-permute-start(f16[96,768]{1,0:T(8,128)(2,1)S(1)} %multiply_convert_fusion), channel_id=1, source_target_pairs={{16,24},{24,16},{48,56},{56,48},{80,88},{88,80},{112,120},{120,112... | collective-permute-start | bytes 442376 | tf_op jit(solution)/shard_map/ppermute | solution.py:237
  270.8 8.4 %collective-permute-start.43 = (f16[768,96]{0,1:T(8,128)(2,1)S(1)}, f16[768,96]{0,1:T(8,128)(2,1)S(1)}, u32[]{:S(2)}, u32[]{:S(2)}) collective-permute-start(f16[768,96]{0,1:T(8,128)(2,1)S(1)} %squeeze.42), channel_id=1, source_target_pairs={{0,104},{8,112},{16,120},{24,0},{32,8},{40,16},{48,24},{56,32},{64... | collective-permute-start | bytes 442376 | tf_op jit(solution)/shard_map/ppermute | solution.py:237
  (27 other events, 293.0 us)
